TPU v7x, 32 devices: a whole 2x2x4 slice. The times are simulated.
32 devices in a mesh: design: 2 (over y), node: 16 (over z, x, core).
Axes of the slice: x: 2, y: 2, z: 4, core: 2. Of those that a mesh axis runs over, the one named last changes fastest.
Arguments:
- feats: bfloat16 [131072, 256], P(('design', 'node')), parts along dimension 0, as said below
- cotangent: bfloat16 [131072, 256], P(('design', 'node')), parts along dimension 0, may hold values from -6 to 6
- valid: int32 [131072], P(('design', 'node')), parts along dimension 0, may hold values 0 or 1
- owned: int32 [32], P(('design', 'node')), parts along dimension 0, may hold values from 2048 to 4096, as said below
- w_mid: bfloat16 [256, 256], replicated, may hold values from -0.375 to 0.375
- w_slice: bfloat16 [32, 32], replicated, may hold values from -1 to 1
- temp_vec: bfloat16 [32], replicated, may hold values from -2 to 2
- w_qkv: bfloat16 [3, 32, 32], replicated, may hold values from -1 to 1
- w_out: bfloat16 [256, 256], replicated, may hold values from -0.375 to 0.375
Outputs:
- attended: bfloat16 [131072, 256], P(('design', 'node')), parts along dimension 0
- feats_grad: bfloat16 [131072, 256], P(('design', 'node')), parts along dimension 0
- grad_w_mid: float32 [512, 256], P('design'), parts along dimension 0
- grad_w_out: float32 [512, 256], P('design'), parts along dimension 0
- grad_w_slice: float32 [64, 32], P('design'), parts along dimension 0
- grad_temp: float32 [64], P('design'), parts along dimension 0
- grad_qkv: float32 [6, 32, 32], P('design'), parts along dimension 0
There are 2 independent parts, one for each index of `design`. A program takes and returns all parts, laid end to end along the dimension named above; an argument that names none is the same for every part. Nothing has to cross between parts.
Inputs may be any that keep to these rules, and one draw needn't show every extreme that they name: `feats`: node features of order one. `owned`: rows of a device at or past its count are padding; some device owns all 4096 rows.
All inputs are finite; a program needn't handle non-finite values. No bound on the sum of `valid` on one device may be relied on, other than what follows from the above.
Results may differ from a plain program's by a relative error of at most 0.04.
The roundings to bfloat16 on the way count: a program that leaves them out, or rounds other values in their place, can miss the bound.
Values sent between devices are 32-bit elements; how exact they have to be, the bound alone decides.
No kernel may reach another device: no remote copies, remote signals or barrier semaphores. Data moves between devices by JAX's collectives and lax.ppermute only.
A program may use at most 128 MiB of HBM per device.

v0:
```python
import math

import jax
import jax.numpy as jnp
from jax import lax
from jax.sharding import PartitionSpec as P

top_precision = lax.Precision.HIGHEST
eps_norm = 1e-05


def mix_slices(token_rows, matrices):
    query_rows = jnp.einsum("nir,ry->niy", token_rows, matrices[0], precision=top_precision)
    every_key = jnp.einsum("nir,ry->niy", token_rows, matrices[1], precision=top_precision)
    every_value = jnp.einsum("nir,ry->niy", token_rows, matrices[2], precision=top_precision)
    scores = jnp.einsum("hme,hke->hmk", query_rows, every_key, precision=top_precision) / math.sqrt(
        query_rows.shape[-1]
    )
    scores = scores - lax.stop_gradient(jnp.max(scores, axis=-1, keepdims=True))
    expo_vals = jnp.exp(scores)
    attn_probs = expo_vals / jnp.sum(expo_vals, axis=-1, keepdims=True)
    return jnp.einsum("hmk,hke->hme", attn_probs, every_value, precision=top_precision)


def contract_rows(left, right):
    return lax.dot_general(
        left, right, (((0,), (0,)), ((), ())), preferred_element_type=jnp.float32
    )


def contract_cols(left, right):
    return lax.dot_general(
        left, right, (((1,), (1,)), ((), ())), preferred_element_type=jnp.float32
    )


def block_of(tiles, heads):
    identity_heads = jnp.eye(heads, dtype=tiles.dtype)
    blocks = tiles[:, :, None, :] * identity_heads[:, None, :, None]
    return blocks.reshape(tiles.shape[0] * tiles.shape[1], heads * tiles.shape[2])


def diagonal_of(full, heads, slices):
    identity_heads = jnp.eye(heads, dtype=jnp.float32)
    reshaped_input = full.reshape(heads, slices, heads, -1)
    return jnp.einsum("puqz,pq->puz", reshaped_input, identity_heads)


def slice_sum(weights_b, mid, heads, slices):
    return diagonal_of(contract_rows(weights_b, mid), heads, slices)


def spread_tokens(weights_b, token_b, heads):
    return jnp.dot(weights_b, block_of(token_b, heads), preferred_element_type=jnp.float32)


def gather_tokens(node_vals, token_b, heads):
    return contract_cols(node_vals, block_of(token_b, heads))


def shards(feats, cotangent, valid, owned, w_mid, w_slice, temp_vec, w_qkv, w_out):
    f32 = jnp.float32
    brain_float_sixteen = jnp.bfloat16
    row_count = feats.shape[0]
    head_dim, slices = w_slice.shape
    heads = feats.shape[1] // head_dim
    identity_heads = jnp.eye(heads, dtype=brain_float_sixteen)
    slice_block = (identity_heads[:, None, :, None] * w_slice[None, :, None, :]).reshape(
        heads * head_dim, heads * slices
    )
    temp_block = (
        identity_heads[:, None, :, None]
        * temp_vec[None, :, None, None]
        * jnp.ones((1, 1, 1, slices), brain_float_sixteen)
    ).reshape(heads * head_dim, heads * slices)
    mid = jnp.dot(feats, w_mid, preferred_element_type=f32).astype(brain_float_sixteen)
    row_index = jnp.arange(row_count, dtype=jnp.int32)
    live = ((valid > 0) & (row_index < owned[0])).astype(f32)[:, None]
    raw_score = jnp.dot(mid, slice_block, preferred_element_type=f32)
    zsum = jnp.dot(mid, temp_block, preferred_element_type=f32)
    tau = 0.5 + jax.nn.softplus(zsum)
    logits = raw_score / tau
    grouped = logits.reshape(row_count, heads, slices)
    peak_value = jnp.max(grouped, axis=-1, keepdims=True)
    expo_vals = jnp.exp(grouped - peak_value)
    probs = (expo_vals / jnp.sum(expo_vals, axis=-1, keepdims=True)).reshape(
        row_count, heads * slices
    )
    weights = probs * live
    weights_b = weights.astype(brain_float_sixteen)
    raw_local = slice_sum(weights_b, mid, heads, slices)
    norm_local = jnp.sum(weights, axis=0).reshape(heads, slices)
    d_merged = contract_cols(cotangent, w_out).astype(brain_float_sixteen)
    mixed_local = slice_sum(weights_b, d_merged, heads, slices)
    unscaled_scores, norm = lax.psum((raw_local, norm_local), "node")
    token_rows = unscaled_scores / (norm[:, :, None] + eps_norm)
    matrices = w_qkv.astype(f32)
    mixed, mix_back = jax.vjp(mix_slices, token_rows, matrices)
    mixed_b = mixed.astype(brain_float_sixteen)
    combined_heads = spread_tokens(weights_b, mixed_b, heads).astype(brain_float_sixteen)
    attended = jnp.dot(combined_heads, w_out, preferred_element_type=f32).astype(
        brain_float_sixteen
    )
    out_local = contract_rows(combined_heads, cotangent)
    mixture_gradient = lax.psum(mixed_local, "node")
    d_tokens, grad_qkv = mix_back(mixture_gradient)
    d_raw = d_tokens / (norm[:, :, None] + eps_norm)
    norm_gradient = -jnp.sum(d_tokens * unscaled_scores, axis=-1) / (norm + eps_norm) ** 2
    d_raw_b = d_raw.astype(brain_float_sixteen)
    weight_cotangents = gather_tokens(d_merged, mixed_b, heads) + gather_tokens(mid, d_raw_b, heads)
    weight_cotangents = weight_cotangents + norm_gradient.reshape(1, heads * slices)
    weighted = (probs * weight_cotangents).reshape(row_count, heads, slices)
    group_total = jnp.sum(weighted, axis=-1, keepdims=True)
    d_logits = live * (weighted - probs.reshape(row_count, heads, slices) * group_total).reshape(
        row_count, heads * slices
    )
    u_b = (d_logits / tau).astype(brain_float_sixteen)
    c_b = (-d_logits * logits / tau * jax.nn.sigmoid(zsum)).astype(brain_float_sixteen)
    middle_gradient = spread_tokens(weights_b, d_raw_b, heads)
    middle_gradient = (
        middle_gradient + contract_cols(u_b, slice_block) + contract_cols(c_b, temp_block)
    )
    d_mid_b = middle_gradient.astype(brain_float_sixteen)
    feats_grad = contract_cols(d_mid_b, w_mid).astype(brain_float_sixteen)
    mid_local = contract_rows(feats, d_mid_b)
    eye_float = jnp.eye(heads, dtype=f32)
    slice_full = contract_rows(mid, u_b).reshape(heads, head_dim, heads, slices)
    slice_local = jnp.einsum("hdgm,hg->dm", slice_full, eye_float)
    temp_full = contract_rows(mid, c_b).reshape(heads, head_dim, heads, slices)
    temp_local = jnp.einsum("hdgm,hg->d", temp_full, eye_float)
    grad_w_mid, grad_w_out, grad_w_slice, grad_temp = lax.psum(
        (mid_local, out_local, slice_local, temp_local), "node"
    )
    return (attended, feats_grad, grad_w_mid, grad_w_out, grad_w_slice, grad_temp, grad_qkv)


def solution(mesh):
    in_specs = (
        P(("design", "node"), None),
        P(("design", "node"), None),
        P(("design", "node")),
        P(("design", "node")),
        P(),
        P(),
        P(),
        P(),
        P(),
    )
    out_specs = (
        P(("design", "node"), None),
        P(("design", "node"), None),
        P("design", None),
        P("design", None),
        P("design", None),
        P("design"),
        P("design", None, None),
    )
    return jax.shard_map(shards, mesh=mesh, in_specs=in_specs, out_specs=out_specs, check_vma=False)
```

profile of v0, /device:TPU:0, one launch (start us, length us, event | category | flops | bytes accessed | tf_op | source)
XLA Modules:
  0.0 341.4 jit_solution(4252367245214678598)
XLA Ops:
  10.7 1.7 convolution_convert_fusion.4
  13.1 3.4 bitcast_reduce_fusion.1
  16.6 8.0 %fusion.1 = f32[4096,8,32]{0,2,1:T(8,128)S(1)} fusion(f32[4096,256]{0,1:T(8,128)S(1)} %get-tuple-element.30, f32[4096,8]{0,1:T(8,128)S(1)} %get-tuple-element.29), kind=kOutput, calls=%fused_computation.1 | output fusion | flops 1081375 | bytes 8519680 | tf_op jit(solution)/shard_map/div | solution.py:86
  26.2 2.3 fusion.53
  29.6 2.5 convolution_convert_fusion.1
  32.2 2.3 fusion.54
  37.0 91.6 %all-reduce.9.cloned.1.call-done = (f32[8,32,32]{1,2,0:T(8,128)}, f32[8,32]{1,0:T(8,128)}, f32[8,32,32]{2,1,0:T(8,128)}) async-done(((f32[8,32,32]{1,2,0:T(8,128)}, f32[8,32]{1,0:T(8,128)}, f32[8,32,32]{2,1,0:T(8,128)}), (f32[8,32,32]{1,2,0:T(8,128)}, f32[8,32]{1,0:T(8,128)}, f32[8,32,32]{2,1,0:T(8,128)})) %all-reduce.9.cloned.1.call-update) | async-done | bytes 66576 | tf_op jit(solution)/shard_map/psum | solution.py:95
  134.5 1.3 multiply_reduce_fusion.2
  141.7 4.4 %fusion.59 = f32[4096,256]{0,1:T(8,128)} fusion(bf16[256,256]{1,0:T(8,128)(2,1)S(1)} %mul.159, bf16[4096,256]{0,1:T(8,128)(2,1)} %copy-done.12), kind=kOutput, calls=%fused_computation.100 | convolution fusion | flops 536870912 | bytes 6422528 | tf_op jit(solution)/shard_map/dot_general | solution.py:32
  146.0 2.1 convolution_convert_fusion.3
  148.6 2.5 fusion.55
  152.1 3.2 fusion.3
  155.3 2.5 fusion
  159.0 1.3 copy-done.8
  160.3 7.0 %multiply_convert_fusion = (bf16[4096,256]{0,1:T(8,128)(2,1)S(1)}, f32[4096,256]{0,1:T(8,128)}) fusion(f32[4096,256]{0,1:T(8,128)S(1)} %copy-done.4, f32[4096,256]{0,1:T(8,128)S(1)} %copy-done.8, f32[4096,256]{0,1:T(8,128)S(1)} %fusion.3, f32[4096,256]{0,1:T(8,128)S(1)} %copy-done.2, f32[4096,8,32]{0,2,1:T(8,128)} %fusion, f32[4096]{0:T(1024)S(1)} %fusion.23), kind=kLoop, calls=%fused_computation.26 | loop fusion | flops 18874368 | bytes 27279360 | tf_op jit(solution)/shard_map/convert_element_type | solution.py:118
  167.3 4.8 %divide_convert_fusion = bf16[4096,256]{0,1:T(8,128)(2,1)S(1)} fusion(f32[4096,256]{0,1:T(8,128)} %get-tuple-element.22, f32[4096,256]{0,1:T(8,128)S(1)} %copy-done.4), kind=kLoop, calls=%fused_computation.27 | loop fusion | flops 9437184 | bytes 10485760 | tf_op jit(solution)/shard_map/convert_element_type | solution.py:117
  175.3 1.5 convolution_bitcast_fusion
  176.7 2.1 convolution_convert_fusion
  179.6 3.7 %fusion.56 = f32[256,256]{1,0:T(8,128)} fusion(bf16[4096,256]{1,0:T(8,128)(2,1)} %convolution_convert_fusion.3, bf16[4096,256]{1,0:T(8,128)(2,1)} %param.10), kind=kOutput, calls=%fused_computation.97 | convolution fusion | flops 536870912 | bytes 4456448 | tf_op jit(solution)/shard_map/dot_general | solution.py:26
  183.8 59.9 %all-reduce.3 = (f32[32,32]{1,0:T(8,128)}, f32[32]{0:T(128)}) all-reduce(f32[32,32]{1,0:T(8,128)S(1)} %bitcast.157, f32[32]{0:T(128)S(1)} %convolution_bitcast_fusion.4), channel_id=1, replica_groups=mesh['design'=2,'node'=16] {'node'}, use_global_device_ids=true, to_apply=%region_13.14 | all-reduce | flops 1056 | bytes 8448 | tf_op jit(solution)/shard_map/psum | solution.py:131
  244.4 3.6 %convolution_convert_fusion.2 = bf16[4096,256]{1,0:T(8,128)(2,1)} fusion(bf16[4096,256]{1,0:T(8,128)(2,1)} %convolution_convert_fusion.3, bf16[256,256]{1,0:T(8,128)(2,1)S(1)} %copy-done.14), kind=kOutput, calls=%fused_computation.11 | convolution fusion | flops 537919488 | bytes 4325376 | tf_op jit(solution)/shard_map/dot_general | solution.py:101
  248.0 83.1 %all-reduce.11.cloned.1.call-done = (f32[256,256]{0,1:T(8,128)}, f32[256,256]{1,0:T(8,128)}) async-done(((f32[256,256]{0,1:T(8,128)}, f32[256,256]{1,0:T(8,128)}), (f32[256,256]{0,1:T(8,128)}, f32[256,256]{1,0:T(8,128)})) %all-reduce.11.cloned.1.call-update) | async-done | bytes 524304 | tf_op jit(solution)/shard_map/psum | solution.py:131
  331.1 1.8 copy.22
  332.9 1.7 copy.54
  (109 shorter events, 28.1 us)
Async XLA Ops:
  7.2 3.5 %copy-start = (bf16[4096,256]{1,0:T(8,128)(2,1)S(1)}, bf16[4096,256]{1,0:T(8,128)(2,1)}, u32[]{:S(2)}) copy-start(bf16[4096,256]{1,0:T(8,128)(2,1)} %param.9) | copy-start | bytes 6291460
  7.2 121.4 %all-reduce.9.cloned.1.call-start = ((), (), s32[]{:S(2)}) async-start(), calls=%async_computation | async-start | bytes 532480 | tf_op jit(solution)/shard_map/psum | solution.py:95
  7.3 27.3 %copy-start.18 = (pred[8,8,1,1]{1,0,2,3:T(8,128)(4,1)}, pred[8,8,1,1]{1,0,2,3:T(8,128)(4,1)S(1)}, u32[]{:S(2)}) copy-start(pred[8,8,1,1]{1,0,2,3:T(8,128)(4,1)S(1)} %fusion.46) | copy-start | bytes 196
  10.0 3.1 copy-start.16
  12.3 13.9 %copy-start.5 = (bf16[4096,256]{0,1:T(8,128)(2,1)}, bf16[4096,256]{0,1:T(8,128)(2,1)S(1)}, u32[]{:S(2)}) copy-start(bf16[4096,256]{0,1:T(8,128)(2,1)S(1)} %convolution_convert_fusion.4) | copy-start | bytes 6291460
  13.1 3.4 %copy-start.3 = (f32[4096,256]{0,1:T(8,128)}, f32[4096,256]{0,1:T(8,128)S(1)}, u32[]{:S(2)}) copy-start(f32[4096,256]{0,1:T(8,128)S(1)} %fusion.52) | copy-start | bytes 12582916
  16.5 8.0 %copy-start.7 = (f32[4096,256]{0,1:T(8,128)}, f32[4096,256]{0,1:T(8,128)S(1)}, u32[]{:S(2)}) copy-start(f32[4096,256]{0,1:T(8,128)S(1)} %get-tuple-element.30) | copy-start | bytes 12582916
  16.6 8.0 %copy-start.21 = (s32[4096]{0:T(1024)S(1)}, s32[4096]{0:T(1024)}, u32[]{:S(2)}) copy-start(s32[4096]{0:T(1024)} %param.11) | copy-start | bytes 49156
  25.8 2.8 copy-start.1
  26.2 3.4 %copy-start.13 = (bf16[256,256]{1,0:T(8,128)(2,1)S(1)}, bf16[256,256]{1,0:T(8,128)(2,1)}, u32[]{:S(2)}) copy-start(bf16[256,256]{1,0:T(8,128)(2,1)} %param.17) | copy-start | bytes 393220
  29.6 2.5 copy-start.10
  32.2 97.1 %copy-start.25 = (bf16[3,32,32]{2,1,0:T(8,128)(2,1)S(1)}, bf16[3,32,32]{2,1,0:T(8,128)(2,1)}, u32[]{:S(2)}) copy-start(bf16[3,32,32]{2,1,0:T(8,128)(2,1)} %param.16) | copy-start | bytes 18436
  36.2 294.9 %all-reduce.11.cloned.1.call-start = ((), (), s32[]{:S(2)}) async-start(), calls=%async_computation.1 | async-start | bytes 1048576 | tf_op jit(solution)/shard_map/psum | solution.py:131
  128.6 7.9 %copy-start.26 = (f32[8,32,32]{1,2,0:T(8,128)S(1)}, f32[8,32,32]{1,2,0:T(8,128)}, u32[]{:S(2)}) copy-start(f32[8,32,32]{1,2,0:T(8,128)} %get-tuple-element.16) | copy-start | bytes 98308
  141.6 4.4 %copy-start.11 = (bf16[4096,256]{0,1:T(8,128)(2,1)S(1)}, bf16[4096,256]{0,1:T(8,128)(2,1)}, u32[]{:S(2)}) copy-start(bf16[4096,256]{0,1:T(8,128)(2,1)} %copy-done.9) | copy-start | bytes 6291460
  148.6 2.8 copy-start.2
  148.6 3.5 %copy-start.6 = (bf16[4096,256]{0,1:T(8,128)(2,1)S(1)}, bf16[4096,256]{0,1:T(8,128)(2,1)}, u32[]{:S(2)}) copy-start(bf16[4096,256]{0,1:T(8,128)(2,1)} %copy-done.5) | copy-start | bytes 6291460
  155.3 3.7 %copy-start.4 = (f32[4096,256]{0,1:T(8,128)S(1)}, f32[4096,256]{0,1:T(8,128)}, u32[]{:S(2)}) copy-start(f32[4096,256]{0,1:T(8,128)} %copy-done.3) | copy-start | bytes 12582916
  155.3 5.0 %copy-start.8 = (f32[4096,256]{0,1:T(8,128)S(1)}, f32[4096,256]{0,1:T(8,128)}, u32[]{:S(2)}) copy-start(f32[4096,256]{0,1:T(8,128)} %copy-done.7) | copy-start | bytes 12582916
  179.3 65.1 %copy-start.14 = (bf16[256,256]{1,0:T(8,128)(2,1)S(1)}, bf16[256,256]{1,0:T(8,128)(2,1)}, u32[]{:S(2)}) copy-start(bf16[256,256]{1,0:T(8,128)(2,1)} %param.17) | copy-start | bytes 393220
  179.6 4.1 %copy-start.27 = (pred[8,8,1]{1,0,2:T(8,128)(4,1)S(1)}, pred[8,8,1]{1,0,2:T(8,128)(4,1)}, u32[]{:S(2)}) copy-start(pred[8,8,1]{1,0,2:T(8,128)(4,1)} %fusion.45) | copy-start | bytes 196
  179.6 64.2 %copy-start.22 = (f32[1,32,32]{2,1,0:T(8,128)S(1)}, f32[1,32,32]{2,1,0:T(8,128)}, u32[]{:S(2)}) copy-start(f32[1,32,32]{2,1,0:T(8,128)} %convolution_bitcast_fusion.3) | copy-start | bytes 12292
  179.6 64.2 %copy-start.23 = (f32[1,32,32]{2,1,0:T(8,128)S(1)}, f32[1,32,32]{2,1,0:T(8,128)}, u32[]{:S(2)}) copy-start(f32[1,32,32]{2,1,0:T(8,128)} %convolution_bitcast_fusion.2) | copy-start | bytes 12292
  179.6 64.2 %copy-start.24 = (f32[1,32,32]{2,1,0:T(8,128)S(1)}, f32[1,32,32]{2,1,0:T(8,128)}, u32[]{:S(2)}) copy-start(f32[1,32,32]{2,1,0:T(8,128)} %convolution_bitcast_fusion.1) | copy-start | bytes 12292
  (6 other events, 12.2 us)
Sparse Core Ops, SparseCore 0:
  36.3 92.2 all-reduce.8
  243.9 87.1 all-reduce.10
where the time goes:
time: 342 us; the launch traced here: 341 us
  waiting for transfers between devices  175 us (51%)
  blocking collectives  59.9 us (18%)
  matrix products  52.3 us (15%)
  other arithmetic  28 us (8%)
  between operations  15.3 us (4%)
  local copies, waits for them, and re-layouts  10.9 us (3%)
    psum x1, waiting for transfers between devices, shards(): unscaled_scores, norm = lax.psum((raw_local, norm_local), 'node')  91.6 us
    psum x1, waiting for transfers between devices, shards(): lax.psum((mid_local, out_local, slice_local, temp_local), 'node')  83.1 us
    psum x1, blocking collectives, shards(): lax.psum((mid_local, out_local, slice_local, temp_local), 'node')  59.9 us
    dot_general x6, matrix products, contract_cols(): lax.dot_general(left, right, (((1,), (1,)), ((), ())), preferred_element_...  13.8 us
    dot_general x6, matrix products, contract_rows(): lax.dot_general(left, right, (((0,), (0,)), ((), ())), preferred_element_...  11.3 us
    div x1, other arithmetic, shards(): expo_vals / jnp.sum(expo_vals, axis=-1, keepdims=True)  7.97 us
    unnamed x58, local copies, waits for them, and re-layouts  7.06 us
    convert_element_type x1, other arithmetic, shards(): (-d_logits * logits / tau * jax.nn.sigmoid(zsum)).astype(brain_float_sixt...  6.97 us
  transfers between devices with their start and end apart: 2, of which 2 were waited for; matrix products, arithmetic and copies ran while one was open for 1% of the time, Pallas kernels for 0%

commit v1 on v0

v1 whole, which is shorter than its diff:
```python
import functools
import math

import jax
import jax.numpy as jnp
from jax import lax
from jax.experimental import pallas as pl
from jax.experimental.pallas import tpu as pltpu
from jax.sharding import PartitionSpec as P

f32 = jnp.float32
bf16 = jnp.bfloat16
eps_norm = 1e-05
exact = lax.Precision.HIGHEST
group = 4
vmem_bytes = 56 * 1024 * 1024


def nn(a, b, precision=None):
    return lax.dot_general(
        a, b, (((1,), (0,)), ((), ())), preferred_element_type=f32, precision=precision
    )


def nt(a, b, precision=None):
    return lax.dot_general(
        a, b, (((1,), (1,)), ((), ())), preferred_element_type=f32, precision=precision
    )


def tn(a, b, precision=None):
    return lax.dot_general(
        a, b, (((0,), (0,)), ((), ())), preferred_element_type=f32, precision=precision
    )


def rows_of(shape):
    return lax.broadcasted_iota(jnp.int32, shape, 0)


def cols_of(shape):
    return lax.broadcasted_iota(jnp.int32, shape, 1)


def spread_matrix(width, small):
    shape = (width, small)
    return jnp.where(rows_of(shape) % small == cols_of(shape), 1.0, 0.0).astype(bf16)


def same_block(rows, cols, row_size, col_size):
    shape = (rows, cols)
    return rows_of(shape) // row_size == cols_of(shape) // col_size


def two_pieces(x):
    high = x.astype(bf16)
    return high, (x - high.astype(f32)).astype(bf16)


def fold_rows(x, heads, size):
    total = x[0:size]
    for h in range(1, heads):
        total = total + x[h * size : (h + 1) * size]
    return total


def group_place():
    return lax.axis_index("node") % group


def stats_kernel(
    heads,
    slices,
    owned_ref,
    valid_ref,
    feats_ref,
    cot_ref,
    w_mid_ref,
    w_slice_ref,
    temp_ref,
    w_out_ref,
    mid_ref,
    wt_ref,
    aux_ref,
    sw_ref,
    sb_ref,
    wc_ref,
    send0,
    send1,
    send2,
    send3,
    raw_acc,
    norm_acc,
    pack,
):
    step = pl.program_id(0)
    width = w_mid_ref.shape[0]
    depth = width // heads
    hm = heads * slices
    block = feats_ref.shape[0]

    @pl.when(step == 0)
    def _():
        spread_d = spread_matrix(width, depth)
        spread_m = spread_matrix(hm, slices)
        w_slice = w_slice_ref[...]
        half = nt(spread_m, w_slice).astype(bf16)
        full = nt(half, spread_d)
        sw_ref[0:hm, :] = jnp.where(same_block(hm, width, slices, depth), full, 0.0).astype(bf16)
        half = nn(spread_d, w_slice).astype(bf16)
        full = nt(half, spread_m)
        sb_ref[...] = jnp.where(same_block(width, hm, depth, slices), full, 0.0).astype(bf16)
        temp = jnp.broadcast_to(temp_ref[...].astype(f32), (16, depth)).astype(bf16)
        full = nt(temp, spread_d)
        sw_ref[hm : hm + 16, :] = jnp.where(same_block(16, width, 1, depth), full, 0.0).astype(
            bf16
        )
        raw_acc[...] = jnp.zeros_like(raw_acc)
        norm_acc[...] = jnp.zeros_like(norm_acc)
        wc_ref[...] = jnp.zeros_like(wc_ref)

    mid = nn(feats_ref[...], w_mid_ref[...]).astype(bf16)
    mid_ref[...] = mid
    scores = nt(sw_ref[...], mid)
    zsum = scores[hm : hm + heads]
    small = jnp.exp(-jnp.abs(zsum))
    inv_tau = 1.0 / (0.5 + (jnp.maximum(zsum, 0.0) + jnp.log(1.0 + small)))
    sig = jnp.where(zsum >= 0.0, 1.0, small) / (1.0 + small)
    position = step * block + cols_of((1, block))
    live = (valid_ref[...] > 0) & (position < owned_ref[0])
    live_f = live.astype(f32)
    aux_ref[0:heads, :] = inv_tau
    aux_ref[2 * heads : 3 * heads, :] = sig * inv_tau
    for h in range(heads):
        span = slice(h * slices, (h + 1) * slices)
        logits = scores[span] * inv_tau[h : h + 1]
        peak = jnp.max(logits, axis=0, keepdims=True)
        expo = jnp.exp(logits - peak)
        total = jnp.sum(expo, axis=0, keepdims=True)
        weights = expo * (live_f / total)
        wt_ref[span, :] = weights.astype(bf16)
        lanes = weights[:, 0:128]
        for c in range(1, block // 128):
            lanes = lanes + weights[:, c * 128 : (c + 1) * 128]
        norm_acc[span, :] += lanes
        aux_ref[heads + h : heads + h + 1, :] = jnp.where(live, peak + jnp.log(total), jnp.inf)
    wt = wt_ref[...]
    raw_acc[...] += nn(wt, mid)
    wc_ref[...] += nn(wt, cot_ref[...])

    @pl.when(step == pl.num_programs(0) - 1)
    def _():
        diagonal = same_block(hm, width, slices, depth)
        raw = fold_rows(jnp.where(diagonal, raw_acc[...], 0.0), heads, slices)
        high, low = two_pieces(wc_ref[...])
        w_out = w_out_ref[...]
        mixed = nt(high, w_out) + nt(low, w_out)
        mixed = fold_rows(jnp.where(diagonal, mixed, 0.0), heads, slices)
        norm = jnp.sum(norm_acc[...].T, axis=0, keepdims=True)
        halves = width // 128
        for j in range(halves):
            part = slice(j * 128, (j + 1) * 128)
            pack[j * slices : (j + 1) * slices, :] = raw[:, part]
            pack[(halves + j) * slices : (halves + j + 1) * slices, :] = mixed[:, part]
        base = 2 * halves * slices
        rest = pack.shape[0] - base
        where_row = rows_of((rest, 128))
        tail = jnp.zeros((rest, 128), f32)
        for j in range(hm // 128):
            tail = jnp.where(where_row == j, norm[:, j * 128 : (j + 1) * 128], tail)
        pack[base:, :] = tail
        place = group_place()
        size = pack.shape[0] // group
        for k, send in enumerate((send0, send1, send2, send3)):
            send[...] = pack[pl.ds(pl.multiple_of((place ^ k) * size, 8), size), :]


def tokens_kernel(
    heads,
    slices,
    own_ref,
    got1,
    got2,
    got3,
    w_qkv_ref,
    w_out_ref,
    sw_ref,
    sb_ref,
    wc_ref,
    lhs_ref,
    mw_ref,
    yt_ref,
    dn_ref,
    grad_qkv_ref,
    send0,
    send1,
    send2,
    send3,
    pack,
    gwo,
):
    width = w_out_ref.shape[0]
    depth = width // heads
    hm = heads * slices
    halves = width // 128
    place = group_place()
    size = own_ref.shape[0]
    for k, got in enumerate((own_ref, got1, got2, got3)):
        pack[pl.ds(pl.multiple_of((place ^ k) * size, 8), size), :] = got[...]

    def compact(first):
        pieces = []
        for h in range(heads):
            per = 128 // depth
            x = pack[(first + h // per) * slices : (first + h // per + 1) * slices, :]
            shift = (h % per) * depth
            pieces.append(pltpu.roll(x, 128 - shift, 1) if shift else x)
        return jnp.concatenate(pieces, axis=0)[:, 0:depth]

    raw = compact(0)
    d_mixed = compact(halves)
    base = 2 * halves * slices
    columns = pack[base : base + 8, :].T
    norm = jnp.concatenate([columns[:, j : j + 1] for j in range(hm // 128)], axis=0)
    inverse = 1.0 / (norm + eps_norm)
    tokens = raw * inverse
    w_q, w_k, w_v = (w_qkv_ref[i].astype(f32) for i in range(3))
    q, k, v = (nn(tokens, w, exact) for w in (w_q, w_k, w_v))
    blocks = same_block(hm, hm, slices, slices)
    scale = 1.0 / math.sqrt(depth)
    scores = jnp.where(blocks, nt(q, k, exact) * scale, -jnp.inf)
    expo = jnp.exp(scores - jnp.max(scores, axis=1, keepdims=True))
    probs = expo / jnp.sum(expo, axis=1, keepdims=True)
    mixed_b = nn(probs, v, exact).astype(bf16)

    spread_d = spread_matrix(width, depth)
    diagonal = same_block(hm, width, slices, depth)
    diagonal_t = same_block(width, hm, depth, slices)
    w_out = w_out_ref[...]
    mixed_block = jnp.where(diagonal, nt(mixed_b, spread_d), 0.0).astype(bf16)
    mw_ref[...] = nn(mixed_block, w_out).astype(bf16)

    d_probs = nt(d_mixed, v, exact)
    d_v = tn(probs, d_mixed, exact)
    d_scores = probs * (d_probs - jnp.sum(probs * d_probs, axis=1, keepdims=True)) * scale
    d_q = nn(d_scores, k, exact)
    d_k = tn(d_scores, q, exact)
    d_tokens = nt(d_q, w_q, exact) + nt(d_k, w_k, exact) + nt(d_v, w_v, exact)
    d_raw_b = (d_tokens * inverse).astype(bf16)
    d_norm = -jnp.sum(d_tokens * raw, axis=1, keepdims=True) * inverse * inverse
    dn_ref[...] = jnp.broadcast_to(d_norm, dn_ref.shape)
    top = sw_ref.shape[0]
    lhs_ref[0:top, :] = sw_ref[...]
    lhs_ref[top : top + hm, :] = jnp.where(diagonal, nt(d_raw_b, spread_d), 0.0).astype(bf16)
    yt_ref[:, 0:hm] = jnp.where(diagonal_t, nt(spread_d, d_raw_b), 0.0).astype(bf16)
    yt_ref[:, hm : 2 * hm] = sb_ref[...]

    for i, grad in enumerate((d_q, d_k, d_v)):
        grad_qkv_ref[i] = tn(tokens, grad, exact)
    mixed_t = jnp.where(diagonal_t, nt(spread_d, mixed_b), 0.0).astype(bf16)
    high, low = two_pieces(wc_ref[...])
    gwo[...] = nn(mixed_t, high) + nn(mixed_t, low)
    rows = width // group
    for k, send in enumerate((send0, send1, send2, send3)):
        send[...] = gwo[pl.ds(pl.multiple_of((place ^ k) * rows, 8), rows), :]


def backward_kernel(
    heads,
    slices,
    aux_ref,
    mid_ref,
    cot_ref,
    feats_ref,
    lhs_ref,
    mw_ref,
    yt_ref,
    dn_ref,
    temp_ref,
    dmt_ref,
    send0,
    send1,
    send2,
    send3,
    stack,
    grad_acc,
    small_acc,
    pack,
):
    step = pl.program_id(0)
    width = mid_ref.shape[1]
    depth = width // heads
    hm = heads * slices
    block = mid_ref.shape[0]

    @pl.when(step == 0)
    def _():
        grad_acc[...] = jnp.zeros_like(grad_acc)
        small_acc[...] = jnp.zeros_like(small_acc)

    mid = mid_ref[...]
    from_mid = nt(lhs_ref[...], mid)
    from_cot = nt(mw_ref[...], cot_ref[...])
    aux = aux_ref[...]
    sums = []
    for h in range(heads):
        span = slice(h * slices, (h + 1) * slices)
        inv_tau = aux[h : h + 1]
        logits = from_mid[span] * inv_tau
        weights = jnp.exp(logits - aux[heads + h : heads + h + 1])
        d_weights = from_cot[span] + from_mid[hm + 16 + h * slices : hm + 16 + (h + 1) * slices]
        d_weights = d_weights + dn_ref[span, 0:1]
        mean = jnp.sum(weights * d_weights, axis=0, keepdims=True)
        d_logits = weights * (d_weights - mean)
        d_tau = jnp.sum(d_logits * logits, axis=0, keepdims=True)
        sums.append(-d_tau * aux[2 * heads + h : 2 * heads + h + 1])
        stack[span, :] = weights.astype(bf16)
        stack[hm + h * slices : hm + (h + 1) * slices, :] = (d_logits * inv_tau).astype(bf16)
    c_sum = jnp.concatenate(sums, axis=0)
    c_high = c_sum.astype(bf16).astype(f32)
    stack[2 * hm : 2 * hm + 2 * heads, :] = jnp.concatenate([c_high, c_sum - c_high], axis=0).astype(bf16)
    d_mid = nn(yt_ref[...], stack[0 : 2 * hm, :])
    temp = temp_ref[...].astype(f32)
    for h in range(heads):
        span = slice(h * depth, (h + 1) * depth)
        dmt_ref[span, :] = (d_mid[span] + temp * sums[h]).astype(bf16)
    grad_acc[...] += nn(dmt_ref[...], feats_ref[...])
    small_acc[...] += nn(stack[hm : 2 * hm + 2 * heads, :], mid)

    @pl.when(step == pl.num_programs(0) - 1)
    def _():
        grad = grad_acc[...].T
        u_part = jnp.where(same_block(hm, width, slices, depth), small_acc[0:hm, :], 0.0)
        u_part = fold_rows(u_part, heads, slices)
        c_part = small_acc[hm : hm + heads, :] + small_acc[hm + heads : hm + 2 * heads, :]
        c_part = jnp.where(same_block(heads, width, 1, depth), c_part, 0.0)
        c_part = jnp.sum(c_part, axis=0, keepdims=True)

        def fold_lanes(x):
            total = x[:, 0:128]
            for j in range(1, width // 128):
                total = total + x[:, j * 128 : (j + 1) * 128]
            shift = 64
            while shift >= depth:
                total = total + pltpu.roll(total, shift, 1)
                shift //= 2
            return total

        u_part = fold_lanes(u_part)
        c_part = fold_lanes(jnp.broadcast_to(c_part, (slices, width)))
        where_lane = cols_of((slices, 128))
        extra = jnp.where(where_lane < depth, u_part, c_part)
        rows = width // group
        more = slices // group
        for j in range(group):
            pack[j, 0:rows, :] = grad[j * rows : (j + 1) * rows]
            pack[j, rows : rows + more, 0:128] = extra[j * more : (j + 1) * more]
            pack[j, rows : rows + more, 128:] = jnp.zeros((more, width - 128), f32)
        place = group_place()
        for k, send in enumerate((send0, send1, send2, send3)):
            send[...] = pack[place ^ k]


def rows_kernel(wt_ref, dmt_ref, mw_ref, w_mid_ref, attended_ref, feats_grad_ref):
    attended_ref[...] = tn(wt_ref[...], mw_ref[...]).astype(bf16)
    feats_grad_ref[...] = lax.dot_general(
        dmt_ref[...], w_mid_ref[...], (((0,), (1,)), ((), ())), preferred_element_type=f32
    ).astype(bf16)


def finish_kernel(
    depth, o0, o1, o2, o3, m0, m1, m2, m3, grad_mid_ref, grad_out_ref, slice_ref, temp_ref, extra
):
    place = group_place()
    rows = o0.shape[0]
    more = m0.shape[0] - rows
    for k, (out_part, mid_part) in enumerate(((o0, m0), (o1, m1), (o2, m2), (o3, m3))):
        at = pl.ds(pl.multiple_of((place ^ k) * rows, 8), rows)
        grad_out_ref[at, :] = out_part[...]
        grad_mid_ref[at, :] = mid_part[0:rows, :]
        extra[pl.ds(pl.multiple_of((place ^ k) * more, 8), more), :] = mid_part[rows:, 0:128]
    slices = slice_ref.shape[1]
    turned = extra[...].T
    slice_ref[...] = turned[0:depth, 0:slices]
    temp_ref[...] = extra[0:1, depth : 2 * depth]


def full(shape):
    zeros = (0,) * len(shape)
    return pl.BlockSpec(shape, lambda *_: zeros)


def params(grid=True):
    if grid:
        return pltpu.CompilerParams(
            dimension_semantics=("arbitrary",), vmem_limit_bytes=vmem_bytes
        )
    return pltpu.CompilerParams(vmem_limit_bytes=vmem_bytes)


def cost(flops, moved, transcendentals=0):
    return pl.CostEstimate(flops=flops, bytes_accessed=moved, transcendentals=transcendentals)


def exchange(x, k, count):
    return lax.ppermute(x, "node", [(i, i ^ k) for i in range(count)])


def sum_over_groups(parts, count):
    got = [parts[0]] + [exchange(parts[k], k, count) for k in range(1, group)]
    total = (got[0] + got[1]) + (got[2] + got[3])
    stride = group
    while stride < count:
        if count // stride % 4 == 0:
            r1, r2, r3 = (exchange(total, stride * j, count) for j in (1, 2, 3))
            total = (total + r1) + (r2 + r3)
            stride *= 4
        else:
            total = total + exchange(total, stride, count)
            stride *= 2
    return total


def gather_group(total, count):
    return [total] + [exchange(total, k, count) for k in range(1, group)]


def shards(count, feats, cotangent, valid, owned, w_mid, w_slice, temp_vec, w_qkv, w_out):
    rows, width = feats.shape
    depth, slices = w_slice.shape
    heads = width // depth
    hm = heads * slices
    block = min(1024, rows)
    grid = (rows // block,)
    unit = 2 * rows * width * width
    smem = pl.BlockSpec(memory_space=pltpu.SMEM)
    by_rows = pl.BlockSpec((block, width), lambda i: (i, 0))
    by_cols = pl.BlockSpec((hm, block), lambda i: (0, i))
    aux_spec = pl.BlockSpec((3 * heads, block), lambda i: (0, i))
    pack_rows = 2 * (width // 128) * slices + 32
    piece = (pack_rows // group, 128)

    def like(shape, dtype):
        return jax.ShapeDtypeStruct(shape, dtype)

    mid, wt, aux, sw, sb, wc, *sends = pl.pallas_call(
        functools.partial(stats_kernel, heads, slices),
        grid=grid,
        in_specs=[
            smem,
            pl.BlockSpec((1, block), lambda i: (0, i)),
            by_rows,
            by_rows,
            full((width, width)),
            full((depth, slices)),
            full((1, depth)),
            full((width, width)),
        ],
        out_specs=[
            by_rows,
            by_cols,
            aux_spec,
            full((hm + 16, width)),
            full((width, hm)),
            full((hm, width)),
        ]
        + [full(piece)] * group,
        out_shape=[
            like((rows, width), bf16),
            like((hm, rows), bf16),
            like((3 * heads, rows), f32),
            like((hm + 16, width), bf16),
            like((width, hm), bf16),
            like((hm, width), f32),
        ]
        + [like(piece, f32)] * group,
        scratch_shapes=[
            pltpu.VMEM((hm, width), f32),
            pltpu.VMEM((hm, 128), f32),
            pltpu.VMEM((pack_rows, 128), f32),
        ],
        compiler_params=params(),
        cost_estimate=cost(4 * unit, rows * width * 8, rows * hm),
    )(owned, valid.reshape(1, rows), feats, cotangent, w_mid, w_slice, temp_vec.reshape(1, depth), w_out)

    pieces = gather_group(sum_over_groups(sends, count), count)

    quarter = (width // group, width)
    lhs, mw, yt, dn, grad_qkv, *sends = pl.pallas_call(
        functools.partial(tokens_kernel, heads, slices),
        out_shape=[
            like((2 * hm + 16, width), bf16),
            like((hm, width), bf16),
            like((width, 2 * hm), bf16),
            like((hm, 128), f32),
            like((3, depth, depth), f32),
        ]
        + [like(quarter, f32)] * group,
        scratch_shapes=[pltpu.VMEM((pack_rows, 128), f32), pltpu.VMEM((width, width), f32)],
        compiler_params=params(False),
        cost_estimate=cost(30 * width**3, 4 * width * width * 4, hm * hm),
    )(*pieces, w_qkv, w_out, sw, sb, wc)

    out_parts = gather_group(sum_over_groups(sends, count), count)

    more = slices // group
    larger = (width // group + more, width)
    dmt, *sends = pl.pallas_call(
        functools.partial(backward_kernel, heads, slices),
        grid=grid,
        in_specs=[
            aux_spec,
            by_rows,
            by_rows,
            by_rows,
            full((2 * hm + 16, width)),
            full((hm, width)),
            full((width, 2 * hm)),
            full((hm, 128)),
            full((depth, 1)),
        ],
        out_specs=[by_cols] + [full(larger)] * group,
        out_shape=[like((width, rows), bf16)] + [like(larger, f32)] * group,
        scratch_shapes=[
            pltpu.VMEM((2 * hm + 16, block), bf16),
            pltpu.VMEM((width, width), f32),
            pltpu.VMEM((hm + 16, width), f32),
            pltpu.VMEM((group,) + larger, f32),
        ],
        compiler_params=params(),
        cost_estimate=cost(8 * unit, rows * width * 8, rows * hm),
    )(aux, mid, cotangent, feats, lhs, mw, yt, dn, temp_vec.reshape(depth, 1))

    mid_parts = gather_group(sum_over_groups(sends, count), count)

    attended, feats_grad = pl.pallas_call(
        rows_kernel,
        grid=grid,
        in_specs=[by_cols, by_cols, full((hm, width)), full((width, width))],
        out_specs=[by_rows, by_rows],
        out_shape=[like((rows, width), bf16)] * 2,
        compiler_params=params(),
        cost_estimate=cost(2 * unit, rows * width * 8),
    )(wt, dmt, mw, w_mid)

    grad_w_mid, grad_w_out, grad_w_slice, grad_temp = pl.pallas_call(
        functools.partial(finish_kernel, depth),
        out_shape=[
            like((width, width), f32),
            like((width, width), f32),
            like((depth, slices), f32),
            like((1, depth), f32),
        ],
        scratch_shapes=[pltpu.VMEM((slices, 128), f32)],
        compiler_params=params(False),
        cost_estimate=cost(0, 4 * width * width * 4),
    )(*out_parts, *mid_parts)
    return (
        attended,
        feats_grad,
        grad_w_mid,
        grad_w_out,
        grad_w_slice,
        grad_temp.reshape(depth),
        grad_qkv,
    )


def solution(mesh):
    in_specs = (
        P(("design", "node"), None),
        P(("design", "node"), None),
        P(("design", "node")),
        P(("design", "node")),
        P(),
        P(),
        P(),
        P(),
        P(),
    )
    out_specs = (
        P(("design", "node"), None),
        P(("design", "node"), None),
        P("design", None),
        P("design", None),
        P("design", None),
        P("design"),
        P("design", None, None),
    )
    return jax.shard_map(
        functools.partial(shards, mesh.shape["node"]),
        mesh=mesh,
        in_specs=in_specs,
        out_specs=out_specs,
        check_vma=False,
    )
```

time: 342 us -> 78 us (0.23)
  waiting for transfers between devices: 175 us -> 13.1 us
  blocking collectives: 59.9 us -> 0 us
  matrix products: 52.3 us -> 0 us
  Pallas kernels: 0 us -> 32.2 us
  other arithmetic: 28 us -> 1.71 us
  starting transfers between devices: 0.26 us -> 26.3 us
  between operations: 15.3 us -> 1.49 us
  local copies, waits for them, and re-layouts: 10.9 us -> 2.6 us
    psum x2 -> x0, waiting for transfers between devices: 175 us -> none  [the longest x1 91.6 us: shards(): unscaled_scores, norm = lax.psum((raw_local, norm_local), 'node')]
    psum x1 -> x0, blocking collectives: 59.9 us -> none  [shards(): lax.psum((mid_local, out_local, slice_local, temp_local), 'node')]
    dot_general x37 -> x0, matrix products: 52.3 us -> none  [the longest x6 13.8 us: contract_cols(): lax.dot_general(left, right, (((1,), (1,)), ((), ())), preferred_element_...]
    pallas_call x0 -> x5, Pallas kernels: none -> 32.2 us  [the longest x1 9.03 us: shards(): pl.pallas_call(functools.partial(backward_kernel, heads, slices), grid=gr...]
    ppermute x0 -> x27, starting transfers between devices: none -> 26.3 us  [exchange(): return lax.ppermute(x, 'node', [(i, i ^ k) for i in range(count)])]
    ppermute x0 -> x27, waiting for transfers between devices: none -> 13.1 us  [exchange(): return lax.ppermute(x, 'node', [(i, i ^ k) for i in range(count)])]
    convert_element_type x5 -> x0, other arithmetic: 12.2 us -> none  [the longest x1 6.97 us: shards(): (-d_logits * logits / tau * jax.nn.sigmoid(zsum)).astype(brain_float_sixt...]
    div x3 -> x0, other arithmetic: 7.98 us -> none  [the longest x1 7.97 us: shards(): expo_vals / jnp.sum(expo_vals, axis=-1, keepdims=True)]
  transfers between devices with their start and end apart: 2 -> 27, of which waited for: 2 -> 7; matrix products, arithmetic and copies ran while one was open for 1% -> 2% of each run, Pallas kernels for 0% -> 19%
where the time goes in v1:
time: 78 us; the launch traced here: 77.4 us
  Pallas kernels  32.2 us (41%)
  starting transfers between devices  26.3 us (34%)
  waiting for transfers between devices  13.1 us (17%)
  local copies, waits for them, and re-layouts  2.6 us (3%)
  other arithmetic  1.71 us (2%)
  between operations  1.49 us (2%)
    ppermute x27, starting transfers between devices, exchange(): return lax.ppermute(x, 'node', [(i, i ^ k) for i in range(count)])  26.3 us
    ppermute x27, waiting for transfers between devices, exchange(): return lax.ppermute(x, 'node', [(i, i ^ k) for i in range(count)])  13.1 us
    pallas_call x1, Pallas kernels, shards(): pl.pallas_call(functools.partial(backward_kernel, heads, slices), grid=gr...  9.03 us
    pallas_call x1, Pallas kernels, shards(): pl.pallas_call(functools.partial(stats_kernel, heads, slices), grid=grid,...  8.96 us
    pallas_call x1, Pallas kernels, shards(): pl.pallas_call(functools.partial(tokens_kernel, heads, slices), out_shape...  6.55 us
    pallas_call x1, Pallas kernels, shards(): pl.pallas_call(rows_kernel, grid=grid, in_specs=[by_cols, by_cols, full((...  5.66 us
    pallas_call x1, Pallas kernels, shards(): pl.pallas_call(functools.partial(finish_kernel, depth), out_shape=[like((...  1.98 us
    unnamed x28, local copies, waits for them, and re-layouts  1.9 us
  transfers between devices with their start and end apart: 27, of which 7 were waited for; matrix products, arithmetic and copies ran while one was open for 2% of the time, Pallas kernels for 19%

profile of v1, /device:TPU:0, one launch (start us, length us, event | category | flops | bytes accessed | tf_op | source)
XLA Modules:
  0.0 77.4 jit_solution(4652728464571274766)
XLA Ops:
  1.3 9.0 %shard_map.144 = (bf16[4096,256]{1,0:T(8,128)(2,1)}, bf16[256,4096]{1,0:T(8,128)(2,1)}, f32[24,4096]{1,0:T(8,128)}, bf16[272,256]{1,0:T(8,128)(2,1)}, bf16[256,2...) custom-call(s32[1]{0:T(128)S(6)} %copy.17.owned_ref, ...), custom_call_target="tpu_custom_call" | custom-call | flops 2147483648 | bytes 8388608 | tf_op jit(solution)/shard_map/pallas_call | solution.py:446
  10.8 2.6 %collective-permute-start.1 = (f32[40,128]{1,0:T(8,128)}, f32[40,128]{1,0:T(8,128)S(1)}, u32[]{:S(2)}, u32[]{:S(2)}) collective-permute-start(f32[40,128]{1,0:T(8,128)} %get-tuple-element.42), channel_id=1, source_target_pairs={{0,2},{1,3},{2,0},{3,1},{4,6},{5,7},{6,4},{7,5},{8,10},{9,11},{10,... | collective-permute-start | bytes 61448 | tf_op jit(solution)/shard_map/ppermute | solution.py:406
  13.4 1.9 %collective-permute-done.1 = f32[40,128]{1,0:T(8,128)S(1)} collective-permute-done((f32[40,128]{1,0:T(8,128)}, f32[40,128]{1,0:T(8,128)S(1)}, u32[]{:S(2)}, u32[]{:S(2)}) %collective-permute-start.1) | collective-permute-done | bytes 20512 | tf_op jit(solution)/shard_map/ppermute | solution.py:406
  15.3 1.4 %collective-permute-done.2 = f32[40,128]{1,0:T(8,128)S(1)} collective-permute-done((f32[40,128]{1,0:T(8,128)}, f32[40,128]{1,0:T(8,128)S(1)}, u32[]{:S(2)}, u32[]{:S(2)}) %collective-permute-start.2) | collective-permute-done | bytes 20512 | tf_op jit(solution)/shard_map/ppermute | solution.py:406
  17.5 1.6 %collective-permute-start.3 = (f32[40,128]{1,0:T(8,128)S(1)}, f32[40,128]{1,0:T(8,128)S(1)}, u32[]{:S(2)}, u32[]{:S(2)}) collective-permute-start(f32[40,128]{1,0:T(8,128)S(1)} %add_add_fusion.5), channel_id=1, source_target_pairs={{0,4},{1,5},{2,6},{3,7},{4,0},{5,1},{6,2},{7,3},{8,12},{9,13},{10,... | collective-permute-start | bytes 61448 | tf_op jit(solution)/shard_map/ppermute | solution.py:406
  19.1 2.6 %collective-permute-start.4 = (f32[40,128]{1,0:T(8,128)S(1)}, f32[40,128]{1,0:T(8,128)S(1)}, u32[]{:S(2)}, u32[]{:S(2)}) collective-permute-start(f32[40,128]{1,0:T(8,128)S(1)} %add_add_fusion.5), channel_id=1, source_target_pairs={{0,8},{1,9},{2,10},{3,11},{4,12},{5,13},{6,14},{7,15},{8,0},{9,1},... | collective-permute-start | bytes 61448 | tf_op jit(solution)/shard_map/ppermute | solution.py:406
  21.9 2.1 %collective-permute-done.4 = f32[40,128]{1,0:T(8,128)S(1)} collective-permute-done((f32[40,128]{1,0:T(8,128)S(1)}, f32[40,128]{1,0:T(8,128)S(1)}, u32[]{:S(2)}, u32[]{:S(2)}) %collective-permute-start.4) | collective-permute-done | bytes 20512 | tf_op jit(solution)/shard_map/ppermute | solution.py:406
  24.0 3.3 %collective-permute-done.5 = f32[40,128]{1,0:T(8,128)S(1)} collective-permute-done((f32[40,128]{1,0:T(8,128)S(1)}, f32[40,128]{1,0:T(8,128)S(1)}, u32[]{:S(2)}, u32[]{:S(2)}) %collective-permute-start.5) | collective-permute-done | bytes 20512 | tf_op jit(solution)/shard_map/ppermute | solution.py:406
  27.3 0.8 %collective-permute-start.7 = (f32[40,128]{1,0:T(8,128)S(1)}, f32[40,128]{1,0:T(8,128)S(1)}, u32[]{:S(2)}, u32[]{:S(2)}) collective-permute-start(f32[40,128]{1,0:T(8,128)S(1)} %add_add_fusion.4.own_ref), channel_id=1, source_target_pairs={{0,2},{1,3},{2,0},{3,1},{4,6},{5,7},{6,4},{7,5},{8,10},{9,11},{10,... | collective-permute-start | bytes 61448 | tf_op jit(solution)/shard_map/ppermute | solution.py:406
  28.2 1.0 %collective-permute-start.8 = (f32[40,128]{1,0:T(8,128)S(1)}, f32[40,128]{1,0:T(8,128)S(1)}, u32[]{:S(2)}, u32[]{:S(2)}) collective-permute-start(f32[40,128]{1,0:T(8,128)S(1)} %add_add_fusion.4.own_ref), channel_id=1, source_target_pairs={{0,3},{1,2},{2,1},{3,0},{4,7},{5,6},{6,5},{7,4},{8,11},{9,10},{10,... | collective-permute-start | bytes 61448 | tf_op jit(solution)/shard_map/ppermute | solution.py:406
  29.9 1.3 %collective-permute-done.7.got2 = f32[40,128]{1,0:T(8,128)S(1)} collective-permute-done((f32[40,128]{1,0:T(8,128)S(1)}, f32[40,128]{1,0:T(8,128)S(1)}, u32[]{:S(2)}, u32[]{:S(2)}) %collective-permute-start.7) | collective-permute-done | bytes 20512 | tf_op jit(solution)/shard_map/ppermute | solution.py:406
  32.0 6.6 %shard_map.145 = (bf16[528,256]{1,0:T(8,128)(2,1)}, bf16[256,256]{1,0:T(8,128)(2,1)}, bf16[256,512]{1,0:T(8,128)(2,1)}, f32[256,128]{1,0:T(8,128)}, f32[3,32,32]...) custom-call(f32[40,128]{1,0:T(8,128)} %copy-done.9, ...), custom_call_target="tpu_custom_call" | custom-call | flops 503316480 | bytes 1048576 | tf_op jit(solution)/shard_map/pallas_call | solution.py:489
  38.6 1.2 %collective-permute-start.10 = (f32[64,256]{1,0:T(8,128)}, f32[64,256]{1,0:T(8,128)S(1)}, u32[]{:S(2)}, u32[]{:S(2)}) collective-permute-start(f32[64,256]{1,0:T(8,128)} %get-tuple-element.56), channel_id=1, source_target_pairs={{0,2},{1,3},{2,0},{3,1},{4,6},{5,7},{6,4},{7,5},{8,10},{9,11},{10,... | collective-permute-start | bytes 196616 | tf_op jit(solution)/shard_map/ppermute | solution.py:406
  40.7 9.0 %shard_map.146 = (bf16[256,4096]{1,0:T(8,128)(2,1)}, f32[72,256]{1,0:T(8,128)}, f32[72,256]{1,0:T(8,128)}, f32[72,256]{1,0:T(8,128)}, f32[72,256]{1,0:T(8,128)}) custom-call(f32[24,4096]{1,0:T(8,128)} %get-tuple-element.38.aux_ref, bf16[4096,256]{1,0:T(8,128)(2,1)} %get-tuple-element.39.mid_ref, bf16[4096,256]{1,0:T(8,128)(2,1)} %cot_ref.3, ...), custom_call_target="tpu_custom_call" | custom-call | flops 4294967296 | bytes 8388608 | tf_op jit(solution)/shard_map/pallas_call | solution.py:508
  49.8 1.3 %collective-permute-start.19 = (f32[72,256]{1,0:T(8,128)}, f32[72,256]{1,0:T(8,128)S(1)}, u32[]{:S(2)}, u32[]{:S(2)}) collective-permute-start(f32[72,256]{1,0:T(8,128)} %get-tuple-element.60), channel_id=1, source_target_pairs={{0,2},{1,3},{2,0},{3,1},{4,6},{5,7},{6,4},{7,5},{8,10},{9,11},{10,... | collective-permute-start | bytes 221192 | tf_op jit(solution)/shard_map/ppermute | solution.py:406
  52.6 3.6 %collective-permute-start.14 = (f32[64,256]{1,0:T(8,128)S(1)}, f32[64,256]{1,0:T(8,128)S(1)}, u32[]{:S(2)}, u32[]{:S(2)}) collective-permute-start(f32[64,256]{1,0:T(8,128)S(1)} %add_add_fusion.3), channel_id=1, source_target_pairs={{0,12},{1,13},{2,14},{3,15},{4,8},{5,9},{6,10},{7,11},{8,4},{9,5},... | collective-permute-start | bytes 196616 | tf_op jit(solution)/shard_map/ppermute | solution.py:406
  56.2 0.9 %add_add_fusion.1 = f32[72,256]{1,0:T(8,128)S(1)} fusion(f32[72,256]{1,0:T(8,128)S(1)} %collective-permute-done.19, f32[72,256]{1,0:T(8,128)S(1)} %collective-permute-done.20, f32[72,256]{1,0:T(8,128)} %get-tuple-element.58, f32[72,256]{1,0:T(8,128)S(1)} %collective-permute-done.18), kind=kLoop, calls=%fused_computation.1 | loop fusion | flops 55296 | bytes 368640 | tf_op jit(solution)/shard_map/add | solution.py:411
  57.2 0.8 collective-permute-start.22
  57.9 3.6 %collective-permute-start.23 = (f32[72,256]{1,0:T(8,128)S(1)}, f32[72,256]{1,0:T(8,128)S(1)}, u32[]{:S(2)}, u32[]{:S(2)}) collective-permute-start(f32[72,256]{1,0:T(8,128)S(1)} %add_add_fusion.1), channel_id=1, source_target_pairs={{0,12},{1,13},{2,14},{3,15},{4,8},{5,9},{6,10},{7,11},{8,4},{9,5},... | collective-permute-start | bytes 221192 | tf_op jit(solution)/shard_map/ppermute | solution.py:406
  61.7 1.3 %collective-permute-start.16 = (f32[64,256]{1,0:T(8,128)S(1)}, f32[64,256]{1,0:T(8,128)S(1)}, u32[]{:S(2)}, u32[]{:S(2)}) collective-permute-start(f32[64,256]{1,0:T(8,128)S(1)} %add_add_fusion.2.o0), channel_id=1, source_target_pairs={{0,2},{1,3},{2,0},{3,1},{4,6},{5,7},{6,4},{7,5},{8,10},{9,11},{10,... | collective-permute-start | bytes 196616 | tf_op jit(solution)/shard_map/ppermute | solution.py:406
  63.5 2.9 %collective-permute-done.22 = f32[72,256]{1,0:T(8,128)S(1)} collective-permute-done((f32[72,256]{1,0:T(8,128)S(1)}, f32[72,256]{1,0:T(8,128)S(1)}, u32[]{:S(2)}, u32[]{:S(2)}) %collective-permute-start.22) | collective-permute-done | bytes 73760 | tf_op jit(solution)/shard_map/ppermute | solution.py:406
  66.5 1.3 %collective-permute-start.25 = (f32[72,256]{1,0:T(8,128)S(1)}, f32[72,256]{1,0:T(8,128)S(1)}, u32[]{:S(2)}, u32[]{:S(2)}) collective-permute-start(f32[72,256]{1,0:T(8,128)S(1)} %add_add_fusion.m0), channel_id=1, source_target_pairs={{0,2},{1,3},{2,0},{3,1},{4,6},{5,7},{6,4},{7,5},{8,10},{9,11},{10,... | collective-permute-start | bytes 221192 | tf_op jit(solution)/shard_map/ppermute | solution.py:406
  68.4 5.7 %shard_map.147 = (bf16[4096,256]{1,0:T(8,128)(2,1)}, bf16[4096,256]{1,0:T(8,128)(2,1)}) custom-call(bf16[256,4096]{1,0:T(8,128)(2,1)} %get-tuple-element.37.wt_ref, bf16[256,4096]{1,0:T(8,128)(2,1)} %get-tuple-element.51.dmt_ref, bf16[256,256]{1,0:T(8,128)(2,1)} %get-tuple-element.48.mw_ref, bf16[256,256]{1,0:T(8,128)(2,1)} %w_mid_ref.3), custom_call_target="tpu_custom_call" | custom-call | flops 1073741824 | bytes 8388608 | tf_op jit(solution)/shard_map/pallas_call | solution.py:536
  75.4 2.0 %shard_map.148 = (f32[256,256]{1,0:T(8,128)}, f32[256,256]{1,0:T(8,128)}, f32[32,32]{1,0:T(8,128)}, f32[1,32]{1,0:T(1,128)}) custom-call(f32[64,256]{1,0:T(8,128)} %copy-done.1, f32[64,256]{1,0:T(8,128)} %copy-done.5, f32[64,256]{1,0:T(8,128)} %copy-done.6, f32[64,256]{1,0:T(8,128)} %copy-done.8, f32[72,256]{1,0:T(8,128)} %copy-done, f32[72,256]{1,0:T(8,128)} %copy-done.2, ...), custom_call_target="tpu_custom_call" | custom-call | bytes 1048576 | tf_op jit(solution)/shard_map/pallas_call | solution.py:546
  (70 shorter events, 8.3 us)
Async XLA Ops:
  10.8 4.5 %collective-permute-start.1 = (f32[40,128]{1,0:T(8,128)}, f32[40,128]{1,0:T(8,128)S(1)}, u32[]{:S(2)}, u32[]{:S(2)}) collective-permute-start(f32[40,128]{1,0:T(8,128)} %get-tuple-element.42), channel_id=1, source_target_pairs={{0,2},{1,3},{2,0},{3,1},{4,6},{5,7},{6,4},{7,5},{8,10},{9,11},{10,... | collective-permute-start | bytes 61448 | tf_op jit(solution)/shard_map/ppermute | solution.py:406
  13.3 3.4 %collective-permute-start.2 = (f32[40,128]{1,0:T(8,128)}, f32[40,128]{1,0:T(8,128)S(1)}, u32[]{:S(2)}, u32[]{:S(2)}) collective-permute-start(f32[40,128]{1,0:T(8,128)} %get-tuple-element.43), channel_id=1, source_target_pairs={{0,3},{1,2},{2,1},{3,0},{4,7},{5,6},{6,5},{7,4},{8,11},{9,10},{10,... | collective-permute-start | bytes 61448 | tf_op jit(solution)/shard_map/ppermute | solution.py:406
  17.5 4.4 %collective-permute-start.3 = (f32[40,128]{1,0:T(8,128)S(1)}, f32[40,128]{1,0:T(8,128)S(1)}, u32[]{:S(2)}, u32[]{:S(2)}) collective-permute-start(f32[40,128]{1,0:T(8,128)S(1)} %add_add_fusion.5), channel_id=1, source_target_pairs={{0,4},{1,5},{2,6},{3,7},{4,0},{5,1},{6,2},{7,3},{8,12},{9,13},{10,... | collective-permute-start | bytes 61448 | tf_op jit(solution)/shard_map/ppermute | solution.py:406
  19.1 4.9 %collective-permute-start.4 = (f32[40,128]{1,0:T(8,128)S(1)}, f32[40,128]{1,0:T(8,128)S(1)}, u32[]{:S(2)}, u32[]{:S(2)}) collective-permute-start(f32[40,128]{1,0:T(8,128)S(1)} %add_add_fusion.5), channel_id=1, source_target_pairs={{0,8},{1,9},{2,10},{3,11},{4,12},{5,13},{6,14},{7,15},{8,0},{9,1},... | collective-permute-start | bytes 61448 | tf_op jit(solution)/shard_map/ppermute | solution.py:406
  21.7 5.6 %collective-permute-start.5 = (f32[40,128]{1,0:T(8,128)S(1)}, f32[40,128]{1,0:T(8,128)S(1)}, u32[]{:S(2)}, u32[]{:S(2)}) collective-permute-start(f32[40,128]{1,0:T(8,128)S(1)} %add_add_fusion.5), channel_id=1, source_target_pairs={{0,12},{1,13},{2,14},{3,15},{4,8},{5,9},{6,10},{7,11},{8,4},{9,5},... | collective-permute-start | bytes 61448 | tf_op jit(solution)/shard_map/ppermute | solution.py:406
  27.3 3.9 %collective-permute-start.7 = (f32[40,128]{1,0:T(8,128)S(1)}, f32[40,128]{1,0:T(8,128)S(1)}, u32[]{:S(2)}, u32[]{:S(2)}) collective-permute-start(f32[40,128]{1,0:T(8,128)S(1)} %add_add_fusion.4.own_ref), channel_id=1, source_target_pairs={{0,2},{1,3},{2,0},{3,1},{4,6},{5,7},{6,4},{7,5},{8,10},{9,11},{10,... | collective-permute-start | bytes 61448 | tf_op jit(solution)/shard_map/ppermute | solution.py:406
  28.2 3.2 %collective-permute-start.8 = (f32[40,128]{1,0:T(8,128)S(1)}, f32[40,128]{1,0:T(8,128)S(1)}, u32[]{:S(2)}, u32[]{:S(2)}) collective-permute-start(f32[40,128]{1,0:T(8,128)S(1)} %add_add_fusion.4.own_ref), channel_id=1, source_target_pairs={{0,3},{1,2},{2,1},{3,0},{4,7},{5,6},{6,5},{7,4},{8,11},{9,10},{10,... | collective-permute-start | bytes 61448 | tf_op jit(solution)/shard_map/ppermute | solution.py:406
  38.6 12.5 %collective-permute-start.10 = (f32[64,256]{1,0:T(8,128)}, f32[64,256]{1,0:T(8,128)S(1)}, u32[]{:S(2)}, u32[]{:S(2)}) collective-permute-start(f32[64,256]{1,0:T(8,128)} %get-tuple-element.56), channel_id=1, source_target_pairs={{0,2},{1,3},{2,0},{3,1},{4,6},{5,7},{6,4},{7,5},{8,10},{9,11},{10,... | collective-permute-start | bytes 196616 | tf_op jit(solution)/shard_map/ppermute | solution.py:406
  39.8 11.9 %collective-permute-start.11 = (f32[64,256]{1,0:T(8,128)}, f32[64,256]{1,0:T(8,128)S(1)}, u32[]{:S(2)}, u32[]{:S(2)}) collective-permute-start(f32[64,256]{1,0:T(8,128)} %get-tuple-element.57), channel_id=1, source_target_pairs={{0,3},{1,2},{2,1},{3,0},{4,7},{5,6},{6,5},{7,4},{8,11},{9,10},{10,... | collective-permute-start | bytes 196616 | tf_op jit(solution)/shard_map/ppermute | solution.py:406
  40.0 11.7 %collective-permute-start.9 = (f32[64,256]{1,0:T(8,128)}, f32[64,256]{1,0:T(8,128)S(1)}, u32[]{:S(2)}, u32[]{:S(2)}) collective-permute-start(f32[64,256]{1,0:T(8,128)} %get-tuple-element.55), channel_id=1, source_target_pairs={{0,1},{1,0},{2,3},{3,2},{4,5},{5,4},{6,7},{7,6},{8,9},{9,8},{10,11... | collective-permute-start | bytes 196616 | tf_op jit(solution)/shard_map/ppermute | solution.py:406
  49.8 6.4 %collective-permute-start.19 = (f32[72,256]{1,0:T(8,128)}, f32[72,256]{1,0:T(8,128)S(1)}, u32[]{:S(2)}, u32[]{:S(2)}) collective-permute-start(f32[72,256]{1,0:T(8,128)} %get-tuple-element.60), channel_id=1, source_target_pairs={{0,2},{1,3},{2,0},{3,1},{4,6},{5,7},{6,4},{7,5},{8,10},{9,11},{10,... | collective-permute-start | bytes 221192 | tf_op jit(solution)/shard_map/ppermute | solution.py:406
  51.1 5.1 %collective-permute-start.20 = (f32[72,256]{1,0:T(8,128)}, f32[72,256]{1,0:T(8,128)S(1)}, u32[]{:S(2)}, u32[]{:S(2)}) collective-permute-start(f32[72,256]{1,0:T(8,128)} %get-tuple-element.61), channel_id=1, source_target_pairs={{0,3},{1,2},{2,1},{3,0},{4,7},{5,6},{6,5},{7,4},{8,11},{9,10},{10,... | collective-permute-start | bytes 221192 | tf_op jit(solution)/shard_map/ppermute | solution.py:406
  51.7 6.2 %collective-permute-start.12 = (f32[64,256]{1,0:T(8,128)S(1)}, f32[64,256]{1,0:T(8,128)S(1)}, u32[]{:S(2)}, u32[]{:S(2)}) collective-permute-start(f32[64,256]{1,0:T(8,128)S(1)} %add_add_fusion.3), channel_id=1, source_target_pairs={{0,4},{1,5},{2,6},{3,7},{4,0},{5,1},{6,2},{7,3},{8,12},{9,13},{10,... | collective-permute-start | bytes 196616 | tf_op jit(solution)/shard_map/ppermute | solution.py:406
  51.8 9.8 %collective-permute-start.13 = (f32[64,256]{1,0:T(8,128)S(1)}, f32[64,256]{1,0:T(8,128)S(1)}, u32[]{:S(2)}, u32[]{:S(2)}) collective-permute-start(f32[64,256]{1,0:T(8,128)S(1)} %add_add_fusion.3), channel_id=1, source_target_pairs={{0,8},{1,9},{2,10},{3,11},{4,12},{5,13},{6,14},{7,15},{8,0},{9,1},... | collective-permute-start | bytes 196616 | tf_op jit(solution)/shard_map/ppermute | solution.py:406
  52.6 9.0 %collective-permute-start.14 = (f32[64,256]{1,0:T(8,128)S(1)}, f32[64,256]{1,0:T(8,128)S(1)}, u32[]{:S(2)}, u32[]{:S(2)}) collective-permute-start(f32[64,256]{1,0:T(8,128)S(1)} %add_add_fusion.3), channel_id=1, source_target_pairs={{0,12},{1,13},{2,14},{3,15},{4,8},{5,9},{6,10},{7,11},{8,4},{9,5},... | collective-permute-start | bytes 196616 | tf_op jit(solution)/shard_map/ppermute | solution.py:406
  57.1 5.9 %collective-permute-start.21 = (f32[72,256]{1,0:T(8,128)S(1)}, f32[72,256]{1,0:T(8,128)S(1)}, u32[]{:S(2)}, u32[]{:S(2)}) collective-permute-start(f32[72,256]{1,0:T(8,128)S(1)} %add_add_fusion.1), channel_id=1, source_target_pairs={{0,4},{1,5},{2,6},{3,7},{4,0},{5,1},{6,2},{7,3},{8,12},{9,13},{10,... | collective-permute-start | bytes 221192 | tf_op jit(solution)/shard_map/ppermute | solution.py:406
  57.2 9.2 %collective-permute-start.22 = (f32[72,256]{1,0:T(8,128)S(1)}, f32[72,256]{1,0:T(8,128)S(1)}, u32[]{:S(2)}, u32[]{:S(2)}) collective-permute-start(f32[72,256]{1,0:T(8,128)S(1)} %add_add_fusion.1), channel_id=1, source_target_pairs={{0,8},{1,9},{2,10},{3,11},{4,12},{5,13},{6,14},{7,15},{8,0},{9,1},... | collective-permute-start | bytes 221192 | tf_op jit(solution)/shard_map/ppermute | solution.py:406
  57.9 8.5 %collective-permute-start.23 = (f32[72,256]{1,0:T(8,128)S(1)}, f32[72,256]{1,0:T(8,128)S(1)}, u32[]{:S(2)}, u32[]{:S(2)}) collective-permute-start(f32[72,256]{1,0:T(8,128)S(1)} %add_add_fusion.1), channel_id=1, source_target_pairs={{0,12},{1,13},{2,14},{3,15},{4,8},{5,9},{6,10},{7,11},{8,4},{9,5},... | collective-permute-start | bytes 221192 | tf_op jit(solution)/shard_map/ppermute | solution.py:406
  61.6 6.2 %collective-permute-start.15 = (f32[64,256]{1,0:T(8,128)S(1)}, f32[64,256]{1,0:T(8,128)S(1)}, u32[]{:S(2)}, u32[]{:S(2)}) collective-permute-start(f32[64,256]{1,0:T(8,128)S(1)} %add_add_fusion.2.o0), channel_id=1, source_target_pairs={{0,1},{1,0},{2,3},{3,2},{4,5},{5,4},{6,7},{7,6},{8,9},{9,8},{10,11... | collective-permute-start | bytes 196616 | tf_op jit(solution)/shard_map/ppermute | solution.py:406
  61.7 12.4 %collective-permute-start.16 = (f32[64,256]{1,0:T(8,128)S(1)}, f32[64,256]{1,0:T(8,128)S(1)}, u32[]{:S(2)}, u32[]{:S(2)}) collective-permute-start(f32[64,256]{1,0:T(8,128)S(1)} %add_add_fusion.2.o0), channel_id=1, source_target_pairs={{0,2},{1,3},{2,0},{3,1},{4,6},{5,7},{6,4},{7,5},{8,10},{9,11},{10,... | collective-permute-start | bytes 196616 | tf_op jit(solution)/shard_map/ppermute | solution.py:406
  63.0 11.1 %collective-permute-start.17 = (f32[64,256]{1,0:T(8,128)S(1)}, f32[64,256]{1,0:T(8,128)S(1)}, u32[]{:S(2)}, u32[]{:S(2)}) collective-permute-start(f32[64,256]{1,0:T(8,128)S(1)} %add_add_fusion.2.o0), channel_id=1, source_target_pairs={{0,3},{1,2},{2,1},{3,0},{4,7},{5,6},{6,5},{7,4},{8,11},{9,10},{10,... | collective-permute-start | bytes 196616 | tf_op jit(solution)/shard_map/ppermute | solution.py:406
  66.4 7.7 %collective-permute-start.24 = (f32[72,256]{1,0:T(8,128)S(1)}, f32[72,256]{1,0:T(8,128)S(1)}, u32[]{:S(2)}, u32[]{:S(2)}) collective-permute-start(f32[72,256]{1,0:T(8,128)S(1)} %add_add_fusion.m0), channel_id=1, source_target_pairs={{0,1},{1,0},{2,3},{3,2},{4,5},{5,4},{6,7},{7,6},{8,9},{9,8},{10,11... | collective-permute-start | bytes 221192 | tf_op jit(solution)/shard_map/ppermute | solution.py:406
  66.5 7.6 %collective-permute-start.25 = (f32[72,256]{1,0:T(8,128)S(1)}, f32[72,256]{1,0:T(8,128)S(1)}, u32[]{:S(2)}, u32[]{:S(2)}) collective-permute-start(f32[72,256]{1,0:T(8,128)S(1)} %add_add_fusion.m0), channel_id=1, source_target_pairs={{0,2},{1,3},{2,0},{3,1},{4,6},{5,7},{6,4},{7,5},{8,10},{9,11},{10,... | collective-permute-start | bytes 221192 | tf_op jit(solution)/shard_map/ppermute | solution.py:406
  67.8 6.3 %collective-permute-start.26 = (f32[72,256]{1,0:T(8,128)S(1)}, f32[72,256]{1,0:T(8,128)S(1)}, u32[]{:S(2)}, u32[]{:S(2)}) collective-permute-start(f32[72,256]{1,0:T(8,128)S(1)} %add_add_fusion.m0), channel_id=1, source_target_pairs={{0,3},{1,2},{2,1},{3,0},{4,7},{5,6},{6,5},{7,4},{8,11},{9,10},{10,... | collective-permute-start | bytes 221192 | tf_op jit(solution)/shard_map/ppermute | solution.py:406
  (17 other events, 83.9 us)

commit v2 on v1

--- a/solution.py
+++ b/solution.py
@@ -85,13 +85,9 @@
     sw_ref,
     sb_ref,
     wc_ref,
-    send0,
-    send1,
-    send2,
-    send3,
+    pack_ref,
     raw_acc,
     norm_acc,
-    pack,
 ):
     step = pl.program_id(0)
     width = w_mid_ref.shape[0]
@@ -157,31 +153,26 @@
         mixed = nt(high, w_out) + nt(low, w_out)
         mixed = fold_rows(jnp.where(diagonal, mixed, 0.0), heads, slices)
         norm = jnp.sum(norm_acc[...].T, axis=0, keepdims=True)
-        halves = width // 128
-        for j in range(halves):
-            part = slice(j * 128, (j + 1) * 128)
-            pack[j * slices : (j + 1) * slices, :] = raw[:, part]
-            pack[(halves + j) * slices : (halves + j + 1) * slices, :] = mixed[:, part]
-        base = 2 * halves * slices
-        rest = pack.shape[0] - base
-        where_row = rows_of((rest, 128))
-        tail = jnp.zeros((rest, 128), f32)
-        for j in range(hm // 128):
-            tail = jnp.where(where_row == j, norm[:, j * 128 : (j + 1) * 128], tail)
-        pack[base:, :] = tail
-        place = group_place()
-        size = pack.shape[0] // group
-        for k, send in enumerate((send0, send1, send2, send3)):
-            send[...] = pack[pl.ds(pl.multiple_of((place ^ k) * size, 8), size), :]
+        tiles = slices // 8
+        count = pack_ref.shape[0] // 2
+        below = rows_of((8, 128))
+        for j in range(count):
+            part = slice(j // tiles * 128, (j // tiles + 1) * 128)
+            at = slice(j % tiles * 8, (j % tiles + 1) * 8)
+            pack_ref[j, 0:8, :] = raw[at, part]
+            pack_ref[count + j, 0:8, :] = mixed[at, part]
+            if j < hm // 128:
+                row = norm[:, j * 128 : (j + 1) * 128]
+                pack_ref[j, 8:16, :] = jnp.where(below == 0, row, 0.0)
+            else:
+                pack_ref[j, 8:16, :] = jnp.zeros((8, 128), f32)
+            pack_ref[count + j, 8:16, :] = jnp.zeros((8, 128), f32)
 
 
 def tokens_kernel(
     heads,
     slices,
-    own_ref,
-    got1,
-    got2,
-    got3,
+    pack_ref,
     w_qkv_ref,
     w_out_ref,
     sw_ref,
@@ -196,32 +187,29 @@
     send1,
     send2,
     send3,
-    pack,
     gwo,
 ):
     width = w_out_ref.shape[0]
     depth = width // heads
     hm = heads * slices
-    halves = width // 128
     place = group_place()
-    size = own_ref.shape[0]
-    for k, got in enumerate((own_ref, got1, got2, got3)):
-        pack[pl.ds(pl.multiple_of((place ^ k) * size, 8), size), :] = got[...]
+    tiles = slices // 8
+    count = pack_ref.shape[0] // 2
 
     def compact(first):
         pieces = []
         for h in range(heads):
             per = 128 // depth
-            x = pack[(first + h // per) * slices : (first + h // per + 1) * slices, :]
+            at = first + h // per * tiles
+            x = pack_ref[at : at + tiles, 0:8, :].reshape(slices, 128)
             shift = (h % per) * depth
             pieces.append(pltpu.roll(x, 128 - shift, 1) if shift else x)
         return jnp.concatenate(pieces, axis=0)[:, 0:depth]
 
     raw = compact(0)
-    d_mixed = compact(halves)
-    base = 2 * halves * slices
-    columns = pack[base : base + 8, :].T
-    norm = jnp.concatenate([columns[:, j : j + 1] for j in range(hm // 128)], axis=0)
+    d_mixed = compact(count)
+    norm = [pack_ref[j, 8:16, :].T[:, 0:1] for j in range(hm // 128)]
+    norm = jnp.concatenate(norm, axis=0)
     inverse = 1.0 / (norm + eps_norm)
     tokens = raw * inverse
     w_q, w_k, w_v = (w_qkv_ref[i].astype(f32) for i in range(3))
@@ -421,6 +409,23 @@
     return total
 
 
+def sum_everywhere(x, count):
+    pieces = x.shape[0]
+    groups = None
+    if count > pieces:
+        groups = [list(range(i, i + pieces)) for i in range(0, count, pieces)]
+
+    def swap(y):
+        return lax.all_to_all(y, "node", 0, 0, axis_index_groups=groups, tiled=True)
+
+    total = jnp.sum(swap(x), axis=0)
+    stride = pieces
+    while stride < count:
+        total = total + exchange(total, stride, count)
+        stride *= 2
+    return swap(jnp.broadcast_to(total, x.shape))
+
+
 def gather_group(total, count):
     return [total] + [exchange(total, k, count) for k in range(1, group)]
 
@@ -437,13 +442,12 @@
     by_rows = pl.BlockSpec((block, width), lambda i: (i, 0))
     by_cols = pl.BlockSpec((hm, block), lambda i: (0, i))
     aux_spec = pl.BlockSpec((3 * heads, block), lambda i: (0, i))
-    pack_rows = 2 * (width // 128) * slices + 32
-    piece = (pack_rows // group, 128)
+    pack = (2 * (slices // 8) * (width // 128), 16, 128)
 
     def like(shape, dtype):
         return jax.ShapeDtypeStruct(shape, dtype)
 
-    mid, wt, aux, sw, sb, wc, *sends = pl.pallas_call(
+    mid, wt, aux, sw, sb, wc, sums = pl.pallas_call(
         functools.partial(stats_kernel, heads, slices),
         grid=grid,
         in_specs=[
@@ -463,8 +467,8 @@
             full((hm + 16, width)),
             full((width, hm)),
             full((hm, width)),
-        ]
-        + [full(piece)] * group,
+            full(pack),
+        ],
         out_shape=[
             like((rows, width), bf16),
             like((hm, rows), bf16),
@@ -472,18 +476,14 @@
             like((hm + 16, width), bf16),
             like((width, hm), bf16),
             like((hm, width), f32),
-        ]
-        + [like(piece, f32)] * group,
-        scratch_shapes=[
-            pltpu.VMEM((hm, width), f32),
-            pltpu.VMEM((hm, 128), f32),
-            pltpu.VMEM((pack_rows, 128), f32),
+            like(pack, f32),
         ],
+        scratch_shapes=[pltpu.VMEM((hm, width), f32), pltpu.VMEM((hm, 128), f32)],
         compiler_params=params(),
         cost_estimate=cost(4 * unit, rows * width * 8, rows * hm),
     )(owned, valid.reshape(1, rows), feats, cotangent, w_mid, w_slice, temp_vec.reshape(1, depth), w_out)
 
-    pieces = gather_group(sum_over_groups(sends, count), count)
+    sums = sum_everywhere(sums, count)
 
     quarter = (width // group, width)
     lhs, mw, yt, dn, grad_qkv, *sends = pl.pallas_call(
@@ -496,10 +496,10 @@
             like((3, depth, depth), f32),
         ]
         + [like(quarter, f32)] * group,
-        scratch_shapes=[pltpu.VMEM((pack_rows, 128), f32), pltpu.VMEM((width, width), f32)],
+        scratch_shapes=[pltpu.VMEM((width, width), f32)],
         compiler_params=params(False),
         cost_estimate=cost(30 * width**3, 4 * width * width * 4, hm * hm),
-    )(*pieces, w_qkv, w_out, sw, sb, wc)
+    )(sums, w_qkv, w_out, sw, sb, wc)
 
     out_parts = gather_group(sum_over_groups(sends, count), count)
 

time: 78 us -> 84.4 us (1.082)
  blocking collectives: 0 us -> 15.3 us
  starting transfers between devices: 26.3 us -> 17.3 us
    all_to_all x0 -> x1, blocking collectives: none -> 15.3 us  [swap(): return lax.all_to_all(y, 'node', 0, 0, axis_index_groups=groups, tiled=True)]
    ppermute x27 -> x18, starting transfers between devices: 26.3 us -> 13.7 us  [exchange(): return lax.ppermute(x, 'node', [(i, i ^ k) for i in range(count)])]
    all_to_all x0 -> x1, waiting for transfers between devices: none -> 7.19 us  [swap(): return lax.all_to_all(y, 'node', 0, 0, axis_index_groups=groups, tiled=True)]
    ppermute x27 -> x18, waiting for transfers between devices: 13.1 us -> 6.08 us  [exchange(): return lax.ppermute(x, 'node', [(i, i ^ k) for i in range(count)])]
    all_to_all x0 -> x1, starting transfers between devices: none -> 3.51 us  [swap(): return lax.all_to_all(y, 'node', 0, 0, axis_index_groups=groups, tiled=True)]
    unnamed x28 -> x22, local copies, waits for them, and re-layouts: 1.9 us -> 1.95 us
  transfers between devices with their start and end apart: 27 -> 19, of which waited for: 7 -> 4; matrix products, arithmetic and copies ran while one was open for 2% -> 2% of each run, Pallas kernels for 19% -> 18%
where the time goes in v2:
time: 84.4 us; the launch traced here: 83.8 us
  Pallas kernels  32.1 us (38%)
  starting transfers between devices  17.3 us (20%)
  blocking collectives  15.3 us (18%)
  waiting for transfers between devices  13.3 us (16%)
  local copies, waits for them, and re-layouts  3.31 us (4%)
  between operations  1.49 us (2%)
  other arithmetic  0.99 us (1%)
    all_to_all x1, blocking collectives, swap(): return lax.all_to_all(y, 'node', 0, 0, axis_index_groups=groups, tiled=True)  15.3 us
    ppermute x18, starting transfers between devices, exchange(): return lax.ppermute(x, 'node', [(i, i ^ k) for i in range(count)])  13.7 us
    pallas_call x1, Pallas kernels, shards(): pl.pallas_call(functools.partial(backward_kernel, heads, slices), grid=gr...  9.03 us
    pallas_call x1, Pallas kernels, shards(): pl.pallas_call(functools.partial(stats_kernel, heads, slices), grid=grid,...  8.97 us
    all_to_all x1, waiting for transfers between devices, swap(): return lax.all_to_all(y, 'node', 0, 0, axis_index_groups=groups, tiled=True)  7.19 us
    pallas_call x1, Pallas kernels, shards(): pl.pallas_call(functools.partial(tokens_kernel, heads, slices), out_shape...  6.51 us
    ppermute x18, waiting for transfers between devices, exchange(): return lax.ppermute(x, 'node', [(i, i ^ k) for i in range(count)])  6.08 us
    pallas_call x1, Pallas kernels, shards(): pl.pallas_call(rows_kernel, grid=grid, in_specs=[by_cols, by_cols, full((...  5.66 us
  transfers between devices with their start and end apart: 19, of which 4 were waited for; matrix products, arithmetic and copies ran while one was open for 2% of the time, Pallas kernels for 18%

profile of v2, /device:TPU:0, one launch (start us, length us, event | category | flops | bytes accessed | tf_op | source)
XLA Modules:
  0.0 83.8 jit_solution(6329400571592804228)
XLA Ops:
  1.3 9.0 %shard_map.144 = (bf16[4096,256]{1,0:T(8,128)(2,1)}, bf16[256,4096]{1,0:T(8,128)(2,1)}, f32[24,4096]{1,0:T(8,128)}, bf16[272,256]{1,0:T(8,128)(2,1)}, bf16[256,2...) custom-call(s32[1]{0:T(128)S(6)} %copy.17.owned_ref, s32[1,4096]{1,0:T(1,128)} %bitcast.6, ...), custom_call_target="tpu_custom_call" | custom-call | flops 2147483648 | bytes 8388608 | tf_op jit(solution)/shard_map/pallas_call | solution.py:450
  10.3 15.3 %all_to_all.10 = f32[16,16,128]{2,1,0:T(8,128)S(1)} all-to-all(f32[16,16,128]{2,1,0:T(8,128)} %get-tuple-element.37), channel_id=1, replica_groups=mesh['design'=2,'node'=16] {'node'}, dimensions={0} | all-to-all | bytes 262144 | tf_op jit(solution)/shard_map/all_to_all | solution.py:419
  25.6 0.7 broadcast_in_dim.3
  26.3 3.5 %all-to-all-start.1 = ((f32[16,16,128]{2,1,0:T(8,128)}), f32[16,16,128]{2,1,0:T(8,128)S(1)}, u32[]{:S(2)}, u32[]{:S(2)}) async-start(f32[16,16,128]{2,1,0:T(8,128)} %broadcast_in_dim.3), calls=%async_computation.1 | async-start | bytes 262144 | tf_op jit(solution)/shard_map/all_to_all | solution.py:419
  29.8 0.7 copy.16.temp_ref
  30.5 7.2 %all-to-all-done.1.pack_ref = f32[16,16,128]{2,1,0:T(8,128)S(1)} async-done(((f32[16,16,128]{2,1,0:T(8,128)}), f32[16,16,128]{2,1,0:T(8,128)S(1)}, u32[]{:S(2)}, u32[]{:S(2)}) %all-to-all-start.1) | async-done | bytes 131104 | tf_op jit(solution)/shard_map/all_to_all | solution.py:419
  37.7 0.7 copy-done.2
  38.3 6.5 %shard_map.145 = (bf16[528,256]{1,0:T(8,128)(2,1)}, bf16[256,256]{1,0:T(8,128)(2,1)}, bf16[256,512]{1,0:T(8,128)(2,1)}, f32[256,128]{1,0:T(8,128)}, f32[3,32,32]...) custom-call(f32[16,16,128]{2,1,0:T(8,128)} %copy-done.2, ...), custom_call_target="tpu_custom_call" | custom-call | flops 503316480 | bytes 1048576 | tf_op jit(solution)/shard_map/pallas_call | solution.py:489
  44.9 1.8 %collective-permute-start.2 = (f32[64,256]{1,0:T(8,128)}, f32[64,256]{1,0:T(8,128)S(1)}, u32[]{:S(2)}, u32[]{:S(2)}) collective-permute-start(f32[64,256]{1,0:T(8,128)} %get-tuple-element.51), channel_id=1, source_target_pairs={{0,3},{1,2},{2,1},{3,0},{4,7},{5,6},{6,5},{7,4},{8,11},{9,10},{10,... | collective-permute-start | bytes 196616 | tf_op jit(solution)/shard_map/ppermute | solution.py:394
  46.7 9.0 %shard_map.146 = (bf16[256,4096]{1,0:T(8,128)(2,1)}, f32[72,256]{1,0:T(8,128)}, f32[72,256]{1,0:T(8,128)}, f32[72,256]{1,0:T(8,128)}, f32[72,256]{1,0:T(8,128)}) custom-call(f32[24,4096]{1,0:T(8,128)} %get-tuple-element.35.aux_ref, bf16[4096,256]{1,0:T(8,128)(2,1)} %get-tuple-element.36.mid_ref, bf16[4096,256]{1,0:T(8,128)(2,1)} %cot_ref.3, ...), custom_call_target="tpu_custom_call" | custom-call | flops 4294967296 | bytes 8388608 | tf_op jit(solution)/shard_map/pallas_call | solution.py:508
  56.1 1.4 %collective-permute-start.11 = (f32[72,256]{1,0:T(8,128)}, f32[72,256]{1,0:T(8,128)S(1)}, u32[]{:S(2)}, u32[]{:S(2)}) collective-permute-start(f32[72,256]{1,0:T(8,128)} %get-tuple-element.55), channel_id=1, source_target_pairs={{0,3},{1,2},{2,1},{3,0},{4,7},{5,6},{6,5},{7,4},{8,11},{9,10},{10,... | collective-permute-start | bytes 221192 | tf_op jit(solution)/shard_map/ppermute | solution.py:394
  58.1 1.2 %collective-permute-start.4 = (f32[64,256]{1,0:T(8,128)S(1)}, f32[64,256]{1,0:T(8,128)S(1)}, u32[]{:S(2)}, u32[]{:S(2)}) collective-permute-start(f32[64,256]{1,0:T(8,128)S(1)} %add_add_fusion.3), channel_id=1, source_target_pairs={{0,8},{1,9},{2,10},{3,11},{4,12},{5,13},{6,14},{7,15},{8,0},{9,1},... | collective-permute-start | bytes 196616 | tf_op jit(solution)/shard_map/ppermute | solution.py:394
  59.3 1.8 %collective-permute-done.10 = f32[72,256]{1,0:T(8,128)S(1)} collective-permute-done((f32[72,256]{1,0:T(8,128)}, f32[72,256]{1,0:T(8,128)S(1)}, u32[]{:S(2)}, u32[]{:S(2)}) %collective-permute-start.10) | collective-permute-done | bytes 73760 | tf_op jit(solution)/shard_map/ppermute | solution.py:394
  61.1 1.3 %collective-permute-start.5 = (f32[64,256]{1,0:T(8,128)S(1)}, f32[64,256]{1,0:T(8,128)S(1)}, u32[]{:S(2)}, u32[]{:S(2)}) collective-permute-start(f32[64,256]{1,0:T(8,128)S(1)} %add_add_fusion.3), channel_id=1, source_target_pairs={{0,12},{1,13},{2,14},{3,15},{4,8},{5,9},{6,10},{7,11},{8,4},{9,5},... | collective-permute-start | bytes 196616 | tf_op jit(solution)/shard_map/ppermute | solution.py:394
  62.5 0.9 %add_add_fusion.1 = f32[72,256]{1,0:T(8,128)S(1)} fusion(f32[72,256]{1,0:T(8,128)S(1)} %collective-permute-done.10, f32[72,256]{1,0:T(8,128)S(1)} %collective-permute-done.11, f32[72,256]{1,0:T(8,128)} %get-tuple-element.52, f32[72,256]{1,0:T(8,128)S(1)} %collective-permute-done.9), kind=kLoop, calls=%fused_computation.1 | loop fusion | flops 55296 | bytes 368640 | tf_op jit(solution)/shard_map/add | solution.py:399
  63.4 3.0 %collective-permute-start.13 = (f32[72,256]{1,0:T(8,128)S(1)}, f32[72,256]{1,0:T(8,128)S(1)}, u32[]{:S(2)}, u32[]{:S(2)}) collective-permute-start(f32[72,256]{1,0:T(8,128)S(1)} %add_add_fusion.1), channel_id=1, source_target_pairs={{0,8},{1,9},{2,10},{3,11},{4,12},{5,13},{6,14},{7,15},{8,0},{9,1},... | collective-permute-start | bytes 221192 | tf_op jit(solution)/shard_map/ppermute | solution.py:394
  66.5 1.3 %collective-permute-start.14 = (f32[72,256]{1,0:T(8,128)S(1)}, f32[72,256]{1,0:T(8,128)S(1)}, u32[]{:S(2)}, u32[]{:S(2)}) collective-permute-start(f32[72,256]{1,0:T(8,128)S(1)} %add_add_fusion.1), channel_id=1, source_target_pairs={{0,12},{1,13},{2,14},{3,15},{4,8},{5,9},{6,10},{7,11},{8,4},{9,5},... | collective-permute-start | bytes 221192 | tf_op jit(solution)/shard_map/ppermute | solution.py:394
  68.3 1.3 %collective-permute-done.12 = f32[72,256]{1,0:T(8,128)S(1)} collective-permute-done((f32[72,256]{1,0:T(8,128)S(1)}, f32[72,256]{1,0:T(8,128)S(1)}, u32[]{:S(2)}, u32[]{:S(2)}) %collective-permute-start.12) | collective-permute-done | bytes 73760 | tf_op jit(solution)/shard_map/ppermute | solution.py:394
  69.8 3.0 %collective-permute-done.13 = f32[72,256]{1,0:T(8,128)S(1)} collective-permute-done((f32[72,256]{1,0:T(8,128)S(1)}, f32[72,256]{1,0:T(8,128)S(1)}, u32[]{:S(2)}, u32[]{:S(2)}) %collective-permute-start.13) | collective-permute-done | bytes 73760 | tf_op jit(solution)/shard_map/ppermute | solution.py:394
  73.2 1.5 %collective-permute-start.17 = (f32[72,256]{1,0:T(8,128)S(1)}, f32[72,256]{1,0:T(8,128)S(1)}, u32[]{:S(2)}, u32[]{:S(2)}) collective-permute-start(f32[72,256]{1,0:T(8,128)S(1)} %add_add_fusion.m0), channel_id=1, source_target_pairs={{0,3},{1,2},{2,1},{3,0},{4,7},{5,6},{6,5},{7,4},{8,11},{9,10},{10,... | collective-permute-start | bytes 221192 | tf_op jit(solution)/shard_map/ppermute | solution.py:394
  74.7 5.7 %shard_map.147 = (bf16[4096,256]{1,0:T(8,128)(2,1)}, bf16[4096,256]{1,0:T(8,128)(2,1)}) custom-call(bf16[256,4096]{1,0:T(8,128)(2,1)} %get-tuple-element.34.wt_ref, bf16[256,4096]{1,0:T(8,128)(2,1)} %get-tuple-element.45.dmt_ref, bf16[256,256]{1,0:T(8,128)(2,1)} %get-tuple-element.42.mw_ref, bf16[256,256]{1,0:T(8,128)(2,1)} %w_mid_ref.3), custom_call_target="tpu_custom_call" | custom-call | flops 1073741824 | bytes 8388608 | tf_op jit(solution)/shard_map/pallas_call | solution.py:536
  80.5 0.5 copy-done.7
  81.2 0.6 copy-done.5
  81.8 2.0 %shard_map.148 = (f32[256,256]{1,0:T(8,128)}, f32[256,256]{1,0:T(8,128)}, f32[32,32]{1,0:T(8,128)}, f32[1,32]{1,0:T(1,128)}) custom-call(f32[64,256]{1,0:T(8,128)} %copy-done.1, f32[64,256]{1,0:T(8,128)} %copy-done.6, f32[64,256]{1,0:T(8,128)} %copy-done.7, f32[64,256]{1,0:T(8,128)} %copy-done.8, f32[72,256]{1,0:T(8,128)} %copy-done, f32[72,256]{1,0:T(8,128)} %copy-done.3, ...), custom_call_target="tpu_custom_call" | custom-call | bytes 1048576 | tf_op jit(solution)/shard_map/pallas_call | solution.py:546
  (49 shorter events, 2.4 us)
Async XLA Ops:
  1.3 28.5 %copy-start.10 = (bf16[32]{0:T(256)(128)(2,1)S(1)}, bf16[32]{0:T(256)(128)(2,1)}, u32[]{:S(2)}) copy-start(bf16[32]{0:T(256)(128)(2,1)} %param.15) | copy-start | bytes 196
  26.3 11.4 %all-to-all-start.1 = ((f32[16,16,128]{2,1,0:T(8,128)}), f32[16,16,128]{2,1,0:T(8,128)S(1)}, u32[]{:S(2)}, u32[]{:S(2)}) async-start(f32[16,16,128]{2,1,0:T(8,128)} %broadcast_in_dim.3), calls=%async_computation.1 | async-start | bytes 262144 | tf_op jit(solution)/shard_map/all_to_all | solution.py:419
  44.8 12.7 %collective-permute-start = (f32[64,256]{1,0:T(8,128)}, f32[64,256]{1,0:T(8,128)S(1)}, u32[]{:S(2)}, u32[]{:S(2)}) collective-permute-start(f32[64,256]{1,0:T(8,128)} %get-tuple-element.49), channel_id=1, source_target_pairs={{0,1},{1,0},{2,3},{3,2},{4,5},{5,4},{6,7},{7,6},{8,9},{9,8},{10,11... | collective-permute-start | bytes 196616 | tf_op jit(solution)/shard_map/ppermute | solution.py:394
  44.9 13.1 %collective-permute-start.1 = (f32[64,256]{1,0:T(8,128)}, f32[64,256]{1,0:T(8,128)S(1)}, u32[]{:S(2)}, u32[]{:S(2)}) collective-permute-start(f32[64,256]{1,0:T(8,128)} %get-tuple-element.50), channel_id=1, source_target_pairs={{0,2},{1,3},{2,0},{3,1},{4,6},{5,7},{6,4},{7,5},{8,10},{9,11},{10,... | collective-permute-start | bytes 196616 | tf_op jit(solution)/shard_map/ppermute | solution.py:394
  44.9 13.0 %collective-permute-start.2 = (f32[64,256]{1,0:T(8,128)}, f32[64,256]{1,0:T(8,128)S(1)}, u32[]{:S(2)}, u32[]{:S(2)}) collective-permute-start(f32[64,256]{1,0:T(8,128)} %get-tuple-element.51), channel_id=1, source_target_pairs={{0,3},{1,2},{2,1},{3,0},{4,7},{5,6},{6,5},{7,4},{8,11},{9,10},{10,... | collective-permute-start | bytes 196616 | tf_op jit(solution)/shard_map/ppermute | solution.py:394
  46.7 11.3 %copy-start.9 = (f32[64,256]{1,0:T(8,128)S(1)}, f32[64,256]{1,0:T(8,128)}, u32[]{:S(2)}) copy-start(f32[64,256]{1,0:T(8,128)} %get-tuple-element.48) | copy-start | bytes 196612
  55.7 5.4 %collective-permute-start.10 = (f32[72,256]{1,0:T(8,128)}, f32[72,256]{1,0:T(8,128)S(1)}, u32[]{:S(2)}, u32[]{:S(2)}) collective-permute-start(f32[72,256]{1,0:T(8,128)} %get-tuple-element.54), channel_id=1, source_target_pairs={{0,2},{1,3},{2,0},{3,1},{4,6},{5,7},{6,4},{7,5},{8,10},{9,11},{10,... | collective-permute-start | bytes 221192 | tf_op jit(solution)/shard_map/ppermute | solution.py:394
  56.1 6.3 %collective-permute-start.11 = (f32[72,256]{1,0:T(8,128)}, f32[72,256]{1,0:T(8,128)S(1)}, u32[]{:S(2)}, u32[]{:S(2)}) collective-permute-start(f32[72,256]{1,0:T(8,128)} %get-tuple-element.55), channel_id=1, source_target_pairs={{0,3},{1,2},{2,1},{3,0},{4,7},{5,6},{6,5},{7,4},{8,11},{9,10},{10,... | collective-permute-start | bytes 221192 | tf_op jit(solution)/shard_map/ppermute | solution.py:394
  57.5 4.9 %collective-permute-start.9 = (f32[72,256]{1,0:T(8,128)}, f32[72,256]{1,0:T(8,128)S(1)}, u32[]{:S(2)}, u32[]{:S(2)}) collective-permute-start(f32[72,256]{1,0:T(8,128)} %get-tuple-element.53), channel_id=1, source_target_pairs={{0,1},{1,0},{2,3},{3,2},{4,5},{5,4},{6,7},{7,6},{8,9},{9,8},{10,11... | collective-permute-start | bytes 221192 | tf_op jit(solution)/shard_map/ppermute | solution.py:394
  58.0 8.5 %collective-permute-start.3 = (f32[64,256]{1,0:T(8,128)S(1)}, f32[64,256]{1,0:T(8,128)S(1)}, u32[]{:S(2)}, u32[]{:S(2)}) collective-permute-start(f32[64,256]{1,0:T(8,128)S(1)} %add_add_fusion.3), channel_id=1, source_target_pairs={{0,4},{1,5},{2,6},{3,7},{4,0},{5,1},{6,2},{7,3},{8,12},{9,13},{10,... | collective-permute-start | bytes 196616 | tf_op jit(solution)/shard_map/ppermute | solution.py:394
  58.1 9.8 %collective-permute-start.4 = (f32[64,256]{1,0:T(8,128)S(1)}, f32[64,256]{1,0:T(8,128)S(1)}, u32[]{:S(2)}, u32[]{:S(2)}) collective-permute-start(f32[64,256]{1,0:T(8,128)S(1)} %add_add_fusion.3), channel_id=1, source_target_pairs={{0,8},{1,9},{2,10},{3,11},{4,12},{5,13},{6,14},{7,15},{8,0},{9,1},... | collective-permute-start | bytes 196616 | tf_op jit(solution)/shard_map/ppermute | solution.py:394
  61.1 6.7 %collective-permute-start.5 = (f32[64,256]{1,0:T(8,128)S(1)}, f32[64,256]{1,0:T(8,128)S(1)}, u32[]{:S(2)}, u32[]{:S(2)}) collective-permute-start(f32[64,256]{1,0:T(8,128)S(1)} %add_add_fusion.3), channel_id=1, source_target_pairs={{0,12},{1,13},{2,14},{3,15},{4,8},{5,9},{6,10},{7,11},{8,4},{9,5},... | collective-permute-start | bytes 196616 | tf_op jit(solution)/shard_map/ppermute | solution.py:394
  63.4 6.2 %collective-permute-start.12 = (f32[72,256]{1,0:T(8,128)S(1)}, f32[72,256]{1,0:T(8,128)S(1)}, u32[]{:S(2)}, u32[]{:S(2)}) collective-permute-start(f32[72,256]{1,0:T(8,128)S(1)} %add_add_fusion.1), channel_id=1, source_target_pairs={{0,4},{1,5},{2,6},{3,7},{4,0},{5,1},{6,2},{7,3},{8,12},{9,13},{10,... | collective-permute-start | bytes 221192 | tf_op jit(solution)/shard_map/ppermute | solution.py:394
  63.4 9.3 %collective-permute-start.13 = (f32[72,256]{1,0:T(8,128)S(1)}, f32[72,256]{1,0:T(8,128)S(1)}, u32[]{:S(2)}, u32[]{:S(2)}) collective-permute-start(f32[72,256]{1,0:T(8,128)S(1)} %add_add_fusion.1), channel_id=1, source_target_pairs={{0,8},{1,9},{2,10},{3,11},{4,12},{5,13},{6,14},{7,15},{8,0},{9,1},... | collective-permute-start | bytes 221192 | tf_op jit(solution)/shard_map/ppermute | solution.py:394
  66.5 6.3 %collective-permute-start.14 = (f32[72,256]{1,0:T(8,128)S(1)}, f32[72,256]{1,0:T(8,128)S(1)}, u32[]{:S(2)}, u32[]{:S(2)}) collective-permute-start(f32[72,256]{1,0:T(8,128)S(1)} %add_add_fusion.1), channel_id=1, source_target_pairs={{0,12},{1,13},{2,14},{3,15},{4,8},{5,9},{6,10},{7,11},{8,4},{9,5},... | collective-permute-start | bytes 221192 | tf_op jit(solution)/shard_map/ppermute | solution.py:394
  67.8 12.6 %copy-start.1 = (f32[64,256]{1,0:T(8,128)}, f32[64,256]{1,0:T(8,128)S(1)}, u32[]{:S(2)}) copy-start(f32[64,256]{1,0:T(8,128)S(1)} %add_add_fusion.2.o0) | copy-start | bytes 196612
  67.9 5.4 %collective-permute-start.6 = (f32[64,256]{1,0:T(8,128)S(1)}, f32[64,256]{1,0:T(8,128)S(1)}, u32[]{:S(2)}, u32[]{:S(2)}) collective-permute-start(f32[64,256]{1,0:T(8,128)S(1)} %add_add_fusion.2.o0), channel_id=1, source_target_pairs={{0,1},{1,0},{2,3},{3,2},{4,5},{5,4},{6,7},{7,6},{8,9},{9,8},{10,11... | collective-permute-start | bytes 196616 | tf_op jit(solution)/shard_map/ppermute | solution.py:394
  67.9 12.5 %collective-permute-start.7 = (f32[64,256]{1,0:T(8,128)S(1)}, f32[64,256]{1,0:T(8,128)S(1)}, u32[]{:S(2)}, u32[]{:S(2)}) collective-permute-start(f32[64,256]{1,0:T(8,128)S(1)} %add_add_fusion.2.o0), channel_id=1, source_target_pairs={{0,2},{1,3},{2,0},{3,1},{4,6},{5,7},{6,4},{7,5},{8,10},{9,11},{10,... | collective-permute-start | bytes 196616 | tf_op jit(solution)/shard_map/ppermute | solution.py:394
  69.6 10.9 %collective-permute-start.8 = (f32[64,256]{1,0:T(8,128)S(1)}, f32[64,256]{1,0:T(8,128)S(1)}, u32[]{:S(2)}, u32[]{:S(2)}) collective-permute-start(f32[64,256]{1,0:T(8,128)S(1)} %add_add_fusion.2.o0), channel_id=1, source_target_pairs={{0,3},{1,2},{2,1},{3,0},{4,7},{5,6},{6,5},{7,4},{8,11},{9,10},{10,... | collective-permute-start | bytes 196616 | tf_op jit(solution)/shard_map/ppermute | solution.py:394
  72.8 7.6 %copy-start = (f32[72,256]{1,0:T(8,128)}, f32[72,256]{1,0:T(8,128)S(1)}, u32[]{:S(2)}) copy-start(f32[72,256]{1,0:T(8,128)S(1)} %add_add_fusion.m0) | copy-start | bytes 221188
  72.8 7.7 %collective-permute-start.15 = (f32[72,256]{1,0:T(8,128)S(1)}, f32[72,256]{1,0:T(8,128)S(1)}, u32[]{:S(2)}, u32[]{:S(2)}) collective-permute-start(f32[72,256]{1,0:T(8,128)S(1)} %add_add_fusion.m0), channel_id=1, source_target_pairs={{0,1},{1,0},{2,3},{3,2},{4,5},{5,4},{6,7},{7,6},{8,9},{9,8},{10,11... | collective-permute-start | bytes 221192 | tf_op jit(solution)/shard_map/ppermute | solution.py:394
  72.9 7.6 %collective-permute-start.16 = (f32[72,256]{1,0:T(8,128)S(1)}, f32[72,256]{1,0:T(8,128)S(1)}, u32[]{:S(2)}, u32[]{:S(2)}) collective-permute-start(f32[72,256]{1,0:T(8,128)S(1)} %add_add_fusion.m0), channel_id=1, source_target_pairs={{0,2},{1,3},{2,0},{3,1},{4,6},{5,7},{6,4},{7,5},{8,10},{9,11},{10,... | collective-permute-start | bytes 221192 | tf_op jit(solution)/shard_map/ppermute | solution.py:394
  73.2 7.2 %copy-start.6 = (f32[64,256]{1,0:T(8,128)}, f32[64,256]{1,0:T(8,128)S(1)}, u32[]{:S(2)}) copy-start(f32[64,256]{1,0:T(8,128)S(1)} %collective-permute-done.6.o1) | copy-start | bytes 196612
  73.2 7.3 %collective-permute-start.17 = (f32[72,256]{1,0:T(8,128)S(1)}, f32[72,256]{1,0:T(8,128)S(1)}, u32[]{:S(2)}, u32[]{:S(2)}) collective-permute-start(f32[72,256]{1,0:T(8,128)S(1)} %add_add_fusion.m0), channel_id=1, source_target_pairs={{0,3},{1,2},{2,1},{3,0},{4,7},{5,6},{6,5},{7,4},{8,11},{9,10},{10,... | collective-permute-start | bytes 221192 | tf_op jit(solution)/shard_map/ppermute | solution.py:394
  (6 other events, 3.9 us)

commit v3 on v1

--- a/solution.py
+++ b/solution.py
@@ -13,7 +13,7 @@
 eps_norm = 1e-05
 exact = lax.Precision.HIGHEST
 group = 4
-vmem_bytes = 56 * 1024 * 1024
+mib = 1024 * 1024
 
 
 def nn(a, b, precision=None):
@@ -79,18 +79,22 @@
     w_slice_ref,
     temp_ref,
     w_out_ref,
+    w_qkv_ref,
     mid_ref,
     wt_ref,
     aux_ref,
     sw_ref,
     sb_ref,
-    wc_ref,
-    send0,
-    send1,
-    send2,
-    send3,
+    w_cat_ref,
+    keep_ref,
+    send_ref,
+    wc0,
+    wc1,
+    wc2,
+    wc3,
     raw_acc,
     norm_acc,
+    wc_acc,
     pack,
 ):
     step = pl.program_id(0)
@@ -115,9 +119,14 @@
         sw_ref[hm : hm + 16, :] = jnp.where(same_block(16, width, 1, depth), full, 0.0).astype(
             bf16
         )
+        w_cat = jnp.zeros((depth, 128), f32)
+        for i in range(3):
+            place_at = jnp.where(rows_of((depth, 128)) + i * depth == cols_of((depth, 128)), 1.0, 0.0)
+            w_cat = w_cat + nn(w_qkv_ref[i], place_at.astype(bf16))
+        w_cat_ref[...] = w_cat.astype(bf16)
         raw_acc[...] = jnp.zeros_like(raw_acc)
         norm_acc[...] = jnp.zeros_like(norm_acc)
-        wc_ref[...] = jnp.zeros_like(wc_ref)
+        wc_acc[...] = jnp.zeros_like(wc_acc)
 
     mid = nn(feats_ref[...], w_mid_ref[...]).astype(bf16)
     mid_ref[...] = mid
@@ -146,123 +155,150 @@
         aux_ref[heads + h : heads + h + 1, :] = jnp.where(live, peak + jnp.log(total), jnp.inf)
     wt = wt_ref[...]
     raw_acc[...] += nn(wt, mid)
-    wc_ref[...] += nn(wt, cot_ref[...])
+    wc_acc[...] += nn(wt, cot_ref[...])
 
     @pl.when(step == pl.num_programs(0) - 1)
     def _():
         diagonal = same_block(hm, width, slices, depth)
         raw = fold_rows(jnp.where(diagonal, raw_acc[...], 0.0), heads, slices)
-        high, low = two_pieces(wc_ref[...])
+        high, low = two_pieces(wc_acc[...])
         w_out = w_out_ref[...]
         mixed = nt(high, w_out) + nt(low, w_out)
         mixed = fold_rows(jnp.where(diagonal, mixed, 0.0), heads, slices)
         norm = jnp.sum(norm_acc[...].T, axis=0, keepdims=True)
-        halves = width // 128
-        for j in range(halves):
+        first = rows_of((8, 128)) == 0
+        for j in range(2):
             part = slice(j * 128, (j + 1) * 128)
-            pack[j * slices : (j + 1) * slices, :] = raw[:, part]
-            pack[(halves + j) * slices : (halves + j + 1) * slices, :] = mixed[:, part]
-        base = 2 * halves * slices
-        rest = pack.shape[0] - base
-        where_row = rows_of((rest, 128))
-        tail = jnp.zeros((rest, 128), f32)
-        for j in range(hm // 128):
-            tail = jnp.where(where_row == j, norm[:, j * 128 : (j + 1) * 128], tail)
-        pack[base:, :] = tail
+            pack[j, 0:slices, :] = raw[:, part]
+            pack[j, slices : 2 * slices, :] = mixed[:, part]
+            pack[j, 2 * slices :, :] = jnp.where(first, norm[:, part], 0.0)
         place = group_place()
-        size = pack.shape[0] // group
-        for k, send in enumerate((send0, send1, send2, send3)):
-            send[...] = pack[pl.ds(pl.multiple_of((place ^ k) * size, 8), size), :]
+        keep_ref[...] = pack[place & 1]
+        send_ref[...] = pack[(place & 1) ^ 1]
+        rows = hm // group
+        for k, send in enumerate((wc0, wc1, wc2, wc3)):
+            send[...] = wc_acc[pl.ds(pl.multiple_of((place ^ k) * rows, 8), rows), :]
+
+
+def lanes_at(x, lane, *where):
+    place = cols_of(x.shape) // lane
+    total = jnp.zeros_like(x)
+    for value, at, to in where:
+        shift = (to - at) * lane % 128
+        moved = pltpu.roll(value, shift, 1) if shift else value
+        total = jnp.where(place == to, moved, total)
+    return total.astype(bf16)
+
+
+def split(x):
+    high = x.astype(bf16).astype(f32)
+    return high, x - high
 
 
 def tokens_kernel(
     heads,
     slices,
     own_ref,
-    got1,
-    got2,
-    got3,
-    w_qkv_ref,
+    got_ref,
+    w_cat_ref,
     w_out_ref,
     sw_ref,
     sb_ref,
-    wc_ref,
     lhs_ref,
     mw_ref,
+    mixed_t_ref,
     yt_ref,
     dn_ref,
     grad_qkv_ref,
-    send0,
-    send1,
-    send2,
-    send3,
     pack,
-    gwo,
 ):
     width = w_out_ref.shape[0]
     depth = width // heads
     hm = heads * slices
-    halves = width // 128
-    place = group_place()
-    size = own_ref.shape[0]
-    for k, got in enumerate((own_ref, got1, got2, got3)):
-        pack[pl.ds(pl.multiple_of((place ^ k) * size, 8), size), :] = got[...]
+    place = group_place() & 1
+    pack[place] = own_ref[...]
+    pack[place ^ 1] = got_ref[...]
+    per = 128 // depth
 
     def compact(first):
         pieces = []
         for h in range(heads):
-            per = 128 // depth
-            x = pack[(first + h // per) * slices : (first + h // per + 1) * slices, :]
+            x = pack[h // per, first : first + slices, :]
             shift = (h % per) * depth
             pieces.append(pltpu.roll(x, 128 - shift, 1) if shift else x)
-        return jnp.concatenate(pieces, axis=0)[:, 0:depth]
+        x = jnp.concatenate(pieces, axis=0)
+        return jnp.where(cols_of(x.shape) < depth, x, 0.0)
 
     raw = compact(0)
-    d_mixed = compact(halves)
-    base = 2 * halves * slices
-    columns = pack[base : base + 8, :].T
-    norm = jnp.concatenate([columns[:, j : j + 1] for j in range(hm // 128)], axis=0)
+    d_mixed = compact(slices)
+    norm = jnp.concatenate([pack[j, 2 * slices :, :].T[:, 0:1] for j in range(2)], axis=0)
     inverse = 1.0 / (norm + eps_norm)
     tokens = raw * inverse
-    w_q, w_k, w_v = (w_qkv_ref[i].astype(f32) for i in range(3))
-    q, k, v = (nn(tokens, w, exact) for w in (w_q, w_k, w_v))
+    w_cat = w_cat_ref[...]
+
+    t_high, rest = split(tokens)
+    t_low, rest = split(rest)
+    left = lanes_at(tokens, depth, (t_high, 0, 0), (t_low, 0, 1), (rest, 0, 2))
+    blank = jnp.zeros((128 - 3 * depth, 128), bf16)
+    qkv = nn(left, jnp.concatenate([w_cat, w_cat, w_cat, blank], axis=0))
+    high, low = split(qkv)
+    q_left = lanes_at(qkv, depth, (high, 0, 0), (high, 0, 1), (low, 0, 2))
+    k_right = lanes_at(qkv, depth, (high, 1, 0), (low, 1, 1), (high, 1, 2))
+    v_right = lanes_at(qkv, depth, (high, 2, 0), (low, 2, 1), (high, 2, 2))
+    q_pair = lanes_at(qkv, depth, (high, 0, 0), (low, 0, 1))
+    k_pair = lanes_at(qkv, depth, (high, 1, 0), (low, 1, 1))
+    v_pair = lanes_at(qkv, depth, (high, 2, 0), (low, 2, 1))
+    g_high, g_low = split(d_mixed)
+    g_left = lanes_at(qkv, depth, (g_high, 0, 0), (g_high, 0, 1), (g_low, 0, 2))
+    g_pair = lanes_at(qkv, depth, (g_high, 0, 0), (g_low, 0, 1))
+
+    def times_pair(dot, x, pair):
+        x_high, x_low = two_pieces(x)
+        both = dot(x_high, pair)
+        low_part = dot(x_low, pair)
+        total = both + pltpu.roll(both, 128 - depth, 1) + low_part
+        return jnp.where(cols_of(total.shape) < depth, total, 0.0)
+
     blocks = same_block(hm, hm, slices, slices)
     scale = 1.0 / math.sqrt(depth)
-    scores = jnp.where(blocks, nt(q, k, exact) * scale, -jnp.inf)
+    scores = jnp.where(blocks, nt(q_left, k_right) * scale, -jnp.inf)
     expo = jnp.exp(scores - jnp.max(scores, axis=1, keepdims=True))
-    probs = expo / jnp.sum(expo, axis=1, keepdims=True)
-    mixed_b = nn(probs, v, exact).astype(bf16)
-
-    spread_d = spread_matrix(width, depth)
+    probs = expo * (1.0 / jnp.sum(expo, axis=1, keepdims=True))
+    mixed_b = times_pair(nn, probs, v_pair).astype(bf16)
+
+    spread_d = jnp.where(
+        (rows_of((width, 128)) % depth == cols_of((width, 128))), 1.0, 0.0
+    ).astype(bf16)
     diagonal = same_block(hm, width, slices, depth)
     diagonal_t = same_block(width, hm, depth, slices)
-    w_out = w_out_ref[...]
     mixed_block = jnp.where(diagonal, nt(mixed_b, spread_d), 0.0).astype(bf16)
-    mw_ref[...] = nn(mixed_block, w_out).astype(bf16)
-
-    d_probs = nt(d_mixed, v, exact)
-    d_v = tn(probs, d_mixed, exact)
+    mw_ref[...] = nn(mixed_block, w_out_ref[...]).astype(bf16)
+    mixed_t_ref[...] = jnp.where(diagonal_t, nt(spread_d, mixed_b), 0.0).astype(bf16)
+
+    d_probs = nt(g_left, v_right)
+    d_v = times_pair(tn, probs, g_pair)
     d_scores = probs * (d_probs - jnp.sum(probs * d_probs, axis=1, keepdims=True)) * scale
-    d_q = nn(d_scores, k, exact)
-    d_k = tn(d_scores, q, exact)
-    d_tokens = nt(d_q, w_q, exact) + nt(d_k, w_k, exact) + nt(d_v, w_v, exact)
+    d_q = times_pair(nn, d_scores, k_pair)
+    d_k = times_pair(tn, d_scores, q_pair)
+    d_qkv = d_q + pltpu.roll(d_k, depth, 1) + pltpu.roll(d_v, 2 * depth, 1)
+    d_high, d_low = two_pieces(d_qkv)
+    d_tokens = nt(d_high, w_cat) + nt(d_low, w_cat)
+    raw = raw[:, 0:depth]
     d_raw_b = (d_tokens * inverse).astype(bf16)
     d_norm = -jnp.sum(d_tokens * raw, axis=1, keepdims=True) * inverse * inverse
     dn_ref[...] = jnp.broadcast_to(d_norm, dn_ref.shape)
     top = sw_ref.shape[0]
     lhs_ref[0:top, :] = sw_ref[...]
+    spread_d = spread_matrix(width, depth)
     lhs_ref[top : top + hm, :] = jnp.where(diagonal, nt(d_raw_b, spread_d), 0.0).astype(bf16)
     yt_ref[:, 0:hm] = jnp.where(diagonal_t, nt(spread_d, d_raw_b), 0.0).astype(bf16)
     yt_ref[:, hm : 2 * hm] = sb_ref[...]
 
-    for i, grad in enumerate((d_q, d_k, d_v)):
-        grad_qkv_ref[i] = tn(tokens, grad, exact)
-    mixed_t = jnp.where(diagonal_t, nt(spread_d, mixed_b), 0.0).astype(bf16)
-    high, low = two_pieces(wc_ref[...])
-    gwo[...] = nn(mixed_t, high) + nn(mixed_t, low)
-    rows = width // group
-    for k, send in enumerate((send0, send1, send2, send3)):
-        send[...] = gwo[pl.ds(pl.multiple_of((place ^ k) * rows, 8), rows), :]
+    t_high, t_low = two_pieces(tokens)
+    grads = tn(t_high, d_high) + tn(t_high, d_low) + tn(t_low, d_high)
+    for i in range(3):
+        at = pltpu.roll(grads, 128 - i * depth, 1) if i else grads
+        grad_qkv_ref[i] = at[0:depth, 0:depth]
 
 
 def backward_kernel(
@@ -277,6 +313,7 @@
     yt_ref,
     dn_ref,
     temp_ref,
+    _,
     dmt_ref,
     send0,
     send1,
@@ -320,7 +357,9 @@
     c_high = c_sum.astype(bf16).astype(f32)
     stack[2 * hm : 2 * hm + 2 * heads, :] = jnp.concatenate([c_high, c_sum - c_high], axis=0).astype(bf16)
     d_mid = nn(yt_ref[...], stack[0 : 2 * hm, :])
-    temp = temp_ref[...].astype(f32)
+    temp = jnp.broadcast_to(temp_ref[...].astype(f32), (16, depth)).astype(bf16)
+    same = (rows_of((depth, depth)) == cols_of((depth, depth))).astype(f32).astype(bf16)
+    temp = nt(same, temp)[:, 0:1]
     for h in range(heads):
         span = slice(h * depth, (h + 1) * depth)
         dmt_ref[span, :] = (d_mid[span] + temp * sums[h]).astype(bf16)
@@ -361,25 +400,33 @@
             send[...] = pack[place ^ k]
 
 
-def rows_kernel(wt_ref, dmt_ref, mw_ref, w_mid_ref, attended_ref, feats_grad_ref):
+def rows_kernel(wt_ref, dmt_ref, mw_ref, w_mid_ref, _, attended_ref, feats_grad_ref, token_ref):
+    token_ref[...] = jnp.zeros_like(token_ref)
     attended_ref[...] = tn(wt_ref[...], mw_ref[...]).astype(bf16)
     feats_grad_ref[...] = lax.dot_general(
         dmt_ref[...], w_mid_ref[...], (((0,), (1,)), ((), ())), preferred_element_type=f32
     ).astype(bf16)
 
 
-def finish_kernel(
-    depth, o0, o1, o2, o3, m0, m1, m2, m3, grad_mid_ref, grad_out_ref, slice_ref, temp_ref, extra
-):
+def grad_out_kernel(o0, o1, o2, o3, mixed_t_ref, grad_out_ref, whole):
     place = group_place()
     rows = o0.shape[0]
-    more = m0.shape[0] - rows
-    for k, (out_part, mid_part) in enumerate(((o0, m0), (o1, m1), (o2, m2), (o3, m3))):
+    for k, part in enumerate((o0, o1, o2, o3)):
+        whole[pl.ds(pl.multiple_of((place ^ k) * rows, 8), rows), :] = part[...]
+    high, low = two_pieces(whole[...])
+    mixed_t = mixed_t_ref[...]
+    grad_out_ref[...] = nn(mixed_t, high) + nn(mixed_t, low)
+
+
+def finish_kernel(depth, m0, m1, m2, m3, grad_mid_ref, slice_ref, temp_ref, extra):
+    place = group_place()
+    slices = slice_ref.shape[1]
+    more = slices // group
+    rows = m0.shape[0] - more
+    for k, part in enumerate((m0, m1, m2, m3)):
         at = pl.ds(pl.multiple_of((place ^ k) * rows, 8), rows)
-        grad_out_ref[at, :] = out_part[...]
-        grad_mid_ref[at, :] = mid_part[0:rows, :]
-        extra[pl.ds(pl.multiple_of((place ^ k) * more, 8), more), :] = mid_part[rows:, 0:128]
-    slices = slice_ref.shape[1]
+        grad_mid_ref[at, :] = part[0:rows, :]
+        extra[pl.ds(pl.multiple_of((place ^ k) * more, 8), more), :] = part[rows:, 0:128]
     turned = extra[...].T
     slice_ref[...] = turned[0:depth, 0:slices]
     temp_ref[...] = extra[0:1, depth : 2 * depth]
@@ -390,12 +437,11 @@
     return pl.BlockSpec(shape, lambda *_: zeros)
 
 
-def params(grid=True):
-    if grid:
-        return pltpu.CompilerParams(
-            dimension_semantics=("arbitrary",), vmem_limit_bytes=vmem_bytes
-        )
-    return pltpu.CompilerParams(vmem_limit_bytes=vmem_bytes)
+def params(mebibytes, grid=True):
+    semantics = ("arbitrary",) if grid else None
+    return pltpu.CompilerParams(
+        dimension_semantics=semantics, vmem_limit_bytes=mebibytes * mib
+    )
 
 
 def cost(flops, moved, transcendentals=0):
@@ -406,14 +452,32 @@
     return lax.ppermute(x, "node", [(i, i ^ k) for i in range(count)])
 
 
-def sum_over_groups(parts, count):
-    got = [parts[0]] + [exchange(parts[k], k, count) for k in range(1, group)]
-    total = (got[0] + got[1]) + (got[2] + got[3])
+def sum_kernel(r0, r1, r2, r3, *rest):
+    rest[-1][...] = (r0[...] + r1[...]) + (r2[...] + r3[...])
+
+
+def sum_four(parts, *before):
+    return pl.pallas_call(
+        sum_kernel,
+        out_shape=jax.ShapeDtypeStruct(parts[0].shape, f32),
+        in_specs=[pl.BlockSpec(memory_space=pltpu.VMEM)] * 4
+        + [pl.BlockSpec(memory_space=pl.ANY)] * len(before),
+        out_specs=pl.BlockSpec(memory_space=pltpu.VMEM),
+        compiler_params=params(2, False),
+        cost_estimate=cost(3 * parts[0].size, 5 * parts[0].size * 4),
+    )(*parts, *before)
+
+
+def scatter_group(parts, count):
+    return sum_four([parts[0]] + [exchange(parts[k], k, count) for k in range(1, group)])
+
+
+def sum_over_groups(total, count, *before):
     stride = group
     while stride < count:
         if count // stride % 4 == 0:
-            r1, r2, r3 = (exchange(total, stride * j, count) for j in (1, 2, 3))
-            total = (total + r1) + (r2 + r3)
+            got = [total] + [exchange(total, stride * j, count) for j in (1, 2, 3)]
+            total = sum_four(got, *before)
             stride *= 4
         else:
             total = total + exchange(total, stride, count)
@@ -430,20 +494,26 @@
     depth, slices = w_slice.shape
     heads = width // depth
     hm = heads * slices
-    block = min(1024, rows)
-    grid = (rows // block,)
     unit = 2 * rows * width * width
     smem = pl.BlockSpec(memory_space=pltpu.SMEM)
-    by_rows = pl.BlockSpec((block, width), lambda i: (i, 0))
-    by_cols = pl.BlockSpec((hm, block), lambda i: (0, i))
-    aux_spec = pl.BlockSpec((3 * heads, block), lambda i: (0, i))
-    pack_rows = 2 * (width // 128) * slices + 32
-    piece = (pack_rows // group, 128)
+
+    def blocks(size):
+        return (
+            (rows // size,),
+            pl.BlockSpec((size, width), lambda i: (i, 0)),
+            pl.BlockSpec((hm, size), lambda i: (0, i)),
+            pl.BlockSpec((3 * heads, size), lambda i: (0, i)),
+        )
 
     def like(shape, dtype):
         return jax.ShapeDtypeStruct(shape, dtype)
 
-    mid, wt, aux, sw, sb, wc, *sends = pl.pallas_call(
+    temp = temp_vec.reshape(1, depth)
+    half = (2 * slices + 8, 128)
+    quarter = (width // group, width)
+    block = min(2048, rows)
+    grid, by_rows, by_cols, aux_spec = blocks(block)
+    mid, wt, aux, sw, sb, w_cat, keep, send, *wc = pl.pallas_call(
         functools.partial(stats_kernel, heads, slices),
         grid=grid,
         in_specs=[
@@ -455,6 +525,7 @@
             full((depth, slices)),
             full((1, depth)),
             full((width, width)),
+            full((3, depth, depth)),
         ],
         out_specs=[
             by_rows,
@@ -462,49 +533,59 @@
             aux_spec,
             full((hm + 16, width)),
             full((width, hm)),
-            full((hm, width)),
+            full((depth, 128)),
+            full(half),
+            full(half),
         ]
-        + [full(piece)] * group,
+        + [full(quarter)] * group,
         out_shape=[
             like((rows, width), bf16),
             like((hm, rows), bf16),
             like((3 * heads, rows), f32),
             like((hm + 16, width), bf16),
             like((width, hm), bf16),
-            like((hm, width), f32),
+            like((depth, 128), bf16),
+            like(half, f32),
+            like(half, f32),
         ]
-        + [like(piece, f32)] * group,
+        + [like(quarter, f32)] * group,
         scratch_shapes=[
             pltpu.VMEM((hm, width), f32),
             pltpu.VMEM((hm, 128), f32),
-            pltpu.VMEM((pack_rows, 128), f32),
+            pltpu.VMEM((hm, width), f32),
+            pltpu.VMEM((2,) + half, f32),
         ],
-        compiler_params=params(),
+        compiler_params=params(56),
         cost_estimate=cost(4 * unit, rows * width * 8, rows * hm),
-    )(owned, valid.reshape(1, rows), feats, cotangent, w_mid, w_slice, temp_vec.reshape(1, depth), w_out)
-
-    pieces = gather_group(sum_over_groups(sends, count), count)
-
-    quarter = (width // group, width)
-    lhs, mw, yt, dn, grad_qkv, *sends = pl.pallas_call(
+    )(owned, valid.reshape(1, rows), feats, cotangent, w_mid, w_slice, temp, w_out, w_qkv)
+
+    own = keep + exchange(send, 1, count)
+    stride = 2
+    while stride < count:
+        own = own + exchange(own, stride, count)
+        stride *= 2
+    other = exchange(own, 1, count)
+
+    parts = lax.optimization_barrier((*wc, other))
+    wc_total = scatter_group(parts[:group], count)
+    lhs, mw, mixed_t, yt, dn, grad_qkv = pl.pallas_call(
         functools.partial(tokens_kernel, heads, slices),
         out_shape=[
             like((2 * hm + 16, width), bf16),
             like((hm, width), bf16),
+            like((width, hm), bf16),
             like((width, 2 * hm), bf16),
             like((hm, 128), f32),
             like((3, depth, depth), f32),
-        ]
-        + [like(quarter, f32)] * group,
-        scratch_shapes=[pltpu.VMEM((pack_rows, 128), f32), pltpu.VMEM((width, width), f32)],
-        compiler_params=params(False),
+        ],
+        scratch_shapes=[pltpu.VMEM((2,) + half, f32)],
+        compiler_params=params(8, False),
         cost_estimate=cost(30 * width**3, 4 * width * width * 4, hm * hm),
-    )(*pieces, w_qkv, w_out, sw, sb, wc)
-
-    out_parts = gather_group(sum_over_groups(sends, count), count)
-
-    more = slices // group
-    larger = (width // group + more, width)
+    )(own, other, w_cat, w_out, sw, sb)
+
+    larger = (width // group + slices // group, width)
+    block = min(512, rows)
+    grid, by_rows, by_cols, aux_spec = blocks(block)
     dmt, *sends = pl.pallas_call(
         functools.partial(backward_kernel, heads, slices),
         grid=grid,
@@ -517,7 +598,8 @@
             full((hm, width)),
             full((width, 2 * hm)),
             full((hm, 128)),
-            full((depth, 1)),
+            full((1, depth)),
+            pl.BlockSpec(memory_space=pl.ANY),
         ],
         out_specs=[by_cols] + [full(larger)] * group,
         out_shape=[like((width, rows), bf16)] + [like(larger, f32)] * group,
@@ -527,34 +609,53 @@
             pltpu.VMEM((hm + 16, width), f32),
             pltpu.VMEM((group,) + larger, f32),
         ],
-        compiler_params=params(),
+        compiler_params=params(56),
         cost_estimate=cost(8 * unit, rows * width * 8, rows * hm),
-    )(aux, mid, cotangent, feats, lhs, mw, yt, dn, temp_vec.reshape(depth, 1))
-
-    mid_parts = gather_group(sum_over_groups(sends, count), count)
-
-    attended, feats_grad = pl.pallas_call(
+    )(aux, mid, cotangent, feats, lhs, mw, yt, dn, temp, wc_total)
+
+    mid_total = scatter_group(sends, count)
+    wc_total = sum_over_groups(wc_total, count, sends[1])
+    out_parts = gather_group(wc_total, count)
+
+    block = min(1024, rows)
+    grid, by_rows, by_cols, aux_spec = blocks(block)
+    attended, feats_grad, token = pl.pallas_call(
         rows_kernel,
         grid=grid,
-        in_specs=[by_cols, by_cols, full((hm, width)), full((width, width))],
-        out_specs=[by_rows, by_rows],
-        out_shape=[like((rows, width), bf16)] * 2,
-        compiler_params=params(),
+        in_specs=[
+            by_cols,
+            by_cols,
+            full((hm, width)),
+            full((width, width)),
+            pl.BlockSpec(memory_space=pl.ANY),
+        ],
+        out_specs=[by_rows, by_rows, full((8, 128))],
+        out_shape=[like((rows, width), bf16)] * 2 + [like((8, 128), f32)],
+        compiler_params=params(56),
         cost_estimate=cost(2 * unit, rows * width * 8),
-    )(wt, dmt, mw, w_mid)
-
-    grad_w_mid, grad_w_out, grad_w_slice, grad_temp = pl.pallas_call(
+    )(wt, dmt, mw, w_mid, mid_total)
+
+    mid_total = sum_over_groups(mid_total, count, token)
+    grad_w_out = pl.pallas_call(
+        grad_out_kernel,
+        out_shape=like((width, width), f32),
+        scratch_shapes=[pltpu.VMEM((hm, width), f32)],
+        compiler_params=params(8, False),
+        cost_estimate=cost(4 * width**3, 3 * width * width * 4),
+    )(*out_parts, mixed_t)
+
+    mid_parts = gather_group(mid_total, count)
+    grad_w_mid, grad_w_slice, grad_temp = pl.pallas_call(
         functools.partial(finish_kernel, depth),
         out_shape=[
-            like((width, width), f32),
             like((width, width), f32),
             like((depth, slices), f32),
             like((1, depth), f32),
         ],
         scratch_shapes=[pltpu.VMEM((slices, 128), f32)],
-        compiler_params=params(False),
-        cost_estimate=cost(0, 4 * width * width * 4),
-    )(*out_parts, *mid_parts)
+        compiler_params=params(8, False),
+        cost_estimate=cost(0, 2 * width * width * 4),
+    )(*mid_parts)
     return (
         attended,
         feats_grad,

time: 78 us -> 86.4 us (1.11)
  local copies, waits for them, and re-layouts: 2.6 us -> 9.39 us
  waiting for transfers between devices: 13.1 us -> 17.3 us
  Pallas kernels: 32.2 us -> 30.8 us
  other arithmetic: 1.71 us -> 0.79 us
    unnamed x28 -> x32, local copies, waits for them, and re-layouts: 1.9 us -> 9.39 us
    ppermute x27 -> x23, waiting for transfers between devices: 13.1 us -> 17.3 us  [exchange(): return lax.ppermute(x, 'node', [(i, i ^ k) for i in range(count)])]
    pallas_call x1, Pallas kernels: 6.55 us -> 3.1 us  [shards(): pl.pallas_call(functools.partial(tokens_kernel, heads, slices), out_shape...]
    pallas_call x1, Pallas kernels: 9.03 us -> 12.1 us  [shards(): pl.pallas_call(functools.partial(backward_kernel, heads, slices), grid=gr...]
    pallas_call x1, Pallas kernels: 1.98 us -> 0.74 us  [shards(): pl.pallas_call(functools.partial(finish_kernel, depth), out_shape=[like((...]
    pallas_call x0 -> x5, Pallas kernels: none -> 1.04 us  [the longest x1 0.97 us: shards(): pl.pallas_call(grad_out_kernel, out_shape=like((width, width), f32), scra...]
    add x6 -> x4, other arithmetic: 1.71 us -> 0.79 us  [the longest x1 0.78 us: shards(): own = keep + exchange(send, 1, count)]
    ppermute x27 -> x23, starting transfers between devices: 26.3 us -> 25.9 us  [exchange(): return lax.ppermute(x, 'node', [(i, i ^ k) for i in range(count)])]
  transfers between devices with their start and end apart: 27 -> 23, of which waited for: 7 -> 8; matrix products, arithmetic and copies ran while one was open for 2% -> 0% of each run, Pallas kernels for 19% -> 26%
where the time goes in v3:
time: 86.4 us; the launch traced here: 85.7 us
  Pallas kernels  30.8 us (36%)
  starting transfers between devices  25.9 us (30%)
  waiting for transfers between devices  17.3 us (20%)
  local copies, waits for them, and re-layouts  9.39 us (11%)
  between operations  1.41 us (2%)
    ppermute x23, starting transfers between devices, exchange(): return lax.ppermute(x, 'node', [(i, i ^ k) for i in range(count)])  25.9 us
    ppermute x23, waiting for transfers between devices, exchange(): return lax.ppermute(x, 'node', [(i, i ^ k) for i in range(count)])  17.3 us
    pallas_call x1, Pallas kernels, shards(): pl.pallas_call(functools.partial(backward_kernel, heads, slices), grid=gr...  12.1 us
    unnamed x32, local copies, waits for them, and re-layouts  9.39 us
    pallas_call x1, Pallas kernels, shards(): pl.pallas_call(functools.partial(stats_kernel, heads, slices), grid=grid,...  8.15 us
    pallas_call x1, Pallas kernels, shards(): pl.pallas_call(rows_kernel, grid=grid, in_specs=[by_cols, by_cols, full((...  5.68 us
    pallas_call x1, Pallas kernels, shards(): pl.pallas_call(functools.partial(tokens_kernel, heads, slices), out_shape...  3.1 us
  transfers between devices with their start and end apart: 23, of which 8 were waited for; matrix products, arithmetic and copies ran while one was open for 0% of the time, Pallas kernels for 26%

profile of v3, /device:TPU:0, one launch (start us, length us, event | category | flops | bytes accessed | tf_op | source)
XLA Modules:
  0.0 85.7 jit_solution(2958446403886385861)
XLA Ops:
  1.3 8.1 %shard_map.144 = (bf16[4096,256]{1,0:T(8,128)(2,1)}, bf16[256,4096]{1,0:T(8,128)(2,1)}, f32[24,4096]{1,0:T(8,128)}, bf16[272,256]{1,0:T(8,128)(2,1)}, bf16[256,2...) custom-call(s32[1]{0:T(128)S(6)} %copy.16.owned_ref, ...), custom_call_target="tpu_custom_call" | custom-call | flops 2147483648 | bytes 8388608 | tf_op jit(solution)/shard_map/pallas_call | solution.py:516
  10.0 1.1 %collective-permute-done = f32[72,128]{1,0:T(8,128)S(1)} collective-permute-done((f32[72,128]{1,0:T(8,128)}, f32[72,128]{1,0:T(8,128)S(1)}, u32[]{:S(2)}, u32[]{:S(2)}) %collective-permute-start) | collective-permute-done | bytes 36896 | tf_op jit(solution)/shard_map/ppermute | solution.py:452
  11.8 2.8 %collective-permute-start.1 = (f32[72,128]{1,0:T(8,128)S(1)}, f32[72,128]{1,0:T(8,128)S(1)}, u32[]{:S(2)}, u32[]{:S(2)}) collective-permute-start(f32[72,128]{1,0:T(8,128)S(1)} %add.12), channel_id=1, source_target_pairs={{0,2},{1,3},{2,0},{3,1},{4,6},{5,7},{6,4},{7,5},{8,10},{9,11},{10,... | collective-permute-start | bytes 110600 | tf_op jit(solution)/shard_map/ppermute | solution.py:452
  14.7 1.9 %collective-permute-done.1 = f32[72,128]{1,0:T(8,128)S(1)} collective-permute-done((f32[72,128]{1,0:T(8,128)S(1)}, f32[72,128]{1,0:T(8,128)S(1)}, u32[]{:S(2)}, u32[]{:S(2)}) %collective-permute-start.1) | collective-permute-done | bytes 36896 | tf_op jit(solution)/shard_map/ppermute | solution.py:452
  16.6 2.1 %collective-permute-start.2 = (f32[72,128]{1,0:T(8,128)S(1)}, f32[72,128]{1,0:T(8,128)S(1)}, u32[]{:S(2)}, u32[]{:S(2)}) collective-permute-start(f32[72,128]{1,0:T(8,128)S(1)} %add.13), channel_id=1, source_target_pairs={{0,4},{1,5},{2,6},{3,7},{4,0},{5,1},{6,2},{7,3},{8,12},{9,13},{10,... | collective-permute-start | bytes 110600 | tf_op jit(solution)/shard_map/ppermute | solution.py:452
  18.7 1.9 %collective-permute-done.2 = f32[72,128]{1,0:T(8,128)S(1)} collective-permute-done((f32[72,128]{1,0:T(8,128)S(1)}, f32[72,128]{1,0:T(8,128)S(1)}, u32[]{:S(2)}, u32[]{:S(2)}) %collective-permute-start.2) | collective-permute-done | bytes 36896 | tf_op jit(solution)/shard_map/ppermute | solution.py:452
  20.7 3.0 %collective-permute-start.3 = (f32[72,128]{1,0:T(8,128)S(1)}, f32[72,128]{1,0:T(8,128)S(1)}, u32[]{:S(2)}, u32[]{:S(2)}) collective-permute-start(f32[72,128]{1,0:T(8,128)S(1)} %add.14), channel_id=1, source_target_pairs={{0,8},{1,9},{2,10},{3,11},{4,12},{5,13},{6,14},{7,15},{8,0},{9,1},... | collective-permute-start | bytes 110600 | tf_op jit(solution)/shard_map/ppermute | solution.py:452
  23.7 1.9 %collective-permute-done.3 = f32[72,128]{1,0:T(8,128)S(1)} collective-permute-done((f32[72,128]{1,0:T(8,128)S(1)}, f32[72,128]{1,0:T(8,128)S(1)}, u32[]{:S(2)}, u32[]{:S(2)}) %collective-permute-start.3) | collective-permute-done | bytes 36896 | tf_op jit(solution)/shard_map/ppermute | solution.py:452
  25.6 1.2 %collective-permute-done.4.got_ref = f32[72,128]{1,0:T(8,128)S(1)} collective-permute-done((f32[72,128]{1,0:T(8,128)S(1)}, f32[72,128]{1,0:T(8,128)S(1)}, u32[]{:S(2)}, u32[]{:S(2)}) %collective-permute-start.4) | collective-permute-done | bytes 36896 | tf_op jit(solution)/shard_map/ppermute | solution.py:452
  27.0 1.8 %collective-permute-start.6 = (f32[64,256]{1,0:T(8,128)}, f32[64,256]{1,0:T(8,128)S(1)}, u32[]{:S(2)}, u32[]{:S(2)}) collective-permute-start(f32[64,256]{1,0:T(8,128)} %get-tuple-element.58), channel_id=1, source_target_pairs={{0,2},{1,3},{2,0},{3,1},{4,6},{5,7},{6,4},{7,5},{8,10},{9,11},{10,... | collective-permute-start | bytes 196616 | tf_op jit(solution)/shard_map/ppermute | solution.py:452
  28.9 0.9 %copy-done.12 = bf16[272,256]{1,0:T(8,128)(2,1)S(1)} copy-done((bf16[272,256]{1,0:T(8,128)(2,1)S(1)}, bf16[272,256]{1,0:T(8,128)(2,1)}, u32[]{:S(2)}) %copy-start.12) | copy-done | bytes 139288
  31.4 3.1 %shard_map.145 = (bf16[528,256]{1,0:T(8,128)(2,1)S(1)}, bf16[256,256]{1,0:T(8,128)(2,1)S(1)}, bf16[256,256]{1,0:T(8,128)(2,1)S(1)}, bf16[256,512]{1,0:T(8,128)(2...) custom-call(f32[72,128]{1,0:T(8,128)S(1)} %add.15.own_ref, f32[72,128]{1,0:T(8,128)S(1)} %collective-permute-done.4.got_ref, ...), custom_call_target="tpu_custom_call" | custom-call | flops 503316480 | bytes 1048576 | tf_op jit(solution)/shard_map/pallas_call | solution.py:571
  37.2 4.1 %collective-permute-start.19 = (f32[64,256]{1,0:T(8,128)S(1)}, f32[64,256]{1,0:T(8,128)S(1)}, u32[]{:S(2)}, u32[]{:S(2)}) collective-permute-start(f32[64,256]{1,0:T(8,128)S(1)} %shard_map.146._.r0), channel_id=1, source_target_pairs={{0,12},{1,13},{2,14},{3,15},{4,8},{5,9},{6,10},{7,11},{8,4},{9,5},... | collective-permute-start | bytes 196616 | tf_op jit(solution)/shard_map/ppermute | solution.py:452
  41.3 12.1 %shard_map.147 = (bf16[256,4096]{1,0:T(8,128)(2,1)}, f32[72,256]{1,0:T(8,128)}, f32[72,256]{1,0:T(8,128)}, f32[72,256]{1,0:T(8,128)}, f32[72,256]{1,0:T(8,128)}) custom-call(f32[24,4096]{1,0:T(8,128)} %get-tuple-element.41.aux_ref, bf16[4096,256]{1,0:T(8,128)(2,1)} %get-tuple-element.42.mid_ref, bf16[4096,256]{1,0:T(8,128)(2,1)} %cot_ref.3, ...), custom_call_target="tpu_custom_call" | custom-call | flops 4294967296 | bytes 8388608 | tf_op jit(solution)/shard_map/pallas_call | solution.py:589
  53.4 1.6 %collective-permute-start.9 = (f32[72,256]{1,0:T(8,128)}, f32[72,256]{1,0:T(8,128)S(1)}, u32[]{:S(2)}, u32[]{:S(2)}) collective-permute-start(f32[72,256]{1,0:T(8,128)} %get-tuple-element.63), channel_id=1, source_target_pairs={{0,2},{1,3},{2,0},{3,1},{4,6},{5,7},{6,4},{7,5},{8,10},{9,11},{10,... | collective-permute-start | bytes 221192 | tf_op jit(solution)/shard_map/ppermute | solution.py:452
  55.6 1.2 %collective-permute-start.17 = (f32[64,256]{1,0:T(8,128)}, f32[64,256]{1,0:T(8,128)S(1)}, u32[]{:S(2)}, u32[]{:S(2)}) collective-permute-start(f32[64,256]{1,0:T(8,128)} %copy-done.2), channel_id=1, source_target_pairs={{0,4},{1,5},{2,6},{3,7},{4,0},{5,1},{6,2},{7,3},{8,12},{9,13},{10,... | collective-permute-start | bytes 196616 | tf_op jit(solution)/shard_map/ppermute | solution.py:452
  56.8 4.4 %collective-permute-done.18.r2 = f32[64,256]{1,0:T(8,128)S(1)} collective-permute-done((f32[64,256]{1,0:T(8,128)}, f32[64,256]{1,0:T(8,128)S(1)}, u32[]{:S(2)}, u32[]{:S(2)}) %collective-permute-start.18) | collective-permute-done | bytes 65568 | tf_op jit(solution)/shard_map/ppermute | solution.py:452
  64.5 1.8 %collective-permute-start.13 = (f32[72,256]{1,0:T(8,128)S(1)}, f32[72,256]{1,0:T(8,128)S(1)}, u32[]{:S(2)}, u32[]{:S(2)}) collective-permute-start(f32[72,256]{1,0:T(8,128)S(1)} %shard_map.148._.r0), channel_id=1, source_target_pairs={{0,12},{1,13},{2,14},{3,15},{4,8},{5,9},{6,10},{7,11},{8,4},{9,5},... | collective-permute-start | bytes 221192 | tf_op jit(solution)/shard_map/ppermute | solution.py:452
  66.4 2.6 %collective-permute-start.11 = (f32[72,256]{1,0:T(8,128)S(1)}, f32[72,256]{1,0:T(8,128)S(1)}, u32[]{:S(2)}, u32[]{:S(2)}) collective-permute-start(f32[72,256]{1,0:T(8,128)S(1)} %shard_map.148._.r0), channel_id=1, source_target_pairs={{0,4},{1,5},{2,6},{3,7},{4,0},{5,1},{6,2},{7,3},{8,12},{9,13},{10,... | collective-permute-start | bytes 221192 | tf_op jit(solution)/shard_map/ppermute | solution.py:452
  69.0 5.7 %shard_map.149 = (bf16[4096,256]{1,0:T(8,128)(2,1)}, bf16[4096,256]{1,0:T(8,128)(2,1)}, f32[8,128]{1,0:T(8,128)}) custom-call(bf16[256,4096]{1,0:T(8,128)(2,1)} %get-tuple-element.40.wt_ref, bf16[256,4096]{1,0:T(8,128)(2,1)} %get-tuple-element.60.dmt_ref, bf16[256,256]{1,0:T(8,128)(2,1)} %copy-done.4, bf16[256,256]{1,0:T(8,128)(2,1)} %w_mid_ref.3, ...), custom_call_target="tpu_custom_call" | custom-call | flops 1073741824 | bytes 8388608 | tf_op jit(solution)/shard_map/pallas_call | solution.py:622
  77.0 1.5 %collective-permute-start.15 = (f32[72,256]{1,0:T(8,128)S(1)}, f32[72,256]{1,0:T(8,128)S(1)}, u32[]{:S(2)}, u32[]{:S(2)}) collective-permute-start(f32[72,256]{1,0:T(8,128)S(1)} %shard_map.150.m0), channel_id=1, source_target_pairs={{0,2},{1,3},{2,0},{3,1},{4,6},{5,7},{6,4},{7,5},{8,10},{9,11},{10,... | collective-permute-start | bytes 221192 | tf_op jit(solution)/shard_map/ppermute | solution.py:452
  78.5 1.0 %collective-permute-start.21 = (f32[64,256]{1,0:T(8,128)S(1)}, f32[64,256]{1,0:T(8,128)S(1)}, u32[]{:S(2)}, u32[]{:S(2)}) collective-permute-start(f32[64,256]{1,0:T(8,128)S(1)} %shard_map.152.o0), channel_id=1, source_target_pairs={{0,2},{1,3},{2,0},{3,1},{4,6},{5,7},{6,4},{7,5},{8,10},{9,11},{10,... | collective-permute-start | bytes 196616 | tf_op jit(solution)/shard_map/ppermute | solution.py:452
  79.5 4.5 %collective-permute-done.21.o2 = f32[64,256]{1,0:T(8,128)S(1)} collective-permute-done((f32[64,256]{1,0:T(8,128)S(1)}, f32[64,256]{1,0:T(8,128)S(1)}, u32[]{:S(2)}, u32[]{:S(2)}) %collective-permute-start.21) | collective-permute-done | bytes 65568 | tf_op jit(solution)/shard_map/ppermute | solution.py:452
  83.9 1.0 %shard_map.153 = f32[256,256]{1,0:T(8,128)} custom-call(f32[64,256]{1,0:T(8,128)S(1)} %shard_map.152.o0, f32[64,256]{1,0:T(8,128)S(1)} %collective-permute-done.20.o1, f32[64,256]{1,0:T(8,128)S(1)} %collective-permute-done.21.o2, f32[64,256]{1,0:T(8,128)S(1)} %collective-permute-done.22.o3, bf16[256,256]{1,0:T(8,128)(2,1)S(1)} %get-tuple-element.69.mixed_t_ref), custom_call_target="tpu_custom_call" | custom-call | flops 67108864 | bytes 786432 | tf_op jit(solution)/shard_map/pallas_call | solution.py:639
  (68 shorter events, 12.9 us)
Async XLA Ops:
  1.3 27.6 %copy-start.9 = (bf16[256,256]{1,0:T(8,128)(2,1)S(1)}, bf16[256,256]{1,0:T(8,128)(2,1)}, u32[]{:S(2)}) copy-start(bf16[256,256]{1,0:T(8,128)(2,1)} %w_out_ref.3) | copy-start | bytes 393220
  9.5 1.6 %collective-permute-start = (f32[72,128]{1,0:T(8,128)}, f32[72,128]{1,0:T(8,128)S(1)}, u32[]{:S(2)}, u32[]{:S(2)}) collective-permute-start(f32[72,128]{1,0:T(8,128)} %get-tuple-element.44), channel_id=1, source_target_pairs={{0,1},{1,0},{2,3},{3,2},{4,5},{5,4},{6,7},{7,6},{8,9},{9,8},{10,11... | collective-permute-start | bytes 110600 | tf_op jit(solution)/shard_map/ppermute | solution.py:452
  11.8 4.8 %collective-permute-start.1 = (f32[72,128]{1,0:T(8,128)S(1)}, f32[72,128]{1,0:T(8,128)S(1)}, u32[]{:S(2)}, u32[]{:S(2)}) collective-permute-start(f32[72,128]{1,0:T(8,128)S(1)} %add.12), channel_id=1, source_target_pairs={{0,2},{1,3},{2,0},{3,1},{4,6},{5,7},{6,4},{7,5},{8,10},{9,11},{10,... | collective-permute-start | bytes 110600 | tf_op jit(solution)/shard_map/ppermute | solution.py:452
  16.6 4.0 %collective-permute-start.2 = (f32[72,128]{1,0:T(8,128)S(1)}, f32[72,128]{1,0:T(8,128)S(1)}, u32[]{:S(2)}, u32[]{:S(2)}) collective-permute-start(f32[72,128]{1,0:T(8,128)S(1)} %add.13), channel_id=1, source_target_pairs={{0,4},{1,5},{2,6},{3,7},{4,0},{5,1},{6,2},{7,3},{8,12},{9,13},{10,... | collective-permute-start | bytes 110600 | tf_op jit(solution)/shard_map/ppermute | solution.py:452
  20.7 5.0 %collective-permute-start.3 = (f32[72,128]{1,0:T(8,128)S(1)}, f32[72,128]{1,0:T(8,128)S(1)}, u32[]{:S(2)}, u32[]{:S(2)}) collective-permute-start(f32[72,128]{1,0:T(8,128)S(1)} %add.14), channel_id=1, source_target_pairs={{0,8},{1,9},{2,10},{3,11},{4,12},{5,13},{6,14},{7,15},{8,0},{9,1},... | collective-permute-start | bytes 110600 | tf_op jit(solution)/shard_map/ppermute | solution.py:452
  25.6 1.2 %collective-permute-start.4 = (f32[72,128]{1,0:T(8,128)S(1)}, f32[72,128]{1,0:T(8,128)S(1)}, u32[]{:S(2)}, u32[]{:S(2)}) collective-permute-start(f32[72,128]{1,0:T(8,128)S(1)} %add.15.own_ref), channel_id=1, source_target_pairs={{0,1},{1,0},{2,3},{3,2},{4,5},{5,4},{6,7},{7,6},{8,9},{9,8},{10,11... | collective-permute-start | bytes 110600 | tf_op jit(solution)/shard_map/ppermute | solution.py:452
  26.8 9.7 %collective-permute-start.5 = (f32[64,256]{1,0:T(8,128)}, f32[64,256]{1,0:T(8,128)S(1)}, u32[]{:S(2)}, u32[]{:S(2)}) collective-permute-start(f32[64,256]{1,0:T(8,128)} %get-tuple-element.57), channel_id=1, source_target_pairs={{0,1},{1,0},{2,3},{3,2},{4,5},{5,4},{6,7},{7,6},{8,9},{9,8},{10,11... | collective-permute-start | bytes 196616 | tf_op jit(solution)/shard_map/ppermute | solution.py:452
  27.0 9.5 %collective-permute-start.6 = (f32[64,256]{1,0:T(8,128)}, f32[64,256]{1,0:T(8,128)S(1)}, u32[]{:S(2)}, u32[]{:S(2)}) collective-permute-start(f32[64,256]{1,0:T(8,128)} %get-tuple-element.58), channel_id=1, source_target_pairs={{0,2},{1,3},{2,0},{3,1},{4,6},{5,7},{6,4},{7,5},{8,10},{9,11},{10,... | collective-permute-start | bytes 196616 | tf_op jit(solution)/shard_map/ppermute | solution.py:452
  28.8 7.7 %collective-permute-start.7 = (f32[64,256]{1,0:T(8,128)}, f32[64,256]{1,0:T(8,128)S(1)}, u32[]{:S(2)}, u32[]{:S(2)}) collective-permute-start(f32[64,256]{1,0:T(8,128)} %get-tuple-element.59), channel_id=1, source_target_pairs={{0,3},{1,2},{2,1},{3,0},{4,7},{5,6},{6,5},{7,4},{8,11},{9,10},{10,... | collective-permute-start | bytes 196616 | tf_op jit(solution)/shard_map/ppermute | solution.py:452
  37.2 18.4 %collective-permute-start.19 = (f32[64,256]{1,0:T(8,128)S(1)}, f32[64,256]{1,0:T(8,128)S(1)}, u32[]{:S(2)}, u32[]{:S(2)}) collective-permute-start(f32[64,256]{1,0:T(8,128)S(1)} %shard_map.146._.r0), channel_id=1, source_target_pairs={{0,12},{1,13},{2,14},{3,15},{4,8},{5,9},{6,10},{7,11},{8,4},{9,5},... | collective-permute-start | bytes 196616 | tf_op jit(solution)/shard_map/ppermute | solution.py:452
  53.4 10.2 %collective-permute-start.9 = (f32[72,256]{1,0:T(8,128)}, f32[72,256]{1,0:T(8,128)S(1)}, u32[]{:S(2)}, u32[]{:S(2)}) collective-permute-start(f32[72,256]{1,0:T(8,128)} %get-tuple-element.63), channel_id=1, source_target_pairs={{0,2},{1,3},{2,0},{3,1},{4,6},{5,7},{6,4},{7,5},{8,10},{9,11},{10,... | collective-permute-start | bytes 221192 | tf_op jit(solution)/shard_map/ppermute | solution.py:452
  55.0 8.6 %collective-permute-start.10 = (f32[72,256]{1,0:T(8,128)}, f32[72,256]{1,0:T(8,128)S(1)}, u32[]{:S(2)}, u32[]{:S(2)}) collective-permute-start(f32[72,256]{1,0:T(8,128)} %get-tuple-element.64), channel_id=1, source_target_pairs={{0,3},{1,2},{2,1},{3,0},{4,7},{5,6},{6,5},{7,4},{8,11},{9,10},{10,... | collective-permute-start | bytes 221192 | tf_op jit(solution)/shard_map/ppermute | solution.py:452
  55.0 8.6 %collective-permute-start.8 = (f32[72,256]{1,0:T(8,128)}, f32[72,256]{1,0:T(8,128)S(1)}, u32[]{:S(2)}, u32[]{:S(2)}) collective-permute-start(f32[72,256]{1,0:T(8,128)} %get-tuple-element.62.rest_0_), channel_id=1, source_target_pairs={{0,1},{1,0},{2,3},{3,2},{4,5},{5,4},{6,7},{7,6},{8,9},{9,8},{10,11... | collective-permute-start | bytes 221192 | tf_op jit(solution)/shard_map/ppermute | solution.py:452
  55.6 5.6 %collective-permute-start.18 = (f32[64,256]{1,0:T(8,128)}, f32[64,256]{1,0:T(8,128)S(1)}, u32[]{:S(2)}, u32[]{:S(2)}) collective-permute-start(f32[64,256]{1,0:T(8,128)} %copy-done.2), channel_id=1, source_target_pairs={{0,8},{1,9},{2,10},{3,11},{4,12},{5,13},{6,14},{7,15},{8,0},{9,1},... | collective-permute-start | bytes 196616 | tf_op jit(solution)/shard_map/ppermute | solution.py:452
  55.6 5.9 %collective-permute-start.17 = (f32[64,256]{1,0:T(8,128)}, f32[64,256]{1,0:T(8,128)S(1)}, u32[]{:S(2)}, u32[]{:S(2)}) collective-permute-start(f32[64,256]{1,0:T(8,128)} %copy-done.2), channel_id=1, source_target_pairs={{0,4},{1,5},{2,6},{3,7},{4,0},{5,1},{6,2},{7,3},{8,12},{9,13},{10,... | collective-permute-start | bytes 196616 | tf_op jit(solution)/shard_map/ppermute | solution.py:452
  63.3 16.2 %collective-permute-start.22 = (f32[64,256]{1,0:T(8,128)S(1)}, f32[64,256]{1,0:T(8,128)S(1)}, u32[]{:S(2)}, u32[]{:S(2)}) collective-permute-start(f32[64,256]{1,0:T(8,128)S(1)} %shard_map.152.o0), channel_id=1, source_target_pairs={{0,3},{1,2},{2,1},{3,0},{4,7},{5,6},{6,5},{7,4},{8,11},{9,10},{10,... | collective-permute-start | bytes 196616 | tf_op jit(solution)/shard_map/ppermute | solution.py:452
  64.5 10.1 %collective-permute-start.13 = (f32[72,256]{1,0:T(8,128)S(1)}, f32[72,256]{1,0:T(8,128)S(1)}, u32[]{:S(2)}, u32[]{:S(2)}) collective-permute-start(f32[72,256]{1,0:T(8,128)S(1)} %shard_map.148._.r0), channel_id=1, source_target_pairs={{0,12},{1,13},{2,14},{3,15},{4,8},{5,9},{6,10},{7,11},{8,4},{9,5},... | collective-permute-start | bytes 221192 | tf_op jit(solution)/shard_map/ppermute | solution.py:452
  66.3 8.4 %collective-permute-start.12 = (f32[72,256]{1,0:T(8,128)S(1)}, f32[72,256]{1,0:T(8,128)S(1)}, u32[]{:S(2)}, u32[]{:S(2)}) collective-permute-start(f32[72,256]{1,0:T(8,128)S(1)} %shard_map.148._.r0), channel_id=1, source_target_pairs={{0,8},{1,9},{2,10},{3,11},{4,12},{5,13},{6,14},{7,15},{8,0},{9,1},... | collective-permute-start | bytes 221192 | tf_op jit(solution)/shard_map/ppermute | solution.py:452
  66.4 8.3 %collective-permute-start.11 = (f32[72,256]{1,0:T(8,128)S(1)}, f32[72,256]{1,0:T(8,128)S(1)}, u32[]{:S(2)}, u32[]{:S(2)}) collective-permute-start(f32[72,256]{1,0:T(8,128)S(1)} %shard_map.148._.r0), channel_id=1, source_target_pairs={{0,4},{1,5},{2,6},{3,7},{4,0},{5,1},{6,2},{7,3},{8,12},{9,13},{10,... | collective-permute-start | bytes 221192 | tf_op jit(solution)/shard_map/ppermute | solution.py:452
  76.3 8.6 %collective-permute-start.16 = (f32[72,256]{1,0:T(8,128)S(1)}, f32[72,256]{1,0:T(8,128)S(1)}, u32[]{:S(2)}, u32[]{:S(2)}) collective-permute-start(f32[72,256]{1,0:T(8,128)S(1)} %shard_map.150.m0), channel_id=1, source_target_pairs={{0,3},{1,2},{2,1},{3,0},{4,7},{5,6},{6,5},{7,4},{8,11},{9,10},{10,... | collective-permute-start | bytes 221192 | tf_op jit(solution)/shard_map/ppermute | solution.py:452
  77.0 7.9 %collective-permute-start.15 = (f32[72,256]{1,0:T(8,128)S(1)}, f32[72,256]{1,0:T(8,128)S(1)}, u32[]{:S(2)}, u32[]{:S(2)}) collective-permute-start(f32[72,256]{1,0:T(8,128)S(1)} %shard_map.150.m0), channel_id=1, source_target_pairs={{0,2},{1,3},{2,0},{3,1},{4,6},{5,7},{6,4},{7,5},{8,10},{9,11},{10,... | collective-permute-start | bytes 221192 | tf_op jit(solution)/shard_map/ppermute | solution.py:452
  78.5 6.4 %collective-permute-start.14 = (f32[72,256]{1,0:T(8,128)S(1)}, f32[72,256]{1,0:T(8,128)S(1)}, u32[]{:S(2)}, u32[]{:S(2)}) collective-permute-start(f32[72,256]{1,0:T(8,128)S(1)} %shard_map.150.m0), channel_id=1, source_target_pairs={{0,1},{1,0},{2,3},{3,2},{4,5},{5,4},{6,7},{7,6},{8,9},{9,8},{10,11... | collective-permute-start | bytes 221192 | tf_op jit(solution)/shard_map/ppermute | solution.py:452
  78.5 5.5 %collective-permute-start.21 = (f32[64,256]{1,0:T(8,128)S(1)}, f32[64,256]{1,0:T(8,128)S(1)}, u32[]{:S(2)}, u32[]{:S(2)}) collective-permute-start(f32[64,256]{1,0:T(8,128)S(1)} %shard_map.152.o0), channel_id=1, source_target_pairs={{0,2},{1,3},{2,0},{3,1},{4,6},{5,7},{6,4},{7,5},{8,10},{9,11},{10,... | collective-permute-start | bytes 196616 | tf_op jit(solution)/shard_map/ppermute | solution.py:452
  79.5 4.5 %collective-permute-start.20 = (f32[64,256]{1,0:T(8,128)S(1)}, f32[64,256]{1,0:T(8,128)S(1)}, u32[]{:S(2)}, u32[]{:S(2)}) collective-permute-start(f32[64,256]{1,0:T(8,128)S(1)} %shard_map.152.o0), channel_id=1, source_target_pairs={{0,1},{1,0},{2,3},{3,2},{4,5},{5,4},{6,7},{7,6},{8,9},{9,8},{10,11... | collective-permute-start | bytes 196616 | tf_op jit(solution)/shard_map/ppermute | solution.py:452
  (15 other events, 45.1 us)

commit v4 on v3

--- a/solution.py
+++ b/solution.py
@@ -13,6 +13,7 @@
 eps_norm = 1e-05
 exact = lax.Precision.HIGHEST
 group = 4
+sub_block = 512
 mib = 1024 * 1024
 
 
@@ -88,10 +89,8 @@
     w_cat_ref,
     keep_ref,
     send_ref,
-    wc0,
-    wc1,
-    wc2,
-    wc3,
+    wc_keep_ref,
+    wc_send_ref,
     raw_acc,
     norm_acc,
     wc_acc,
@@ -175,9 +174,9 @@
         place = group_place()
         keep_ref[...] = pack[place & 1]
         send_ref[...] = pack[(place & 1) ^ 1]
-        rows = hm // group
-        for k, send in enumerate((wc0, wc1, wc2, wc3)):
-            send[...] = wc_acc[pl.ds(pl.multiple_of((place ^ k) * rows, 8), rows), :]
+        rows = hm // 2
+        for k, out in enumerate((wc_keep_ref, wc_send_ref)):
+            out[...] = wc_acc[pl.ds(pl.multiple_of(((place & 1) ^ k) * rows, 8), rows), :]
 
 
 def lanes_at(x, lane, *where):
@@ -202,12 +201,10 @@
     got_ref,
     w_cat_ref,
     w_out_ref,
-    sw_ref,
-    sb_ref,
-    lhs_ref,
     mw_ref,
     mixed_t_ref,
-    yt_ref,
+    dr_ref,
+    drt_ref,
     dn_ref,
     grad_qkv_ref,
     pack,
@@ -287,12 +284,9 @@
     d_raw_b = (d_tokens * inverse).astype(bf16)
     d_norm = -jnp.sum(d_tokens * raw, axis=1, keepdims=True) * inverse * inverse
     dn_ref[...] = jnp.broadcast_to(d_norm, dn_ref.shape)
-    top = sw_ref.shape[0]
-    lhs_ref[0:top, :] = sw_ref[...]
     spread_d = spread_matrix(width, depth)
-    lhs_ref[top : top + hm, :] = jnp.where(diagonal, nt(d_raw_b, spread_d), 0.0).astype(bf16)
-    yt_ref[:, 0:hm] = jnp.where(diagonal_t, nt(spread_d, d_raw_b), 0.0).astype(bf16)
-    yt_ref[:, hm : 2 * hm] = sb_ref[...]
+    dr_ref[...] = jnp.where(diagonal, nt(d_raw_b, spread_d), 0.0).astype(bf16)
+    drt_ref[...] = jnp.where(diagonal_t, nt(spread_d, d_raw_b), 0.0).astype(bf16)
 
     t_high, t_low = two_pieces(tokens)
     grads = tn(t_high, d_high) + tn(t_high, d_low) + tn(t_low, d_high)
@@ -308,9 +302,11 @@
     mid_ref,
     cot_ref,
     feats_ref,
-    lhs_ref,
+    sw_ref,
+    sb_ref,
     mw_ref,
-    yt_ref,
+    dr_ref,
+    drt_ref,
     dn_ref,
     temp_ref,
     _,
@@ -319,7 +315,8 @@
     send1,
     send2,
     send3,
-    stack,
+    lhs,
+    yt,
     grad_acc,
     small_acc,
     pack,
@@ -329,42 +326,60 @@
     depth = width // heads
     hm = heads * slices
     block = mid_ref.shape[0]
+    top = hm + 16
 
     @pl.when(step == 0)
     def _():
         grad_acc[...] = jnp.zeros_like(grad_acc)
         small_acc[...] = jnp.zeros_like(small_acc)
-
-    mid = mid_ref[...]
-    from_mid = nt(lhs_ref[...], mid)
-    from_cot = nt(mw_ref[...], cot_ref[...])
-    aux = aux_ref[...]
-    sums = []
-    for h in range(heads):
-        span = slice(h * slices, (h + 1) * slices)
-        inv_tau = aux[h : h + 1]
-        logits = from_mid[span] * inv_tau
-        weights = jnp.exp(logits - aux[heads + h : heads + h + 1])
-        d_weights = from_cot[span] + from_mid[hm + 16 + h * slices : hm + 16 + (h + 1) * slices]
-        d_weights = d_weights + dn_ref[span, 0:1]
-        mean = jnp.sum(weights * d_weights, axis=0, keepdims=True)
-        d_logits = weights * (d_weights - mean)
-        d_tau = jnp.sum(d_logits * logits, axis=0, keepdims=True)
-        sums.append(-d_tau * aux[2 * heads + h : 2 * heads + h + 1])
-        stack[span, :] = weights.astype(bf16)
-        stack[hm + h * slices : hm + (h + 1) * slices, :] = (d_logits * inv_tau).astype(bf16)
-    c_sum = jnp.concatenate(sums, axis=0)
-    c_high = c_sum.astype(bf16).astype(f32)
-    stack[2 * hm : 2 * hm + 2 * heads, :] = jnp.concatenate([c_high, c_sum - c_high], axis=0).astype(bf16)
-    d_mid = nn(yt_ref[...], stack[0 : 2 * hm, :])
+        lhs[0:top, :] = sw_ref[...]
+        lhs[top:, :] = dr_ref[...]
+        yt[:, 0:hm] = drt_ref[...]
+        yt[:, hm:] = sb_ref[...]
+
     temp = jnp.broadcast_to(temp_ref[...].astype(f32), (16, depth)).astype(bf16)
     same = (rows_of((depth, depth)) == cols_of((depth, depth))).astype(f32).astype(bf16)
     temp = nt(same, temp)[:, 0:1]
-    for h in range(heads):
-        span = slice(h * depth, (h + 1) * depth)
-        dmt_ref[span, :] = (d_mid[span] + temp * sums[h]).astype(bf16)
-    grad_acc[...] += nn(dmt_ref[...], feats_ref[...])
-    small_acc[...] += nn(stack[hm : 2 * hm + 2 * heads, :], mid)
+    piece = min(sub_block, block)
+    pieces = [slice(i * piece, (i + 1) * piece) for i in range(block // piece)]
+
+    def products(at):
+        return nt(lhs[...], mid_ref[at, :]), nt(mw_ref[...], cot_ref[at, :])
+
+    def per_head(at, from_mid, from_cot):
+        weights_b, u_b, sums = [], [], []
+        for h in range(heads):
+            span = slice(h * slices, (h + 1) * slices)
+            inv_tau = aux_ref[h : h + 1, at]
+            logits = from_mid[span] * inv_tau
+            weights = jnp.exp(logits - aux_ref[heads + h : heads + h + 1, at])
+            d_weights = from_cot[span] + from_mid[top + h * slices : top + (h + 1) * slices]
+            d_weights = d_weights + dn_ref[span, 0:1]
+            mean = jnp.sum(weights * d_weights, axis=0, keepdims=True)
+            d_logits = weights * (d_weights - mean)
+            d_tau = jnp.sum(d_logits * logits, axis=0, keepdims=True)
+            sums.append(-d_tau * aux_ref[2 * heads + h : 2 * heads + h + 1, at])
+            weights_b.append(weights.astype(bf16))
+            u_b.append((d_logits * inv_tau).astype(bf16))
+        c_sum = jnp.concatenate(sums, axis=0)
+        c_high = c_sum.astype(bf16).astype(f32)
+        u_b.append(jnp.concatenate([c_high, c_sum - c_high], axis=0).astype(bf16))
+        return jnp.concatenate(weights_b, axis=0), jnp.concatenate(u_b, axis=0), sums
+
+    def outputs(at, weights_b, u_b, sums):
+        d_mid = nn(yt[...], jnp.concatenate([weights_b, u_b[0:hm]], axis=0))
+        for h in range(heads):
+            span = slice(h * depth, (h + 1) * depth)
+            dmt_ref[span, at] = (d_mid[span] + temp * sums[h]).astype(bf16)
+        grad_acc[...] += nn(dmt_ref[:, at], feats_ref[at, :])
+        small_acc[...] += nn(u_b, mid_ref[at, :])
+
+    ready = products(pieces[0])
+    for i, at in enumerate(pieces):
+        current = ready
+        if i + 1 < len(pieces):
+            ready = products(pieces[i + 1])
+        outputs(at, *per_head(at, *current))
 
     @pl.when(step == pl.num_programs(0) - 1)
     def _():
@@ -408,10 +423,10 @@
     ).astype(bf16)
 
 
-def grad_out_kernel(o0, o1, o2, o3, mixed_t_ref, grad_out_ref, whole):
-    place = group_place()
-    rows = o0.shape[0]
-    for k, part in enumerate((o0, o1, o2, o3)):
+def grad_out_kernel(own_ref, other_ref, mixed_t_ref, grad_out_ref, whole):
+    place = group_place() & 1
+    rows = own_ref.shape[0]
+    for k, part in enumerate((own_ref, other_ref)):
         whole[pl.ds(pl.multiple_of((place ^ k) * rows, 8), rows), :] = part[...]
     high, low = two_pieces(whole[...])
     mixed_t = mixed_t_ref[...]
@@ -452,15 +467,18 @@
     return lax.ppermute(x, "node", [(i, i ^ k) for i in range(count)])
 
 
-def sum_kernel(r0, r1, r2, r3, *rest):
-    rest[-1][...] = (r0[...] + r1[...]) + (r2[...] + r3[...])
-
-
-def sum_four(parts, *before):
+def sum_kernel(count, *refs):
+    total = refs[0][...] + refs[1][...]
+    if count == 4:
+        total = total + (refs[2][...] + refs[3][...])
+    refs[-1][...] = total
+
+
+def sum_behind(parts, *before):
     return pl.pallas_call(
-        sum_kernel,
+        functools.partial(sum_kernel, len(parts)),
         out_shape=jax.ShapeDtypeStruct(parts[0].shape, f32),
-        in_specs=[pl.BlockSpec(memory_space=pltpu.VMEM)] * 4
+        in_specs=[pl.BlockSpec(memory_space=pltpu.VMEM)] * len(parts)
         + [pl.BlockSpec(memory_space=pl.ANY)] * len(before),
         out_specs=pl.BlockSpec(memory_space=pltpu.VMEM),
         compiler_params=params(2, False),
@@ -469,7 +487,8 @@
 
 
 def scatter_group(parts, count):
-    return sum_four([parts[0]] + [exchange(parts[k], k, count) for k in range(1, group)])
+    got = [parts[0]] + [exchange(parts[k], k, count) for k in range(1, group)]
+    return (got[0] + got[1]) + (got[2] + got[3])
 
 
 def sum_over_groups(total, count, *before):
@@ -477,7 +496,10 @@
     while stride < count:
         if count // stride % 4 == 0:
             got = [total] + [exchange(total, stride * j, count) for j in (1, 2, 3)]
-            total = sum_four(got, *before)
+            if before:
+                total = sum_behind(got, *before)
+            else:
+                total = (got[0] + got[1]) + (got[2] + got[3])
             stride *= 4
         else:
             total = total + exchange(total, stride, count)
@@ -510,10 +532,10 @@
 
     temp = temp_vec.reshape(1, depth)
     half = (2 * slices + 8, 128)
-    quarter = (width // group, width)
+    wide = (hm // 2, width)
     block = min(2048, rows)
     grid, by_rows, by_cols, aux_spec = blocks(block)
-    mid, wt, aux, sw, sb, w_cat, keep, send, *wc = pl.pallas_call(
+    mid, wt, aux, sw, sb, w_cat, keep, send, wc_keep, wc_send = pl.pallas_call(
         functools.partial(stats_kernel, heads, slices),
         grid=grid,
         in_specs=[
@@ -536,8 +558,9 @@
             full((depth, 128)),
             full(half),
             full(half),
-        ]
-        + [full(quarter)] * group,
+            full(wide),
+            full(wide),
+        ],
         out_shape=[
             like((rows, width), bf16),
             like((hm, rows), bf16),
@@ -547,44 +570,52 @@
             like((depth, 128), bf16),
             like(half, f32),
             like(half, f32),
-        ]
-        + [like(quarter, f32)] * group,
+            like(wide, f32),
+            like(wide, f32),
+        ],
         scratch_shapes=[
             pltpu.VMEM((hm, width), f32),
             pltpu.VMEM((hm, 128), f32),
             pltpu.VMEM((hm, width), f32),
             pltpu.VMEM((2,) + half, f32),
         ],
-        compiler_params=params(56),
+        compiler_params=params(60),
         cost_estimate=cost(4 * unit, rows * width * 8, rows * hm),
     )(owned, valid.reshape(1, rows), feats, cotangent, w_mid, w_slice, temp, w_out, w_qkv)
 
     own = keep + exchange(send, 1, count)
-    stride = 2
-    while stride < count:
-        own = own + exchange(own, stride, count)
-        stride *= 2
+    wc_got = exchange(wc_send, 1, count)
+    own = own + exchange(own, 2, count)
+    wc_sum = sum_behind([wc_keep, wc_got], own)
+    wc_got = exchange(wc_sum, 2, count)
+    own = sum_over_groups(own, count)
+    wc_sum = sum_behind([wc_sum, wc_got], own)
     other = exchange(own, 1, count)
-
-    parts = lax.optimization_barrier((*wc, other))
-    wc_total = scatter_group(parts[:group], count)
-    lhs, mw, mixed_t, yt, dn, grad_qkv = pl.pallas_call(
+    strides = [stride for stride in (1 << i for i in range(2, 30)) if stride < count]
+    for stride in strides[:-1]:
+        wc_got = exchange(wc_sum, stride, count)
+        if stride != strides[-2]:
+            wc_sum = wc_sum + wc_got
+
+    mw, mixed_t, dr, drt, dn, grad_qkv = pl.pallas_call(
         functools.partial(tokens_kernel, heads, slices),
         out_shape=[
-            like((2 * hm + 16, width), bf16),
             like((hm, width), bf16),
             like((width, hm), bf16),
-            like((width, 2 * hm), bf16),
+            like((hm, width), bf16),
+            like((width, hm), bf16),
             like((hm, 128), f32),
             like((3, depth, depth), f32),
         ],
         scratch_shapes=[pltpu.VMEM((2,) + half, f32)],
-        compiler_params=params(8, False),
+        compiler_params=params(16, False),
         cost_estimate=cost(30 * width**3, 4 * width * width * 4, hm * hm),
-    )(own, other, w_cat, w_out, sw, sb)
+    )(own, other, w_cat, w_out)
+    wc_sum = sum_behind([wc_sum, wc_got], mw)
+    wc_got = exchange(wc_sum, strides[-1], count)
 
     larger = (width // group + slices // group, width)
-    block = min(512, rows)
+    block = min(2048, rows)
     grid, by_rows, by_cols, aux_spec = blocks(block)
     dmt, *sends = pl.pallas_call(
         functools.partial(backward_kernel, heads, slices),
@@ -594,9 +625,11 @@
             by_rows,
             by_rows,
             by_rows,
-            full((2 * hm + 16, width)),
+            full((hm + 16, width)),
+            full((width, hm)),
             full((hm, width)),
-            full((width, 2 * hm)),
+            full((hm, width)),
+            full((width, hm)),
             full((hm, 128)),
             full((1, depth)),
             pl.BlockSpec(memory_space=pl.ANY),
@@ -604,18 +637,19 @@
         out_specs=[by_cols] + [full(larger)] * group,
         out_shape=[like((width, rows), bf16)] + [like(larger, f32)] * group,
         scratch_shapes=[
-            pltpu.VMEM((2 * hm + 16, block), bf16),
+            pltpu.VMEM((2 * hm + 16, width), bf16),
+            pltpu.VMEM((width, 2 * hm), bf16),
             pltpu.VMEM((width, width), f32),
             pltpu.VMEM((hm + 16, width), f32),
             pltpu.VMEM((group,) + larger, f32),
         ],
-        compiler_params=params(56),
+        compiler_params=params(32),
         cost_estimate=cost(8 * unit, rows * width * 8, rows * hm),
-    )(aux, mid, cotangent, feats, lhs, mw, yt, dn, temp, wc_total)
+    )(aux, mid, cotangent, feats, sw, sb, mw, dr, drt, dn, temp, wc_sum)
 
     mid_total = scatter_group(sends, count)
-    wc_total = sum_over_groups(wc_total, count, sends[1])
-    out_parts = gather_group(wc_total, count)
+    wc_sum = sum_behind([wc_sum, wc_got], sends[1])
+    wc_other = exchange(wc_sum, 1, count)
 
     block = min(1024, rows)
     grid, by_rows, by_cols, aux_spec = blocks(block)
@@ -631,7 +665,7 @@
         ],
         out_specs=[by_rows, by_rows, full((8, 128))],
         out_shape=[like((rows, width), bf16)] * 2 + [like((8, 128), f32)],
-        compiler_params=params(56),
+        compiler_params=params(20),
         cost_estimate=cost(2 * unit, rows * width * 8),
     )(wt, dmt, mw, w_mid, mid_total)
 
@@ -642,7 +676,7 @@
         scratch_shapes=[pltpu.VMEM((hm, width), f32)],
         compiler_params=params(8, False),
         cost_estimate=cost(4 * width**3, 3 * width * width * 4),
-    )(*out_parts, mixed_t)
+    )(wc_sum, wc_other, mixed_t)
 
     mid_parts = gather_group(mid_total, count)
     grad_w_mid, grad_w_slice, grad_temp = pl.pallas_call(

time: 86.4 us -> 66.4 us (0.77)
  Pallas kernels: 30.8 us -> 22.6 us
  local copies, waits for them, and re-layouts: 9.39 us -> 3.23 us
  waiting for transfers between devices: 17.3 us -> 14.1 us
  starting transfers between devices: 25.9 us -> 23.4 us
    pallas_call x1, Pallas kernels: 12.1 us -> 5.77 us  [shards(): pl.pallas_call(functools.partial(backward_kernel, heads, slices), grid=gr...]
    unnamed x32 -> x24, local copies, waits for them, and re-layouts: 9.39 us -> 3.23 us
    ppermute x23 -> x20, waiting for transfers between devices: 17.3 us -> 14.1 us  [exchange(): return lax.ppermute(x, 'node', [(i, i ^ k) for i in range(count)])]
    ppermute x23 -> x20, starting transfers between devices: 25.9 us -> 23.4 us  [exchange(): return lax.ppermute(x, 'node', [(i, i ^ k) for i in range(count)])]
    pallas_call x1, Pallas kernels: 5.68 us -> 3.66 us  [shards(): pl.pallas_call(rows_kernel, grid=grid, in_specs=[by_cols, by_cols, full((...]
  transfers between devices with their start and end apart: 23 -> 20, of which waited for: 8 -> 10; matrix products, arithmetic and copies ran while one was open for 0% -> 1% of each run, Pallas kernels for 26% -> 12%
where the time goes in v4:
time: 66.4 us; the launch traced here: 65.6 us
  starting transfers between devices  23.4 us (35%)
  Pallas kernels  22.6 us (34%)
  waiting for transfers between devices  14.1 us (21%)
  local copies, waits for them, and re-layouts  3.23 us (5%)
  between operations  1.46 us (2%)
  other arithmetic  0.81 us (1%)
    ppermute x20, starting transfers between devices, exchange(): return lax.ppermute(x, 'node', [(i, i ^ k) for i in range(count)])  23.4 us
    ppermute x20, waiting for transfers between devices, exchange(): return lax.ppermute(x, 'node', [(i, i ^ k) for i in range(count)])  14.1 us
    pallas_call x1, Pallas kernels, shards(): pl.pallas_call(functools.partial(stats_kernel, heads, slices), grid=grid,...  8.26 us
    pallas_call x1, Pallas kernels, shards(): pl.pallas_call(functools.partial(backward_kernel, heads, slices), grid=gr...  5.77 us
    pallas_call x1, Pallas kernels, shards(): pl.pallas_call(rows_kernel, grid=grid, in_specs=[by_cols, by_cols, full((...  3.66 us
    unnamed x24, local copies, waits for them, and re-layouts  3.23 us
    pallas_call x1, Pallas kernels, shards(): pl.pallas_call(functools.partial(tokens_kernel, heads, slices), out_shape...  3.1 us
  transfers between devices with their start and end apart: 20, of which 10 were waited for; matrix products, arithmetic and copies ran while one was open for 1% of the time, Pallas kernels for 12%

profile of v4, /device:TPU:0, one launch (start us, length us, event | category | flops | bytes accessed | tf_op | source)
XLA Modules:
  0.0 65.6 jit_solution(16671564715964596039)
XLA Ops:
  1.3 8.3 %shard_map.144 = (bf16[4096,256]{1,0:T(8,128)(2,1)}, bf16[256,4096]{1,0:T(8,128)(2,1)}, f32[24,4096]{1,0:T(8,128)}, bf16[272,256]{1,0:T(8,128)(2,1)}, bf16[256,2...) custom-call(s32[1]{0:T(128)S(6)} %copy.16.owned_ref, ...), custom_call_target="tpu_custom_call" | custom-call | flops 2147483648 | bytes 8388608 | tf_op jit(solution)/shard_map/pallas_call | solution.py:538
  10.2 1.3 %collective-permute-done = f32[72,128]{1,0:T(8,128)S(1)} collective-permute-done((f32[72,128]{1,0:T(8,128)}, f32[72,128]{1,0:T(8,128)S(1)}, u32[]{:S(2)}, u32[]{:S(2)}) %collective-permute-start) | collective-permute-done | bytes 36896 | tf_op jit(solution)/shard_map/ppermute | solution.py:467
  12.3 2.7 %collective-permute-start.1 = (f32[72,128]{1,0:T(8,128)S(1)}, f32[72,128]{1,0:T(8,128)S(1)}, u32[]{:S(2)}, u32[]{:S(2)}) collective-permute-start(f32[72,128]{1,0:T(8,128)S(1)} %add.24), channel_id=1, source_target_pairs={{0,2},{1,3},{2,0},{3,1},{4,6},{5,7},{6,4},{7,5},{8,10},{9,11},{10,... | collective-permute-start | bytes 110600 | tf_op jit(solution)/shard_map/ppermute | solution.py:467
  15.0 2.0 %collective-permute-done.1 = f32[72,128]{1,0:T(8,128)S(1)} collective-permute-done((f32[72,128]{1,0:T(8,128)S(1)}, f32[72,128]{1,0:T(8,128)S(1)}, u32[]{:S(2)}, u32[]{:S(2)}) %collective-permute-start.1) | collective-permute-done | bytes 36896 | tf_op jit(solution)/shard_map/ppermute | solution.py:467
  16.9 2.1 %collective-permute-start.2 = (f32[72,128]{1,0:T(8,128)S(1)}, f32[72,128]{1,0:T(8,128)S(1)}, u32[]{:S(2)}, u32[]{:S(2)}) collective-permute-start(f32[72,128]{1,0:T(8,128)S(1)} %add.25.refs_2_), channel_id=1, source_target_pairs={{0,4},{1,5},{2,6},{3,7},{4,0},{5,1},{6,2},{7,3},{8,12},{9,13},{10,... | collective-permute-start | bytes 110600 | tf_op jit(solution)/shard_map/ppermute | solution.py:467
  19.0 2.6 %collective-permute-start.3 = (f32[72,128]{1,0:T(8,128)S(1)}, f32[72,128]{1,0:T(8,128)S(1)}, u32[]{:S(2)}, u32[]{:S(2)}) collective-permute-start(f32[72,128]{1,0:T(8,128)S(1)} %add.25.refs_2_), channel_id=1, source_target_pairs={{0,8},{1,9},{2,10},{3,11},{4,12},{5,13},{6,14},{7,15},{8,0},{9,1},... | collective-permute-start | bytes 110600 | tf_op jit(solution)/shard_map/ppermute | solution.py:467
  22.6 1.8 %collective-permute-start.7 = (f32[128,256]{1,0:T(8,128)S(1)}, f32[128,256]{1,0:T(8,128)S(1)}, u32[]{:S(2)}, u32[]{:S(2)}) collective-permute-start(f32[128,256]{1,0:T(8,128)S(1)} %shard_map.146.refs_0_), channel_id=1, source_target_pairs={{0,2},{1,3},{2,0},{3,1},{4,6},{5,7},{6,4},{7,5},{8,10},{9,11},{10,... | collective-permute-start | bytes 393224 | tf_op jit(solution)/shard_map/ppermute | solution.py:467
  24.3 3.0 %collective-permute-done.4 = f32[72,128]{1,0:T(8,128)S(1)} collective-permute-done((f32[72,128]{1,0:T(8,128)S(1)}, f32[72,128]{1,0:T(8,128)S(1)}, u32[]{:S(2)}, u32[]{:S(2)}) %collective-permute-start.4) | collective-permute-done | bytes 36896 | tf_op jit(solution)/shard_map/ppermute | solution.py:467
  27.6 1.0 %collective-permute-start.8 = (f32[128,256]{1,0:T(8,128)S(1)}, f32[128,256]{1,0:T(8,128)S(1)}, u32[]{:S(2)}, u32[]{:S(2)}) collective-permute-start(f32[128,256]{1,0:T(8,128)S(1)} %shard_map.147.refs_0_), channel_id=1, source_target_pairs={{0,4},{1,5},{2,6},{3,7},{4,0},{5,1},{6,2},{7,3},{8,12},{9,13},{10,... | collective-permute-start | bytes 393224 | tf_op jit(solution)/shard_map/ppermute | solution.py:467
  28.6 1.2 %collective-permute-done.5.got_ref = f32[72,128]{1,0:T(8,128)S(1)} collective-permute-done((f32[72,128]{1,0:T(8,128)S(1)}, f32[72,128]{1,0:T(8,128)S(1)}, u32[]{:S(2)}, u32[]{:S(2)}) %collective-permute-start.5) | collective-permute-done | bytes 36896 | tf_op jit(solution)/shard_map/ppermute | solution.py:467
  30.5 3.1 %shard_map.145 = (bf16[256,256]{1,0:T(8,128)(2,1)S(1)}, bf16[256,256]{1,0:T(8,128)(2,1)S(1)}, bf16[256,256]{1,0:T(8,128)(2,1)S(1)}, bf16[256,256]{1,0:T(8,128)(2...) custom-call(f32[72,128]{1,0:T(8,128)S(1)} %add_add_fusion.1.own_ref.refs_2_, ...), custom_call_target="tpu_custom_call" | custom-call | flops 503316480 | bytes 1048576 | tf_op jit(solution)/shard_map/pallas_call | solution.py:600
  33.7 1.6 %copy-done.7 = bf16[4096,256]{1,0:T(8,128)(2,1)S(1)} copy-done((bf16[4096,256]{1,0:T(8,128)(2,1)S(1)}, bf16[4096,256]{1,0:T(8,128)(2,1)}, u32[]{:S(2)}) %copy-start.7) | copy-done | bytes 2097176
  35.3 5.8 %shard_map.149 = (bf16[256,4096]{1,0:T(8,128)(2,1)S(1)}, f32[72,256]{1,0:T(8,128)S(1)}, f32[72,256]{1,0:T(8,128)S(1)}, f32[72,256]{1,0:T(8,128)S(1)}, f32[72,256]{1,0:T(8,128)S(1)}) custom-call(f32[24,4096]{1,0:T(8,128)S(1)} %copy-done.8, bf16[4096,256]{1,0:T(8,128)(2,1)S(1)} %copy-done.7, bf16[4096,256]{1,0:T(8,128)(2,1)S(1)} %copy-done.4, ...), custom_call_target="tpu_custom_call" | custom-call | flops 4294967296 | bytes 8388608 | tf_op jit(solution)/shard_map/pallas_call | solution.py:620
  41.0 1.6 %collective-permute-start.10 = (f32[72,256]{1,0:T(8,128)S(1)}, f32[72,256]{1,0:T(8,128)S(1)}, u32[]{:S(2)}, u32[]{:S(2)}) collective-permute-start(f32[72,256]{1,0:T(8,128)S(1)} %get-tuple-element.51), channel_id=1, source_target_pairs={{0,2},{1,3},{2,0},{3,1},{4,6},{5,7},{6,4},{7,5},{8,10},{9,11},{10,... | collective-permute-start | bytes 221192 | tf_op jit(solution)/shard_map/ppermute | solution.py:467
  43.2 3.5 %collective-permute-start.18 = (f32[128,256]{1,0:T(8,128)S(1)}, f32[128,256]{1,0:T(8,128)S(1)}, u32[]{:S(2)}, u32[]{:S(2)}) collective-permute-start(f32[128,256]{1,0:T(8,128)S(1)} %shard_map.148._.refs_0_), channel_id=1, source_target_pairs={{0,8},{1,9},{2,10},{3,11},{4,12},{5,13},{6,14},{7,15},{8,0},{9,1},... | collective-permute-start | bytes 393224 | tf_op jit(solution)/shard_map/ppermute | solution.py:467
  47.1 1.4 %collective-permute-start.12 = (f32[72,256]{1,0:T(8,128)S(1)}, f32[72,256]{1,0:T(8,128)S(1)}, u32[]{:S(2)}, u32[]{:S(2)}) collective-permute-start(f32[72,256]{1,0:T(8,128)S(1)} %add_add_fusion._.refs_0_), channel_id=1, source_target_pairs={{0,4},{1,5},{2,6},{3,7},{4,0},{5,1},{6,2},{7,3},{8,12},{9,13},{10,... | collective-permute-start | bytes 221192 | tf_op jit(solution)/shard_map/ppermute | solution.py:467
  48.5 2.2 %collective-permute-start.13 = (f32[72,256]{1,0:T(8,128)S(1)}, f32[72,256]{1,0:T(8,128)S(1)}, u32[]{:S(2)}, u32[]{:S(2)}) collective-permute-start(f32[72,256]{1,0:T(8,128)S(1)} %add_add_fusion._.refs_0_), channel_id=1, source_target_pairs={{0,8},{1,9},{2,10},{3,11},{4,12},{5,13},{6,14},{7,15},{8,0},{9,1},... | collective-permute-start | bytes 221192 | tf_op jit(solution)/shard_map/ppermute | solution.py:467
  50.8 1.4 %collective-permute-start.14 = (f32[72,256]{1,0:T(8,128)S(1)}, f32[72,256]{1,0:T(8,128)S(1)}, u32[]{:S(2)}, u32[]{:S(2)}) collective-permute-start(f32[72,256]{1,0:T(8,128)S(1)} %add_add_fusion._.refs_0_), channel_id=1, source_target_pairs={{0,12},{1,13},{2,14},{3,15},{4,8},{5,9},{6,10},{7,11},{8,4},{9,5},... | collective-permute-start | bytes 221192 | tf_op jit(solution)/shard_map/ppermute | solution.py:467
  52.1 1.0 %collective-permute-done.18.refs_1_ = f32[128,256]{1,0:T(8,128)S(1)} collective-permute-done((f32[128,256]{1,0:T(8,128)S(1)}, f32[128,256]{1,0:T(8,128)S(1)}, u32[]{:S(2)}, u32[]{:S(2)}) %collective-permute-start.18) | collective-permute-done | bytes 131104 | tf_op jit(solution)/shard_map/ppermute | solution.py:467
  53.3 3.7 %shard_map.150 = (bf16[4096,256]{1,0:T(8,128)(2,1)}, bf16[4096,256]{1,0:T(8,128)(2,1)}, f32[8,128]{1,0:T(8,128)S(1)}) custom-call(bf16[256,4096]{1,0:T(8,128)(2,1)S(1)} %copy-done, bf16[256,4096]{1,0:T(8,128)(2,1)S(1)} %get-tuple-element.48.dmt_ref, bf16[256,256]{1,0:T(8,128)(2,1)S(1)} %get-tuple-element.42.refs_2_.mw_ref, bf16[256,256]{1,0:T(8,128)(2,1)S(1)} %copy-done.1, ...), custom_call_target="tpu_custom_call" | custom-call | flops 1073741824 | bytes 8388608 | tf_op jit(solution)/shard_map/pallas_call | solution.py:656
  58.0 1.7 %collective-permute-start.16 = (f32[72,256]{1,0:T(8,128)S(1)}, f32[72,256]{1,0:T(8,128)S(1)}, u32[]{:S(2)}, u32[]{:S(2)}) collective-permute-start(f32[72,256]{1,0:T(8,128)S(1)} %shard_map.151.m0), channel_id=1, source_target_pairs={{0,2},{1,3},{2,0},{3,1},{4,6},{5,7},{6,4},{7,5},{8,10},{9,11},{10,... | collective-permute-start | bytes 221192 | tf_op jit(solution)/shard_map/ppermute | solution.py:467
  59.8 2.8 %collective-permute-done.16.m2 = f32[72,256]{1,0:T(8,128)S(1)} collective-permute-done((f32[72,256]{1,0:T(8,128)S(1)}, f32[72,256]{1,0:T(8,128)S(1)}, u32[]{:S(2)}, u32[]{:S(2)}) %collective-permute-start.16) | collective-permute-done | bytes 73760 | tf_op jit(solution)/shard_map/ppermute | solution.py:467
  62.6 1.2 %collective-permute-done.17.m3 = f32[72,256]{1,0:T(8,128)S(1)} collective-permute-done((f32[72,256]{1,0:T(8,128)S(1)}, f32[72,256]{1,0:T(8,128)S(1)}, u32[]{:S(2)}, u32[]{:S(2)}) %collective-permute-start.17) | collective-permute-done | bytes 73760 | tf_op jit(solution)/shard_map/ppermute | solution.py:467
  64.6 1.0 %shard_map.154 = f32[256,256]{1,0:T(8,128)} custom-call(f32[128,256]{1,0:T(8,128)S(1)} %shard_map.153.own_ref, f32[128,256]{1,0:T(8,128)S(1)} %collective-permute-done.19.other_ref, bf16[256,256]{1,0:T(8,128)(2,1)S(1)} %get-tuple-element.57.mixed_t_ref), custom_call_target="tpu_custom_call" | custom-call | flops 67108864 | bytes 786432 | tf_op jit(solution)/shard_map/pallas_call | solution.py:673
  (55 shorter events, 6.3 us)
Async XLA Ops:
  1.3 28.5 %copy-start.5 = (bf16[256,256]{1,0:T(8,128)(2,1)S(1)}, bf16[256,256]{1,0:T(8,128)(2,1)}, u32[]{:S(2)}) copy-start(bf16[256,256]{1,0:T(8,128)(2,1)} %w_out_ref.3) | copy-start | bytes 393220
  1.3 32.3 %copy-start.3 = (bf16[4096,256]{1,0:T(8,128)(2,1)S(1)}, bf16[4096,256]{1,0:T(8,128)(2,1)}, u32[]{:S(2)}) copy-start(bf16[4096,256]{1,0:T(8,128)(2,1)} %feats_ref.3) | copy-start | bytes 6291460
  9.6 24.1 %copy-start.6 = (bf16[32]{0:T(256)(128)(2,1)S(1)}, bf16[32]{0:T(256)(128)(2,1)}, u32[]{:S(2)}) copy-start(bf16[32]{0:T(256)(128)(2,1)} %param.15) | copy-start | bytes 196
  9.6 24.1 %copy-start.9 = (bf16[272,256]{1,0:T(8,128)(2,1)S(1)}, bf16[272,256]{1,0:T(8,128)(2,1)}, u32[]{:S(2)}) copy-start(bf16[272,256]{1,0:T(8,128)(2,1)} %get-tuple-element.37.sw_ref) | copy-start | bytes 417796
  9.6 12.0 %collective-permute-start.6 = (f32[128,256]{1,0:T(8,128)}, f32[128,256]{1,0:T(8,128)S(1)}, u32[]{:S(2)}, u32[]{:S(2)}) collective-permute-start(f32[128,256]{1,0:T(8,128)} %get-tuple-element.47), channel_id=1, source_target_pairs={{0,1},{1,0},{2,3},{3,2},{4,5},{5,4},{6,7},{7,6},{8,9},{9,8},{10,11... | collective-permute-start | bytes 393224 | tf_op jit(solution)/shard_map/ppermute | solution.py:467
  10.1 1.4 %collective-permute-start = (f32[72,128]{1,0:T(8,128)}, f32[72,128]{1,0:T(8,128)S(1)}, u32[]{:S(2)}, u32[]{:S(2)}) collective-permute-start(f32[72,128]{1,0:T(8,128)} %get-tuple-element.40), channel_id=1, source_target_pairs={{0,1},{1,0},{2,3},{3,2},{4,5},{5,4},{6,7},{7,6},{8,9},{9,8},{10,11... | collective-permute-start | bytes 110600 | tf_op jit(solution)/shard_map/ppermute | solution.py:467
  12.3 4.6 %collective-permute-start.1 = (f32[72,128]{1,0:T(8,128)S(1)}, f32[72,128]{1,0:T(8,128)S(1)}, u32[]{:S(2)}, u32[]{:S(2)}) collective-permute-start(f32[72,128]{1,0:T(8,128)S(1)} %add.24), channel_id=1, source_target_pairs={{0,2},{1,3},{2,0},{3,1},{4,6},{5,7},{6,4},{7,5},{8,10},{9,11},{10,... | collective-permute-start | bytes 110600 | tf_op jit(solution)/shard_map/ppermute | solution.py:467
  16.9 7.4 %collective-permute-start.2 = (f32[72,128]{1,0:T(8,128)S(1)}, f32[72,128]{1,0:T(8,128)S(1)}, u32[]{:S(2)}, u32[]{:S(2)}) collective-permute-start(f32[72,128]{1,0:T(8,128)S(1)} %add.25.refs_2_), channel_id=1, source_target_pairs={{0,4},{1,5},{2,6},{3,7},{4,0},{5,1},{6,2},{7,3},{8,12},{9,13},{10,... | collective-permute-start | bytes 110600 | tf_op jit(solution)/shard_map/ppermute | solution.py:467
  19.0 5.3 %collective-permute-start.3 = (f32[72,128]{1,0:T(8,128)S(1)}, f32[72,128]{1,0:T(8,128)S(1)}, u32[]{:S(2)}, u32[]{:S(2)}) collective-permute-start(f32[72,128]{1,0:T(8,128)S(1)} %add.25.refs_2_), channel_id=1, source_target_pairs={{0,8},{1,9},{2,10},{3,11},{4,12},{5,13},{6,14},{7,15},{8,0},{9,1},... | collective-permute-start | bytes 110600 | tf_op jit(solution)/shard_map/ppermute | solution.py:467
  21.6 5.8 %collective-permute-start.4 = (f32[72,128]{1,0:T(8,128)S(1)}, f32[72,128]{1,0:T(8,128)S(1)}, u32[]{:S(2)}, u32[]{:S(2)}) collective-permute-start(f32[72,128]{1,0:T(8,128)S(1)} %add.25.refs_2_), channel_id=1, source_target_pairs={{0,12},{1,13},{2,14},{3,15},{4,8},{5,9},{6,10},{7,11},{8,4},{9,5},... | collective-permute-start | bytes 110600 | tf_op jit(solution)/shard_map/ppermute | solution.py:467
  22.6 5.0 %collective-permute-start.7 = (f32[128,256]{1,0:T(8,128)S(1)}, f32[128,256]{1,0:T(8,128)S(1)}, u32[]{:S(2)}, u32[]{:S(2)}) collective-permute-start(f32[128,256]{1,0:T(8,128)S(1)} %shard_map.146.refs_0_), channel_id=1, source_target_pairs={{0,2},{1,3},{2,0},{3,1},{4,6},{5,7},{6,4},{7,5},{8,10},{9,11},{10,... | collective-permute-start | bytes 393224 | tf_op jit(solution)/shard_map/ppermute | solution.py:467
  27.6 6.0 %collective-permute-start.8 = (f32[128,256]{1,0:T(8,128)S(1)}, f32[128,256]{1,0:T(8,128)S(1)}, u32[]{:S(2)}, u32[]{:S(2)}) collective-permute-start(f32[128,256]{1,0:T(8,128)S(1)} %shard_map.147.refs_0_), channel_id=1, source_target_pairs={{0,4},{1,5},{2,6},{3,7},{4,0},{5,1},{6,2},{7,3},{8,12},{9,13},{10,... | collective-permute-start | bytes 393224 | tf_op jit(solution)/shard_map/ppermute | solution.py:467
  28.6 1.2 %collective-permute-start.5 = (f32[72,128]{1,0:T(8,128)S(1)}, f32[72,128]{1,0:T(8,128)S(1)}, u32[]{:S(2)}, u32[]{:S(2)}) collective-permute-start(f32[72,128]{1,0:T(8,128)S(1)} %add_add_fusion.1.own_ref.refs_2_), channel_id=1, source_target_pairs={{0,1},{1,0},{2,3},{3,2},{4,5},{5,4},{6,7},{7,6},{8,9},{9,8},{10,11... | collective-permute-start | bytes 110600 | tf_op jit(solution)/shard_map/ppermute | solution.py:467
  41.0 5.7 %collective-permute-start.10 = (f32[72,256]{1,0:T(8,128)S(1)}, f32[72,256]{1,0:T(8,128)S(1)}, u32[]{:S(2)}, u32[]{:S(2)}) collective-permute-start(f32[72,256]{1,0:T(8,128)S(1)} %get-tuple-element.51), channel_id=1, source_target_pairs={{0,2},{1,3},{2,0},{3,1},{4,6},{5,7},{6,4},{7,5},{8,10},{9,11},{10,... | collective-permute-start | bytes 221192 | tf_op jit(solution)/shard_map/ppermute | solution.py:467
  42.6 4.5 %collective-permute-start.11 = (f32[72,256]{1,0:T(8,128)S(1)}, f32[72,256]{1,0:T(8,128)S(1)}, u32[]{:S(2)}, u32[]{:S(2)}) collective-permute-start(f32[72,256]{1,0:T(8,128)S(1)} %get-tuple-element.52), channel_id=1, source_target_pairs={{0,3},{1,2},{2,1},{3,0},{4,7},{5,6},{6,5},{7,4},{8,11},{9,10},{10,... | collective-permute-start | bytes 221192 | tf_op jit(solution)/shard_map/ppermute | solution.py:467
  42.6 4.5 %collective-permute-start.9 = (f32[72,256]{1,0:T(8,128)S(1)}, f32[72,256]{1,0:T(8,128)S(1)}, u32[]{:S(2)}, u32[]{:S(2)}) collective-permute-start(f32[72,256]{1,0:T(8,128)S(1)} %get-tuple-element.50.refs_2_), channel_id=1, source_target_pairs={{0,1},{1,0},{2,3},{3,2},{4,5},{5,4},{6,7},{7,6},{8,9},{9,8},{10,11... | collective-permute-start | bytes 221192 | tf_op jit(solution)/shard_map/ppermute | solution.py:467
  43.2 9.9 %collective-permute-start.18 = (f32[128,256]{1,0:T(8,128)S(1)}, f32[128,256]{1,0:T(8,128)S(1)}, u32[]{:S(2)}, u32[]{:S(2)}) collective-permute-start(f32[128,256]{1,0:T(8,128)S(1)} %shard_map.148._.refs_0_), channel_id=1, source_target_pairs={{0,8},{1,9},{2,10},{3,11},{4,12},{5,13},{6,14},{7,15},{8,0},{9,1},... | collective-permute-start | bytes 393224 | tf_op jit(solution)/shard_map/ppermute | solution.py:467
  47.1 9.8 %collective-permute-start.12 = (f32[72,256]{1,0:T(8,128)S(1)}, f32[72,256]{1,0:T(8,128)S(1)}, u32[]{:S(2)}, u32[]{:S(2)}) collective-permute-start(f32[72,256]{1,0:T(8,128)S(1)} %add_add_fusion._.refs_0_), channel_id=1, source_target_pairs={{0,4},{1,5},{2,6},{3,7},{4,0},{5,1},{6,2},{7,3},{8,12},{9,13},{10,... | collective-permute-start | bytes 221192 | tf_op jit(solution)/shard_map/ppermute | solution.py:467
  48.5 9.3 %collective-permute-start.13 = (f32[72,256]{1,0:T(8,128)S(1)}, f32[72,256]{1,0:T(8,128)S(1)}, u32[]{:S(2)}, u32[]{:S(2)}) collective-permute-start(f32[72,256]{1,0:T(8,128)S(1)} %add_add_fusion._.refs_0_), channel_id=1, source_target_pairs={{0,8},{1,9},{2,10},{3,11},{4,12},{5,13},{6,14},{7,15},{8,0},{9,1},... | collective-permute-start | bytes 221192 | tf_op jit(solution)/shard_map/ppermute | solution.py:467
  50.8 7.1 %collective-permute-start.14 = (f32[72,256]{1,0:T(8,128)S(1)}, f32[72,256]{1,0:T(8,128)S(1)}, u32[]{:S(2)}, u32[]{:S(2)}) collective-permute-start(f32[72,256]{1,0:T(8,128)S(1)} %add_add_fusion._.refs_0_), channel_id=1, source_target_pairs={{0,12},{1,13},{2,14},{3,15},{4,8},{5,9},{6,10},{7,11},{8,4},{9,5},... | collective-permute-start | bytes 221192 | tf_op jit(solution)/shard_map/ppermute | solution.py:467
  53.2 11.4 %collective-permute-start.19 = (f32[128,256]{1,0:T(8,128)S(1)}, f32[128,256]{1,0:T(8,128)S(1)}, u32[]{:S(2)}, u32[]{:S(2)}) collective-permute-start(f32[128,256]{1,0:T(8,128)S(1)} %shard_map.153.own_ref), channel_id=1, source_target_pairs={{0,1},{1,0},{2,3},{3,2},{4,5},{5,4},{6,7},{7,6},{8,9},{9,8},{10,11... | collective-permute-start | bytes 393224 | tf_op jit(solution)/shard_map/ppermute | solution.py:467
  57.9 1.9 %collective-permute-start.15 = (f32[72,256]{1,0:T(8,128)S(1)}, f32[72,256]{1,0:T(8,128)S(1)}, u32[]{:S(2)}, u32[]{:S(2)}) collective-permute-start(f32[72,256]{1,0:T(8,128)S(1)} %shard_map.151.m0), channel_id=1, source_target_pairs={{0,1},{1,0},{2,3},{3,2},{4,5},{5,4},{6,7},{7,6},{8,9},{9,8},{10,11... | collective-permute-start | bytes 221192 | tf_op jit(solution)/shard_map/ppermute | solution.py:467
  58.0 4.7 %collective-permute-start.16 = (f32[72,256]{1,0:T(8,128)S(1)}, f32[72,256]{1,0:T(8,128)S(1)}, u32[]{:S(2)}, u32[]{:S(2)}) collective-permute-start(f32[72,256]{1,0:T(8,128)S(1)} %shard_map.151.m0), channel_id=1, source_target_pairs={{0,2},{1,3},{2,0},{3,1},{4,6},{5,7},{6,4},{7,5},{8,10},{9,11},{10,... | collective-permute-start | bytes 221192 | tf_op jit(solution)/shard_map/ppermute | solution.py:467
  59.7 4.2 %collective-permute-start.17 = (f32[72,256]{1,0:T(8,128)S(1)}, f32[72,256]{1,0:T(8,128)S(1)}, u32[]{:S(2)}, u32[]{:S(2)}) collective-permute-start(f32[72,256]{1,0:T(8,128)S(1)} %shard_map.151.m0), channel_id=1, source_target_pairs={{0,3},{1,2},{2,1},{3,0},{4,7},{5,6},{6,5},{7,4},{8,11},{9,10},{10,... | collective-permute-start | bytes 221192 | tf_op jit(solution)/shard_map/ppermute | solution.py:467
  (8 other events, 72.6 us)

commit v5 on v4

--- a/solution.py
+++ b/solution.py
@@ -127,34 +127,53 @@
         norm_acc[...] = jnp.zeros_like(norm_acc)
         wc_acc[...] = jnp.zeros_like(wc_acc)
 
-    mid = nn(feats_ref[...], w_mid_ref[...]).astype(bf16)
-    mid_ref[...] = mid
-    scores = nt(sw_ref[...], mid)
-    zsum = scores[hm : hm + heads]
-    small = jnp.exp(-jnp.abs(zsum))
-    inv_tau = 1.0 / (0.5 + (jnp.maximum(zsum, 0.0) + jnp.log(1.0 + small)))
-    sig = jnp.where(zsum >= 0.0, 1.0, small) / (1.0 + small)
-    position = step * block + cols_of((1, block))
-    live = (valid_ref[...] > 0) & (position < owned_ref[0])
-    live_f = live.astype(f32)
-    aux_ref[0:heads, :] = inv_tau
-    aux_ref[2 * heads : 3 * heads, :] = sig * inv_tau
-    for h in range(heads):
-        span = slice(h * slices, (h + 1) * slices)
-        logits = scores[span] * inv_tau[h : h + 1]
-        peak = jnp.max(logits, axis=0, keepdims=True)
-        expo = jnp.exp(logits - peak)
-        total = jnp.sum(expo, axis=0, keepdims=True)
-        weights = expo * (live_f / total)
-        wt_ref[span, :] = weights.astype(bf16)
-        lanes = weights[:, 0:128]
-        for c in range(1, block // 128):
-            lanes = lanes + weights[:, c * 128 : (c + 1) * 128]
-        norm_acc[span, :] += lanes
-        aux_ref[heads + h : heads + h + 1, :] = jnp.where(live, peak + jnp.log(total), jnp.inf)
-    wt = wt_ref[...]
-    raw_acc[...] += nn(wt, mid)
-    wc_acc[...] += nn(wt, cot_ref[...])
+    piece = min(sub_block, block)
+    base = step * block
+    owned = owned_ref[0]
+
+    def products(i):
+        at = slice(i * piece, (i + 1) * piece)
+        mid = nn(feats_ref[at, :], w_mid_ref[...]).astype(bf16)
+        mid_ref[pl.ds(pl.multiple_of(base + i * piece, piece), piece), :] = mid
+        return mid, nt(sw_ref[...], mid)
+
+    def statistics(i, mid, scores):
+        at = slice(i * piece, (i + 1) * piece)
+        span_all = pl.ds(pl.multiple_of(base + i * piece, piece), piece)
+        zsum = scores[hm : hm + heads]
+        small = jnp.exp(-jnp.abs(zsum))
+        inv_tau = 1.0 / (0.5 + (jnp.maximum(zsum, 0.0) + jnp.log(1.0 + small)))
+        sig = jnp.where(zsum >= 0.0, 1.0, small) / (1.0 + small)
+        position = base + i * piece + cols_of((1, piece))
+        live = (valid_ref[:, at] > 0) & (position < owned)
+        live_f = live.astype(f32)
+        rounded, sums, logs = [], [], []
+        for h in range(heads):
+            span = slice(h * slices, (h + 1) * slices)
+            logits = scores[span] * inv_tau[h : h + 1]
+            peak = jnp.max(logits, axis=0, keepdims=True)
+            expo = jnp.exp(logits - peak)
+            total = jnp.sum(expo, axis=0, keepdims=True)
+            weights = expo * (live_f / total)
+            rounded.append(weights.astype(bf16))
+            lanes = weights[:, 0:128]
+            for c in range(1, piece // 128):
+                lanes = lanes + weights[:, c * 128 : (c + 1) * 128]
+            sums.append(lanes)
+            logs.append(jnp.where(live, peak + jnp.log(total), jnp.inf))
+        wt = jnp.concatenate(rounded, axis=0)
+        wt_ref[:, span_all] = wt
+        norm_acc[...] += jnp.concatenate(sums, axis=0)
+        aux_ref[:, span_all] = jnp.concatenate([inv_tau] + logs + [sig * inv_tau], axis=0)
+        raw_acc[...] += nn(wt, mid)
+        wc_acc[...] += nn(wt, cot_ref[at, :])
+
+    ready = products(0)
+    for i in range(block // piece):
+        current = ready
+        if (i + 1) * piece < block:
+            ready = products(i + 1)
+        statistics(i, *current)
 
     @pl.when(step == pl.num_programs(0) - 1)
     def _():
@@ -325,7 +344,7 @@
     width = mid_ref.shape[1]
     depth = width // heads
     hm = heads * slices
-    block = mid_ref.shape[0]
+    block = feats_ref.shape[0]
     top = hm + 16
 
     @pl.when(step == 0)
@@ -343,22 +362,26 @@
     piece = min(sub_block, block)
     pieces = [slice(i * piece, (i + 1) * piece) for i in range(block // piece)]
 
+    def whole(at):
+        return pl.ds(pl.multiple_of(step * block + at.start, piece), piece)
+
     def products(at):
-        return nt(lhs[...], mid_ref[at, :]), nt(mw_ref[...], cot_ref[at, :])
+        return nt(lhs[...], mid_ref[whole(at), :]), nt(mw_ref[...], cot_ref[at, :])
 
     def per_head(at, from_mid, from_cot):
         weights_b, u_b, sums = [], [], []
+        aux = aux_ref[:, whole(at)]
         for h in range(heads):
             span = slice(h * slices, (h + 1) * slices)
-            inv_tau = aux_ref[h : h + 1, at]
+            inv_tau = aux[h : h + 1]
             logits = from_mid[span] * inv_tau
-            weights = jnp.exp(logits - aux_ref[heads + h : heads + h + 1, at])
+            weights = jnp.exp(logits - aux[heads + h : heads + h + 1])
             d_weights = from_cot[span] + from_mid[top + h * slices : top + (h + 1) * slices]
             d_weights = d_weights + dn_ref[span, 0:1]
             mean = jnp.sum(weights * d_weights, axis=0, keepdims=True)
             d_logits = weights * (d_weights - mean)
             d_tau = jnp.sum(d_logits * logits, axis=0, keepdims=True)
-            sums.append(-d_tau * aux_ref[2 * heads + h : 2 * heads + h + 1, at])
+            sums.append(-d_tau * aux[2 * heads + h : 2 * heads + h + 1])
             weights_b.append(weights.astype(bf16))
             u_b.append((d_logits * inv_tau).astype(bf16))
         c_sum = jnp.concatenate(sums, axis=0)
@@ -368,11 +391,14 @@
 
     def outputs(at, weights_b, u_b, sums):
         d_mid = nn(yt[...], jnp.concatenate([weights_b, u_b[0:hm]], axis=0))
-        for h in range(heads):
-            span = slice(h * depth, (h + 1) * depth)
-            dmt_ref[span, at] = (d_mid[span] + temp * sums[h]).astype(bf16)
-        grad_acc[...] += nn(dmt_ref[:, at], feats_ref[at, :])
-        small_acc[...] += nn(u_b, mid_ref[at, :])
+        d_mid = [
+            (d_mid[h * depth : (h + 1) * depth] + temp * sums[h]).astype(bf16)
+            for h in range(heads)
+        ]
+        d_mid = jnp.concatenate(d_mid, axis=0)
+        dmt_ref[:, whole(at)] = d_mid
+        grad_acc[...] += nn(d_mid, feats_ref[at, :])
+        small_acc[...] += nn(u_b, mid_ref[whole(at), :])
 
     ready = products(pieces[0])
     for i, at in enumerate(pieces):
@@ -416,14 +442,17 @@
 
 
 def rows_kernel(wt_ref, dmt_ref, mw_ref, w_mid_ref, _, attended_ref, feats_grad_ref, token_ref):
+    block = attended_ref.shape[0]
+    at = pl.ds(pl.multiple_of(pl.program_id(0) * block, block), block)
     token_ref[...] = jnp.zeros_like(token_ref)
-    attended_ref[...] = tn(wt_ref[...], mw_ref[...]).astype(bf16)
+    attended_ref[...] = tn(wt_ref[:, at], mw_ref[...]).astype(bf16)
     feats_grad_ref[...] = lax.dot_general(
-        dmt_ref[...], w_mid_ref[...], (((0,), (1,)), ((), ())), preferred_element_type=f32
+        dmt_ref[:, at], w_mid_ref[...], (((0,), (1,)), ((), ())), preferred_element_type=f32
     ).astype(bf16)
 
 
-def grad_out_kernel(own_ref, other_ref, mixed_t_ref, grad_out_ref, whole):
+def grad_out_kernel(own_ref, other_ref, mixed_t_ref, grad_out_ref, token_ref, whole):
+    token_ref[...] = jnp.zeros_like(token_ref)
     place = group_place() & 1
     rows = own_ref.shape[0]
     for k, part in enumerate((own_ref, other_ref)):
@@ -468,9 +497,9 @@
 
 
 def sum_kernel(count, *refs):
-    total = refs[0][...] + refs[1][...]
+    total = refs[0][...] + refs[count - 1][...]
     if count == 4:
-        total = total + (refs[2][...] + refs[3][...])
+        total = total + (refs[1][...] + refs[2][...])
     refs[-1][...] = total
 
 
@@ -491,19 +520,20 @@
     return (got[0] + got[1]) + (got[2] + got[3])
 
 
-def sum_over_groups(total, count, *before):
-    stride = group
+def sum_stage(total, stride, others, count, *before):
+    got = [total] + [exchange(total, stride * j, count) for j in range(others, 0, -1)]
+    if before:
+        return sum_behind(got, *before)
+    if others == 1:
+        return got[0] + got[1]
+    return (got[0] + got[3]) + (got[1] + got[2])
+
+
+def sum_over_groups(total, stride, count, *before):
     while stride < count:
-        if count // stride % 4 == 0:
-            got = [total] + [exchange(total, stride * j, count) for j in (1, 2, 3)]
-            if before:
-                total = sum_behind(got, *before)
-            else:
-                total = (got[0] + got[1]) + (got[2] + got[3])
-            stride *= 4
-        else:
-            total = total + exchange(total, stride, count)
-            stride *= 2
+        others = 3 if count // stride % 4 == 0 else 1
+        total = sum_stage(total, stride, others, count, *before)
+        stride *= others + 1
     return total
 
 
@@ -520,21 +550,22 @@
     smem = pl.BlockSpec(memory_space=pltpu.SMEM)
 
     def blocks(size):
-        return (
-            (rows // size,),
-            pl.BlockSpec((size, width), lambda i: (i, 0)),
-            pl.BlockSpec((hm, size), lambda i: (0, i)),
-            pl.BlockSpec((3 * heads, size), lambda i: (0, i)),
-        )
+        return (rows // size,), pl.BlockSpec((size, width), lambda i: (i, 0))
 
     def like(shape, dtype):
         return jax.ShapeDtypeStruct(shape, dtype)
+
+    def far(x):
+        return pltpu.with_memory_space_constraint(x, pltpu.HBM)
+
+    near = pltpu.VMEM
+    whole = pl.BlockSpec(memory_space=pltpu.VMEM)
 
     temp = temp_vec.reshape(1, depth)
     half = (2 * slices + 8, 128)
     wide = (hm // 2, width)
     block = min(2048, rows)
-    grid, by_rows, by_cols, aux_spec = blocks(block)
+    grid, by_rows = blocks(block)
     mid, wt, aux, sw, sb, w_cat, keep, send, wc_keep, wc_send = pl.pallas_call(
         functools.partial(stats_kernel, heads, slices),
         grid=grid,
@@ -549,29 +580,18 @@
             full((width, width)),
             full((3, depth, depth)),
         ],
-        out_specs=[
-            by_rows,
-            by_cols,
-            aux_spec,
-            full((hm + 16, width)),
-            full((width, hm)),
-            full((depth, 128)),
-            full(half),
-            full(half),
-            full(wide),
-            full(wide),
-        ],
+        out_specs=[whole] * 10,
         out_shape=[
-            like((rows, width), bf16),
-            like((hm, rows), bf16),
-            like((3 * heads, rows), f32),
-            like((hm + 16, width), bf16),
-            like((width, hm), bf16),
-            like((depth, 128), bf16),
-            like(half, f32),
-            like(half, f32),
-            like(wide, f32),
-            like(wide, f32),
+            near((rows, width), bf16),
+            near((hm, rows), bf16),
+            near((3 * heads, rows), f32),
+            near((hm + 16, width), bf16),
+            near((width, hm), bf16),
+            near((depth, 128), bf16),
+            near(half, f32),
+            near(half, f32),
+            near(wide, f32),
+            near(wide, f32),
         ],
         scratch_shapes=[
             pltpu.VMEM((hm, width), f32),
@@ -579,16 +599,16 @@
             pltpu.VMEM((hm, width), f32),
             pltpu.VMEM((2,) + half, f32),
         ],
-        compiler_params=params(60),
+        compiler_params=params(32),
         cost_estimate=cost(4 * unit, rows * width * 8, rows * hm),
-    )(owned, valid.reshape(1, rows), feats, cotangent, w_mid, w_slice, temp, w_out, w_qkv)
+    )(owned, *map(far, (valid.reshape(1, rows), feats, cotangent, w_mid, w_slice, temp, w_out, w_qkv)))
 
     own = keep + exchange(send, 1, count)
     wc_got = exchange(wc_send, 1, count)
-    own = own + exchange(own, 2, count)
+    own = sum_stage(own, 2, 3, count)
     wc_sum = sum_behind([wc_keep, wc_got], own)
     wc_got = exchange(wc_sum, 2, count)
-    own = sum_over_groups(own, count)
+    own = sum_over_groups(own, 8, count)
     wc_sum = sum_behind([wc_sum, wc_got], own)
     other = exchange(own, 1, count)
     strides = [stride for stride in (1 << i for i in range(2, 30)) if stride < count]
@@ -600,11 +620,11 @@
     mw, mixed_t, dr, drt, dn, grad_qkv = pl.pallas_call(
         functools.partial(tokens_kernel, heads, slices),
         out_shape=[
-            like((hm, width), bf16),
-            like((width, hm), bf16),
-            like((hm, width), bf16),
-            like((width, hm), bf16),
-            like((hm, 128), f32),
+            near((hm, width), bf16),
+            near((width, hm), bf16),
+            near((hm, width), bf16),
+            near((width, hm), bf16),
+            near((hm, 128), f32),
             like((3, depth, depth), f32),
         ],
         scratch_shapes=[pltpu.VMEM((2,) + half, f32)],
@@ -616,26 +636,15 @@
 
     larger = (width // group + slices // group, width)
     block = min(2048, rows)
-    grid, by_rows, by_cols, aux_spec = blocks(block)
+    grid, by_rows = blocks(block)
     dmt, *sends = pl.pallas_call(
         functools.partial(backward_kernel, heads, slices),
         grid=grid,
-        in_specs=[
-            aux_spec,
-            by_rows,
-            by_rows,
-            by_rows,
-            full((hm + 16, width)),
-            full((width, hm)),
-            full((hm, width)),
-            full((hm, width)),
-            full((width, hm)),
-            full((hm, 128)),
-            full((1, depth)),
-            pl.BlockSpec(memory_space=pl.ANY),
-        ],
-        out_specs=[by_cols] + [full(larger)] * group,
-        out_shape=[like((width, rows), bf16)] + [like(larger, f32)] * group,
+        in_specs=[whole, whole, by_rows, by_rows]
+        + [whole] * 7
+        + [pl.BlockSpec(memory_space=pl.ANY)],
+        out_specs=[whole] * (1 + group),
+        out_shape=[near((width, rows), bf16)] + [near(larger, f32)] * group,
         scratch_shapes=[
             pltpu.VMEM((2 * hm + 16, width), bf16),
             pltpu.VMEM((width, 2 * hm), bf16),
@@ -652,14 +661,14 @@
     wc_other = exchange(wc_sum, 1, count)
 
     block = min(1024, rows)
-    grid, by_rows, by_cols, aux_spec = blocks(block)
+    grid, by_rows = blocks(block)
     attended, feats_grad, token = pl.pallas_call(
         rows_kernel,
         grid=grid,
         in_specs=[
-            by_cols,
-            by_cols,
-            full((hm, width)),
+            whole,
+            whole,
+            whole,
             full((width, width)),
             pl.BlockSpec(memory_space=pl.ANY),
         ],
@@ -669,15 +678,15 @@
         cost_estimate=cost(2 * unit, rows * width * 8),
     )(wt, dmt, mw, w_mid, mid_total)
 
-    mid_total = sum_over_groups(mid_total, count, token)
-    grad_w_out = pl.pallas_call(
+    grad_w_out, token_out = pl.pallas_call(
         grad_out_kernel,
-        out_shape=like((width, width), f32),
+        out_shape=[like((width, width), f32), like((8, 128), f32)],
         scratch_shapes=[pltpu.VMEM((hm, width), f32)],
         compiler_params=params(8, False),
         cost_estimate=cost(4 * width**3, 3 * width * width * 4),
     )(wc_sum, wc_other, mixed_t)
 
+    mid_total = sum_over_groups(mid_total, group, count, token, token_out)
     mid_parts = gather_group(mid_total, count)
     grad_w_mid, grad_w_slice, grad_temp = pl.pallas_call(
         functools.partial(finish_kernel, depth),

time: 66.4 us -> 61 us (0.919)
  waiting for transfers between devices: 14.1 us -> 17.5 us
  local copies, waits for them, and re-layouts: 3.23 us -> 0.02 us
  starting transfers between devices: 23.4 us -> 20.6 us
  Pallas kernels: 22.6 us -> 21.3 us
  other arithmetic: 0.81 us -> 0.04 us
    ppermute x20, waiting for transfers between devices: 14.1 us -> 17.5 us  [exchange(): return lax.ppermute(x, 'node', [(i, i ^ k) for i in range(count)])]
    unnamed x24 -> x10, local copies, waits for them, and re-layouts: 3.23 us -> 0.02 us
    ppermute x20, starting transfers between devices: 23.4 us -> 20.6 us  [exchange(): return lax.ppermute(x, 'node', [(i, i ^ k) for i in range(count)])]
    pallas_call x1, Pallas kernels: 8.26 us -> 7.25 us  [shards(): pl.pallas_call(functools.partial(stats_kernel, heads, slices), grid=grid,...]
    add x1, other arithmetic: 0.78 us -> 0.01 us  [shards(): own = keep + exchange(send, 1, count)]
  transfers between devices with their start and end apart: 20 -> 20, of which waited for: 10 -> 11; matrix products, arithmetic and copies ran while one was open for 1% -> 0% of each run, Pallas kernels for 12% -> 22%
where the time goes in v5:
time: 61 us; the launch traced here: 60.8 us
  Pallas kernels  21.3 us (35%)
  starting transfers between devices  20.6 us (34%)
  waiting for transfers between devices  17.5 us (29%)
  between operations  1.42 us (2%)
    ppermute x20, starting transfers between devices, exchange(): return lax.ppermute(x, 'node', [(i, i ^ k) for i in range(count)])  20.6 us
    ppermute x20, waiting for transfers between devices, exchange(): return lax.ppermute(x, 'node', [(i, i ^ k) for i in range(count)])  17.5 us
    pallas_call x1, Pallas kernels, shards(): pl.pallas_call(functools.partial(stats_kernel, heads, slices), grid=grid,...  7.25 us
    pallas_call x1, Pallas kernels, shards(): pl.pallas_call(functools.partial(backward_kernel, heads, slices), grid=gr...  5.72 us
    pallas_call x1, Pallas kernels, shards(): pl.pallas_call(rows_kernel, grid=grid, in_specs=[whole, whole, whole, ful...  3.42 us
    pallas_call x1, Pallas kernels, shards(): pl.pallas_call(functools.partial(tokens_kernel, heads, slices), out_shape...  3.1 us
  transfers between devices with their start and end apart: 20, of which 11 were waited for; matrix products, arithmetic and copies ran while one was open for 0% of the time, Pallas kernels for 22%

profile of v5, /device:TPU:0, one launch (start us, length us, event | category | flops | bytes accessed | tf_op | source)
XLA Modules:
  0.0 60.8 jit_solution(4144359255099616921)
XLA Ops:
  1.3 7.3 %shard_map.144 = (bf16[4096,256]{1,0:T(8,128)(2,1)S(1)}, bf16[256,4096]{1,0:T(8,128)(2,1)S(1)}, f32[24,4096]{1,0:T(8,128)S(1)}, bf16[272,256]{1,0:T(8,128)(2,1)S...) custom-call(s32[1]{0:T(128)S(6)} %copy.16.owned_ref, ...), custom_call_target="tpu_custom_call" | custom-call | flops 2147483648 | bytes 8388608 | tf_op jit(solution)/shard_map/pallas_call | solution.py:569
  9.1 0.9 %collective-permute-done = f32[72,128]{1,0:T(8,128)S(1)} collective-permute-done((f32[72,128]{1,0:T(8,128)S(1)}, f32[72,128]{1,0:T(8,128)S(1)}, u32[]{:S(2)}, u32[]{:S(2)}) %collective-permute-start) | collective-permute-done | bytes 36896 | tf_op jit(solution)/shard_map/ppermute | solution.py:496
  10.0 2.8 %collective-permute-start.1 = (f32[72,128]{1,0:T(8,128)S(1)}, f32[72,128]{1,0:T(8,128)S(1)}, u32[]{:S(2)}, u32[]{:S(2)}) collective-permute-start(f32[72,128]{1,0:T(8,128)S(1)} %add.24), channel_id=1, source_target_pairs={{0,2},{1,3},{2,0},{3,1},{4,6},{5,7},{6,4},{7,5},{8,10},{9,11},{10,... | collective-permute-start | bytes 110600 | tf_op jit(solution)/shard_map/ppermute | solution.py:496
  12.8 1.5 %collective-permute-start.2 = (f32[72,128]{1,0:T(8,128)S(1)}, f32[72,128]{1,0:T(8,128)S(1)}, u32[]{:S(2)}, u32[]{:S(2)}) collective-permute-start(f32[72,128]{1,0:T(8,128)S(1)} %add.24), channel_id=1, source_target_pairs={{0,6},{1,7},{2,4},{3,5},{4,2},{5,3},{6,0},{7,1},{8,14},{9,15},{10,... | collective-permute-start | bytes 110600 | tf_op jit(solution)/shard_map/ppermute | solution.py:496
  14.8 3.1 %collective-permute-done.2 = f32[72,128]{1,0:T(8,128)S(1)} collective-permute-done((f32[72,128]{1,0:T(8,128)S(1)}, f32[72,128]{1,0:T(8,128)S(1)}, u32[]{:S(2)}, u32[]{:S(2)}) %collective-permute-start.2) | collective-permute-done | bytes 36896 | tf_op jit(solution)/shard_map/ppermute | solution.py:496
  18.4 1.6 %collective-permute-start.7 = (f32[128,256]{1,0:T(8,128)S(1)}, f32[128,256]{1,0:T(8,128)S(1)}, u32[]{:S(2)}, u32[]{:S(2)}) collective-permute-start(f32[128,256]{1,0:T(8,128)S(1)} %shard_map.146.refs_0_), channel_id=1, source_target_pairs={{0,2},{1,3},{2,0},{3,1},{4,6},{5,7},{6,4},{7,5},{8,10},{9,11},{10,... | collective-permute-start | bytes 393224 | tf_op jit(solution)/shard_map/ppermute | solution.py:496
  19.9 2.6 %collective-permute-start.4 = (f32[72,128]{1,0:T(8,128)S(1)}, f32[72,128]{1,0:T(8,128)S(1)}, u32[]{:S(2)}, u32[]{:S(2)}) collective-permute-start(f32[72,128]{1,0:T(8,128)S(1)} %add_add_fusion.1.refs_2_), channel_id=1, source_target_pairs={{0,8},{1,9},{2,10},{3,11},{4,12},{5,13},{6,14},{7,15},{8,0},{9,1},... | collective-permute-start | bytes 110600 | tf_op jit(solution)/shard_map/ppermute | solution.py:496
  22.5 2.6 %collective-permute-done.4 = f32[72,128]{1,0:T(8,128)S(1)} collective-permute-done((f32[72,128]{1,0:T(8,128)S(1)}, f32[72,128]{1,0:T(8,128)S(1)}, u32[]{:S(2)}, u32[]{:S(2)}) %collective-permute-start.4) | collective-permute-done | bytes 36896 | tf_op jit(solution)/shard_map/ppermute | solution.py:496
  25.4 1.2 %collective-permute-done.5.got_ref = f32[72,128]{1,0:T(8,128)S(1)} collective-permute-done((f32[72,128]{1,0:T(8,128)S(1)}, f32[72,128]{1,0:T(8,128)S(1)}, u32[]{:S(2)}, u32[]{:S(2)}) %collective-permute-start.5) | collective-permute-done | bytes 36896 | tf_op jit(solution)/shard_map/ppermute | solution.py:496
  26.6 3.1 %shard_map.145 = (bf16[256,256]{1,0:T(8,128)(2,1)S(1)}, bf16[256,256]{1,0:T(8,128)(2,1)S(1)}, bf16[256,256]{1,0:T(8,128)(2,1)S(1)}, bf16[256,256]{1,0:T(8,128)(2...) custom-call(f32[72,128]{1,0:T(8,128)S(1)} %add.28.own_ref.refs_2_, f32[72,128]{1,0:T(8,128)S(1)} %collective-permute-done.5.got_ref, ...), custom_call_target="tpu_custom_call" | custom-call | flops 503316480 | bytes 1048576 | tf_op jit(solution)/shard_map/pallas_call | solution.py:620
  30.2 2.6 %collective-permute-start.15 = (f32[128,256]{1,0:T(8,128)S(1)}, f32[128,256]{1,0:T(8,128)S(1)}, u32[]{:S(2)}, u32[]{:S(2)}) collective-permute-start(f32[128,256]{1,0:T(8,128)S(1)} %shard_map.148._.refs_0_), channel_id=1, source_target_pairs={{0,8},{1,9},{2,10},{3,11},{4,12},{5,13},{6,14},{7,15},{8,0},{9,1},... | collective-permute-start | bytes 393224 | tf_op jit(solution)/shard_map/ppermute | solution.py:496
  32.9 5.7 %shard_map.149 = (bf16[256,4096]{1,0:T(8,128)(2,1)S(1)}, f32[72,256]{1,0:T(8,128)S(1)}, f32[72,256]{1,0:T(8,128)S(1)}, f32[72,256]{1,0:T(8,128)S(1)}, f32[72,256]{1,0:T(8,128)S(1)}) custom-call(f32[24,4096]{1,0:T(8,128)S(1)} %get-tuple-element.37.aux_ref, bf16[4096,256]{1,0:T(8,128)(2,1)S(1)} %get-tuple-element.38.mid_ref, bf16[4096,256]{1,0:T(8,128)(2,1)S(1)} %copy-done.2, ...), custom_call_target="tpu_custom_call" | custom-call | flops 4294967296 | bytes 8388608 | tf_op jit(solution)/shard_map/pallas_call | solution.py:640
  39.4 1.4 %collective-permute-start.9 = (f32[72,256]{1,0:T(8,128)S(1)}, f32[72,256]{1,0:T(8,128)S(1)}, u32[]{:S(2)}, u32[]{:S(2)}) collective-permute-start(f32[72,256]{1,0:T(8,128)S(1)} %get-tuple-element.52.refs_2_), channel_id=1, source_target_pairs={{0,1},{1,0},{2,3},{3,2},{4,5},{5,4},{6,7},{7,6},{8,9},{9,8},{10,11... | collective-permute-start | bytes 221192 | tf_op jit(solution)/shard_map/ppermute | solution.py:496
  40.9 2.8 %collective-permute-done.10 = f32[72,256]{1,0:T(8,128)S(1)} collective-permute-done((f32[72,256]{1,0:T(8,128)S(1)}, f32[72,256]{1,0:T(8,128)S(1)}, u32[]{:S(2)}, u32[]{:S(2)}) %collective-permute-start.10) | collective-permute-done | bytes 73760 | tf_op jit(solution)/shard_map/ppermute | solution.py:496
  43.8 1.0 %collective-permute-start.12 = (f32[72,256]{1,0:T(8,128)S(1)}, f32[72,256]{1,0:T(8,128)S(1)}, u32[]{:S(2)}, u32[]{:S(2)}) collective-permute-start(f32[72,256]{1,0:T(8,128)S(1)} %add_add_fusion._.refs_0_), channel_id=1, source_target_pairs={{0,12},{1,13},{2,14},{3,15},{4,8},{5,9},{6,10},{7,11},{8,4},{9,5},... | collective-permute-start | bytes 221192 | tf_op jit(solution)/shard_map/ppermute | solution.py:496
  44.8 1.9 %collective-permute-start.13 = (f32[72,256]{1,0:T(8,128)S(1)}, f32[72,256]{1,0:T(8,128)S(1)}, u32[]{:S(2)}, u32[]{:S(2)}) collective-permute-start(f32[72,256]{1,0:T(8,128)S(1)} %add_add_fusion._.refs_0_), channel_id=1, source_target_pairs={{0,8},{1,9},{2,10},{3,11},{4,12},{5,13},{6,14},{7,15},{8,0},{9,1},... | collective-permute-start | bytes 221192 | tf_op jit(solution)/shard_map/ppermute | solution.py:496
  46.7 1.5 %collective-permute-start.14 = (f32[72,256]{1,0:T(8,128)S(1)}, f32[72,256]{1,0:T(8,128)S(1)}, u32[]{:S(2)}, u32[]{:S(2)}) collective-permute-start(f32[72,256]{1,0:T(8,128)S(1)} %add_add_fusion._.refs_0_), channel_id=1, source_target_pairs={{0,4},{1,5},{2,6},{3,7},{4,0},{5,1},{6,2},{7,3},{8,12},{9,13},{10,... | collective-permute-start | bytes 221192 | tf_op jit(solution)/shard_map/ppermute | solution.py:496
  48.2 3.4 %shard_map.150 = (bf16[4096,256]{1,0:T(8,128)(2,1)}, bf16[4096,256]{1,0:T(8,128)(2,1)}, f32[8,128]{1,0:T(8,128)S(1)}) custom-call(bf16[256,4096]{1,0:T(8,128)(2,1)S(1)} %get-tuple-element.36.wt_ref, bf16[256,4096]{1,0:T(8,128)(2,1)S(1)} %get-tuple-element.50.dmt_ref, bf16[256,256]{1,0:T(8,128)(2,1)S(1)} %get-tuple-element.44.refs_2_.mw_ref, ...), custom_call_target="tpu_custom_call" | custom-call | flops 1073741824 | bytes 8388608 | tf_op jit(solution)/shard_map/pallas_call | solution.py:665
  51.7 1.0 %shard_map.152 = (f32[256,256]{1,0:T(8,128)}, f32[8,128]{1,0:T(8,128)S(1)}) custom-call(f32[128,256]{1,0:T(8,128)S(1)} %shard_map.151.own_ref, f32[128,256]{1,0:T(8,128)S(1)} %collective-permute-done.16.other_ref, bf16[256,256]{1,0:T(8,128)(2,1)S(1)} %get-tuple-element.58.mixed_t_ref), custom_call_target="tpu_custom_call" | custom-call | flops 67108864 | bytes 786432 | tf_op jit(solution)/shard_map/pallas_call | solution.py:681
  52.6 1.5 %collective-permute-done.13.refs_2_ = f32[72,256]{1,0:T(8,128)S(1)} collective-permute-done((f32[72,256]{1,0:T(8,128)S(1)}, f32[72,256]{1,0:T(8,128)S(1)}, u32[]{:S(2)}, u32[]{:S(2)}) %collective-permute-start.13) | collective-permute-done | bytes 73760 | tf_op jit(solution)/shard_map/ppermute | solution.py:496
  54.3 0.8 %collective-permute-start.18 = (f32[72,256]{1,0:T(8,128)S(1)}, f32[72,256]{1,0:T(8,128)S(1)}, u32[]{:S(2)}, u32[]{:S(2)}) collective-permute-start(f32[72,256]{1,0:T(8,128)S(1)} %shard_map.153.m0), channel_id=1, source_target_pairs={{0,2},{1,3},{2,0},{3,1},{4,6},{5,7},{6,4},{7,5},{8,10},{9,11},{10,... | collective-permute-start | bytes 221192 | tf_op jit(solution)/shard_map/ppermute | solution.py:496
  55.1 1.0 %collective-permute-start.19 = (f32[72,256]{1,0:T(8,128)S(1)}, f32[72,256]{1,0:T(8,128)S(1)}, u32[]{:S(2)}, u32[]{:S(2)}) collective-permute-start(f32[72,256]{1,0:T(8,128)S(1)} %shard_map.153.m0), channel_id=1, source_target_pairs={{0,3},{1,2},{2,1},{3,0},{4,7},{5,6},{6,5},{7,4},{8,11},{9,10},{10,... | collective-permute-start | bytes 221192 | tf_op jit(solution)/shard_map/ppermute | solution.py:496
  56.1 3.3 %collective-permute-done.18.m2 = f32[72,256]{1,0:T(8,128)S(1)} collective-permute-done((f32[72,256]{1,0:T(8,128)S(1)}, f32[72,256]{1,0:T(8,128)S(1)}, u32[]{:S(2)}, u32[]{:S(2)}) %collective-permute-start.18) | collective-permute-done | bytes 73760 | tf_op jit(solution)/shard_map/ppermute | solution.py:496
  60.1 0.7 %shard_map.154 = (f32[256,256]{1,0:T(8,128)}, f32[32,32]{1,0:T(8,128)}, f32[1,32]{1,0:T(1,128)}) custom-call(f32[72,256]{1,0:T(8,128)S(1)} %shard_map.153.m0, f32[72,256]{1,0:T(8,128)S(1)} %collective-permute-done.17.m1, f32[72,256]{1,0:T(8,128)S(1)} %collective-permute-done.18.m2, f32[72,256]{1,0:T(8,128)S(1)} %collective-permute-done.19.m3), custom_call_target="tpu_custom_call" | custom-call | bytes 524288 | tf_op jit(solution)/shard_map/pallas_call | solution.py:691
  (41 shorter events, 3.9 us)
Async XLA Ops:
  1.3 25.3 %copy-start.3 = (bf16[256,256]{1,0:T(8,128)(2,1)S(1)}, bf16[256,256]{1,0:T(8,128)(2,1)}, u32[]{:S(2)}) copy-start(bf16[256,256]{1,0:T(8,128)(2,1)} %w_out_ref.3) | copy-start | bytes 393220
  1.3 31.6 %copy-start.2 = (bf16[4096,256]{1,0:T(8,128)(2,1)S(1)}, bf16[4096,256]{1,0:T(8,128)(2,1)}, u32[]{:S(2)}) copy-start(bf16[4096,256]{1,0:T(8,128)(2,1)} %cot_ref.3) | copy-start | bytes 6291460
  8.6 24.3 %copy-start.1 = (bf16[4096,256]{1,0:T(8,128)(2,1)S(1)}, bf16[4096,256]{1,0:T(8,128)(2,1)}, u32[]{:S(2)}) copy-start(bf16[4096,256]{1,0:T(8,128)(2,1)} %feats_ref.3) | copy-start | bytes 6291460
  8.6 24.3 %copy-start.4 = (bf16[32]{0:T(256)(128)(2,1)S(1)}, bf16[32]{0:T(256)(128)(2,1)}, u32[]{:S(2)}) copy-start(bf16[32]{0:T(256)(128)(2,1)} %param.15) | copy-start | bytes 196
  8.6 1.4 %collective-permute-start = (f32[72,128]{1,0:T(8,128)S(1)}, f32[72,128]{1,0:T(8,128)S(1)}, u32[]{:S(2)}, u32[]{:S(2)}) collective-permute-start(f32[72,128]{1,0:T(8,128)S(1)} %get-tuple-element.42), channel_id=1, source_target_pairs={{0,1},{1,0},{2,3},{3,2},{4,5},{5,4},{6,7},{7,6},{8,9},{9,8},{10,11... | collective-permute-start | bytes 110600 | tf_op jit(solution)/shard_map/ppermute | solution.py:496
  10.0 4.8 %collective-permute-start.1 = (f32[72,128]{1,0:T(8,128)S(1)}, f32[72,128]{1,0:T(8,128)S(1)}, u32[]{:S(2)}, u32[]{:S(2)}) collective-permute-start(f32[72,128]{1,0:T(8,128)S(1)} %add.24), channel_id=1, source_target_pairs={{0,2},{1,3},{2,0},{3,1},{4,6},{5,7},{6,4},{7,5},{8,10},{9,11},{10,... | collective-permute-start | bytes 110600 | tf_op jit(solution)/shard_map/ppermute | solution.py:496
  12.8 5.1 %collective-permute-start.2 = (f32[72,128]{1,0:T(8,128)S(1)}, f32[72,128]{1,0:T(8,128)S(1)}, u32[]{:S(2)}, u32[]{:S(2)}) collective-permute-start(f32[72,128]{1,0:T(8,128)S(1)} %add.24), channel_id=1, source_target_pairs={{0,6},{1,7},{2,4},{3,5},{4,2},{5,3},{6,0},{7,1},{8,14},{9,15},{10,... | collective-permute-start | bytes 110600 | tf_op jit(solution)/shard_map/ppermute | solution.py:496
  14.4 4.0 %collective-permute-start.3 = (f32[72,128]{1,0:T(8,128)S(1)}, f32[72,128]{1,0:T(8,128)S(1)}, u32[]{:S(2)}, u32[]{:S(2)}) collective-permute-start(f32[72,128]{1,0:T(8,128)S(1)} %add.24), channel_id=1, source_target_pairs={{0,4},{1,5},{2,6},{3,7},{4,0},{5,1},{6,2},{7,3},{8,12},{9,13},{10,... | collective-permute-start | bytes 110600 | tf_op jit(solution)/shard_map/ppermute | solution.py:496
  14.4 3.9 %collective-permute-start.6 = (f32[128,256]{1,0:T(8,128)S(1)}, f32[128,256]{1,0:T(8,128)S(1)}, u32[]{:S(2)}, u32[]{:S(2)}) collective-permute-start(f32[128,256]{1,0:T(8,128)S(1)} %get-tuple-element.49), channel_id=1, source_target_pairs={{0,1},{1,0},{2,3},{3,2},{4,5},{5,4},{6,7},{7,6},{8,9},{9,8},{10,11... | collective-permute-start | bytes 393224 | tf_op jit(solution)/shard_map/ppermute | solution.py:496
  18.4 6.8 %collective-permute-start.7 = (f32[128,256]{1,0:T(8,128)S(1)}, f32[128,256]{1,0:T(8,128)S(1)}, u32[]{:S(2)}, u32[]{:S(2)}) collective-permute-start(f32[128,256]{1,0:T(8,128)S(1)} %shard_map.146.refs_0_), channel_id=1, source_target_pairs={{0,2},{1,3},{2,0},{3,1},{4,6},{5,7},{6,4},{7,5},{8,10},{9,11},{10,... | collective-permute-start | bytes 393224 | tf_op jit(solution)/shard_map/ppermute | solution.py:496
  19.9 5.2 %collective-permute-start.4 = (f32[72,128]{1,0:T(8,128)S(1)}, f32[72,128]{1,0:T(8,128)S(1)}, u32[]{:S(2)}, u32[]{:S(2)}) collective-permute-start(f32[72,128]{1,0:T(8,128)S(1)} %add_add_fusion.1.refs_2_), channel_id=1, source_target_pairs={{0,8},{1,9},{2,10},{3,11},{4,12},{5,13},{6,14},{7,15},{8,0},{9,1},... | collective-permute-start | bytes 110600 | tf_op jit(solution)/shard_map/ppermute | solution.py:496
  25.2 5.0 %collective-permute-start.8 = (f32[128,256]{1,0:T(8,128)S(1)}, f32[128,256]{1,0:T(8,128)S(1)}, u32[]{:S(2)}, u32[]{:S(2)}) collective-permute-start(f32[128,256]{1,0:T(8,128)S(1)} %shard_map.147.refs_0_), channel_id=1, source_target_pairs={{0,4},{1,5},{2,6},{3,7},{4,0},{5,1},{6,2},{7,3},{8,12},{9,13},{10,... | collective-permute-start | bytes 393224 | tf_op jit(solution)/shard_map/ppermute | solution.py:496
  25.4 1.2 %collective-permute-start.5 = (f32[72,128]{1,0:T(8,128)S(1)}, f32[72,128]{1,0:T(8,128)S(1)}, u32[]{:S(2)}, u32[]{:S(2)}) collective-permute-start(f32[72,128]{1,0:T(8,128)S(1)} %add.28.own_ref.refs_2_), channel_id=1, source_target_pairs={{0,1},{1,0},{2,3},{3,2},{4,5},{5,4},{6,7},{7,6},{8,9},{9,8},{10,11... | collective-permute-start | bytes 110600 | tf_op jit(solution)/shard_map/ppermute | solution.py:496
  30.2 10.6 %collective-permute-start.15 = (f32[128,256]{1,0:T(8,128)S(1)}, f32[128,256]{1,0:T(8,128)S(1)}, u32[]{:S(2)}, u32[]{:S(2)}) collective-permute-start(f32[128,256]{1,0:T(8,128)S(1)} %shard_map.148._.refs_0_), channel_id=1, source_target_pairs={{0,8},{1,9},{2,10},{3,11},{4,12},{5,13},{6,14},{7,15},{8,0},{9,1},... | collective-permute-start | bytes 393224 | tf_op jit(solution)/shard_map/ppermute | solution.py:496
  38.6 5.2 %collective-permute-start.10 = (f32[72,256]{1,0:T(8,128)S(1)}, f32[72,256]{1,0:T(8,128)S(1)}, u32[]{:S(2)}, u32[]{:S(2)}) collective-permute-start(f32[72,256]{1,0:T(8,128)S(1)} %get-tuple-element.53), channel_id=1, source_target_pairs={{0,2},{1,3},{2,0},{3,1},{4,6},{5,7},{6,4},{7,5},{8,10},{9,11},{10,... | collective-permute-start | bytes 221192 | tf_op jit(solution)/shard_map/ppermute | solution.py:496
  39.2 4.6 %collective-permute-start.11 = (f32[72,256]{1,0:T(8,128)S(1)}, f32[72,256]{1,0:T(8,128)S(1)}, u32[]{:S(2)}, u32[]{:S(2)}) collective-permute-start(f32[72,256]{1,0:T(8,128)S(1)} %get-tuple-element.54), channel_id=1, source_target_pairs={{0,3},{1,2},{2,1},{3,0},{4,7},{5,6},{6,5},{7,4},{8,11},{9,10},{10,... | collective-permute-start | bytes 221192 | tf_op jit(solution)/shard_map/ppermute | solution.py:496
  39.4 4.4 %collective-permute-start.9 = (f32[72,256]{1,0:T(8,128)S(1)}, f32[72,256]{1,0:T(8,128)S(1)}, u32[]{:S(2)}, u32[]{:S(2)}) collective-permute-start(f32[72,256]{1,0:T(8,128)S(1)} %get-tuple-element.52.refs_2_), channel_id=1, source_target_pairs={{0,1},{1,0},{2,3},{3,2},{4,5},{5,4},{6,7},{7,6},{8,9},{9,8},{10,11... | collective-permute-start | bytes 221192 | tf_op jit(solution)/shard_map/ppermute | solution.py:496
  40.8 10.8 %collective-permute-start.16 = (f32[128,256]{1,0:T(8,128)S(1)}, f32[128,256]{1,0:T(8,128)S(1)}, u32[]{:S(2)}, u32[]{:S(2)}) collective-permute-start(f32[128,256]{1,0:T(8,128)S(1)} %shard_map.151.own_ref), channel_id=1, source_target_pairs={{0,1},{1,0},{2,3},{3,2},{4,5},{5,4},{6,7},{7,6},{8,9},{9,8},{10,11... | collective-permute-start | bytes 393224 | tf_op jit(solution)/shard_map/ppermute | solution.py:496
  43.8 8.9 %collective-permute-start.12 = (f32[72,256]{1,0:T(8,128)S(1)}, f32[72,256]{1,0:T(8,128)S(1)}, u32[]{:S(2)}, u32[]{:S(2)}) collective-permute-start(f32[72,256]{1,0:T(8,128)S(1)} %add_add_fusion._.refs_0_), channel_id=1, source_target_pairs={{0,12},{1,13},{2,14},{3,15},{4,8},{5,9},{6,10},{7,11},{8,4},{9,5},... | collective-permute-start | bytes 221192 | tf_op jit(solution)/shard_map/ppermute | solution.py:496
  44.8 9.4 %collective-permute-start.13 = (f32[72,256]{1,0:T(8,128)S(1)}, f32[72,256]{1,0:T(8,128)S(1)}, u32[]{:S(2)}, u32[]{:S(2)}) collective-permute-start(f32[72,256]{1,0:T(8,128)S(1)} %add_add_fusion._.refs_0_), channel_id=1, source_target_pairs={{0,8},{1,9},{2,10},{3,11},{4,12},{5,13},{6,14},{7,15},{8,0},{9,1},... | collective-permute-start | bytes 221192 | tf_op jit(solution)/shard_map/ppermute | solution.py:496
  46.7 7.5 %collective-permute-start.14 = (f32[72,256]{1,0:T(8,128)S(1)}, f32[72,256]{1,0:T(8,128)S(1)}, u32[]{:S(2)}, u32[]{:S(2)}) collective-permute-start(f32[72,256]{1,0:T(8,128)S(1)} %add_add_fusion._.refs_0_), channel_id=1, source_target_pairs={{0,4},{1,5},{2,6},{3,7},{4,0},{5,1},{6,2},{7,3},{8,12},{9,13},{10,... | collective-permute-start | bytes 221192 | tf_op jit(solution)/shard_map/ppermute | solution.py:496
  54.2 1.9 %collective-permute-start.17 = (f32[72,256]{1,0:T(8,128)S(1)}, f32[72,256]{1,0:T(8,128)S(1)}, u32[]{:S(2)}, u32[]{:S(2)}) collective-permute-start(f32[72,256]{1,0:T(8,128)S(1)} %shard_map.153.m0), channel_id=1, source_target_pairs={{0,1},{1,0},{2,3},{3,2},{4,5},{5,4},{6,7},{7,6},{8,9},{9,8},{10,11... | collective-permute-start | bytes 221192 | tf_op jit(solution)/shard_map/ppermute | solution.py:496
  54.3 5.1 %collective-permute-start.18 = (f32[72,256]{1,0:T(8,128)S(1)}, f32[72,256]{1,0:T(8,128)S(1)}, u32[]{:S(2)}, u32[]{:S(2)}) collective-permute-start(f32[72,256]{1,0:T(8,128)S(1)} %shard_map.153.m0), channel_id=1, source_target_pairs={{0,2},{1,3},{2,0},{3,1},{4,6},{5,7},{6,4},{7,5},{8,10},{9,11},{10,... | collective-permute-start | bytes 221192 | tf_op jit(solution)/shard_map/ppermute | solution.py:496
  55.1 5.0 %collective-permute-start.19 = (f32[72,256]{1,0:T(8,128)S(1)}, f32[72,256]{1,0:T(8,128)S(1)}, u32[]{:S(2)}, u32[]{:S(2)}) collective-permute-start(f32[72,256]{1,0:T(8,128)S(1)} %shard_map.153.m0), channel_id=1, source_target_pairs={{0,3},{1,2},{2,1},{3,0},{4,7},{5,6},{6,5},{7,4},{8,11},{9,10},{10,... | collective-permute-start | bytes 221192 | tf_op jit(solution)/shard_map/ppermute | solution.py:496
  (1 other events, 15.4 us)

commit v6 on v5

--- a/solution.py
+++ b/solution.py
@@ -73,14 +73,14 @@
     heads,
     slices,
     owned_ref,
-    valid_ref,
-    feats_ref,
-    cot_ref,
-    w_mid_ref,
-    w_slice_ref,
     temp_ref,
-    w_out_ref,
-    w_qkv_ref,
+    valid_far,
+    feats_far,
+    cot_far,
+    w_mid_far,
+    w_slice_far,
+    w_out_far,
+    w_qkv_far,
     mid_ref,
     wt_ref,
     aux_ref,
@@ -91,60 +91,92 @@
     send_ref,
     wc_keep_ref,
     wc_send_ref,
+    feats_ref,
+    cot_ref,
+    valid_ref,
+    w_mid_ref,
+    w_slice_ref,
+    w_out_ref,
+    w_qkv_ref,
     raw_acc,
     norm_acc,
     wc_acc,
     pack,
+    sems,
 ):
-    step = pl.program_id(0)
     width = w_mid_ref.shape[0]
     depth = width // heads
     hm = heads * slices
-    block = feats_ref.shape[0]
-
-    @pl.when(step == 0)
-    def _():
-        spread_d = spread_matrix(width, depth)
-        spread_m = spread_matrix(hm, slices)
-        w_slice = w_slice_ref[...]
-        half = nt(spread_m, w_slice).astype(bf16)
-        full = nt(half, spread_d)
-        sw_ref[0:hm, :] = jnp.where(same_block(hm, width, slices, depth), full, 0.0).astype(bf16)
-        half = nn(spread_d, w_slice).astype(bf16)
-        full = nt(half, spread_m)
-        sb_ref[...] = jnp.where(same_block(width, hm, depth, slices), full, 0.0).astype(bf16)
-        temp = jnp.broadcast_to(temp_ref[...].astype(f32), (16, depth)).astype(bf16)
-        full = nt(temp, spread_d)
-        sw_ref[hm : hm + 16, :] = jnp.where(same_block(16, width, 1, depth), full, 0.0).astype(
-            bf16
+    rows = feats_ref.shape[0]
+    piece = min(sub_block, rows)
+    count = rows // piece
+    small = [
+        pltpu.make_async_copy(source, target, sems.at[i])
+        for i, (source, target) in enumerate(
+            (
+                (w_slice_far, w_slice_ref),
+                (w_qkv_far, w_qkv_ref),
+                (w_mid_far, w_mid_ref),
+                (valid_far, valid_ref),
+                (w_out_far, w_out_ref),
+            )
         )
-        w_cat = jnp.zeros((depth, 128), f32)
-        for i in range(3):
-            place_at = jnp.where(rows_of((depth, 128)) + i * depth == cols_of((depth, 128)), 1.0, 0.0)
-            w_cat = w_cat + nn(w_qkv_ref[i], place_at.astype(bf16))
-        w_cat_ref[...] = w_cat.astype(bf16)
-        raw_acc[...] = jnp.zeros_like(raw_acc)
-        norm_acc[...] = jnp.zeros_like(norm_acc)
-        wc_acc[...] = jnp.zeros_like(wc_acc)
-
-    piece = min(sub_block, block)
-    base = step * block
+    ]
+    feats_in, cot_in = [], []
+    for i in range(count):
+        at = pl.ds(i * piece, piece)
+        for j, (source, target, into) in enumerate(
+            ((feats_far, feats_ref, feats_in), (cot_far, cot_ref, cot_in))
+        ):
+            sem = sems.at[len(small) + 2 * i + j]
+            into.append(pltpu.make_async_copy(source.at[at, :], target.at[at, :], sem))
+    for copy in small[:3] + feats_in[:1] + small[3:] + cot_in[:1]:
+        copy.start()
+    for i in range(1, count):
+        feats_in[i].start()
+        cot_in[i].start()
+
+    raw_acc[...] = jnp.zeros_like(raw_acc)
+    norm_acc[...] = jnp.zeros_like(norm_acc)
+    wc_acc[...] = jnp.zeros_like(wc_acc)
+    spread_d = spread_matrix(width, depth)
+    spread_m = spread_matrix(hm, slices)
+    temp = jnp.broadcast_to(temp_ref[...].astype(f32), (16, depth)).astype(bf16)
+    small[0].wait()
+    w_slice = w_slice_ref[...]
+    half = nt(spread_m, w_slice).astype(bf16)
+    full = nt(half, spread_d)
+    sw_ref[0:hm, :] = jnp.where(same_block(hm, width, slices, depth), full, 0.0).astype(bf16)
+    half = nn(spread_d, w_slice).astype(bf16)
+    full = nt(half, spread_m)
+    sb_ref[...] = jnp.where(same_block(width, hm, depth, slices), full, 0.0).astype(bf16)
+    full = nt(temp, spread_d)
+    sw_ref[hm : hm + 16, :] = jnp.where(same_block(16, width, 1, depth), full, 0.0).astype(bf16)
+    small[1].wait()
+    w_cat = jnp.zeros((depth, 128), f32)
+    for i in range(3):
+        place_at = jnp.where(rows_of((depth, 128)) + i * depth == cols_of((depth, 128)), 1.0, 0.0)
+        w_cat = w_cat + nn(w_qkv_ref[i], place_at.astype(bf16))
+    w_cat_ref[...] = w_cat.astype(bf16)
+    small[2].wait()
+    small[3].wait()
+    small[4].wait()
     owned = owned_ref[0]
 
     def products(i):
         at = slice(i * piece, (i + 1) * piece)
+        feats_in[i].wait()
         mid = nn(feats_ref[at, :], w_mid_ref[...]).astype(bf16)
-        mid_ref[pl.ds(pl.multiple_of(base + i * piece, piece), piece), :] = mid
+        mid_ref[at, :] = mid
         return mid, nt(sw_ref[...], mid)
 
     def statistics(i, mid, scores):
         at = slice(i * piece, (i + 1) * piece)
-        span_all = pl.ds(pl.multiple_of(base + i * piece, piece), piece)
         zsum = scores[hm : hm + heads]
         small = jnp.exp(-jnp.abs(zsum))
         inv_tau = 1.0 / (0.5 + (jnp.maximum(zsum, 0.0) + jnp.log(1.0 + small)))
         sig = jnp.where(zsum >= 0.0, 1.0, small) / (1.0 + small)
-        position = base + i * piece + cols_of((1, piece))
+        position = i * piece + cols_of((1, piece))
         live = (valid_ref[:, at] > 0) & (position < owned)
         live_f = live.astype(f32)
         rounded, sums, logs = [], [], []
@@ -162,40 +194,39 @@
             sums.append(lanes)
             logs.append(jnp.where(live, peak + jnp.log(total), jnp.inf))
         wt = jnp.concatenate(rounded, axis=0)
-        wt_ref[:, span_all] = wt
+        wt_ref[:, at] = wt
         norm_acc[...] += jnp.concatenate(sums, axis=0)
-        aux_ref[:, span_all] = jnp.concatenate([inv_tau] + logs + [sig * inv_tau], axis=0)
+        aux_ref[:, at] = jnp.concatenate([inv_tau] + logs + [sig * inv_tau], axis=0)
         raw_acc[...] += nn(wt, mid)
+        cot_in[i].wait()
         wc_acc[...] += nn(wt, cot_ref[at, :])
 
     ready = products(0)
-    for i in range(block // piece):
+    for i in range(count):
         current = ready
-        if (i + 1) * piece < block:
+        if i + 1 < count:
             ready = products(i + 1)
         statistics(i, *current)
 
-    @pl.when(step == pl.num_programs(0) - 1)
-    def _():
-        diagonal = same_block(hm, width, slices, depth)
-        raw = fold_rows(jnp.where(diagonal, raw_acc[...], 0.0), heads, slices)
-        high, low = two_pieces(wc_acc[...])
-        w_out = w_out_ref[...]
-        mixed = nt(high, w_out) + nt(low, w_out)
-        mixed = fold_rows(jnp.where(diagonal, mixed, 0.0), heads, slices)
-        norm = jnp.sum(norm_acc[...].T, axis=0, keepdims=True)
-        first = rows_of((8, 128)) == 0
-        for j in range(2):
-            part = slice(j * 128, (j + 1) * 128)
-            pack[j, 0:slices, :] = raw[:, part]
-            pack[j, slices : 2 * slices, :] = mixed[:, part]
-            pack[j, 2 * slices :, :] = jnp.where(first, norm[:, part], 0.0)
-        place = group_place()
-        keep_ref[...] = pack[place & 1]
-        send_ref[...] = pack[(place & 1) ^ 1]
-        rows = hm // 2
-        for k, out in enumerate((wc_keep_ref, wc_send_ref)):
-            out[...] = wc_acc[pl.ds(pl.multiple_of(((place & 1) ^ k) * rows, 8), rows), :]
+    diagonal = same_block(hm, width, slices, depth)
+    raw = fold_rows(jnp.where(diagonal, raw_acc[...], 0.0), heads, slices)
+    high, low = two_pieces(wc_acc[...])
+    w_out = w_out_ref[...]
+    mixed = nt(high, w_out) + nt(low, w_out)
+    mixed = fold_rows(jnp.where(diagonal, mixed, 0.0), heads, slices)
+    norm = jnp.sum(norm_acc[...].T, axis=0, keepdims=True)
+    first = rows_of((8, 128)) == 0
+    for j in range(2):
+        part = slice(j * 128, (j + 1) * 128)
+        pack[j, 0:slices, :] = raw[:, part]
+        pack[j, slices : 2 * slices, :] = mixed[:, part]
+        pack[j, 2 * slices :, :] = jnp.where(first, norm[:, part], 0.0)
+    place = group_place()
+    keep_ref[...] = pack[place & 1]
+    send_ref[...] = pack[(place & 1) ^ 1]
+    rows = hm // 2
+    for k, out in enumerate((wc_keep_ref, wc_send_ref)):
+        out[...] = wc_acc[pl.ds(pl.multiple_of(((place & 1) ^ k) * rows, 8), rows), :]
 
 
 def lanes_at(x, lane, *where):
@@ -340,21 +371,18 @@
     small_acc,
     pack,
 ):
-    step = pl.program_id(0)
     width = mid_ref.shape[1]
     depth = width // heads
     hm = heads * slices
     block = feats_ref.shape[0]
     top = hm + 16
 
-    @pl.when(step == 0)
-    def _():
-        grad_acc[...] = jnp.zeros_like(grad_acc)
-        small_acc[...] = jnp.zeros_like(small_acc)
-        lhs[0:top, :] = sw_ref[...]
-        lhs[top:, :] = dr_ref[...]
-        yt[:, 0:hm] = drt_ref[...]
-        yt[:, hm:] = sb_ref[...]
+    grad_acc[...] = jnp.zeros_like(grad_acc)
+    small_acc[...] = jnp.zeros_like(small_acc)
+    lhs[0:top, :] = sw_ref[...]
+    lhs[top:, :] = dr_ref[...]
+    yt[:, 0:hm] = drt_ref[...]
+    yt[:, hm:] = sb_ref[...]
 
     temp = jnp.broadcast_to(temp_ref[...].astype(f32), (16, depth)).astype(bf16)
     same = (rows_of((depth, depth)) == cols_of((depth, depth))).astype(f32).astype(bf16)
@@ -362,15 +390,12 @@
     piece = min(sub_block, block)
     pieces = [slice(i * piece, (i + 1) * piece) for i in range(block // piece)]
 
-    def whole(at):
-        return pl.ds(pl.multiple_of(step * block + at.start, piece), piece)
-
     def products(at):
-        return nt(lhs[...], mid_ref[whole(at), :]), nt(mw_ref[...], cot_ref[at, :])
+        return nt(lhs[...], mid_ref[at, :]), nt(mw_ref[...], cot_ref[at, :])
 
     def per_head(at, from_mid, from_cot):
         weights_b, u_b, sums = [], [], []
-        aux = aux_ref[:, whole(at)]
+        aux = aux_ref[:, at]
         for h in range(heads):
             span = slice(h * slices, (h + 1) * slices)
             inv_tau = aux[h : h + 1]
@@ -396,9 +421,9 @@
             for h in range(heads)
         ]
         d_mid = jnp.concatenate(d_mid, axis=0)
-        dmt_ref[:, whole(at)] = d_mid
+        dmt_ref[:, at] = d_mid
         grad_acc[...] += nn(d_mid, feats_ref[at, :])
-        small_acc[...] += nn(u_b, mid_ref[whole(at), :])
+        small_acc[...] += nn(u_b, mid_ref[at, :])
 
     ready = products(pieces[0])
     for i, at in enumerate(pieces):
@@ -407,38 +432,36 @@
             ready = products(pieces[i + 1])
         outputs(at, *per_head(at, *current))
 
-    @pl.when(step == pl.num_programs(0) - 1)
-    def _():
-        grad = grad_acc[...].T
-        u_part = jnp.where(same_block(hm, width, slices, depth), small_acc[0:hm, :], 0.0)
-        u_part = fold_rows(u_part, heads, slices)
-        c_part = small_acc[hm : hm + heads, :] + small_acc[hm + heads : hm + 2 * heads, :]
-        c_part = jnp.where(same_block(heads, width, 1, depth), c_part, 0.0)
-        c_part = jnp.sum(c_part, axis=0, keepdims=True)
-
-        def fold_lanes(x):
-            total = x[:, 0:128]
-            for j in range(1, width // 128):
-                total = total + x[:, j * 128 : (j + 1) * 128]
-            shift = 64
-            while shift >= depth:
-                total = total + pltpu.roll(total, shift, 1)
-                shift //= 2
-            return total
-
-        u_part = fold_lanes(u_part)
-        c_part = fold_lanes(jnp.broadcast_to(c_part, (slices, width)))
-        where_lane = cols_of((slices, 128))
-        extra = jnp.where(where_lane < depth, u_part, c_part)
-        rows = width // group
-        more = slices // group
-        for j in range(group):
-            pack[j, 0:rows, :] = grad[j * rows : (j + 1) * rows]
-            pack[j, rows : rows + more, 0:128] = extra[j * more : (j + 1) * more]
-            pack[j, rows : rows + more, 128:] = jnp.zeros((more, width - 128), f32)
-        place = group_place()
-        for k, send in enumerate((send0, send1, send2, send3)):
-            send[...] = pack[place ^ k]
+    grad = grad_acc[...].T
+    u_part = jnp.where(same_block(hm, width, slices, depth), small_acc[0:hm, :], 0.0)
+    u_part = fold_rows(u_part, heads, slices)
+    c_part = small_acc[hm : hm + heads, :] + small_acc[hm + heads : hm + 2 * heads, :]
+    c_part = jnp.where(same_block(heads, width, 1, depth), c_part, 0.0)
+    c_part = jnp.sum(c_part, axis=0, keepdims=True)
+
+    def fold_lanes(x):
+        total = x[:, 0:128]
+        for j in range(1, width // 128):
+            total = total + x[:, j * 128 : (j + 1) * 128]
+        shift = 64
+        while shift >= depth:
+            total = total + pltpu.roll(total, shift, 1)
+            shift //= 2
+        return total
+
+    u_part = fold_lanes(u_part)
+    c_part = fold_lanes(jnp.broadcast_to(c_part, (slices, width)))
+    where_lane = cols_of((slices, 128))
+    extra = jnp.where(where_lane < depth, u_part, c_part)
+    rows = width // group
+    more = slices // group
+    for j in range(group):
+        pack[j, 0:rows, :] = grad[j * rows : (j + 1) * rows]
+        pack[j, rows : rows + more, 0:128] = extra[j * more : (j + 1) * more]
+        pack[j, rows : rows + more, 128:] = jnp.zeros((more, width - 128), f32)
+    place = group_place()
+    for k, send in enumerate((send0, send1, send2, send3)):
+        send[...] = pack[place ^ k]
 
 
 def rows_kernel(wt_ref, dmt_ref, mw_ref, w_mid_ref, _, attended_ref, feats_grad_ref, token_ref):
@@ -564,23 +587,25 @@
     temp = temp_vec.reshape(1, depth)
     half = (2 * slices + 8, 128)
     wide = (hm // 2, width)
-    block = min(2048, rows)
-    grid, by_rows = blocks(block)
-    mid, wt, aux, sw, sb, w_cat, keep, send, wc_keep, wc_send = pl.pallas_call(
+    inputs = (valid.reshape(1, rows), feats, cotangent, w_mid, w_slice, w_out, w_qkv)
+    pieces = rows // min(sub_block, rows)
+    (
+        mid,
+        wt,
+        aux,
+        sw,
+        sb,
+        w_cat,
+        keep,
+        send,
+        wc_keep,
+        wc_send,
+        feats_near,
+        cot_near,
+    ) = pl.pallas_call(
         functools.partial(stats_kernel, heads, slices),
-        grid=grid,
-        in_specs=[
-            smem,
-            pl.BlockSpec((1, block), lambda i: (0, i)),
-            by_rows,
-            by_rows,
-            full((width, width)),
-            full((depth, slices)),
-            full((1, depth)),
-            full((width, width)),
-            full((3, depth, depth)),
-        ],
-        out_specs=[whole] * 10,
+        in_specs=[smem, whole] + [pl.BlockSpec(memory_space=pltpu.HBM)] * len(inputs),
+        out_specs=[whole] * 12,
         out_shape=[
             near((rows, width), bf16),
             near((hm, rows), bf16),
@@ -592,30 +617,32 @@
             near(half, f32),
             near(wide, f32),
             near(wide, f32),
+            near((rows, width), bf16),
+            near((rows, width), bf16),
         ],
         scratch_shapes=[
+            pltpu.VMEM((1, rows), jnp.int32),
+            pltpu.VMEM((width, width), bf16),
+            pltpu.VMEM((depth, slices), bf16),
+            pltpu.VMEM((width, width), bf16),
+            pltpu.VMEM((3, depth, depth), bf16),
             pltpu.VMEM((hm, width), f32),
             pltpu.VMEM((hm, 128), f32),
             pltpu.VMEM((hm, width), f32),
             pltpu.VMEM((2,) + half, f32),
+            pltpu.SemaphoreType.DMA((5 + 2 * pieces,)),
         ],
-        compiler_params=params(32),
+        compiler_params=params(24, False),
         cost_estimate=cost(4 * unit, rows * width * 8, rows * hm),
-    )(owned, *map(far, (valid.reshape(1, rows), feats, cotangent, w_mid, w_slice, temp, w_out, w_qkv)))
+    )(owned, far(temp), *map(far, inputs))
 
     own = keep + exchange(send, 1, count)
     wc_got = exchange(wc_send, 1, count)
     own = sum_stage(own, 2, 3, count)
+    own = sum_over_groups(own, 8, count)
+    other = exchange(own, 1, count)
     wc_sum = sum_behind([wc_keep, wc_got], own)
     wc_got = exchange(wc_sum, 2, count)
-    own = sum_over_groups(own, 8, count)
-    wc_sum = sum_behind([wc_sum, wc_got], own)
-    other = exchange(own, 1, count)
-    strides = [stride for stride in (1 << i for i in range(2, 30)) if stride < count]
-    for stride in strides[:-1]:
-        wc_got = exchange(wc_sum, stride, count)
-        if stride != strides[-2]:
-            wc_sum = wc_sum + wc_got
 
     mw, mixed_t, dr, drt, dn, grad_qkv = pl.pallas_call(
         functools.partial(tokens_kernel, heads, slices),
@@ -632,17 +659,17 @@
         cost_estimate=cost(30 * width**3, 4 * width * width * 4, hm * hm),
     )(own, other, w_cat, w_out)
     wc_sum = sum_behind([wc_sum, wc_got], mw)
-    wc_got = exchange(wc_sum, strides[-1], count)
+    stride = 4
+    while stride < count // 2:
+        if stride > 4:
+            wc_sum = wc_sum + wc_got
+        wc_got = exchange(wc_sum, stride, count)
+        stride *= 2
 
     larger = (width // group + slices // group, width)
-    block = min(2048, rows)
-    grid, by_rows = blocks(block)
     dmt, *sends = pl.pallas_call(
         functools.partial(backward_kernel, heads, slices),
-        grid=grid,
-        in_specs=[whole, whole, by_rows, by_rows]
-        + [whole] * 7
-        + [pl.BlockSpec(memory_space=pl.ANY)],
+        in_specs=[whole] * 11 + [pl.BlockSpec(memory_space=pl.ANY)],
         out_specs=[whole] * (1 + group),
         out_shape=[near((width, rows), bf16)] + [near(larger, f32)] * group,
         scratch_shapes=[
@@ -652,12 +679,14 @@
             pltpu.VMEM((hm + 16, width), f32),
             pltpu.VMEM((group,) + larger, f32),
         ],
-        compiler_params=params(32),
+        compiler_params=params(24, False),
         cost_estimate=cost(8 * unit, rows * width * 8, rows * hm),
-    )(aux, mid, cotangent, feats, sw, sb, mw, dr, drt, dn, temp, wc_sum)
+    )(aux, mid, cot_near, feats_near, sw, sb, mw, dr, drt, dn, temp, wc_sum)
 
     mid_total = scatter_group(sends, count)
     wc_sum = sum_behind([wc_sum, wc_got], sends[1])
+    wc_got = exchange(wc_sum, count // 2, count)
+    wc_sum = sum_behind([wc_sum, wc_got], mid_total)
     wc_other = exchange(wc_sum, 1, count)
 
     block = min(1024, rows)

time: 61 us -> 64.5 us (1.057)
  waiting for transfers between devices: 17.5 us -> 18.8 us
  Pallas kernels: 21.3 us -> 22.5 us
  starting transfers between devices: 20.6 us -> 21.6 us
    ppermute x20, waiting for transfers between devices: 17.5 us -> 18.8 us  [exchange(): return lax.ppermute(x, 'node', [(i, i ^ k) for i in range(count)])]
    pallas_call x2, Pallas kernels: 13 us -> 14.2 us  [the longest x1 8.71 us: shards(): pl.pallas_call(functools.partial(stats_kernel, heads, slices), in_specs=[...]
    ppermute x20, starting transfers between devices: 20.6 us -> 21.6 us  [exchange(): return lax.ppermute(x, 'node', [(i, i ^ k) for i in range(count)])]
  transfers between devices with their start and end apart: 20 -> 20, of which waited for: 11 -> 11; matrix products, arithmetic and copies ran while one was open for 0% -> 0% of each run, Pallas kernels for 22% -> 20%
where the time goes in v6:
time: 64.5 us; the launch traced here: 64.3 us
  Pallas kernels  22.5 us (35%)
  starting transfers between devices  21.6 us (33%)
  waiting for transfers between devices  18.8 us (29%)
  between operations  1.38 us (2%)
    ppermute x20, starting transfers between devices, exchange(): return lax.ppermute(x, 'node', [(i, i ^ k) for i in range(count)])  21.6 us
    ppermute x20, waiting for transfers between devices, exchange(): return lax.ppermute(x, 'node', [(i, i ^ k) for i in range(count)])  18.8 us
    pallas_call x1, Pallas kernels, shards(): pl.pallas_call(functools.partial(stats_kernel, heads, slices), in_specs=[...  8.71 us
    pallas_call x1, Pallas kernels, shards(): pl.pallas_call(functools.partial(backward_kernel, heads, slices), in_spec...  5.52 us
    pallas_call x1, Pallas kernels, shards(): pl.pallas_call(rows_kernel, grid=grid, in_specs=[whole, whole, whole, ful...  3.43 us
    pallas_call x1, Pallas kernels, shards(): pl.pallas_call(functools.partial(tokens_kernel, heads, slices), out_shape...  3.1 us
  transfers between devices with their start and end apart: 20, of which 11 were waited for; matrix products, arithmetic and copies ran while one was open for 0% of the time, Pallas kernels for 20%

profile of v6, /device:TPU:0, one launch (start us, length us, event | category | flops | bytes accessed | tf_op | source)
XLA Modules:
  0.0 64.3 jit_solution(12018261728315633316)
XLA Ops:
  1.3 8.7 %shard_map.144 = (bf16[4096,256]{1,0:T(8,128)(2,1)S(1)}, bf16[256,4096]{1,0:T(8,128)(2,1)S(1)}, f32[24,4096]{1,0:T(8,128)S(1)}, bf16[272,256]{1,0:T(8,128)(2,1)S...) custom-call(s32[1]{0:T(128)S(6)} %copy.16.owned_ref, ...), custom_call_target="tpu_custom_call" | custom-call | flops 2147483648 | bytes 8388608 | tf_op jit(solution)/shard_map/pallas_call | solution.py:605
  10.5 0.9 %collective-permute-done = f32[72,128]{1,0:T(8,128)S(1)} collective-permute-done((f32[72,128]{1,0:T(8,128)S(1)}, f32[72,128]{1,0:T(8,128)S(1)}, u32[]{:S(2)}, u32[]{:S(2)}) %collective-permute-start) | collective-permute-done | bytes 36896 | tf_op jit(solution)/shard_map/ppermute | solution.py:519
  11.4 2.9 %collective-permute-start.3 = (f32[72,128]{1,0:T(8,128)S(1)}, f32[72,128]{1,0:T(8,128)S(1)}, u32[]{:S(2)}, u32[]{:S(2)}) collective-permute-start(f32[72,128]{1,0:T(8,128)S(1)} %add.24), channel_id=1, source_target_pairs={{0,4},{1,5},{2,6},{3,7},{4,0},{5,1},{6,2},{7,3},{8,12},{9,13},{10,... | collective-permute-start | bytes 110600 | tf_op jit(solution)/shard_map/ppermute | solution.py:519
  14.3 1.4 %collective-permute-start.2 = (f32[72,128]{1,0:T(8,128)S(1)}, f32[72,128]{1,0:T(8,128)S(1)}, u32[]{:S(2)}, u32[]{:S(2)}) collective-permute-start(f32[72,128]{1,0:T(8,128)S(1)} %add.24), channel_id=1, source_target_pairs={{0,6},{1,7},{2,4},{3,5},{4,2},{5,3},{6,0},{7,1},{8,14},{9,15},{10,... | collective-permute-start | bytes 110600 | tf_op jit(solution)/shard_map/ppermute | solution.py:519
  16.3 2.9 %collective-permute-done.2 = f32[72,128]{1,0:T(8,128)S(1)} collective-permute-done((f32[72,128]{1,0:T(8,128)S(1)}, f32[72,128]{1,0:T(8,128)S(1)}, u32[]{:S(2)}, u32[]{:S(2)}) %collective-permute-start.2) | collective-permute-done | bytes 36896 | tf_op jit(solution)/shard_map/ppermute | solution.py:519
  19.7 2.7 %collective-permute-start.4 = (f32[72,128]{1,0:T(8,128)S(1)}, f32[72,128]{1,0:T(8,128)S(1)}, u32[]{:S(2)}, u32[]{:S(2)}) collective-permute-start(f32[72,128]{1,0:T(8,128)S(1)} %add_add_fusion.1), channel_id=1, source_target_pairs={{0,8},{1,9},{2,10},{3,11},{4,12},{5,13},{6,14},{7,15},{8,0},{9,1},... | collective-permute-start | bytes 110600 | tf_op jit(solution)/shard_map/ppermute | solution.py:519
  22.3 2.3 %collective-permute-done.4 = f32[72,128]{1,0:T(8,128)S(1)} collective-permute-done((f32[72,128]{1,0:T(8,128)S(1)}, f32[72,128]{1,0:T(8,128)S(1)}, u32[]{:S(2)}, u32[]{:S(2)}) %collective-permute-start.4) | collective-permute-done | bytes 36896 | tf_op jit(solution)/shard_map/ppermute | solution.py:519
  24.6 1.1 %collective-permute-start.7 = (f32[128,256]{1,0:T(8,128)S(1)}, f32[128,256]{1,0:T(8,128)S(1)}, u32[]{:S(2)}, u32[]{:S(2)}) collective-permute-start(f32[128,256]{1,0:T(8,128)S(1)} %shard_map.146.refs_0_), channel_id=1, source_target_pairs={{0,2},{1,3},{2,0},{3,1},{4,6},{5,7},{6,4},{7,5},{8,10},{9,11},{10,... | collective-permute-start | bytes 393224 | tf_op jit(solution)/shard_map/ppermute | solution.py:519
  25.7 1.2 %collective-permute-done.5.got_ref = f32[72,128]{1,0:T(8,128)S(1)} collective-permute-done((f32[72,128]{1,0:T(8,128)S(1)}, f32[72,128]{1,0:T(8,128)S(1)}, u32[]{:S(2)}, u32[]{:S(2)}) %collective-permute-start.5) | collective-permute-done | bytes 36896 | tf_op jit(solution)/shard_map/ppermute | solution.py:519
  26.9 3.1 %shard_map.145 = (bf16[256,256]{1,0:T(8,128)(2,1)S(1)}, bf16[256,256]{1,0:T(8,128)(2,1)S(1)}, bf16[256,256]{1,0:T(8,128)(2,1)S(1)}, bf16[256,256]{1,0:T(8,128)(2...) custom-call(f32[72,128]{1,0:T(8,128)S(1)} %add.28.own_ref.refs_2_, f32[72,128]{1,0:T(8,128)S(1)} %collective-permute-done.5.got_ref, ...), custom_call_target="tpu_custom_call" | custom-call | flops 503316480 | bytes 1048576 | tf_op jit(solution)/shard_map/pallas_call | solution.py:647
  30.1 1.3 %collective-permute-start.14 = (f32[128,256]{1,0:T(8,128)S(1)}, f32[128,256]{1,0:T(8,128)S(1)}, u32[]{:S(2)}, u32[]{:S(2)}) collective-permute-start(f32[128,256]{1,0:T(8,128)S(1)} %shard_map.147._.refs_0_), channel_id=1, source_target_pairs={{0,4},{1,5},{2,6},{3,7},{4,0},{5,1},{6,2},{7,3},{8,12},{9,13},{10,... | collective-permute-start | bytes 393224 | tf_op jit(solution)/shard_map/ppermute | solution.py:519
  31.3 5.5 %shard_map.148 = (bf16[256,4096]{1,0:T(8,128)(2,1)S(1)}, f32[72,256]{1,0:T(8,128)S(1)}, f32[72,256]{1,0:T(8,128)S(1)}, f32[72,256]{1,0:T(8,128)S(1)}, f32[72,256]{1,0:T(8,128)S(1)}) custom-call(f32[24,4096]{1,0:T(8,128)S(1)} %get-tuple-element.39.aux_ref, bf16[4096,256]{1,0:T(8,128)(2,1)S(1)} %get-tuple-element.40.mid_ref, ...), custom_call_target="tpu_custom_call" | custom-call | flops 4294967296 | bytes 8388608 | tf_op jit(solution)/shard_map/pallas_call | solution.py:670
  36.9 1.4 %collective-permute-start.9 = (f32[72,256]{1,0:T(8,128)S(1)}, f32[72,256]{1,0:T(8,128)S(1)}, u32[]{:S(2)}, u32[]{:S(2)}) collective-permute-start(f32[72,256]{1,0:T(8,128)S(1)} %get-tuple-element.57), channel_id=1, source_target_pairs={{0,2},{1,3},{2,0},{3,1},{4,6},{5,7},{6,4},{7,5},{8,10},{9,11},{10,... | collective-permute-start | bytes 221192 | tf_op jit(solution)/shard_map/ppermute | solution.py:519
  39.1 2.9 %collective-permute-start.15 = (f32[128,256]{1,0:T(8,128)S(1)}, f32[128,256]{1,0:T(8,128)S(1)}, u32[]{:S(2)}, u32[]{:S(2)}) collective-permute-start(f32[128,256]{1,0:T(8,128)S(1)} %shard_map.150.refs_0_), channel_id=1, source_target_pairs={{0,8},{1,9},{2,10},{3,11},{4,12},{5,13},{6,14},{7,15},{8,0},{9,1},... | collective-permute-start | bytes 393224 | tf_op jit(solution)/shard_map/ppermute | solution.py:519
  42.0 0.8 %collective-permute-done.10 = f32[72,256]{1,0:T(8,128)S(1)} collective-permute-done((f32[72,256]{1,0:T(8,128)S(1)}, f32[72,256]{1,0:T(8,128)S(1)}, u32[]{:S(2)}, u32[]{:S(2)}) %collective-permute-start.10) | collective-permute-done | bytes 73760 | tf_op jit(solution)/shard_map/ppermute | solution.py:519
  42.9 5.6 %collective-permute-done.15.refs_1_ = f32[128,256]{1,0:T(8,128)S(1)} collective-permute-done((f32[128,256]{1,0:T(8,128)S(1)}, f32[128,256]{1,0:T(8,128)S(1)}, u32[]{:S(2)}, u32[]{:S(2)}) %collective-permute-start.15) | collective-permute-done | bytes 131104 | tf_op jit(solution)/shard_map/ppermute | solution.py:519
  48.7 3.2 %collective-permute-start.12 = (f32[72,256]{1,0:T(8,128)S(1)}, f32[72,256]{1,0:T(8,128)S(1)}, u32[]{:S(2)}, u32[]{:S(2)}) collective-permute-start(f32[72,256]{1,0:T(8,128)S(1)} %add_add_fusion._.refs_2_.refs_0_), channel_id=1, source_target_pairs={{0,8},{1,9},{2,10},{3,11},{4,12},{5,13},{6,14},{7,15},{8,0},{9,1},... | collective-permute-start | bytes 221192 | tf_op jit(solution)/shard_map/ppermute | solution.py:519
  51.9 1.2 %collective-permute-start.11 = (f32[72,256]{1,0:T(8,128)S(1)}, f32[72,256]{1,0:T(8,128)S(1)}, u32[]{:S(2)}, u32[]{:S(2)}) collective-permute-start(f32[72,256]{1,0:T(8,128)S(1)} %add_add_fusion._.refs_2_.refs_0_), channel_id=1, source_target_pairs={{0,12},{1,13},{2,14},{3,15},{4,8},{5,9},{6,10},{7,11},{8,4},{9,5},... | collective-permute-start | bytes 221192 | tf_op jit(solution)/shard_map/ppermute | solution.py:519
  53.1 3.4 %shard_map.149 = (bf16[4096,256]{1,0:T(8,128)(2,1)}, bf16[4096,256]{1,0:T(8,128)(2,1)}, f32[8,128]{1,0:T(8,128)S(1)}) custom-call(bf16[256,4096]{1,0:T(8,128)(2,1)S(1)} %get-tuple-element.38.wt_ref, bf16[256,4096]{1,0:T(8,128)(2,1)S(1)} %get-tuple-element.54.dmt_ref, bf16[256,256]{1,0:T(8,128)(2,1)S(1)} %get-tuple-element.48.refs_2_.mw_ref, ...), custom_call_target="tpu_custom_call" | custom-call | flops 1073741824 | bytes 8388608 | tf_op jit(solution)/shard_map/pallas_call | solution.py:694
  56.5 1.0 %shard_map.152 = (f32[256,256]{1,0:T(8,128)}, f32[8,128]{1,0:T(8,128)S(1)}) custom-call(f32[128,256]{1,0:T(8,128)S(1)} %shard_map.151.own_ref, f32[128,256]{1,0:T(8,128)S(1)} %collective-permute-done.16.other_ref, bf16[256,256]{1,0:T(8,128)(2,1)S(1)} %get-tuple-element.62.mixed_t_ref), custom_call_target="tpu_custom_call" | custom-call | flops 67108864 | bytes 786432 | tf_op jit(solution)/shard_map/pallas_call | solution.py:710
  58.2 1.1 %collective-permute-start.18 = (f32[72,256]{1,0:T(8,128)S(1)}, f32[72,256]{1,0:T(8,128)S(1)}, u32[]{:S(2)}, u32[]{:S(2)}) collective-permute-start(f32[72,256]{1,0:T(8,128)S(1)} %shard_map.153.m0), channel_id=1, source_target_pairs={{0,2},{1,3},{2,0},{3,1},{4,6},{5,7},{6,4},{7,5},{8,10},{9,11},{10,... | collective-permute-start | bytes 221192 | tf_op jit(solution)/shard_map/ppermute | solution.py:519
  59.3 0.8 %collective-permute-start.17 = (f32[72,256]{1,0:T(8,128)S(1)}, f32[72,256]{1,0:T(8,128)S(1)}, u32[]{:S(2)}, u32[]{:S(2)}) collective-permute-start(f32[72,256]{1,0:T(8,128)S(1)} %shard_map.153.m0), channel_id=1, source_target_pairs={{0,1},{1,0},{2,3},{3,2},{4,5},{5,4},{6,7},{7,6},{8,9},{9,8},{10,11... | collective-permute-start | bytes 221192 | tf_op jit(solution)/shard_map/ppermute | solution.py:519
  60.1 2.6 %collective-permute-done.19.m3 = f32[72,256]{1,0:T(8,128)S(1)} collective-permute-done((f32[72,256]{1,0:T(8,128)S(1)}, f32[72,256]{1,0:T(8,128)S(1)}, u32[]{:S(2)}, u32[]{:S(2)}) %collective-permute-start.19) | collective-permute-done | bytes 73760 | tf_op jit(solution)/shard_map/ppermute | solution.py:519
  62.7 0.9 %collective-permute-done.18.m2 = f32[72,256]{1,0:T(8,128)S(1)} collective-permute-done((f32[72,256]{1,0:T(8,128)S(1)}, f32[72,256]{1,0:T(8,128)S(1)}, u32[]{:S(2)}, u32[]{:S(2)}) %collective-permute-start.18) | collective-permute-done | bytes 73760 | tf_op jit(solution)/shard_map/ppermute | solution.py:519
  (37 shorter events, 4.1 us)
Async XLA Ops:
  1.3 25.7 %copy-start.1 = (bf16[256,256]{1,0:T(8,128)(2,1)S(1)}, bf16[256,256]{1,0:T(8,128)(2,1)}, u32[]{:S(2)}) copy-start(bf16[256,256]{1,0:T(8,128)(2,1)} %w_out_ref.1) | copy-start | bytes 393220
  10.0 21.3 %copy-start.2 = (bf16[32]{0:T(256)(128)(2,1)S(1)}, bf16[32]{0:T(256)(128)(2,1)}, u32[]{:S(2)}) copy-start(bf16[32]{0:T(256)(128)(2,1)} %param.15) | copy-start | bytes 196
  10.0 1.4 %collective-permute-start = (f32[72,128]{1,0:T(8,128)S(1)}, f32[72,128]{1,0:T(8,128)S(1)}, u32[]{:S(2)}, u32[]{:S(2)}) collective-permute-start(f32[72,128]{1,0:T(8,128)S(1)} %get-tuple-element.46), channel_id=1, source_target_pairs={{0,1},{1,0},{2,3},{3,2},{4,5},{5,4},{6,7},{7,6},{8,9},{9,8},{10,11... | collective-permute-start | bytes 110600 | tf_op jit(solution)/shard_map/ppermute | solution.py:519
  11.4 4.9 %collective-permute-start.3 = (f32[72,128]{1,0:T(8,128)S(1)}, f32[72,128]{1,0:T(8,128)S(1)}, u32[]{:S(2)}, u32[]{:S(2)}) collective-permute-start(f32[72,128]{1,0:T(8,128)S(1)} %add.24), channel_id=1, source_target_pairs={{0,4},{1,5},{2,6},{3,7},{4,0},{5,1},{6,2},{7,3},{8,12},{9,13},{10,... | collective-permute-start | bytes 110600 | tf_op jit(solution)/shard_map/ppermute | solution.py:519
  14.3 4.9 %collective-permute-start.2 = (f32[72,128]{1,0:T(8,128)S(1)}, f32[72,128]{1,0:T(8,128)S(1)}, u32[]{:S(2)}, u32[]{:S(2)}) collective-permute-start(f32[72,128]{1,0:T(8,128)S(1)} %add.24), channel_id=1, source_target_pairs={{0,6},{1,7},{2,4},{3,5},{4,2},{5,3},{6,0},{7,1},{8,14},{9,15},{10,... | collective-permute-start | bytes 110600 | tf_op jit(solution)/shard_map/ppermute | solution.py:519
  15.7 4.0 %collective-permute-start.1 = (f32[72,128]{1,0:T(8,128)S(1)}, f32[72,128]{1,0:T(8,128)S(1)}, u32[]{:S(2)}, u32[]{:S(2)}) collective-permute-start(f32[72,128]{1,0:T(8,128)S(1)} %add.24), channel_id=1, source_target_pairs={{0,2},{1,3},{2,0},{3,1},{4,6},{5,7},{6,4},{7,5},{8,10},{9,11},{10,... | collective-permute-start | bytes 110600 | tf_op jit(solution)/shard_map/ppermute | solution.py:519
  15.9 8.7 %collective-permute-start.6 = (f32[128,256]{1,0:T(8,128)S(1)}, f32[128,256]{1,0:T(8,128)S(1)}, u32[]{:S(2)}, u32[]{:S(2)}) collective-permute-start(f32[128,256]{1,0:T(8,128)S(1)} %get-tuple-element.53), channel_id=1, source_target_pairs={{0,1},{1,0},{2,3},{3,2},{4,5},{5,4},{6,7},{7,6},{8,9},{9,8},{10,11... | collective-permute-start | bytes 393224 | tf_op jit(solution)/shard_map/ppermute | solution.py:519
  19.7 4.9 %collective-permute-start.4 = (f32[72,128]{1,0:T(8,128)S(1)}, f32[72,128]{1,0:T(8,128)S(1)}, u32[]{:S(2)}, u32[]{:S(2)}) collective-permute-start(f32[72,128]{1,0:T(8,128)S(1)} %add_add_fusion.1), channel_id=1, source_target_pairs={{0,8},{1,9},{2,10},{3,11},{4,12},{5,13},{6,14},{7,15},{8,0},{9,1},... | collective-permute-start | bytes 110600 | tf_op jit(solution)/shard_map/ppermute | solution.py:519
  24.6 5.4 %collective-permute-start.7 = (f32[128,256]{1,0:T(8,128)S(1)}, f32[128,256]{1,0:T(8,128)S(1)}, u32[]{:S(2)}, u32[]{:S(2)}) collective-permute-start(f32[128,256]{1,0:T(8,128)S(1)} %shard_map.146.refs_0_), channel_id=1, source_target_pairs={{0,2},{1,3},{2,0},{3,1},{4,6},{5,7},{6,4},{7,5},{8,10},{9,11},{10,... | collective-permute-start | bytes 393224 | tf_op jit(solution)/shard_map/ppermute | solution.py:519
  25.7 1.2 %collective-permute-start.5 = (f32[72,128]{1,0:T(8,128)S(1)}, f32[72,128]{1,0:T(8,128)S(1)}, u32[]{:S(2)}, u32[]{:S(2)}) collective-permute-start(f32[72,128]{1,0:T(8,128)S(1)} %add.28.own_ref.refs_2_), channel_id=1, source_target_pairs={{0,1},{1,0},{2,3},{3,2},{4,5},{5,4},{6,7},{7,6},{8,9},{9,8},{10,11... | collective-permute-start | bytes 110600 | tf_op jit(solution)/shard_map/ppermute | solution.py:519
  30.1 9.0 %collective-permute-start.14 = (f32[128,256]{1,0:T(8,128)S(1)}, f32[128,256]{1,0:T(8,128)S(1)}, u32[]{:S(2)}, u32[]{:S(2)}) collective-permute-start(f32[128,256]{1,0:T(8,128)S(1)} %shard_map.147._.refs_0_), channel_id=1, source_target_pairs={{0,4},{1,5},{2,6},{3,7},{4,0},{5,1},{6,2},{7,3},{8,12},{9,13},{10,... | collective-permute-start | bytes 393224 | tf_op jit(solution)/shard_map/ppermute | solution.py:519
  31.3 21.7 %copy-start = (bf16[256,256]{1,0:T(8,128)(2,1)S(1)}, bf16[256,256]{1,0:T(8,128)(2,1)}, u32[]{:S(2)}) copy-start(bf16[256,256]{1,0:T(8,128)(2,1)} %w_mid_ref.1) | copy-start | bytes 393220
  36.9 5.2 %collective-permute-start.9 = (f32[72,256]{1,0:T(8,128)S(1)}, f32[72,256]{1,0:T(8,128)S(1)}, u32[]{:S(2)}, u32[]{:S(2)}) collective-permute-start(f32[72,256]{1,0:T(8,128)S(1)} %get-tuple-element.57), channel_id=1, source_target_pairs={{0,2},{1,3},{2,0},{3,1},{4,6},{5,7},{6,4},{7,5},{8,10},{9,11},{10,... | collective-permute-start | bytes 221192 | tf_op jit(solution)/shard_map/ppermute | solution.py:519
  38.3 4.5 %collective-permute-start.10 = (f32[72,256]{1,0:T(8,128)S(1)}, f32[72,256]{1,0:T(8,128)S(1)}, u32[]{:S(2)}, u32[]{:S(2)}) collective-permute-start(f32[72,256]{1,0:T(8,128)S(1)} %get-tuple-element.58), channel_id=1, source_target_pairs={{0,3},{1,2},{2,1},{3,0},{4,7},{5,6},{6,5},{7,4},{8,11},{9,10},{10,... | collective-permute-start | bytes 221192 | tf_op jit(solution)/shard_map/ppermute | solution.py:519
  38.3 4.5 %collective-permute-start.8 = (f32[72,256]{1,0:T(8,128)S(1)}, f32[72,256]{1,0:T(8,128)S(1)}, u32[]{:S(2)}, u32[]{:S(2)}) collective-permute-start(f32[72,256]{1,0:T(8,128)S(1)} %get-tuple-element.56.refs_2_), channel_id=1, source_target_pairs={{0,1},{1,0},{2,3},{3,2},{4,5},{5,4},{6,7},{7,6},{8,9},{9,8},{10,11... | collective-permute-start | bytes 221192 | tf_op jit(solution)/shard_map/ppermute | solution.py:519
  39.1 9.4 %collective-permute-start.15 = (f32[128,256]{1,0:T(8,128)S(1)}, f32[128,256]{1,0:T(8,128)S(1)}, u32[]{:S(2)}, u32[]{:S(2)}) collective-permute-start(f32[128,256]{1,0:T(8,128)S(1)} %shard_map.150.refs_0_), channel_id=1, source_target_pairs={{0,8},{1,9},{2,10},{3,11},{4,12},{5,13},{6,14},{7,15},{8,0},{9,1},... | collective-permute-start | bytes 393224 | tf_op jit(solution)/shard_map/ppermute | solution.py:519
  48.5 8.0 %collective-permute-start.16 = (f32[128,256]{1,0:T(8,128)S(1)}, f32[128,256]{1,0:T(8,128)S(1)}, u32[]{:S(2)}, u32[]{:S(2)}) collective-permute-start(f32[128,256]{1,0:T(8,128)S(1)} %shard_map.151.own_ref), channel_id=1, source_target_pairs={{0,1},{1,0},{2,3},{3,2},{4,5},{5,4},{6,7},{7,6},{8,9},{9,8},{10,11... | collective-permute-start | bytes 393224 | tf_op jit(solution)/shard_map/ppermute | solution.py:519
  48.6 8.9 %collective-permute-start.13 = (f32[72,256]{1,0:T(8,128)S(1)}, f32[72,256]{1,0:T(8,128)S(1)}, u32[]{:S(2)}, u32[]{:S(2)}) collective-permute-start(f32[72,256]{1,0:T(8,128)S(1)} %add_add_fusion._.refs_2_.refs_0_), channel_id=1, source_target_pairs={{0,4},{1,5},{2,6},{3,7},{4,0},{5,1},{6,2},{7,3},{8,12},{9,13},{10,... | collective-permute-start | bytes 221192 | tf_op jit(solution)/shard_map/ppermute | solution.py:519
  48.7 9.5 %collective-permute-start.12 = (f32[72,256]{1,0:T(8,128)S(1)}, f32[72,256]{1,0:T(8,128)S(1)}, u32[]{:S(2)}, u32[]{:S(2)}) collective-permute-start(f32[72,256]{1,0:T(8,128)S(1)} %add_add_fusion._.refs_2_.refs_0_), channel_id=1, source_target_pairs={{0,8},{1,9},{2,10},{3,11},{4,12},{5,13},{6,14},{7,15},{8,0},{9,1},... | collective-permute-start | bytes 221192 | tf_op jit(solution)/shard_map/ppermute | solution.py:519
  51.9 6.3 %collective-permute-start.11 = (f32[72,256]{1,0:T(8,128)S(1)}, f32[72,256]{1,0:T(8,128)S(1)}, u32[]{:S(2)}, u32[]{:S(2)}) collective-permute-start(f32[72,256]{1,0:T(8,128)S(1)} %add_add_fusion._.refs_2_.refs_0_), channel_id=1, source_target_pairs={{0,12},{1,13},{2,14},{3,15},{4,8},{5,9},{6,10},{7,11},{8,4},{9,5},... | collective-permute-start | bytes 221192 | tf_op jit(solution)/shard_map/ppermute | solution.py:519
  58.2 4.5 %collective-permute-start.19 = (f32[72,256]{1,0:T(8,128)S(1)}, f32[72,256]{1,0:T(8,128)S(1)}, u32[]{:S(2)}, u32[]{:S(2)}) collective-permute-start(f32[72,256]{1,0:T(8,128)S(1)} %shard_map.153.m0), channel_id=1, source_target_pairs={{0,3},{1,2},{2,1},{3,0},{4,7},{5,6},{6,5},{7,4},{8,11},{9,10},{10,... | collective-permute-start | bytes 221192 | tf_op jit(solution)/shard_map/ppermute | solution.py:519
  58.2 5.3 %collective-permute-start.18 = (f32[72,256]{1,0:T(8,128)S(1)}, f32[72,256]{1,0:T(8,128)S(1)}, u32[]{:S(2)}, u32[]{:S(2)}) collective-permute-start(f32[72,256]{1,0:T(8,128)S(1)} %shard_map.153.m0), channel_id=1, source_target_pairs={{0,2},{1,3},{2,0},{3,1},{4,6},{5,7},{6,4},{7,5},{8,10},{9,11},{10,... | collective-permute-start | bytes 221192 | tf_op jit(solution)/shard_map/ppermute | solution.py:519
  59.3 4.3 %collective-permute-start.17 = (f32[72,256]{1,0:T(8,128)S(1)}, f32[72,256]{1,0:T(8,128)S(1)}, u32[]{:S(2)}, u32[]{:S(2)}) collective-permute-start(f32[72,256]{1,0:T(8,128)S(1)} %shard_map.153.m0), channel_id=1, source_target_pairs={{0,1},{1,0},{2,3},{3,2},{4,5},{5,4},{6,7},{7,6},{8,9},{9,8},{10,11... | collective-permute-start | bytes 221192 | tf_op jit(solution)/shard_map/ppermute | solution.py:519

commit v7 on v6

--- a/solution.py
+++ b/solution.py
@@ -35,6 +35,10 @@
     )
 
 
+def log2(size):
+    return size.bit_length() - 1
+
+
 def rows_of(shape):
     return lax.broadcasted_iota(jnp.int32, shape, 0)
 
@@ -45,12 +49,12 @@
 
 def spread_matrix(width, small):
     shape = (width, small)
-    return jnp.where(rows_of(shape) % small == cols_of(shape), 1.0, 0.0).astype(bf16)
+    return jnp.where((rows_of(shape) & (small - 1)) == cols_of(shape), 1.0, 0.0).astype(bf16)
 
 
 def same_block(rows, cols, row_size, col_size):
     shape = (rows, cols)
-    return rows_of(shape) // row_size == cols_of(shape) // col_size
+    return rows_of(shape) >> log2(row_size) == cols_of(shape) >> log2(col_size)
 
 
 def two_pieces(x):
@@ -165,7 +169,6 @@
 
     def products(i):
         at = slice(i * piece, (i + 1) * piece)
-        feats_in[i].wait()
         mid = nn(feats_ref[at, :], w_mid_ref[...]).astype(bf16)
         mid_ref[at, :] = mid
         return mid, nt(sw_ref[...], mid)
@@ -198,13 +201,15 @@
         norm_acc[...] += jnp.concatenate(sums, axis=0)
         aux_ref[:, at] = jnp.concatenate([inv_tau] + logs + [sig * inv_tau], axis=0)
         raw_acc[...] += nn(wt, mid)
-        cot_in[i].wait()
         wc_acc[...] += nn(wt, cot_ref[at, :])
 
+    feats_in[0].wait()
     ready = products(0)
     for i in range(count):
         current = ready
+        cot_in[i].wait()
         if i + 1 < count:
+            feats_in[i + 1].wait()
             ready = products(i + 1)
         statistics(i, *current)
 
@@ -230,7 +235,7 @@
 
 
 def lanes_at(x, lane, *where):
-    place = cols_of(x.shape) // lane
+    place = cols_of(x.shape) >> log2(lane)
     total = jnp.zeros_like(x)
     for value, at, to in where:
         shift = (to - at) * lane % 128
@@ -314,7 +319,7 @@
     mixed_b = times_pair(nn, probs, v_pair).astype(bf16)
 
     spread_d = jnp.where(
-        (rows_of((width, 128)) % depth == cols_of((width, 128))), 1.0, 0.0
+        (rows_of((width, 128)) & (depth - 1)) == cols_of((width, 128)), 1.0, 0.0
     ).astype(bf16)
     diagonal = same_block(hm, width, slices, depth)
     diagonal_t = same_block(width, hm, depth, slices)
@@ -387,7 +392,7 @@
     temp = jnp.broadcast_to(temp_ref[...].astype(f32), (16, depth)).astype(bf16)
     same = (rows_of((depth, depth)) == cols_of((depth, depth))).astype(f32).astype(bf16)
     temp = nt(same, temp)[:, 0:1]
-    piece = min(sub_block, block)
+    piece = min(2 * sub_block, block)
     pieces = [slice(i * piece, (i + 1) * piece) for i in range(block // piece)]
 
     def products(at):
@@ -474,7 +479,7 @@
     ).astype(bf16)
 
 
-def grad_out_kernel(own_ref, other_ref, mixed_t_ref, grad_out_ref, token_ref, whole):
+def grad_out_kernel(own_ref, other_ref, mixed_t_ref, _, grad_out_ref, token_ref, whole):
     token_ref[...] = jnp.zeros_like(token_ref)
     place = group_place() & 1
     rows = own_ref.shape[0]
@@ -485,7 +490,7 @@
     grad_out_ref[...] = nn(mixed_t, high) + nn(mixed_t, low)
 
 
-def finish_kernel(depth, m0, m1, m2, m3, grad_mid_ref, slice_ref, temp_ref, extra):
+def finish_kernel(depth, m0, m1, m2, m3, _, grad_mid_ref, slice_ref, temp_ref, extra):
     place = group_place()
     slices = slice_ref.shape[1]
     more = slices // group
@@ -686,8 +691,6 @@
     mid_total = scatter_group(sends, count)
     wc_sum = sum_behind([wc_sum, wc_got], sends[1])
     wc_got = exchange(wc_sum, count // 2, count)
-    wc_sum = sum_behind([wc_sum, wc_got], mid_total)
-    wc_other = exchange(wc_sum, 1, count)
 
     block = min(1024, rows)
     grid, by_rows = blocks(block)
@@ -707,18 +710,24 @@
         cost_estimate=cost(2 * unit, rows * width * 8),
     )(wt, dmt, mw, w_mid, mid_total)
 
-    grad_w_out, token_out = pl.pallas_call(
+    wc_sum = sum_behind([wc_sum, wc_got], token)
+    wc_other = exchange(wc_sum, 1, count)
+    mid_total = sum_over_groups(mid_total, group, count, token)
+    grad_w_out, token = pl.pallas_call(
         grad_out_kernel,
         out_shape=[like((width, width), f32), like((8, 128), f32)],
+        in_specs=[whole] * 3 + [pl.BlockSpec(memory_space=pl.ANY)],
+        out_specs=[whole] * 2,
         scratch_shapes=[pltpu.VMEM((hm, width), f32)],
         compiler_params=params(8, False),
         cost_estimate=cost(4 * width**3, 3 * width * width * 4),
-    )(wc_sum, wc_other, mixed_t)
-
-    mid_total = sum_over_groups(mid_total, group, count, token, token_out)
+    )(wc_sum, wc_other, mixed_t, mid_total)
+
     mid_parts = gather_group(mid_total, count)
     grad_w_mid, grad_w_slice, grad_temp = pl.pallas_call(
         functools.partial(finish_kernel, depth),
+        in_specs=[whole] * group + [pl.BlockSpec(memory_space=pl.ANY)],
+        out_specs=[whole] * 3,
         out_shape=[
             like((width, width), f32),
             like((depth, slices), f32),
@@ -727,7 +736,7 @@
         scratch_shapes=[pltpu.VMEM((slices, 128), f32)],
         compiler_params=params(8, False),
         cost_estimate=cost(0, 2 * width * width * 4),
-    )(*mid_parts)
+    )(*mid_parts, token)
     return (
         attended,
         feats_grad,

time: 64.5 us -> 59.9 us (0.929)
  waiting for transfers between devices: 18.8 us -> 14.8 us
  Pallas kernels: 22.5 us -> 21.8 us
    ppermute x20, waiting for transfers between devices: 18.8 us -> 14.8 us  [exchange(): return lax.ppermute(x, 'node', [(i, i ^ k) for i in range(count)])]
    pallas_call x1, Pallas kernels: 8.71 us -> 7.92 us  [shards(): pl.pallas_call(functools.partial(stats_kernel, heads, slices), in_specs=[...]
  transfers between devices with their start and end apart: 20 -> 20, of which waited for: 11 -> 11; matrix products, arithmetic and copies ran while one was open for 0% -> 0% of each run, Pallas kernels for 20% -> 22%
where the time goes in v7:
time: 59.9 us; the launch traced here: 59.7 us
  Pallas kernels  21.8 us (36%)
  starting transfers between devices  21.6 us (36%)
  waiting for transfers between devices  14.8 us (25%)
  between operations  1.37 us (2%)
    ppermute x20, starting transfers between devices, exchange(): return lax.ppermute(x, 'node', [(i, i ^ k) for i in range(count)])  21.6 us
    ppermute x20, waiting for transfers between devices, exchange(): return lax.ppermute(x, 'node', [(i, i ^ k) for i in range(count)])  14.8 us
    pallas_call x1, Pallas kernels, shards(): pl.pallas_call(functools.partial(stats_kernel, heads, slices), in_specs=[...  7.92 us
    pallas_call x1, Pallas kernels, shards(): pl.pallas_call(functools.partial(backward_kernel, heads, slices), in_spec...  5.58 us
    pallas_call x1, Pallas kernels, shards(): pl.pallas_call(rows_kernel, grid=grid, in_specs=[whole, whole, whole, ful...  3.42 us
    pallas_call x1, Pallas kernels, shards(): pl.pallas_call(functools.partial(tokens_kernel, heads, slices), out_shape...  3.1 us
  transfers between devices with their start and end apart: 20, of which 11 were waited for; matrix products, arithmetic and copies ran while one was open for 0% of the time, Pallas kernels for 22%

profile of v7, /device:TPU:0, one launch (start us, length us, event | category | flops | bytes accessed | tf_op | source)
XLA Modules:
  0.0 59.7 jit_solution(7580725922374415037)
XLA Ops:
  1.3 7.9 %shard_map.144 = (bf16[4096,256]{1,0:T(8,128)(2,1)S(1)}, bf16[256,4096]{1,0:T(8,128)(2,1)S(1)}, f32[24,4096]{1,0:T(8,128)S(1)}, bf16[272,256]{1,0:T(8,128)(2,1)S...) custom-call(s32[1]{0:T(128)S(6)} %copy.16.owned_ref, ...), custom_call_target="tpu_custom_call" | custom-call | flops 2147483648 | bytes 8388608 | tf_op jit(solution)/shard_map/pallas_call | solution.py:610
  9.7 0.9 %collective-permute-done = f32[72,128]{1,0:T(8,128)S(1)} collective-permute-done((f32[72,128]{1,0:T(8,128)S(1)}, f32[72,128]{1,0:T(8,128)S(1)}, u32[]{:S(2)}, u32[]{:S(2)}) %collective-permute-start) | collective-permute-done | bytes 36896 | tf_op jit(solution)/shard_map/ppermute | solution.py:524
  10.6 2.9 %collective-permute-start.3 = (f32[72,128]{1,0:T(8,128)S(1)}, f32[72,128]{1,0:T(8,128)S(1)}, u32[]{:S(2)}, u32[]{:S(2)}) collective-permute-start(f32[72,128]{1,0:T(8,128)S(1)} %add.24), channel_id=1, source_target_pairs={{0,4},{1,5},{2,6},{3,7},{4,0},{5,1},{6,2},{7,3},{8,12},{9,13},{10,... | collective-permute-start | bytes 110600 | tf_op jit(solution)/shard_map/ppermute | solution.py:524
  13.5 1.4 %collective-permute-start.2 = (f32[72,128]{1,0:T(8,128)S(1)}, f32[72,128]{1,0:T(8,128)S(1)}, u32[]{:S(2)}, u32[]{:S(2)}) collective-permute-start(f32[72,128]{1,0:T(8,128)S(1)} %add.24), channel_id=1, source_target_pairs={{0,6},{1,7},{2,4},{3,5},{4,2},{5,3},{6,0},{7,1},{8,14},{9,15},{10,... | collective-permute-start | bytes 110600 | tf_op jit(solution)/shard_map/ppermute | solution.py:524
  15.5 2.9 %collective-permute-done.2 = f32[72,128]{1,0:T(8,128)S(1)} collective-permute-done((f32[72,128]{1,0:T(8,128)S(1)}, f32[72,128]{1,0:T(8,128)S(1)}, u32[]{:S(2)}, u32[]{:S(2)}) %collective-permute-start.2) | collective-permute-done | bytes 36896 | tf_op jit(solution)/shard_map/ppermute | solution.py:524
  18.9 2.7 %collective-permute-start.4 = (f32[72,128]{1,0:T(8,128)S(1)}, f32[72,128]{1,0:T(8,128)S(1)}, u32[]{:S(2)}, u32[]{:S(2)}) collective-permute-start(f32[72,128]{1,0:T(8,128)S(1)} %add_add_fusion.1), channel_id=1, source_target_pairs={{0,8},{1,9},{2,10},{3,11},{4,12},{5,13},{6,14},{7,15},{8,0},{9,1},... | collective-permute-start | bytes 110600 | tf_op jit(solution)/shard_map/ppermute | solution.py:524
  21.5 2.3 %collective-permute-done.4 = f32[72,128]{1,0:T(8,128)S(1)} collective-permute-done((f32[72,128]{1,0:T(8,128)S(1)}, f32[72,128]{1,0:T(8,128)S(1)}, u32[]{:S(2)}, u32[]{:S(2)}) %collective-permute-start.4) | collective-permute-done | bytes 36896 | tf_op jit(solution)/shard_map/ppermute | solution.py:524
  23.8 1.1 %collective-permute-start.7 = (f32[128,256]{1,0:T(8,128)S(1)}, f32[128,256]{1,0:T(8,128)S(1)}, u32[]{:S(2)}, u32[]{:S(2)}) collective-permute-start(f32[128,256]{1,0:T(8,128)S(1)} %shard_map.146.refs_0_), channel_id=1, source_target_pairs={{0,2},{1,3},{2,0},{3,1},{4,6},{5,7},{6,4},{7,5},{8,10},{9,11},{10,... | collective-permute-start | bytes 393224 | tf_op jit(solution)/shard_map/ppermute | solution.py:524
  24.9 1.2 %collective-permute-done.5.got_ref = f32[72,128]{1,0:T(8,128)S(1)} collective-permute-done((f32[72,128]{1,0:T(8,128)S(1)}, f32[72,128]{1,0:T(8,128)S(1)}, u32[]{:S(2)}, u32[]{:S(2)}) %collective-permute-start.5) | collective-permute-done | bytes 36896 | tf_op jit(solution)/shard_map/ppermute | solution.py:524
  26.1 3.1 %shard_map.145 = (bf16[256,256]{1,0:T(8,128)(2,1)S(1)}, bf16[256,256]{1,0:T(8,128)(2,1)S(1)}, bf16[256,256]{1,0:T(8,128)(2,1)S(1)}, bf16[256,256]{1,0:T(8,128)(2...) custom-call(f32[72,128]{1,0:T(8,128)S(1)} %add.28.own_ref.refs_2_, f32[72,128]{1,0:T(8,128)S(1)} %collective-permute-done.5.got_ref, ...), custom_call_target="tpu_custom_call" | custom-call | flops 503316480 | bytes 1048576 | tf_op jit(solution)/shard_map/pallas_call | solution.py:652
  29.3 1.3 %collective-permute-start.17 = (f32[128,256]{1,0:T(8,128)S(1)}, f32[128,256]{1,0:T(8,128)S(1)}, u32[]{:S(2)}, u32[]{:S(2)}) collective-permute-start(f32[128,256]{1,0:T(8,128)S(1)} %shard_map.147._.refs_0_), channel_id=1, source_target_pairs={{0,4},{1,5},{2,6},{3,7},{4,0},{5,1},{6,2},{7,3},{8,12},{9,13},{10,... | collective-permute-start | bytes 393224 | tf_op jit(solution)/shard_map/ppermute | solution.py:524
  30.5 5.6 %shard_map.148 = (bf16[256,4096]{1,0:T(8,128)(2,1)S(1)}, f32[72,256]{1,0:T(8,128)S(1)}, f32[72,256]{1,0:T(8,128)S(1)}, f32[72,256]{1,0:T(8,128)S(1)}, f32[72,256]{1,0:T(8,128)S(1)}) custom-call(f32[24,4096]{1,0:T(8,128)S(1)} %get-tuple-element.39.aux_ref, bf16[4096,256]{1,0:T(8,128)(2,1)S(1)} %get-tuple-element.40.mid_ref, ...), custom_call_target="tpu_custom_call" | custom-call | flops 4294967296 | bytes 8388608 | tf_op jit(solution)/shard_map/pallas_call | solution.py:675
  36.1 1.4 %collective-permute-start.9 = (f32[72,256]{1,0:T(8,128)S(1)}, f32[72,256]{1,0:T(8,128)S(1)}, u32[]{:S(2)}, u32[]{:S(2)}) collective-permute-start(f32[72,256]{1,0:T(8,128)S(1)} %get-tuple-element.57), channel_id=1, source_target_pairs={{0,2},{1,3},{2,0},{3,1},{4,6},{5,7},{6,4},{7,5},{8,10},{9,11},{10,... | collective-permute-start | bytes 221192 | tf_op jit(solution)/shard_map/ppermute | solution.py:524
  37.6 0.8 %collective-permute-start.8 = (f32[72,256]{1,0:T(8,128)S(1)}, f32[72,256]{1,0:T(8,128)S(1)}, u32[]{:S(2)}, u32[]{:S(2)}) collective-permute-start(f32[72,256]{1,0:T(8,128)S(1)} %get-tuple-element.56.refs_2_), channel_id=1, source_target_pairs={{0,1},{1,0},{2,3},{3,2},{4,5},{5,4},{6,7},{7,6},{8,9},{9,8},{10,11... | collective-permute-start | bytes 221192 | tf_op jit(solution)/shard_map/ppermute | solution.py:524
  38.4 2.9 %collective-permute-start.18 = (f32[128,256]{1,0:T(8,128)S(1)}, f32[128,256]{1,0:T(8,128)S(1)}, u32[]{:S(2)}, u32[]{:S(2)}) collective-permute-start(f32[128,256]{1,0:T(8,128)S(1)} %shard_map.151.refs_0_), channel_id=1, source_target_pairs={{0,8},{1,9},{2,10},{3,11},{4,12},{5,13},{6,14},{7,15},{8,0},{9,1},... | collective-permute-start | bytes 393224 | tf_op jit(solution)/shard_map/ppermute | solution.py:524
  41.3 0.8 %collective-permute-done.10 = f32[72,256]{1,0:T(8,128)S(1)} collective-permute-done((f32[72,256]{1,0:T(8,128)S(1)}, f32[72,256]{1,0:T(8,128)S(1)}, u32[]{:S(2)}, u32[]{:S(2)}) %collective-permute-start.10) | collective-permute-done | bytes 73760 | tf_op jit(solution)/shard_map/ppermute | solution.py:524
  42.6 2.6 %collective-permute-start.12 = (f32[72,256]{1,0:T(8,128)S(1)}, f32[72,256]{1,0:T(8,128)S(1)}, u32[]{:S(2)}, u32[]{:S(2)}) collective-permute-start(f32[72,256]{1,0:T(8,128)S(1)} %add_add_fusion._.refs_0_), channel_id=1, source_target_pairs={{0,8},{1,9},{2,10},{3,11},{4,12},{5,13},{6,14},{7,15},{8,0},{9,1},... | collective-permute-start | bytes 221192 | tf_op jit(solution)/shard_map/ppermute | solution.py:524
  45.2 1.4 %collective-permute-start.11 = (f32[72,256]{1,0:T(8,128)S(1)}, f32[72,256]{1,0:T(8,128)S(1)}, u32[]{:S(2)}, u32[]{:S(2)}) collective-permute-start(f32[72,256]{1,0:T(8,128)S(1)} %add_add_fusion._.refs_0_), channel_id=1, source_target_pairs={{0,12},{1,13},{2,14},{3,15},{4,8},{5,9},{6,10},{7,11},{8,4},{9,5},... | collective-permute-start | bytes 221192 | tf_op jit(solution)/shard_map/ppermute | solution.py:524
  46.6 3.4 %shard_map.149 = (bf16[4096,256]{1,0:T(8,128)(2,1)}, bf16[4096,256]{1,0:T(8,128)(2,1)}, f32[8,128]{1,0:T(8,128)S(1)}) custom-call(bf16[256,4096]{1,0:T(8,128)(2,1)S(1)} %get-tuple-element.38.wt_ref, bf16[256,4096]{1,0:T(8,128)(2,1)S(1)} %get-tuple-element.54.dmt_ref, bf16[256,256]{1,0:T(8,128)(2,1)S(1)} %get-tuple-element.48.refs_2_.mw_ref, ...), custom_call_target="tpu_custom_call" | custom-call | flops 1073741824 | bytes 8388608 | tf_op jit(solution)/shard_map/pallas_call | solution.py:697
  50.8 1.9 %collective-permute-done.12.refs_2_ = f32[72,256]{1,0:T(8,128)S(1)} collective-permute-done((f32[72,256]{1,0:T(8,128)S(1)}, f32[72,256]{1,0:T(8,128)S(1)}, u32[]{:S(2)}, u32[]{:S(2)}) %collective-permute-start.12) | collective-permute-done | bytes 73760 | tf_op jit(solution)/shard_map/ppermute | solution.py:524
  53.3 0.9 %collective-permute-start.15 = (f32[72,256]{1,0:T(8,128)S(1)}, f32[72,256]{1,0:T(8,128)S(1)}, u32[]{:S(2)}, u32[]{:S(2)}) collective-permute-start(f32[72,256]{1,0:T(8,128)S(1)} %shard_map.150._.m0), channel_id=1, source_target_pairs={{0,2},{1,3},{2,0},{3,1},{4,6},{5,7},{6,4},{7,5},{8,10},{9,11},{10,... | collective-permute-start | bytes 221192 | tf_op jit(solution)/shard_map/ppermute | solution.py:524
  54.6 1.0 %shard_map.153 = (f32[256,256]{1,0:T(8,128)}, f32[8,128]{1,0:T(8,128)S(1)}) custom-call(f32[128,256]{1,0:T(8,128)S(1)} %shard_map.152.own_ref, f32[128,256]{1,0:T(8,128)S(1)} %collective-permute-done.19.other_ref, bf16[256,256]{1,0:T(8,128)(2,1)S(1)} %get-tuple-element.62.mixed_t_ref, f32[72,256]{1,0:T(8,128)S(1)} %shard_map.150._.m0), custom_call_target="tpu_custom_call" | custom-call | flops 67108864 | bytes 786432 | tf_op jit(solution)/shard_map/pallas_call | solution.py:716
  55.6 1.7 %collective-permute-done.16.m3 = f32[72,256]{1,0:T(8,128)S(1)} collective-permute-done((f32[72,256]{1,0:T(8,128)S(1)}, f32[72,256]{1,0:T(8,128)S(1)}, u32[]{:S(2)}, u32[]{:S(2)}) %collective-permute-start.16) | collective-permute-done | bytes 73760 | tf_op jit(solution)/shard_map/ppermute | solution.py:524
  57.3 1.6 %collective-permute-done.15.m2 = f32[72,256]{1,0:T(8,128)S(1)} collective-permute-done((f32[72,256]{1,0:T(8,128)S(1)}, f32[72,256]{1,0:T(8,128)S(1)}, u32[]{:S(2)}, u32[]{:S(2)}) %collective-permute-start.15) | collective-permute-done | bytes 73760 | tf_op jit(solution)/shard_map/ppermute | solution.py:524
  (37 shorter events, 4.6 us)
Async XLA Ops:
  1.3 24.9 %copy-start.1 = (bf16[256,256]{1,0:T(8,128)(2,1)S(1)}, bf16[256,256]{1,0:T(8,128)(2,1)}, u32[]{:S(2)}) copy-start(bf16[256,256]{1,0:T(8,128)(2,1)} %w_out_ref.1) | copy-start | bytes 393220
  9.2 21.3 %copy-start.2 = (bf16[32]{0:T(256)(128)(2,1)S(1)}, bf16[32]{0:T(256)(128)(2,1)}, u32[]{:S(2)}) copy-start(bf16[32]{0:T(256)(128)(2,1)} %param.15) | copy-start | bytes 196
  9.2 1.4 %collective-permute-start = (f32[72,128]{1,0:T(8,128)S(1)}, f32[72,128]{1,0:T(8,128)S(1)}, u32[]{:S(2)}, u32[]{:S(2)}) collective-permute-start(f32[72,128]{1,0:T(8,128)S(1)} %get-tuple-element.46), channel_id=1, source_target_pairs={{0,1},{1,0},{2,3},{3,2},{4,5},{5,4},{6,7},{7,6},{8,9},{9,8},{10,11... | collective-permute-start | bytes 110600 | tf_op jit(solution)/shard_map/ppermute | solution.py:524
  10.6 4.9 %collective-permute-start.3 = (f32[72,128]{1,0:T(8,128)S(1)}, f32[72,128]{1,0:T(8,128)S(1)}, u32[]{:S(2)}, u32[]{:S(2)}) collective-permute-start(f32[72,128]{1,0:T(8,128)S(1)} %add.24), channel_id=1, source_target_pairs={{0,4},{1,5},{2,6},{3,7},{4,0},{5,1},{6,2},{7,3},{8,12},{9,13},{10,... | collective-permute-start | bytes 110600 | tf_op jit(solution)/shard_map/ppermute | solution.py:524
  13.5 4.9 %collective-permute-start.2 = (f32[72,128]{1,0:T(8,128)S(1)}, f32[72,128]{1,0:T(8,128)S(1)}, u32[]{:S(2)}, u32[]{:S(2)}) collective-permute-start(f32[72,128]{1,0:T(8,128)S(1)} %add.24), channel_id=1, source_target_pairs={{0,6},{1,7},{2,4},{3,5},{4,2},{5,3},{6,0},{7,1},{8,14},{9,15},{10,... | collective-permute-start | bytes 110600 | tf_op jit(solution)/shard_map/ppermute | solution.py:524
  14.9 4.0 %collective-permute-start.1 = (f32[72,128]{1,0:T(8,128)S(1)}, f32[72,128]{1,0:T(8,128)S(1)}, u32[]{:S(2)}, u32[]{:S(2)}) collective-permute-start(f32[72,128]{1,0:T(8,128)S(1)} %add.24), channel_id=1, source_target_pairs={{0,2},{1,3},{2,0},{3,1},{4,6},{5,7},{6,4},{7,5},{8,10},{9,11},{10,... | collective-permute-start | bytes 110600 | tf_op jit(solution)/shard_map/ppermute | solution.py:524
  15.1 8.7 %collective-permute-start.6 = (f32[128,256]{1,0:T(8,128)S(1)}, f32[128,256]{1,0:T(8,128)S(1)}, u32[]{:S(2)}, u32[]{:S(2)}) collective-permute-start(f32[128,256]{1,0:T(8,128)S(1)} %get-tuple-element.53), channel_id=1, source_target_pairs={{0,1},{1,0},{2,3},{3,2},{4,5},{5,4},{6,7},{7,6},{8,9},{9,8},{10,11... | collective-permute-start | bytes 393224 | tf_op jit(solution)/shard_map/ppermute | solution.py:524
  18.9 4.9 %collective-permute-start.4 = (f32[72,128]{1,0:T(8,128)S(1)}, f32[72,128]{1,0:T(8,128)S(1)}, u32[]{:S(2)}, u32[]{:S(2)}) collective-permute-start(f32[72,128]{1,0:T(8,128)S(1)} %add_add_fusion.1), channel_id=1, source_target_pairs={{0,8},{1,9},{2,10},{3,11},{4,12},{5,13},{6,14},{7,15},{8,0},{9,1},... | collective-permute-start | bytes 110600 | tf_op jit(solution)/shard_map/ppermute | solution.py:524
  23.8 5.4 %collective-permute-start.7 = (f32[128,256]{1,0:T(8,128)S(1)}, f32[128,256]{1,0:T(8,128)S(1)}, u32[]{:S(2)}, u32[]{:S(2)}) collective-permute-start(f32[128,256]{1,0:T(8,128)S(1)} %shard_map.146.refs_0_), channel_id=1, source_target_pairs={{0,2},{1,3},{2,0},{3,1},{4,6},{5,7},{6,4},{7,5},{8,10},{9,11},{10,... | collective-permute-start | bytes 393224 | tf_op jit(solution)/shard_map/ppermute | solution.py:524
  24.9 1.2 %collective-permute-start.5 = (f32[72,128]{1,0:T(8,128)S(1)}, f32[72,128]{1,0:T(8,128)S(1)}, u32[]{:S(2)}, u32[]{:S(2)}) collective-permute-start(f32[72,128]{1,0:T(8,128)S(1)} %add.28.own_ref.refs_2_), channel_id=1, source_target_pairs={{0,1},{1,0},{2,3},{3,2},{4,5},{5,4},{6,7},{7,6},{8,9},{9,8},{10,11... | collective-permute-start | bytes 110600 | tf_op jit(solution)/shard_map/ppermute | solution.py:524
  29.3 9.1 %collective-permute-start.17 = (f32[128,256]{1,0:T(8,128)S(1)}, f32[128,256]{1,0:T(8,128)S(1)}, u32[]{:S(2)}, u32[]{:S(2)}) collective-permute-start(f32[128,256]{1,0:T(8,128)S(1)} %shard_map.147._.refs_0_), channel_id=1, source_target_pairs={{0,4},{1,5},{2,6},{3,7},{4,0},{5,1},{6,2},{7,3},{8,12},{9,13},{10,... | collective-permute-start | bytes 393224 | tf_op jit(solution)/shard_map/ppermute | solution.py:524
  30.5 16.1 %copy-start = (bf16[256,256]{1,0:T(8,128)(2,1)S(1)}, bf16[256,256]{1,0:T(8,128)(2,1)}, u32[]{:S(2)}) copy-start(bf16[256,256]{1,0:T(8,128)(2,1)} %w_mid_ref.1) | copy-start | bytes 393220
  36.1 5.2 %collective-permute-start.9 = (f32[72,256]{1,0:T(8,128)S(1)}, f32[72,256]{1,0:T(8,128)S(1)}, u32[]{:S(2)}, u32[]{:S(2)}) collective-permute-start(f32[72,256]{1,0:T(8,128)S(1)} %get-tuple-element.57), channel_id=1, source_target_pairs={{0,2},{1,3},{2,0},{3,1},{4,6},{5,7},{6,4},{7,5},{8,10},{9,11},{10,... | collective-permute-start | bytes 221192 | tf_op jit(solution)/shard_map/ppermute | solution.py:524
  37.6 4.5 %collective-permute-start.10 = (f32[72,256]{1,0:T(8,128)S(1)}, f32[72,256]{1,0:T(8,128)S(1)}, u32[]{:S(2)}, u32[]{:S(2)}) collective-permute-start(f32[72,256]{1,0:T(8,128)S(1)} %get-tuple-element.58), channel_id=1, source_target_pairs={{0,3},{1,2},{2,1},{3,0},{4,7},{5,6},{6,5},{7,4},{8,11},{9,10},{10,... | collective-permute-start | bytes 221192 | tf_op jit(solution)/shard_map/ppermute | solution.py:524
  37.6 4.5 %collective-permute-start.8 = (f32[72,256]{1,0:T(8,128)S(1)}, f32[72,256]{1,0:T(8,128)S(1)}, u32[]{:S(2)}, u32[]{:S(2)}) collective-permute-start(f32[72,256]{1,0:T(8,128)S(1)} %get-tuple-element.56.refs_2_), channel_id=1, source_target_pairs={{0,1},{1,0},{2,3},{3,2},{4,5},{5,4},{6,7},{7,6},{8,9},{9,8},{10,11... | collective-permute-start | bytes 221192 | tf_op jit(solution)/shard_map/ppermute | solution.py:524
  38.4 11.7 %collective-permute-start.18 = (f32[128,256]{1,0:T(8,128)S(1)}, f32[128,256]{1,0:T(8,128)S(1)}, u32[]{:S(2)}, u32[]{:S(2)}) collective-permute-start(f32[128,256]{1,0:T(8,128)S(1)} %shard_map.151.refs_0_), channel_id=1, source_target_pairs={{0,8},{1,9},{2,10},{3,11},{4,12},{5,13},{6,14},{7,15},{8,0},{9,1},... | collective-permute-start | bytes 393224 | tf_op jit(solution)/shard_map/ppermute | solution.py:524
  42.2 8.6 %collective-permute-start.13 = (f32[72,256]{1,0:T(8,128)S(1)}, f32[72,256]{1,0:T(8,128)S(1)}, u32[]{:S(2)}, u32[]{:S(2)}) collective-permute-start(f32[72,256]{1,0:T(8,128)S(1)} %add_add_fusion._.refs_0_), channel_id=1, source_target_pairs={{0,4},{1,5},{2,6},{3,7},{4,0},{5,1},{6,2},{7,3},{8,12},{9,13},{10,... | collective-permute-start | bytes 221192 | tf_op jit(solution)/shard_map/ppermute | solution.py:524
  42.6 10.1 %collective-permute-start.12 = (f32[72,256]{1,0:T(8,128)S(1)}, f32[72,256]{1,0:T(8,128)S(1)}, u32[]{:S(2)}, u32[]{:S(2)}) collective-permute-start(f32[72,256]{1,0:T(8,128)S(1)} %add_add_fusion._.refs_0_), channel_id=1, source_target_pairs={{0,8},{1,9},{2,10},{3,11},{4,12},{5,13},{6,14},{7,15},{8,0},{9,1},... | collective-permute-start | bytes 221192 | tf_op jit(solution)/shard_map/ppermute | solution.py:524
  45.2 7.5 %collective-permute-start.11 = (f32[72,256]{1,0:T(8,128)S(1)}, f32[72,256]{1,0:T(8,128)S(1)}, u32[]{:S(2)}, u32[]{:S(2)}) collective-permute-start(f32[72,256]{1,0:T(8,128)S(1)} %add_add_fusion._.refs_0_), channel_id=1, source_target_pairs={{0,12},{1,13},{2,14},{3,15},{4,8},{5,9},{6,10},{7,11},{8,4},{9,5},... | collective-permute-start | bytes 221192 | tf_op jit(solution)/shard_map/ppermute | solution.py:524
  50.1 4.6 %collective-permute-start.19 = (f32[128,256]{1,0:T(8,128)S(1)}, f32[128,256]{1,0:T(8,128)S(1)}, u32[]{:S(2)}, u32[]{:S(2)}) collective-permute-start(f32[128,256]{1,0:T(8,128)S(1)} %shard_map.152.own_ref), channel_id=1, source_target_pairs={{0,1},{1,0},{2,3},{3,2},{4,5},{5,4},{6,7},{7,6},{8,9},{9,8},{10,11... | collective-permute-start | bytes 393224 | tf_op jit(solution)/shard_map/ppermute | solution.py:524
  52.7 4.6 %collective-permute-start.16 = (f32[72,256]{1,0:T(8,128)S(1)}, f32[72,256]{1,0:T(8,128)S(1)}, u32[]{:S(2)}, u32[]{:S(2)}) collective-permute-start(f32[72,256]{1,0:T(8,128)S(1)} %shard_map.150._.m0), channel_id=1, source_target_pairs={{0,3},{1,2},{2,1},{3,0},{4,7},{5,6},{6,5},{7,4},{8,11},{9,10},{10,... | collective-permute-start | bytes 221192 | tf_op jit(solution)/shard_map/ppermute | solution.py:524
  53.3 5.6 %collective-permute-start.15 = (f32[72,256]{1,0:T(8,128)S(1)}, f32[72,256]{1,0:T(8,128)S(1)}, u32[]{:S(2)}, u32[]{:S(2)}) collective-permute-start(f32[72,256]{1,0:T(8,128)S(1)} %shard_map.150._.m0), channel_id=1, source_target_pairs={{0,2},{1,3},{2,0},{3,1},{4,6},{5,7},{6,4},{7,5},{8,10},{9,11},{10,... | collective-permute-start | bytes 221192 | tf_op jit(solution)/shard_map/ppermute | solution.py:524
  54.3 4.7 %collective-permute-start.14 = (f32[72,256]{1,0:T(8,128)S(1)}, f32[72,256]{1,0:T(8,128)S(1)}, u32[]{:S(2)}, u32[]{:S(2)}) collective-permute-start(f32[72,256]{1,0:T(8,128)S(1)} %shard_map.150._.m0), channel_id=1, source_target_pairs={{0,1},{1,0},{2,3},{3,2},{4,5},{5,4},{6,7},{7,6},{8,9},{9,8},{10,11... | collective-permute-start | bytes 221192 | tf_op jit(solution)/shard_map/ppermute | solution.py:524

commit v8 on v7

--- a/solution.py
+++ b/solution.py
@@ -126,19 +126,19 @@
             )
         )
     ]
-    feats_in, cot_in = [], []
-    for i in range(count):
-        at = pl.ds(i * piece, piece)
-        for j, (source, target, into) in enumerate(
-            ((feats_far, feats_ref, feats_in), (cot_far, cot_ref, cot_in))
-        ):
-            sem = sems.at[len(small) + 2 * i + j]
-            into.append(pltpu.make_async_copy(source.at[at, :], target.at[at, :], sem))
-    for copy in small[:3] + feats_in[:1] + small[3:] + cot_in[:1]:
+    first, rest = pl.ds(0, piece), pl.ds(piece, rows - piece)
+    large = [
+        pltpu.make_async_copy(source, target, sems.at[len(small) + i])
+        for i, (source, target) in enumerate(
+            (
+                (feats_far.at[first, :], feats_ref.at[first, :]),
+                (feats_far.at[rest, :], feats_ref.at[rest, :]),
+                (cot_far, cot_ref),
+            )
+        )
+    ]
+    for copy in small[:3] + large[:1] + small[3:] + large[1:]:
         copy.start()
-    for i in range(1, count):
-        feats_in[i].start()
-        cot_in[i].start()
 
     raw_acc[...] = jnp.zeros_like(raw_acc)
     norm_acc[...] = jnp.zeros_like(norm_acc)
@@ -203,13 +203,13 @@
         raw_acc[...] += nn(wt, mid)
         wc_acc[...] += nn(wt, cot_ref[at, :])
 
-    feats_in[0].wait()
+    large[0].wait()
     ready = products(0)
+    large[1].wait()
+    large[2].wait()
     for i in range(count):
         current = ready
-        cot_in[i].wait()
         if i + 1 < count:
-            feats_in[i + 1].wait()
             ready = products(i + 1)
         statistics(i, *current)
 
@@ -593,7 +593,6 @@
     half = (2 * slices + 8, 128)
     wide = (hm // 2, width)
     inputs = (valid.reshape(1, rows), feats, cotangent, w_mid, w_slice, w_out, w_qkv)
-    pieces = rows // min(sub_block, rows)
     (
         mid,
         wt,
@@ -635,7 +634,7 @@
             pltpu.VMEM((hm, 128), f32),
             pltpu.VMEM((hm, width), f32),
             pltpu.VMEM((2,) + half, f32),
-            pltpu.SemaphoreType.DMA((5 + 2 * pieces,)),
+            pltpu.SemaphoreType.DMA((8,)),
         ],
         compiler_params=params(24, False),
         cost_estimate=cost(4 * unit, rows * width * 8, rows * hm),
@@ -643,11 +642,18 @@
 
     own = keep + exchange(send, 1, count)
     wc_got = exchange(wc_send, 1, count)
+    wc_sum = sum_behind([wc_keep, wc_got], own)
     own = sum_stage(own, 2, 3, count)
+    wc_got = exchange(wc_sum, 2, count)
+    wc_sum = sum_behind([wc_sum, wc_got], own)
     own = sum_over_groups(own, 8, count)
     other = exchange(own, 1, count)
-    wc_sum = sum_behind([wc_keep, wc_got], own)
-    wc_got = exchange(wc_sum, 2, count)
+    stride = 4
+    while stride < count // 2:
+        wc_got = exchange(wc_sum, stride, count)
+        stride *= 2
+        if stride < count // 2:
+            wc_sum = wc_sum + wc_got
 
     mw, mixed_t, dr, drt, dn, grad_qkv = pl.pallas_call(
         functools.partial(tokens_kernel, heads, slices),
@@ -661,16 +667,8 @@
         ],
         scratch_shapes=[pltpu.VMEM((2,) + half, f32)],
         compiler_params=params(16, False),
-        cost_estimate=cost(30 * width**3, 4 * width * width * 4, hm * hm),
+        cost_estimate=cost(3 * width**3, 4 * width * width * 4, hm * hm),
     )(own, other, w_cat, w_out)
-    wc_sum = sum_behind([wc_sum, wc_got], mw)
-    stride = 4
-    while stride < count // 2:
-        if stride > 4:
-            wc_sum = wc_sum + wc_got
-        wc_got = exchange(wc_sum, stride, count)
-        stride *= 2
-
     larger = (width // group + slices // group, width)
     dmt, *sends = pl.pallas_call(
         functools.partial(backward_kernel, heads, slices),
@@ -685,7 +683,7 @@
             pltpu.VMEM((group,) + larger, f32),
         ],
         compiler_params=params(24, False),
-        cost_estimate=cost(8 * unit, rows * width * 8, rows * hm),
+        cost_estimate=cost(width**3, rows * width, rows),
     )(aux, mid, cot_near, feats_near, sw, sb, mw, dr, drt, dn, temp, wc_sum)
 
     mid_total = scatter_group(sends, count)

time: 59.9 us -> 58.5 us (0.977)
  waiting for transfers between devices: 14.8 us -> 13.1 us
  starting transfers between devices: 21.6 us -> 22.5 us
    ppermute x20, waiting for transfers between devices: 14.8 us -> 13.1 us  [exchange(): return lax.ppermute(x, 'node', [(i, i ^ k) for i in range(count)])]
    ppermute x20, starting transfers between devices: 21.6 us -> 22.5 us  [exchange(): return lax.ppermute(x, 'node', [(i, i ^ k) for i in range(count)])]
  transfers between devices with their start and end apart: 20 -> 20, of which waited for: 11 -> 10; matrix products, arithmetic and copies ran while one was open for 0% -> 0% of each run, Pallas kernels for 22% -> 23%
where the time goes in v8:
time: 58.5 us; the launch traced here: 58.3 us
  starting transfers between devices  22.5 us (38%)
  Pallas kernels  21.3 us (36%)
  waiting for transfers between devices  13.1 us (22%)
  between operations  1.38 us (2%)
    ppermute x20, starting transfers between devices, exchange(): return lax.ppermute(x, 'node', [(i, i ^ k) for i in range(count)])  22.5 us
    ppermute x20, waiting for transfers between devices, exchange(): return lax.ppermute(x, 'node', [(i, i ^ k) for i in range(count)])  13.1 us
    pallas_call x1, Pallas kernels, shards(): pl.pallas_call(functools.partial(stats_kernel, heads, slices), in_specs=[...  7.41 us
    pallas_call x1, Pallas kernels, shards(): pl.pallas_call(functools.partial(backward_kernel, heads, slices), in_spec...  5.58 us
    pallas_call x1, Pallas kernels, shards(): pl.pallas_call(rows_kernel, grid=grid, in_specs=[whole, whole, whole, ful...  3.44 us
    pallas_call x1, Pallas kernels, shards(): pl.pallas_call(functools.partial(tokens_kernel, heads, slices), out_shape...  3.1 us
  transfers between devices with their start and end apart: 20, of which 10 were waited for; matrix products, arithmetic and copies ran while one was open for 0% of the time, Pallas kernels for 23%

profile of v8, /device:TPU:0, one launch (start us, length us, event | category | flops | bytes accessed | tf_op | source)
XLA Modules:
  0.0 58.3 jit_solution(4801700789753117809)
XLA Ops:
  1.3 7.4 %shard_map.144 = (bf16[4096,256]{1,0:T(8,128)(2,1)S(1)}, bf16[256,4096]{1,0:T(8,128)(2,1)S(1)}, f32[24,4096]{1,0:T(8,128)S(1)}, bf16[272,256]{1,0:T(8,128)(2,1)S...) custom-call(s32[1]{0:T(128)S(6)} %copy.16.owned_ref, ...), custom_call_target="tpu_custom_call" | custom-call | flops 2147483648 | bytes 8388608 | tf_op jit(solution)/shard_map/pallas_call | solution.py:609
  9.3 1.1 %collective-permute-done = f32[72,128]{1,0:T(8,128)S(1)} collective-permute-done((f32[72,128]{1,0:T(8,128)S(1)}, f32[72,128]{1,0:T(8,128)S(1)}, u32[]{:S(2)}, u32[]{:S(2)}) %collective-permute-start) | collective-permute-done | bytes 36896 | tf_op jit(solution)/shard_map/ppermute | solution.py:524
  10.5 3.7 %collective-permute-start.2 = (f32[72,128]{1,0:T(8,128)S(1)}, f32[72,128]{1,0:T(8,128)S(1)}, u32[]{:S(2)}, u32[]{:S(2)}) collective-permute-start(f32[72,128]{1,0:T(8,128)S(1)} %add.24.refs_2_), channel_id=1, source_target_pairs={{0,6},{1,7},{2,4},{3,5},{4,2},{5,3},{6,0},{7,1},{8,14},{9,15},{10,... | collective-permute-start | bytes 110600 | tf_op jit(solution)/shard_map/ppermute | solution.py:524
  14.8 1.9 %collective-permute-start.7 = (f32[128,256]{1,0:T(8,128)S(1)}, f32[128,256]{1,0:T(8,128)S(1)}, u32[]{:S(2)}, u32[]{:S(2)}) collective-permute-start(f32[128,256]{1,0:T(8,128)S(1)} %shard_map.146.refs_0_), channel_id=1, source_target_pairs={{0,2},{1,3},{2,0},{3,1},{4,6},{5,7},{6,4},{7,5},{8,10},{9,11},{10,... | collective-permute-start | bytes 393224 | tf_op jit(solution)/shard_map/ppermute | solution.py:524
  16.7 1.4 %collective-permute-done.3 = f32[72,128]{1,0:T(8,128)S(1)} collective-permute-done((f32[72,128]{1,0:T(8,128)S(1)}, f32[72,128]{1,0:T(8,128)S(1)}, u32[]{:S(2)}, u32[]{:S(2)}) %collective-permute-start.3) | collective-permute-done | bytes 36896 | tf_op jit(solution)/shard_map/ppermute | solution.py:524
  18.1 0.9 %collective-permute-done.1 = f32[72,128]{1,0:T(8,128)S(1)} collective-permute-done((f32[72,128]{1,0:T(8,128)S(1)}, f32[72,128]{1,0:T(8,128)S(1)}, u32[]{:S(2)}, u32[]{:S(2)}) %collective-permute-start.1) | collective-permute-done | bytes 36896 | tf_op jit(solution)/shard_map/ppermute | solution.py:524
  19.0 2.7 %collective-permute-start.4 = (f32[72,128]{1,0:T(8,128)S(1)}, f32[72,128]{1,0:T(8,128)S(1)}, u32[]{:S(2)}, u32[]{:S(2)}) collective-permute-start(f32[72,128]{1,0:T(8,128)S(1)} %add_add_fusion.1.refs_2_), channel_id=1, source_target_pairs={{0,8},{1,9},{2,10},{3,11},{4,12},{5,13},{6,14},{7,15},{8,0},{9,1},... | collective-permute-start | bytes 110600 | tf_op jit(solution)/shard_map/ppermute | solution.py:524
  21.7 1.6 %collective-permute-start.17 = (f32[128,256]{1,0:T(8,128)S(1)}, f32[128,256]{1,0:T(8,128)S(1)}, u32[]{:S(2)}, u32[]{:S(2)}) collective-permute-start(f32[128,256]{1,0:T(8,128)S(1)} %shard_map.147._.refs_0_), channel_id=1, source_target_pairs={{0,4},{1,5},{2,6},{3,7},{4,0},{5,1},{6,2},{7,3},{8,12},{9,13},{10,... | collective-permute-start | bytes 393224 | tf_op jit(solution)/shard_map/ppermute | solution.py:524
  23.3 0.7 %collective-permute-done.4 = f32[72,128]{1,0:T(8,128)S(1)} collective-permute-done((f32[72,128]{1,0:T(8,128)S(1)}, f32[72,128]{1,0:T(8,128)S(1)}, u32[]{:S(2)}, u32[]{:S(2)}) %collective-permute-start.4) | collective-permute-done | bytes 36896 | tf_op jit(solution)/shard_map/ppermute | solution.py:524
  24.0 1.2 %collective-permute-done.5.got_ref = f32[72,128]{1,0:T(8,128)S(1)} collective-permute-done((f32[72,128]{1,0:T(8,128)S(1)}, f32[72,128]{1,0:T(8,128)S(1)}, u32[]{:S(2)}, u32[]{:S(2)}) %collective-permute-start.5) | collective-permute-done | bytes 36896 | tf_op jit(solution)/shard_map/ppermute | solution.py:524
  25.2 3.1 %shard_map.145 = (bf16[256,256]{1,0:T(8,128)(2,1)S(1)}, bf16[256,256]{1,0:T(8,128)(2,1)S(1)}, bf16[256,256]{1,0:T(8,128)(2,1)S(1)}, bf16[256,256]{1,0:T(8,128)(2...) custom-call(f32[72,128]{1,0:T(8,128)S(1)} %add.28.own_ref, f32[72,128]{1,0:T(8,128)S(1)} %collective-permute-done.5.got_ref, ...), custom_call_target="tpu_custom_call" | custom-call | flops 50331648 | bytes 1048576 | tf_op jit(solution)/shard_map/pallas_call | solution.py:658
  28.3 5.6 %shard_map.148 = (bf16[256,4096]{1,0:T(8,128)(2,1)S(1)}, f32[72,256]{1,0:T(8,128)S(1)}, f32[72,256]{1,0:T(8,128)S(1)}, f32[72,256]{1,0:T(8,128)S(1)}, f32[72,256]{1,0:T(8,128)S(1)}) custom-call(f32[24,4096]{1,0:T(8,128)S(1)} %get-tuple-element.39.aux_ref, bf16[4096,256]{1,0:T(8,128)(2,1)S(1)} %get-tuple-element.40.mid_ref, ...), custom_call_target="tpu_custom_call" | custom-call | flops 16777216 | bytes 1048576 | tf_op jit(solution)/shard_map/pallas_call | solution.py:673
  34.1 1.4 %collective-permute-start.10 = (f32[72,256]{1,0:T(8,128)S(1)}, f32[72,256]{1,0:T(8,128)S(1)}, u32[]{:S(2)}, u32[]{:S(2)}) collective-permute-start(f32[72,256]{1,0:T(8,128)S(1)} %get-tuple-element.58), channel_id=1, source_target_pairs={{0,3},{1,2},{2,1},{3,0},{4,7},{5,6},{6,5},{7,4},{8,11},{9,10},{10,... | collective-permute-start | bytes 221192 | tf_op jit(solution)/shard_map/ppermute | solution.py:524
  36.2 2.6 %collective-permute-start.18 = (f32[128,256]{1,0:T(8,128)S(1)}, f32[128,256]{1,0:T(8,128)S(1)}, u32[]{:S(2)}, u32[]{:S(2)}) collective-permute-start(f32[128,256]{1,0:T(8,128)S(1)} %shard_map.151.refs_0_), channel_id=1, source_target_pairs={{0,8},{1,9},{2,10},{3,11},{4,12},{5,13},{6,14},{7,15},{8,0},{9,1},... | collective-permute-start | bytes 393224 | tf_op jit(solution)/shard_map/ppermute | solution.py:524
  39.2 3.9 %collective-permute-start.11 = (f32[72,256]{1,0:T(8,128)S(1)}, f32[72,256]{1,0:T(8,128)S(1)}, u32[]{:S(2)}, u32[]{:S(2)}) collective-permute-start(f32[72,256]{1,0:T(8,128)S(1)} %add_add_fusion._.refs_0_), channel_id=1, source_target_pairs={{0,12},{1,13},{2,14},{3,15},{4,8},{5,9},{6,10},{7,11},{8,4},{9,5},... | collective-permute-start | bytes 221192 | tf_op jit(solution)/shard_map/ppermute | solution.py:524
  43.7 3.4 %shard_map.149 = (bf16[4096,256]{1,0:T(8,128)(2,1)}, bf16[4096,256]{1,0:T(8,128)(2,1)}, f32[8,128]{1,0:T(8,128)S(1)}) custom-call(bf16[256,4096]{1,0:T(8,128)(2,1)S(1)} %get-tuple-element.38.wt_ref, bf16[256,4096]{1,0:T(8,128)(2,1)S(1)} %get-tuple-element.54.dmt_ref, bf16[256,256]{1,0:T(8,128)(2,1)S(1)} %get-tuple-element.48.mw_ref, ...), custom_call_target="tpu_custom_call" | custom-call | flops 1073741824 | bytes 8388608 | tf_op jit(solution)/shard_map/pallas_call | solution.py:695
  47.1 2.3 %collective-permute-done.18.refs_1_ = f32[128,256]{1,0:T(8,128)S(1)} collective-permute-done((f32[128,256]{1,0:T(8,128)S(1)}, f32[128,256]{1,0:T(8,128)S(1)}, u32[]{:S(2)}, u32[]{:S(2)}) %collective-permute-start.18) | collective-permute-done | bytes 131104 | tf_op jit(solution)/shard_map/ppermute | solution.py:524
  49.6 2.1 %collective-permute-done.12.refs_2_ = f32[72,256]{1,0:T(8,128)S(1)} collective-permute-done((f32[72,256]{1,0:T(8,128)S(1)}, f32[72,256]{1,0:T(8,128)S(1)}, u32[]{:S(2)}, u32[]{:S(2)}) %collective-permute-start.12) | collective-permute-done | bytes 73760 | tf_op jit(solution)/shard_map/ppermute | solution.py:524
  51.8 0.7 %collective-permute-start.15 = (f32[72,256]{1,0:T(8,128)S(1)}, f32[72,256]{1,0:T(8,128)S(1)}, u32[]{:S(2)}, u32[]{:S(2)}) collective-permute-start(f32[72,256]{1,0:T(8,128)S(1)} %shard_map.150._.m0), channel_id=1, source_target_pairs={{0,2},{1,3},{2,0},{3,1},{4,6},{5,7},{6,4},{7,5},{8,10},{9,11},{10,... | collective-permute-start | bytes 221192 | tf_op jit(solution)/shard_map/ppermute | solution.py:524
  52.4 1.2 %collective-permute-start.16 = (f32[72,256]{1,0:T(8,128)S(1)}, f32[72,256]{1,0:T(8,128)S(1)}, u32[]{:S(2)}, u32[]{:S(2)}) collective-permute-start(f32[72,256]{1,0:T(8,128)S(1)} %shard_map.150._.m0), channel_id=1, source_target_pairs={{0,3},{1,2},{2,1},{3,0},{4,7},{5,6},{6,5},{7,4},{8,11},{9,10},{10,... | collective-permute-start | bytes 221192 | tf_op jit(solution)/shard_map/ppermute | solution.py:524
  53.6 1.0 %shard_map.153 = (f32[256,256]{1,0:T(8,128)}, f32[8,128]{1,0:T(8,128)S(1)}) custom-call(f32[128,256]{1,0:T(8,128)S(1)} %shard_map.152.own_ref, f32[128,256]{1,0:T(8,128)S(1)} %collective-permute-done.19.other_ref, bf16[256,256]{1,0:T(8,128)(2,1)S(1)} %get-tuple-element.62.mixed_t_ref, f32[72,256]{1,0:T(8,128)S(1)} %shard_map.150._.m0), custom_call_target="tpu_custom_call" | custom-call | flops 67108864 | bytes 786432 | tf_op jit(solution)/shard_map/pallas_call | solution.py:714
  54.6 2.3 %collective-permute-done.15.m2 = f32[72,256]{1,0:T(8,128)S(1)} collective-permute-done((f32[72,256]{1,0:T(8,128)S(1)}, f32[72,256]{1,0:T(8,128)S(1)}, u32[]{:S(2)}, u32[]{:S(2)}) %collective-permute-start.15) | collective-permute-done | bytes 73760 | tf_op jit(solution)/shard_map/ppermute | solution.py:524
  56.9 0.7 %collective-permute-done.16.m3 = f32[72,256]{1,0:T(8,128)S(1)} collective-permute-done((f32[72,256]{1,0:T(8,128)S(1)}, f32[72,256]{1,0:T(8,128)S(1)}, u32[]{:S(2)}, u32[]{:S(2)}) %collective-permute-start.16) | collective-permute-done | bytes 73760 | tf_op jit(solution)/shard_map/ppermute | solution.py:524
  57.6 0.7 %shard_map.154 = (f32[256,256]{1,0:T(8,128)}, f32[32,32]{1,0:T(8,128)}, f32[1,32]{1,0:T(1,128)}) custom-call(f32[72,256]{1,0:T(8,128)S(1)} %shard_map.150._.m0, f32[72,256]{1,0:T(8,128)S(1)} %collective-permute-done.14.m1, f32[72,256]{1,0:T(8,128)S(1)} %collective-permute-done.15.m2, f32[72,256]{1,0:T(8,128)S(1)} %collective-permute-done.16.m3, ...), custom_call_target="tpu_custom_call" | custom-call | bytes 524288 | tf_op jit(solution)/shard_map/pallas_call | solution.py:725
  (37 shorter events, 3.3 us)
Async XLA Ops:
  1.3 24.0 %copy-start.1 = (bf16[256,256]{1,0:T(8,128)(2,1)S(1)}, bf16[256,256]{1,0:T(8,128)(2,1)}, u32[]{:S(2)}) copy-start(bf16[256,256]{1,0:T(8,128)(2,1)} %w_out_ref.1) | copy-start | bytes 393220
  1.3 27.0 %copy-start.2 = (bf16[32]{0:T(256)(128)(2,1)S(1)}, bf16[32]{0:T(256)(128)(2,1)}, u32[]{:S(2)}) copy-start(bf16[32]{0:T(256)(128)(2,1)} %param.15) | copy-start | bytes 196
  8.7 6.1 %collective-permute-start.6 = (f32[128,256]{1,0:T(8,128)S(1)}, f32[128,256]{1,0:T(8,128)S(1)}, u32[]{:S(2)}, u32[]{:S(2)}) collective-permute-start(f32[128,256]{1,0:T(8,128)S(1)} %get-tuple-element.53), channel_id=1, source_target_pairs={{0,1},{1,0},{2,3},{3,2},{4,5},{5,4},{6,7},{7,6},{8,9},{9,8},{10,11... | collective-permute-start | bytes 393224 | tf_op jit(solution)/shard_map/ppermute | solution.py:524
  9.2 1.2 %collective-permute-start = (f32[72,128]{1,0:T(8,128)S(1)}, f32[72,128]{1,0:T(8,128)S(1)}, u32[]{:S(2)}, u32[]{:S(2)}) collective-permute-start(f32[72,128]{1,0:T(8,128)S(1)} %get-tuple-element.46), channel_id=1, source_target_pairs={{0,1},{1,0},{2,3},{3,2},{4,5},{5,4},{6,7},{7,6},{8,9},{9,8},{10,11... | collective-permute-start | bytes 110600 | tf_op jit(solution)/shard_map/ppermute | solution.py:524
  10.5 6.3 %collective-permute-start.2 = (f32[72,128]{1,0:T(8,128)S(1)}, f32[72,128]{1,0:T(8,128)S(1)}, u32[]{:S(2)}, u32[]{:S(2)}) collective-permute-start(f32[72,128]{1,0:T(8,128)S(1)} %add.24.refs_2_), channel_id=1, source_target_pairs={{0,6},{1,7},{2,4},{3,5},{4,2},{5,3},{6,0},{7,1},{8,14},{9,15},{10,... | collective-permute-start | bytes 110600 | tf_op jit(solution)/shard_map/ppermute | solution.py:524
  14.1 4.0 %collective-permute-start.3 = (f32[72,128]{1,0:T(8,128)S(1)}, f32[72,128]{1,0:T(8,128)S(1)}, u32[]{:S(2)}, u32[]{:S(2)}) collective-permute-start(f32[72,128]{1,0:T(8,128)S(1)} %add.24.refs_2_), channel_id=1, source_target_pairs={{0,4},{1,5},{2,6},{3,7},{4,0},{5,1},{6,2},{7,3},{8,12},{9,13},{10,... | collective-permute-start | bytes 110600 | tf_op jit(solution)/shard_map/ppermute | solution.py:524
  14.6 4.4 %collective-permute-start.1 = (f32[72,128]{1,0:T(8,128)S(1)}, f32[72,128]{1,0:T(8,128)S(1)}, u32[]{:S(2)}, u32[]{:S(2)}) collective-permute-start(f32[72,128]{1,0:T(8,128)S(1)} %add.24.refs_2_), channel_id=1, source_target_pairs={{0,2},{1,3},{2,0},{3,1},{4,6},{5,7},{6,4},{7,5},{8,10},{9,11},{10,... | collective-permute-start | bytes 110600 | tf_op jit(solution)/shard_map/ppermute | solution.py:524
  14.8 6.8 %collective-permute-start.7 = (f32[128,256]{1,0:T(8,128)S(1)}, f32[128,256]{1,0:T(8,128)S(1)}, u32[]{:S(2)}, u32[]{:S(2)}) collective-permute-start(f32[128,256]{1,0:T(8,128)S(1)} %shard_map.146.refs_0_), channel_id=1, source_target_pairs={{0,2},{1,3},{2,0},{3,1},{4,6},{5,7},{6,4},{7,5},{8,10},{9,11},{10,... | collective-permute-start | bytes 393224 | tf_op jit(solution)/shard_map/ppermute | solution.py:524
  19.0 5.0 %collective-permute-start.4 = (f32[72,128]{1,0:T(8,128)S(1)}, f32[72,128]{1,0:T(8,128)S(1)}, u32[]{:S(2)}, u32[]{:S(2)}) collective-permute-start(f32[72,128]{1,0:T(8,128)S(1)} %add_add_fusion.1.refs_2_), channel_id=1, source_target_pairs={{0,8},{1,9},{2,10},{3,11},{4,12},{5,13},{6,14},{7,15},{8,0},{9,1},... | collective-permute-start | bytes 110600 | tf_op jit(solution)/shard_map/ppermute | solution.py:524
  21.7 14.5 %collective-permute-start.17 = (f32[128,256]{1,0:T(8,128)S(1)}, f32[128,256]{1,0:T(8,128)S(1)}, u32[]{:S(2)}, u32[]{:S(2)}) collective-permute-start(f32[128,256]{1,0:T(8,128)S(1)} %shard_map.147._.refs_0_), channel_id=1, source_target_pairs={{0,4},{1,5},{2,6},{3,7},{4,0},{5,1},{6,2},{7,3},{8,12},{9,13},{10,... | collective-permute-start | bytes 393224 | tf_op jit(solution)/shard_map/ppermute | solution.py:524
  24.0 1.2 %collective-permute-start.5 = (f32[72,128]{1,0:T(8,128)S(1)}, f32[72,128]{1,0:T(8,128)S(1)}, u32[]{:S(2)}, u32[]{:S(2)}) collective-permute-start(f32[72,128]{1,0:T(8,128)S(1)} %add.28.own_ref), channel_id=1, source_target_pairs={{0,1},{1,0},{2,3},{3,2},{4,5},{5,4},{6,7},{7,6},{8,9},{9,8},{10,11... | collective-permute-start | bytes 110600 | tf_op jit(solution)/shard_map/ppermute | solution.py:524
  28.3 15.3 %copy-start = (bf16[256,256]{1,0:T(8,128)(2,1)S(1)}, bf16[256,256]{1,0:T(8,128)(2,1)}, u32[]{:S(2)}) copy-start(bf16[256,256]{1,0:T(8,128)(2,1)} %w_mid_ref.1) | copy-start | bytes 393220
  33.9 5.2 %collective-permute-start.9 = (f32[72,256]{1,0:T(8,128)S(1)}, f32[72,256]{1,0:T(8,128)S(1)}, u32[]{:S(2)}, u32[]{:S(2)}) collective-permute-start(f32[72,256]{1,0:T(8,128)S(1)} %get-tuple-element.57), channel_id=1, source_target_pairs={{0,2},{1,3},{2,0},{3,1},{4,6},{5,7},{6,4},{7,5},{8,10},{9,11},{10,... | collective-permute-start | bytes 221192 | tf_op jit(solution)/shard_map/ppermute | solution.py:524
  34.1 5.1 %collective-permute-start.10 = (f32[72,256]{1,0:T(8,128)S(1)}, f32[72,256]{1,0:T(8,128)S(1)}, u32[]{:S(2)}, u32[]{:S(2)}) collective-permute-start(f32[72,256]{1,0:T(8,128)S(1)} %get-tuple-element.58), channel_id=1, source_target_pairs={{0,3},{1,2},{2,1},{3,0},{4,7},{5,6},{6,5},{7,4},{8,11},{9,10},{10,... | collective-permute-start | bytes 221192 | tf_op jit(solution)/shard_map/ppermute | solution.py:524
  35.5 3.6 %collective-permute-start.8 = (f32[72,256]{1,0:T(8,128)S(1)}, f32[72,256]{1,0:T(8,128)S(1)}, u32[]{:S(2)}, u32[]{:S(2)}) collective-permute-start(f32[72,256]{1,0:T(8,128)S(1)} %get-tuple-element.56.refs_2_), channel_id=1, source_target_pairs={{0,1},{1,0},{2,3},{3,2},{4,5},{5,4},{6,7},{7,6},{8,9},{9,8},{10,11... | collective-permute-start | bytes 221192 | tf_op jit(solution)/shard_map/ppermute | solution.py:524
  36.2 13.3 %collective-permute-start.18 = (f32[128,256]{1,0:T(8,128)S(1)}, f32[128,256]{1,0:T(8,128)S(1)}, u32[]{:S(2)}, u32[]{:S(2)}) collective-permute-start(f32[128,256]{1,0:T(8,128)S(1)} %shard_map.151.refs_0_), channel_id=1, source_target_pairs={{0,8},{1,9},{2,10},{3,11},{4,12},{5,13},{6,14},{7,15},{8,0},{9,1},... | collective-permute-start | bytes 393224 | tf_op jit(solution)/shard_map/ppermute | solution.py:524
  39.2 10.4 %collective-permute-start.11 = (f32[72,256]{1,0:T(8,128)S(1)}, f32[72,256]{1,0:T(8,128)S(1)}, u32[]{:S(2)}, u32[]{:S(2)}) collective-permute-start(f32[72,256]{1,0:T(8,128)S(1)} %add_add_fusion._.refs_0_), channel_id=1, source_target_pairs={{0,12},{1,13},{2,14},{3,15},{4,8},{5,9},{6,10},{7,11},{8,4},{9,5},... | collective-permute-start | bytes 221192 | tf_op jit(solution)/shard_map/ppermute | solution.py:524
  43.0 8.6 %collective-permute-start.12 = (f32[72,256]{1,0:T(8,128)S(1)}, f32[72,256]{1,0:T(8,128)S(1)}, u32[]{:S(2)}, u32[]{:S(2)}) collective-permute-start(f32[72,256]{1,0:T(8,128)S(1)} %add_add_fusion._.refs_0_), channel_id=1, source_target_pairs={{0,8},{1,9},{2,10},{3,11},{4,12},{5,13},{6,14},{7,15},{8,0},{9,1},... | collective-permute-start | bytes 221192 | tf_op jit(solution)/shard_map/ppermute | solution.py:524
  43.0 8.6 %collective-permute-start.13 = (f32[72,256]{1,0:T(8,128)S(1)}, f32[72,256]{1,0:T(8,128)S(1)}, u32[]{:S(2)}, u32[]{:S(2)}) collective-permute-start(f32[72,256]{1,0:T(8,128)S(1)} %add_add_fusion._.refs_0_), channel_id=1, source_target_pairs={{0,4},{1,5},{2,6},{3,7},{4,0},{5,1},{6,2},{7,3},{8,12},{9,13},{10,... | collective-permute-start | bytes 221192 | tf_op jit(solution)/shard_map/ppermute | solution.py:524
  49.5 4.2 %collective-permute-start.19 = (f32[128,256]{1,0:T(8,128)S(1)}, f32[128,256]{1,0:T(8,128)S(1)}, u32[]{:S(2)}, u32[]{:S(2)}) collective-permute-start(f32[128,256]{1,0:T(8,128)S(1)} %shard_map.152.own_ref), channel_id=1, source_target_pairs={{0,1},{1,0},{2,3},{3,2},{4,5},{5,4},{6,7},{7,6},{8,9},{9,8},{10,11... | collective-permute-start | bytes 393224 | tf_op jit(solution)/shard_map/ppermute | solution.py:524
  51.7 2.9 %collective-permute-start.14 = (f32[72,256]{1,0:T(8,128)S(1)}, f32[72,256]{1,0:T(8,128)S(1)}, u32[]{:S(2)}, u32[]{:S(2)}) collective-permute-start(f32[72,256]{1,0:T(8,128)S(1)} %shard_map.150._.m0), channel_id=1, source_target_pairs={{0,1},{1,0},{2,3},{3,2},{4,5},{5,4},{6,7},{7,6},{8,9},{9,8},{10,11... | collective-permute-start | bytes 221192 | tf_op jit(solution)/shard_map/ppermute | solution.py:524
  51.8 5.1 %collective-permute-start.15 = (f32[72,256]{1,0:T(8,128)S(1)}, f32[72,256]{1,0:T(8,128)S(1)}, u32[]{:S(2)}, u32[]{:S(2)}) collective-permute-start(f32[72,256]{1,0:T(8,128)S(1)} %shard_map.150._.m0), channel_id=1, source_target_pairs={{0,2},{1,3},{2,0},{3,1},{4,6},{5,7},{6,4},{7,5},{8,10},{9,11},{10,... | collective-permute-start | bytes 221192 | tf_op jit(solution)/shard_map/ppermute | solution.py:524
  52.4 5.2 %collective-permute-start.16 = (f32[72,256]{1,0:T(8,128)S(1)}, f32[72,256]{1,0:T(8,128)S(1)}, u32[]{:S(2)}, u32[]{:S(2)}) collective-permute-start(f32[72,256]{1,0:T(8,128)S(1)} %shard_map.150._.m0), channel_id=1, source_target_pairs={{0,3},{1,2},{2,1},{3,0},{4,7},{5,6},{6,5},{7,4},{8,11},{9,10},{10,... | collective-permute-start | bytes 221192 | tf_op jit(solution)/shard_map/ppermute | solution.py:524

commit v9 on v8

--- a/solution.py
+++ b/solution.py
@@ -84,13 +84,10 @@
     w_mid_far,
     w_slice_far,
     w_out_far,
-    w_qkv_far,
     mid_ref,
     wt_ref,
     aux_ref,
     sw_ref,
-    sb_ref,
-    w_cat_ref,
     keep_ref,
     send_ref,
     wc_keep_ref,
@@ -101,7 +98,6 @@
     w_mid_ref,
     w_slice_ref,
     w_out_ref,
-    w_qkv_ref,
     raw_acc,
     norm_acc,
     wc_acc,
@@ -119,7 +115,6 @@
         for i, (source, target) in enumerate(
             (
                 (w_slice_far, w_slice_ref),
-                (w_qkv_far, w_qkv_ref),
                 (w_mid_far, w_mid_ref),
                 (valid_far, valid_ref),
                 (w_out_far, w_out_ref),
@@ -137,7 +132,7 @@
             )
         )
     ]
-    for copy in small[:3] + large[:1] + small[3:] + large[1:]:
+    for copy in small[:2] + large[:1] + small[2:] + large[1:]:
         copy.start()
 
     raw_acc[...] = jnp.zeros_like(raw_acc)
@@ -145,26 +140,14 @@
     wc_acc[...] = jnp.zeros_like(wc_acc)
     spread_d = spread_matrix(width, depth)
     spread_m = spread_matrix(hm, slices)
+    for copy in small + large[:1]:
+        copy.wait()
     temp = jnp.broadcast_to(temp_ref[...].astype(f32), (16, depth)).astype(bf16)
-    small[0].wait()
-    w_slice = w_slice_ref[...]
-    half = nt(spread_m, w_slice).astype(bf16)
+    half = nt(spread_m, w_slice_ref[...]).astype(bf16)
     full = nt(half, spread_d)
     sw_ref[0:hm, :] = jnp.where(same_block(hm, width, slices, depth), full, 0.0).astype(bf16)
-    half = nn(spread_d, w_slice).astype(bf16)
-    full = nt(half, spread_m)
-    sb_ref[...] = jnp.where(same_block(width, hm, depth, slices), full, 0.0).astype(bf16)
     full = nt(temp, spread_d)
     sw_ref[hm : hm + 16, :] = jnp.where(same_block(16, width, 1, depth), full, 0.0).astype(bf16)
-    small[1].wait()
-    w_cat = jnp.zeros((depth, 128), f32)
-    for i in range(3):
-        place_at = jnp.where(rows_of((depth, 128)) + i * depth == cols_of((depth, 128)), 1.0, 0.0)
-        w_cat = w_cat + nn(w_qkv_ref[i], place_at.astype(bf16))
-    w_cat_ref[...] = w_cat.astype(bf16)
-    small[2].wait()
-    small[3].wait()
-    small[4].wait()
     owned = owned_ref[0]
 
     def products(i):
@@ -203,7 +186,6 @@
         raw_acc[...] += nn(wt, mid)
         wc_acc[...] += nn(wt, cot_ref[at, :])
 
-    large[0].wait()
     ready = products(0)
     large[1].wait()
     large[2].wait()
@@ -232,6 +214,47 @@
     rows = hm // 2
     for k, out in enumerate((wc_keep_ref, wc_send_ref)):
         out[...] = wc_acc[pl.ds(pl.multiple_of(((place & 1) ^ k) * rows, 8), rows), :]
+
+
+def between_kernel(
+    heads,
+    slices,
+    mid_ref,
+    sw_ref,
+    aux_ref,
+    w_slice_ref,
+    w_qkv_ref,
+    _,
+    logits_ref,
+    weights_ref,
+    sb_ref,
+    w_cat_ref,
+    token_ref,
+):
+    depth = w_slice_ref.shape[0]
+    width = heads * depth
+    hm = heads * slices
+    rows = mid_ref.shape[0]
+    piece = min(sub_block, rows)
+    token_ref[...] = jnp.zeros_like(token_ref)
+    spread_d = spread_matrix(width, depth)
+    spread_m = spread_matrix(hm, slices)
+    half = nn(spread_d, w_slice_ref[...]).astype(bf16)
+    full = nt(half, spread_m)
+    sb_ref[...] = jnp.where(same_block(width, hm, depth, slices), full, 0.0).astype(bf16)
+    w_cat = jnp.zeros((depth, 128), f32)
+    for i in range(3):
+        place_at = jnp.where(rows_of((depth, 128)) + i * depth == cols_of((depth, 128)), 1.0, 0.0)
+        w_cat = w_cat + nn(w_qkv_ref[i], place_at.astype(bf16))
+    w_cat_ref[...] = w_cat.astype(bf16)
+    for i in range(rows // piece):
+        at = slice(i * piece, (i + 1) * piece)
+        scores = nt(sw_ref[0:hm, :], mid_ref[at, :])
+        for h in range(heads):
+            span = slice(h * slices, (h + 1) * slices)
+            logits = scores[span] * aux_ref[h : h + 1, at]
+            logits_ref[span, at] = logits
+            weights_ref[span, at] = jnp.exp(logits - aux_ref[heads + h : heads + h + 1, at])
 
 
 def lanes_at(x, lane, *where):
@@ -354,10 +377,12 @@
     heads,
     slices,
     aux_ref,
+    wt_ref,
+    logits_ref,
+    weights_ref,
     mid_ref,
     cot_ref,
     feats_ref,
-    sw_ref,
     sb_ref,
     mw_ref,
     dr_ref,
@@ -370,7 +395,6 @@
     send1,
     send2,
     send3,
-    lhs,
     yt,
     grad_acc,
     small_acc,
@@ -380,47 +404,42 @@
     depth = width // heads
     hm = heads * slices
     block = feats_ref.shape[0]
-    top = hm + 16
 
     grad_acc[...] = jnp.zeros_like(grad_acc)
     small_acc[...] = jnp.zeros_like(small_acc)
-    lhs[0:top, :] = sw_ref[...]
-    lhs[top:, :] = dr_ref[...]
     yt[:, 0:hm] = drt_ref[...]
     yt[:, hm:] = sb_ref[...]
 
     temp = jnp.broadcast_to(temp_ref[...].astype(f32), (16, depth)).astype(bf16)
     same = (rows_of((depth, depth)) == cols_of((depth, depth))).astype(f32).astype(bf16)
     temp = nt(same, temp)[:, 0:1]
-    piece = min(2 * sub_block, block)
+    piece = min(sub_block, block)
     pieces = [slice(i * piece, (i + 1) * piece) for i in range(block // piece)]
 
     def products(at):
-        return nt(lhs[...], mid_ref[at, :]), nt(mw_ref[...], cot_ref[at, :])
-
-    def per_head(at, from_mid, from_cot):
-        weights_b, u_b, sums = [], [], []
+        return nt(dr_ref[...], mid_ref[at, :]) + nt(mw_ref[...], cot_ref[at, :])
+
+    def per_head(at, products):
+        u_b, sums = [], []
         aux = aux_ref[:, at]
         for h in range(heads):
             span = slice(h * slices, (h + 1) * slices)
             inv_tau = aux[h : h + 1]
-            logits = from_mid[span] * inv_tau
-            weights = jnp.exp(logits - aux[heads + h : heads + h + 1])
-            d_weights = from_cot[span] + from_mid[top + h * slices : top + (h + 1) * slices]
-            d_weights = d_weights + dn_ref[span, 0:1]
+            logits = logits_ref[span, at]
+            weights = weights_ref[span, at]
+            d_weights = products[span] + dn_ref[span, 0:1]
             mean = jnp.sum(weights * d_weights, axis=0, keepdims=True)
             d_logits = weights * (d_weights - mean)
             d_tau = jnp.sum(d_logits * logits, axis=0, keepdims=True)
             sums.append(-d_tau * aux[2 * heads + h : 2 * heads + h + 1])
-            weights_b.append(weights.astype(bf16))
             u_b.append((d_logits * inv_tau).astype(bf16))
         c_sum = jnp.concatenate(sums, axis=0)
         c_high = c_sum.astype(bf16).astype(f32)
         u_b.append(jnp.concatenate([c_high, c_sum - c_high], axis=0).astype(bf16))
-        return jnp.concatenate(weights_b, axis=0), jnp.concatenate(u_b, axis=0), sums
-
-    def outputs(at, weights_b, u_b, sums):
-        d_mid = nn(yt[...], jnp.concatenate([weights_b, u_b[0:hm]], axis=0))
+        return jnp.concatenate(u_b, axis=0), sums
+
+    def outputs(at, u_b, sums):
+        d_mid = nn(yt[...], jnp.concatenate([wt_ref[:, at], u_b[0:hm]], axis=0))
         d_mid = [
             (d_mid[h * depth : (h + 1) * depth] + temp * sums[h]).astype(bf16)
             for h in range(heads)
@@ -435,7 +454,7 @@
         current = ready
         if i + 1 < len(pieces):
             ready = products(pieces[i + 1])
-        outputs(at, *per_head(at, *current))
+        outputs(at, *per_head(at, current))
 
     grad = grad_acc[...].T
     u_part = jnp.where(same_block(hm, width, slices, depth), small_acc[0:hm, :], 0.0)
@@ -479,7 +498,7 @@
     ).astype(bf16)
 
 
-def grad_out_kernel(own_ref, other_ref, mixed_t_ref, _, grad_out_ref, token_ref, whole):
+def grad_out_kernel(own_ref, other_ref, mixed_t_ref, grad_out_ref, token_ref, whole):
     token_ref[...] = jnp.zeros_like(token_ref)
     place = group_place() & 1
     rows = own_ref.shape[0]
@@ -490,7 +509,7 @@
     grad_out_ref[...] = nn(mixed_t, high) + nn(mixed_t, low)
 
 
-def finish_kernel(depth, m0, m1, m2, m3, _, grad_mid_ref, slice_ref, temp_ref, extra):
+def finish_kernel(depth, m0, m1, m2, m3, grad_mid_ref, slice_ref, temp_ref, extra):
     place = group_place()
     slices = slice_ref.shape[1]
     more = slices // group
@@ -549,12 +568,12 @@
 
 
 def sum_stage(total, stride, others, count, *before):
-    got = [total] + [exchange(total, stride * j, count) for j in range(others, 0, -1)]
+    parts = [total] + [exchange(total, stride * j, count) for j in range(others, 0, -1)]
     if before:
-        return sum_behind(got, *before)
+        return sum_behind(parts, *before)
     if others == 1:
-        return got[0] + got[1]
-    return (got[0] + got[3]) + (got[1] + got[2])
+        return parts[0] + parts[1]
+    return (parts[0] + parts[3]) + (parts[1] + parts[2])
 
 
 def sum_over_groups(total, stride, count, *before):
@@ -592,14 +611,12 @@
     temp = temp_vec.reshape(1, depth)
     half = (2 * slices + 8, 128)
     wide = (hm // 2, width)
-    inputs = (valid.reshape(1, rows), feats, cotangent, w_mid, w_slice, w_out, w_qkv)
+    inputs = (valid.reshape(1, rows), feats, cotangent, w_mid, w_slice, w_out)
     (
         mid,
         wt,
         aux,
         sw,
-        sb,
-        w_cat,
         keep,
         send,
         wc_keep,
@@ -609,14 +626,12 @@
     ) = pl.pallas_call(
         functools.partial(stats_kernel, heads, slices),
         in_specs=[smem, whole] + [pl.BlockSpec(memory_space=pltpu.HBM)] * len(inputs),
-        out_specs=[whole] * 12,
+        out_specs=[whole] * 10,
         out_shape=[
             near((rows, width), bf16),
             near((hm, rows), bf16),
             near((3 * heads, rows), f32),
             near((hm + 16, width), bf16),
-            near((width, hm), bf16),
-            near((depth, 128), bf16),
             near(half, f32),
             near(half, f32),
             near(wide, f32),
@@ -629,12 +644,11 @@
             pltpu.VMEM((width, width), bf16),
             pltpu.VMEM((depth, slices), bf16),
             pltpu.VMEM((width, width), bf16),
-            pltpu.VMEM((3, depth, depth), bf16),
             pltpu.VMEM((hm, width), f32),
             pltpu.VMEM((hm, 128), f32),
             pltpu.VMEM((hm, width), f32),
             pltpu.VMEM((2,) + half, f32),
-            pltpu.SemaphoreType.DMA((8,)),
+            pltpu.SemaphoreType.DMA((7,)),
         ],
         compiler_params=params(24, False),
         cost_estimate=cost(4 * unit, rows * width * 8, rows * hm),
@@ -643,10 +657,24 @@
     own = keep + exchange(send, 1, count)
     wc_got = exchange(wc_send, 1, count)
     wc_sum = sum_behind([wc_keep, wc_got], own)
+    logits, weights, sb, w_cat, token = pl.pallas_call(
+        functools.partial(between_kernel, heads, slices),
+        in_specs=[whole] * 5 + [pl.BlockSpec(memory_space=pl.ANY)],
+        out_specs=[whole] * 5,
+        out_shape=[
+            near((hm, rows), f32),
+            near((hm, rows), f32),
+            near((width, hm), bf16),
+            near((depth, 128), bf16),
+            near((8, 128), f32),
+        ],
+        compiler_params=params(16, False),
+        cost_estimate=cost(unit // 10, rows, rows),
+    )(mid, sw, aux, w_slice, w_qkv, wc_sum)
     own = sum_stage(own, 2, 3, count)
     wc_got = exchange(wc_sum, 2, count)
     wc_sum = sum_behind([wc_sum, wc_got], own)
-    own = sum_over_groups(own, 8, count)
+    own = sum_over_groups(own, 8, count, token)
     other = exchange(own, 1, count)
     stride = 4
     while stride < count // 2:
@@ -667,28 +695,29 @@
         ],
         scratch_shapes=[pltpu.VMEM((2,) + half, f32)],
         compiler_params=params(16, False),
-        cost_estimate=cost(3 * width**3, 4 * width * width * 4, hm * hm),
+        cost_estimate=cost(100 * width**3, 4 * width * width * 4, hm * hm),
     )(own, other, w_cat, w_out)
+    wc_sum = sum_behind([wc_sum, wc_got], mw)
+    wc_got = exchange(wc_sum, count // 2, count)
     larger = (width // group + slices // group, width)
     dmt, *sends = pl.pallas_call(
         functools.partial(backward_kernel, heads, slices),
-        in_specs=[whole] * 11 + [pl.BlockSpec(memory_space=pl.ANY)],
+        in_specs=[whole] * 13 + [pl.BlockSpec(memory_space=pl.ANY)],
         out_specs=[whole] * (1 + group),
         out_shape=[near((width, rows), bf16)] + [near(larger, f32)] * group,
         scratch_shapes=[
-            pltpu.VMEM((2 * hm + 16, width), bf16),
             pltpu.VMEM((width, 2 * hm), bf16),
             pltpu.VMEM((width, width), f32),
             pltpu.VMEM((hm + 16, width), f32),
             pltpu.VMEM((group,) + larger, f32),
         ],
         compiler_params=params(24, False),
-        cost_estimate=cost(width**3, rows * width, rows),
-    )(aux, mid, cot_near, feats_near, sw, sb, mw, dr, drt, dn, temp, wc_sum)
+        cost_estimate=cost(unit, rows * width, rows),
+    )(aux, wt, logits, weights, mid, cot_near, feats_near, sb, mw, dr, drt, dn, temp, wc_sum)
 
     mid_total = scatter_group(sends, count)
     wc_sum = sum_behind([wc_sum, wc_got], sends[1])
-    wc_got = exchange(wc_sum, count // 2, count)
+    wc_other = exchange(wc_sum, 1, count)
 
     block = min(1024, rows)
     grid, by_rows = blocks(block)
@@ -708,24 +737,18 @@
         cost_estimate=cost(2 * unit, rows * width * 8),
     )(wt, dmt, mw, w_mid, mid_total)
 
-    wc_sum = sum_behind([wc_sum, wc_got], token)
-    wc_other = exchange(wc_sum, 1, count)
-    mid_total = sum_over_groups(mid_total, group, count, token)
-    grad_w_out, token = pl.pallas_call(
+    grad_w_out, token_out = pl.pallas_call(
         grad_out_kernel,
         out_shape=[like((width, width), f32), like((8, 128), f32)],
-        in_specs=[whole] * 3 + [pl.BlockSpec(memory_space=pl.ANY)],
-        out_specs=[whole] * 2,
         scratch_shapes=[pltpu.VMEM((hm, width), f32)],
         compiler_params=params(8, False),
         cost_estimate=cost(4 * width**3, 3 * width * width * 4),
-    )(wc_sum, wc_other, mixed_t, mid_total)
+    )(wc_sum, wc_other, mixed_t)
+    mid_total = sum_over_groups(mid_total, group, count, token, token_out)
 
     mid_parts = gather_group(mid_total, count)
     grad_w_mid, grad_w_slice, grad_temp = pl.pallas_call(
         functools.partial(finish_kernel, depth),
-        in_specs=[whole] * group + [pl.BlockSpec(memory_space=pl.ANY)],
-        out_specs=[whole] * 3,
         out_shape=[
             like((width, width), f32),
             like((depth, slices), f32),
@@ -734,7 +757,7 @@
         scratch_shapes=[pltpu.VMEM((slices, 128), f32)],
         compiler_params=params(8, False),
         cost_estimate=cost(0, 2 * width * width * 4),
-    )(*mid_parts, token)
+    )(*mid_parts)
     return (
         attended,
         feats_grad,

time: 58.5 us -> 59.5 us (1.017)
  waiting for transfers between devices: 13.1 us -> 13.9 us
    pallas_call x1 -> x2, Pallas kernels: 0.73 us -> 1.72 us  [the longest x1 0.98 us: shards(): pl.pallas_call(functools.partial(between_kernel, heads, slices), in_specs...]
    ppermute x20, waiting for transfers between devices: 13.1 us -> 13.9 us  [exchange(): return lax.ppermute(x, 'node', [(i, i ^ k) for i in range(count)])]
    pallas_call x1, Pallas kernels: 5.58 us -> 4.93 us  [shards(): pl.pallas_call(functools.partial(backward_kernel, heads, slices), in_spec...]
where the time goes in v9:
time: 59.5 us; the launch traced here: 59.3 us
  starting transfers between devices  22.5 us (38%)
  Pallas kernels  21.5 us (36%)
  waiting for transfers between devices  13.9 us (23%)
  between operations  1.4 us (2%)
    ppermute x20, starting transfers between devices, exchange(): return lax.ppermute(x, 'node', [(i, i ^ k) for i in range(count)])  22.5 us
    ppermute x20, waiting for transfers between devices, exchange(): return lax.ppermute(x, 'node', [(i, i ^ k) for i in range(count)])  13.9 us
    pallas_call x1, Pallas kernels, shards(): pl.pallas_call(functools.partial(stats_kernel, heads, slices), in_specs=[...  7.23 us
    pallas_call x1, Pallas kernels, shards(): pl.pallas_call(functools.partial(backward_kernel, heads, slices), in_spec...  4.93 us
    pallas_call x1, Pallas kernels, shards(): pl.pallas_call(rows_kernel, grid=grid, in_specs=[whole, whole, whole, ful...  3.42 us
    pallas_call x1, Pallas kernels, shards(): pl.pallas_call(functools.partial(tokens_kernel, heads, slices), out_shape...  3.11 us
  transfers between devices with their start and end apart: 20, of which 10 were waited for; matrix products, arithmetic and copies ran while one was open for 0% of the time, Pallas kernels for 23%

profile of v9, /device:TPU:0, one launch (start us, length us, event | category | flops | bytes accessed | tf_op | source)
XLA Modules:
  0.0 59.3 jit_solution(11517462481695921757)
XLA Ops:
  1.3 7.2 %shard_map.144 = (bf16[4096,256]{1,0:T(8,128)(2,1)S(1)}, bf16[256,4096]{1,0:T(8,128)(2,1)S(1)}, f32[24,4096]{1,0:T(8,128)S(1)}, bf16[272,256]{1,0:T(8,128)(2,1)S...) custom-call(s32[1]{0:T(128)S(6)} %copy.16.owned_ref, ...), custom_call_target="tpu_custom_call" | custom-call | flops 2147483648 | bytes 8388608 | tf_op jit(solution)/shard_map/pallas_call | solution.py:626
  9.2 1.1 %collective-permute-done.1 = f32[72,128]{1,0:T(8,128)S(1)} collective-permute-done((f32[72,128]{1,0:T(8,128)S(1)}, f32[72,128]{1,0:T(8,128)S(1)}, u32[]{:S(2)}, u32[]{:S(2)}) %collective-permute-start.1) | collective-permute-done | bytes 36896 | tf_op jit(solution)/shard_map/ppermute | solution.py:543
  10.3 2.8 %collective-permute-start.4 = (f32[72,128]{1,0:T(8,128)S(1)}, f32[72,128]{1,0:T(8,128)S(1)}, u32[]{:S(2)}, u32[]{:S(2)}) collective-permute-start(f32[72,128]{1,0:T(8,128)S(1)} %add.21.refs_2_), channel_id=1, source_target_pairs={{0,4},{1,5},{2,6},{3,7},{4,0},{5,1},{6,2},{7,3},{8,12},{9,13},{10,... | collective-permute-start | bytes 110600 | tf_op jit(solution)/shard_map/ppermute | solution.py:543
  13.1 1.4 %collective-permute-start.3 = (f32[72,128]{1,0:T(8,128)S(1)}, f32[72,128]{1,0:T(8,128)S(1)}, u32[]{:S(2)}, u32[]{:S(2)}) collective-permute-start(f32[72,128]{1,0:T(8,128)S(1)} %add.21.refs_2_), channel_id=1, source_target_pairs={{0,6},{1,7},{2,4},{3,5},{4,2},{5,3},{6,0},{7,1},{8,14},{9,15},{10,... | collective-permute-start | bytes 110600 | tf_op jit(solution)/shard_map/ppermute | solution.py:543
  14.6 1.9 %collective-permute-start.7 = (f32[128,256]{1,0:T(8,128)S(1)}, f32[128,256]{1,0:T(8,128)S(1)}, u32[]{:S(2)}, u32[]{:S(2)}) collective-permute-start(f32[128,256]{1,0:T(8,128)S(1)} %shard_map.145._.refs_0_), channel_id=1, source_target_pairs={{0,2},{1,3},{2,0},{3,1},{4,6},{5,7},{6,4},{7,5},{8,10},{9,11},{10,... | collective-permute-start | bytes 393224 | tf_op jit(solution)/shard_map/ppermute | solution.py:543
  16.5 1.5 %collective-permute-done.3 = f32[72,128]{1,0:T(8,128)S(1)} collective-permute-done((f32[72,128]{1,0:T(8,128)S(1)}, f32[72,128]{1,0:T(8,128)S(1)}, u32[]{:S(2)}, u32[]{:S(2)}) %collective-permute-start.3) | collective-permute-done | bytes 36896 | tf_op jit(solution)/shard_map/ppermute | solution.py:543
  18.8 2.6 %collective-permute-start.5 = (f32[72,128]{1,0:T(8,128)S(1)}, f32[72,128]{1,0:T(8,128)S(1)}, u32[]{:S(2)}, u32[]{:S(2)}) collective-permute-start(f32[72,128]{1,0:T(8,128)S(1)} %add_add_fusion.1.refs_0_.refs_2_), channel_id=1, source_target_pairs={{0,8},{1,9},{2,10},{3,11},{4,12},{5,13},{6,14},{7,15},{8,0},{9,1},... | collective-permute-start | bytes 110600 | tf_op jit(solution)/shard_map/ppermute | solution.py:543
  21.5 1.0 %shard_map.146 = (f32[256,4096]{1,0:T(8,128)S(1)}, f32[256,4096]{1,0:T(8,128)S(1)}, bf16[256,256]{1,0:T(8,128)(2,1)S(1)}, bf16[32,128]{1,0:T(8,128)(2,1)S(1)}, f32[8,128]{1,0:T(8,128)S(1)}) custom-call(bf16[4096,256]{1,0:T(8,128)(2,1)S(1)} %get-tuple-element.43.mid_ref, bf16[272,256]{1,0:T(8,128)(2,1)S(1)} %get-tuple-element.44.sw_ref, ...), custom_call_target="tpu_custom_call" | custom-call | flops 53687092 | bytes 4096 | tf_op jit(solution)/shard_map/pallas_call | solution.py:660
  22.5 1.3 %collective-permute-done.5.refs_1_ = f32[72,128]{1,0:T(8,128)S(1)} collective-permute-done((f32[72,128]{1,0:T(8,128)S(1)}, f32[72,128]{1,0:T(8,128)S(1)}, u32[]{:S(2)}, u32[]{:S(2)}) %collective-permute-start.5) | collective-permute-done | bytes 36896 | tf_op jit(solution)/shard_map/ppermute | solution.py:543
  23.8 1.6 %collective-permute-start.8 = (f32[128,256]{1,0:T(8,128)S(1)}, f32[128,256]{1,0:T(8,128)S(1)}, u32[]{:S(2)}, u32[]{:S(2)}) collective-permute-start(f32[128,256]{1,0:T(8,128)S(1)} %shard_map.149.refs_0_), channel_id=1, source_target_pairs={{0,4},{1,5},{2,6},{3,7},{4,0},{5,1},{6,2},{7,3},{8,12},{9,13},{10,... | collective-permute-start | bytes 393224 | tf_op jit(solution)/shard_map/ppermute | solution.py:543
  25.4 3.1 %shard_map.148 = (bf16[256,256]{1,0:T(8,128)(2,1)S(1)}, bf16[256,256]{1,0:T(8,128)(2,1)S(1)}, bf16[256,256]{1,0:T(8,128)(2,1)S(1)}, bf16[256,256]{1,0:T(8,128)(2...) custom-call(f32[72,128]{1,0:T(8,128)S(1)} %shard_map.147.own_ref, f32[72,128]{1,0:T(8,128)S(1)} %collective-permute-done.6.got_ref, ...), custom_call_target="tpu_custom_call" | custom-call | flops 1677721600 | bytes 1048576 | tf_op jit(solution)/shard_map/pallas_call | solution.py:686
  28.6 1.2 %collective-permute-done.8.refs_1_ = f32[128,256]{1,0:T(8,128)S(1)} collective-permute-done((f32[128,256]{1,0:T(8,128)S(1)}, f32[128,256]{1,0:T(8,128)S(1)}, u32[]{:S(2)}, u32[]{:S(2)}) %collective-permute-start.8) | collective-permute-done | bytes 131104 | tf_op jit(solution)/shard_map/ppermute | solution.py:543
  29.8 2.8 %collective-permute-start.15 = (f32[128,256]{1,0:T(8,128)S(1)}, f32[128,256]{1,0:T(8,128)S(1)}, u32[]{:S(2)}, u32[]{:S(2)}) collective-permute-start(f32[128,256]{1,0:T(8,128)S(1)} %shard_map.150._.refs_0_), channel_id=1, source_target_pairs={{0,8},{1,9},{2,10},{3,11},{4,12},{5,13},{6,14},{7,15},{8,0},{9,1},... | collective-permute-start | bytes 393224 | tf_op jit(solution)/shard_map/ppermute | solution.py:543
  32.6 4.9 %shard_map.151 = (bf16[256,4096]{1,0:T(8,128)(2,1)S(1)}, f32[72,256]{1,0:T(8,128)S(1)}, f32[72,256]{1,0:T(8,128)S(1)}, f32[72,256]{1,0:T(8,128)S(1)}, f32[72,256]{1,0:T(8,128)S(1)}) custom-call(f32[24,4096]{1,0:T(8,128)S(1)} %get-tuple-element.42.aux_ref, bf16[256,4096]{1,0:T(8,128)(2,1)S(1)} %get-tuple-element.41.wt_ref, ...), custom_call_target="tpu_custom_call" | custom-call | flops 536870912 | bytes 1048576 | tf_op jit(solution)/shard_map/pallas_call | solution.py:703
  38.4 1.3 %collective-permute-start.9 = (f32[72,256]{1,0:T(8,128)S(1)}, f32[72,256]{1,0:T(8,128)S(1)}, u32[]{:S(2)}, u32[]{:S(2)}) collective-permute-start(f32[72,256]{1,0:T(8,128)S(1)} %get-tuple-element.62.refs_2_), channel_id=1, source_target_pairs={{0,1},{1,0},{2,3},{3,2},{4,5},{5,4},{6,7},{7,6},{8,9},{9,8},{10,11... | collective-permute-start | bytes 221192 | tf_op jit(solution)/shard_map/ppermute | solution.py:543
  39.8 2.7 %collective-permute-done.10 = f32[72,256]{1,0:T(8,128)S(1)} collective-permute-done((f32[72,256]{1,0:T(8,128)S(1)}, f32[72,256]{1,0:T(8,128)S(1)}, u32[]{:S(2)}, u32[]{:S(2)}) %collective-permute-start.10) | collective-permute-done | bytes 73760 | tf_op jit(solution)/shard_map/ppermute | solution.py:543
  42.9 1.1 %collective-permute-start.14 = (f32[72,256]{1,0:T(8,128)S(1)}, f32[72,256]{1,0:T(8,128)S(1)}, u32[]{:S(2)}, u32[]{:S(2)}) collective-permute-start(f32[72,256]{1,0:T(8,128)S(1)} %add_add_fusion._.refs_0_), channel_id=1, source_target_pairs={{0,4},{1,5},{2,6},{3,7},{4,0},{5,1},{6,2},{7,3},{8,12},{9,13},{10,... | collective-permute-start | bytes 221192 | tf_op jit(solution)/shard_map/ppermute | solution.py:543
  44.4 3.0 %collective-permute-start.12 = (f32[72,256]{1,0:T(8,128)S(1)}, f32[72,256]{1,0:T(8,128)S(1)}, u32[]{:S(2)}, u32[]{:S(2)}) collective-permute-start(f32[72,256]{1,0:T(8,128)S(1)} %add_add_fusion._.refs_0_), channel_id=1, source_target_pairs={{0,12},{1,13},{2,14},{3,15},{4,8},{5,9},{6,10},{7,11},{8,4},{9,5},... | collective-permute-start | bytes 221192 | tf_op jit(solution)/shard_map/ppermute | solution.py:543
  47.4 3.4 %shard_map.152 = (bf16[4096,256]{1,0:T(8,128)(2,1)}, bf16[4096,256]{1,0:T(8,128)(2,1)}, f32[8,128]{1,0:T(8,128)S(1)}) custom-call(bf16[256,4096]{1,0:T(8,128)(2,1)S(1)} %get-tuple-element.41.wt_ref, bf16[256,4096]{1,0:T(8,128)(2,1)S(1)} %get-tuple-element.60.dmt_ref, bf16[256,256]{1,0:T(8,128)(2,1)S(1)} %get-tuple-element.56.refs_2_.mw_ref, ...), custom_call_target="tpu_custom_call" | custom-call | flops 1073741824 | bytes 8388608 | tf_op jit(solution)/shard_map/pallas_call | solution.py:724
  50.8 1.0 %shard_map.154 = (f32[256,256]{1,0:T(8,128)}, f32[8,128]{1,0:T(8,128)S(1)}) custom-call(f32[128,256]{1,0:T(8,128)S(1)} %shard_map.153.own_ref, f32[128,256]{1,0:T(8,128)S(1)} %collective-permute-done.16.other_ref, bf16[256,256]{1,0:T(8,128)(2,1)S(1)} %get-tuple-element.68.mixed_t_ref), custom_call_target="tpu_custom_call" | custom-call | flops 67108864 | bytes 786432 | tf_op jit(solution)/shard_map/pallas_call | solution.py:740
  51.8 1.2 %collective-permute-done.13.refs_2_ = f32[72,256]{1,0:T(8,128)S(1)} collective-permute-done((f32[72,256]{1,0:T(8,128)S(1)}, f32[72,256]{1,0:T(8,128)S(1)}, u32[]{:S(2)}, u32[]{:S(2)}) %collective-permute-start.13) | collective-permute-done | bytes 73760 | tf_op jit(solution)/shard_map/ppermute | solution.py:543
  53.0 1.1 %collective-permute-start.18 = (f32[72,256]{1,0:T(8,128)S(1)}, f32[72,256]{1,0:T(8,128)S(1)}, u32[]{:S(2)}, u32[]{:S(2)}) collective-permute-start(f32[72,256]{1,0:T(8,128)S(1)} %shard_map.155.m0), channel_id=1, source_target_pairs={{0,2},{1,3},{2,0},{3,1},{4,6},{5,7},{6,4},{7,5},{8,10},{9,11},{10,... | collective-permute-start | bytes 221192 | tf_op jit(solution)/shard_map/ppermute | solution.py:543
  54.9 2.7 %collective-permute-done.19.m3 = f32[72,256]{1,0:T(8,128)S(1)} collective-permute-done((f32[72,256]{1,0:T(8,128)S(1)}, f32[72,256]{1,0:T(8,128)S(1)}, u32[]{:S(2)}, u32[]{:S(2)}) %collective-permute-start.19) | collective-permute-done | bytes 73760 | tf_op jit(solution)/shard_map/ppermute | solution.py:543
  57.6 1.0 %collective-permute-done.18.m2 = f32[72,256]{1,0:T(8,128)S(1)} collective-permute-done((f32[72,256]{1,0:T(8,128)S(1)}, f32[72,256]{1,0:T(8,128)S(1)}, u32[]{:S(2)}, u32[]{:S(2)}) %collective-permute-start.18) | collective-permute-done | bytes 73760 | tf_op jit(solution)/shard_map/ppermute | solution.py:543
  (42 shorter events, 5.1 us)
Async XLA Ops:
  1.3 20.2 %copy-start.1 = (bf16[3,32,32]{2,1,0:T(8,128)(2,1)S(1)}, bf16[3,32,32]{2,1,0:T(8,128)(2,1)}, u32[]{:S(2)}) copy-start(bf16[3,32,32]{2,1,0:T(8,128)(2,1)} %w_qkv_ref.1) | copy-start | bytes 18436
  1.3 20.2 %copy-start.2 = (bf16[32,32]{1,0:T(8,128)(2,1)S(1)}, bf16[32,32]{1,0:T(8,128)(2,1)}, u32[]{:S(2)}) copy-start(bf16[32,32]{1,0:T(8,128)(2,1)} %w_slice_ref.1) | copy-start | bytes 6148
  8.5 16.9 %copy-start.4 = (bf16[256,256]{1,0:T(8,128)(2,1)S(1)}, bf16[256,256]{1,0:T(8,128)(2,1)}, u32[]{:S(2)}) copy-start(bf16[256,256]{1,0:T(8,128)(2,1)} %w_out_ref.1) | copy-start | bytes 393220
  8.6 6.0 %collective-permute-start = (f32[128,256]{1,0:T(8,128)S(1)}, f32[128,256]{1,0:T(8,128)S(1)}, u32[]{:S(2)}, u32[]{:S(2)}) collective-permute-start(f32[128,256]{1,0:T(8,128)S(1)} %get-tuple-element.46), channel_id=1, source_target_pairs={{0,1},{1,0},{2,3},{3,2},{4,5},{5,4},{6,7},{7,6},{8,9},{9,8},{10,11... | collective-permute-start | bytes 393224 | tf_op jit(solution)/shard_map/ppermute | solution.py:543
  9.1 1.2 %collective-permute-start.1 = (f32[72,128]{1,0:T(8,128)S(1)}, f32[72,128]{1,0:T(8,128)S(1)}, u32[]{:S(2)}, u32[]{:S(2)}) collective-permute-start(f32[72,128]{1,0:T(8,128)S(1)} %get-tuple-element.48), channel_id=1, source_target_pairs={{0,1},{1,0},{2,3},{3,2},{4,5},{5,4},{6,7},{7,6},{8,9},{9,8},{10,11... | collective-permute-start | bytes 110600 | tf_op jit(solution)/shard_map/ppermute | solution.py:543
  10.3 6.3 %collective-permute-start.4 = (f32[72,128]{1,0:T(8,128)S(1)}, f32[72,128]{1,0:T(8,128)S(1)}, u32[]{:S(2)}, u32[]{:S(2)}) collective-permute-start(f32[72,128]{1,0:T(8,128)S(1)} %add.21.refs_2_), channel_id=1, source_target_pairs={{0,4},{1,5},{2,6},{3,7},{4,0},{5,1},{6,2},{7,3},{8,12},{9,13},{10,... | collective-permute-start | bytes 110600 | tf_op jit(solution)/shard_map/ppermute | solution.py:543
  13.1 5.0 %collective-permute-start.3 = (f32[72,128]{1,0:T(8,128)S(1)}, f32[72,128]{1,0:T(8,128)S(1)}, u32[]{:S(2)}, u32[]{:S(2)}) collective-permute-start(f32[72,128]{1,0:T(8,128)S(1)} %add.21.refs_2_), channel_id=1, source_target_pairs={{0,6},{1,7},{2,4},{3,5},{4,2},{5,3},{6,0},{7,1},{8,14},{9,15},{10,... | collective-permute-start | bytes 110600 | tf_op jit(solution)/shard_map/ppermute | solution.py:543
  14.4 4.4 %collective-permute-start.2 = (f32[72,128]{1,0:T(8,128)S(1)}, f32[72,128]{1,0:T(8,128)S(1)}, u32[]{:S(2)}, u32[]{:S(2)}) collective-permute-start(f32[72,128]{1,0:T(8,128)S(1)} %add.21.refs_2_), channel_id=1, source_target_pairs={{0,2},{1,3},{2,0},{3,1},{4,6},{5,7},{6,4},{7,5},{8,10},{9,11},{10,... | collective-permute-start | bytes 110600 | tf_op jit(solution)/shard_map/ppermute | solution.py:543
  14.6 9.2 %collective-permute-start.7 = (f32[128,256]{1,0:T(8,128)S(1)}, f32[128,256]{1,0:T(8,128)S(1)}, u32[]{:S(2)}, u32[]{:S(2)}) collective-permute-start(f32[128,256]{1,0:T(8,128)S(1)} %shard_map.145._.refs_0_), channel_id=1, source_target_pairs={{0,2},{1,3},{2,0},{3,1},{4,6},{5,7},{6,4},{7,5},{8,10},{9,11},{10,... | collective-permute-start | bytes 393224 | tf_op jit(solution)/shard_map/ppermute | solution.py:543
  18.8 4.9 %collective-permute-start.5 = (f32[72,128]{1,0:T(8,128)S(1)}, f32[72,128]{1,0:T(8,128)S(1)}, u32[]{:S(2)}, u32[]{:S(2)}) collective-permute-start(f32[72,128]{1,0:T(8,128)S(1)} %add_add_fusion.1.refs_0_.refs_2_), channel_id=1, source_target_pairs={{0,8},{1,9},{2,10},{3,11},{4,12},{5,13},{6,14},{7,15},{8,0},{9,1},... | collective-permute-start | bytes 110600 | tf_op jit(solution)/shard_map/ppermute | solution.py:543
  23.8 1.7 %collective-permute-start.6 = (f32[72,128]{1,0:T(8,128)S(1)}, f32[72,128]{1,0:T(8,128)S(1)}, u32[]{:S(2)}, u32[]{:S(2)}) collective-permute-start(f32[72,128]{1,0:T(8,128)S(1)} %shard_map.147.own_ref), channel_id=1, source_target_pairs={{0,1},{1,0},{2,3},{3,2},{4,5},{5,4},{6,7},{7,6},{8,9},{9,8},{10,11... | collective-permute-start | bytes 110600 | tf_op jit(solution)/shard_map/ppermute | solution.py:543
  23.8 6.0 %collective-permute-start.8 = (f32[128,256]{1,0:T(8,128)S(1)}, f32[128,256]{1,0:T(8,128)S(1)}, u32[]{:S(2)}, u32[]{:S(2)}) collective-permute-start(f32[128,256]{1,0:T(8,128)S(1)} %shard_map.149.refs_0_), channel_id=1, source_target_pairs={{0,4},{1,5},{2,6},{3,7},{4,0},{5,1},{6,2},{7,3},{8,12},{9,13},{10,... | collective-permute-start | bytes 393224 | tf_op jit(solution)/shard_map/ppermute | solution.py:543
  29.8 9.9 %collective-permute-start.15 = (f32[128,256]{1,0:T(8,128)S(1)}, f32[128,256]{1,0:T(8,128)S(1)}, u32[]{:S(2)}, u32[]{:S(2)}) collective-permute-start(f32[128,256]{1,0:T(8,128)S(1)} %shard_map.150._.refs_0_), channel_id=1, source_target_pairs={{0,8},{1,9},{2,10},{3,11},{4,12},{5,13},{6,14},{7,15},{8,0},{9,1},... | collective-permute-start | bytes 393224 | tf_op jit(solution)/shard_map/ppermute | solution.py:543
  32.6 14.8 %copy-start = (bf16[256,256]{1,0:T(8,128)(2,1)S(1)}, bf16[256,256]{1,0:T(8,128)(2,1)}, u32[]{:S(2)}) copy-start(bf16[256,256]{1,0:T(8,128)(2,1)} %w_mid_ref.1) | copy-start | bytes 393220
  37.5 5.0 %collective-permute-start.10 = (f32[72,256]{1,0:T(8,128)S(1)}, f32[72,256]{1,0:T(8,128)S(1)}, u32[]{:S(2)}, u32[]{:S(2)}) collective-permute-start(f32[72,256]{1,0:T(8,128)S(1)} %get-tuple-element.63), channel_id=1, source_target_pairs={{0,2},{1,3},{2,0},{3,1},{4,6},{5,7},{6,4},{7,5},{8,10},{9,11},{10,... | collective-permute-start | bytes 221192 | tf_op jit(solution)/shard_map/ppermute | solution.py:543
  38.3 4.6 %collective-permute-start.11 = (f32[72,256]{1,0:T(8,128)S(1)}, f32[72,256]{1,0:T(8,128)S(1)}, u32[]{:S(2)}, u32[]{:S(2)}) collective-permute-start(f32[72,256]{1,0:T(8,128)S(1)} %get-tuple-element.64), channel_id=1, source_target_pairs={{0,3},{1,2},{2,1},{3,0},{4,7},{5,6},{6,5},{7,4},{8,11},{9,10},{10,... | collective-permute-start | bytes 221192 | tf_op jit(solution)/shard_map/ppermute | solution.py:543
  38.4 4.5 %collective-permute-start.9 = (f32[72,256]{1,0:T(8,128)S(1)}, f32[72,256]{1,0:T(8,128)S(1)}, u32[]{:S(2)}, u32[]{:S(2)}) collective-permute-start(f32[72,256]{1,0:T(8,128)S(1)} %get-tuple-element.62.refs_2_), channel_id=1, source_target_pairs={{0,1},{1,0},{2,3},{3,2},{4,5},{5,4},{6,7},{7,6},{8,9},{9,8},{10,11... | collective-permute-start | bytes 221192 | tf_op jit(solution)/shard_map/ppermute | solution.py:543
  39.7 11.1 %collective-permute-start.16 = (f32[128,256]{1,0:T(8,128)S(1)}, f32[128,256]{1,0:T(8,128)S(1)}, u32[]{:S(2)}, u32[]{:S(2)}) collective-permute-start(f32[128,256]{1,0:T(8,128)S(1)} %shard_map.153.own_ref), channel_id=1, source_target_pairs={{0,1},{1,0},{2,3},{3,2},{4,5},{5,4},{6,7},{7,6},{8,9},{9,8},{10,11... | collective-permute-start | bytes 393224 | tf_op jit(solution)/shard_map/ppermute | solution.py:543
  42.9 8.8 %collective-permute-start.14 = (f32[72,256]{1,0:T(8,128)S(1)}, f32[72,256]{1,0:T(8,128)S(1)}, u32[]{:S(2)}, u32[]{:S(2)}) collective-permute-start(f32[72,256]{1,0:T(8,128)S(1)} %add_add_fusion._.refs_0_), channel_id=1, source_target_pairs={{0,4},{1,5},{2,6},{3,7},{4,0},{5,1},{6,2},{7,3},{8,12},{9,13},{10,... | collective-permute-start | bytes 221192 | tf_op jit(solution)/shard_map/ppermute | solution.py:543
  44.1 8.9 %collective-permute-start.13 = (f32[72,256]{1,0:T(8,128)S(1)}, f32[72,256]{1,0:T(8,128)S(1)}, u32[]{:S(2)}, u32[]{:S(2)}) collective-permute-start(f32[72,256]{1,0:T(8,128)S(1)} %add_add_fusion._.refs_0_), channel_id=1, source_target_pairs={{0,8},{1,9},{2,10},{3,11},{4,12},{5,13},{6,14},{7,15},{8,0},{9,1},... | collective-permute-start | bytes 221192 | tf_op jit(solution)/shard_map/ppermute | solution.py:543
  44.4 8.5 %collective-permute-start.12 = (f32[72,256]{1,0:T(8,128)S(1)}, f32[72,256]{1,0:T(8,128)S(1)}, u32[]{:S(2)}, u32[]{:S(2)}) collective-permute-start(f32[72,256]{1,0:T(8,128)S(1)} %add_add_fusion._.refs_0_), channel_id=1, source_target_pairs={{0,12},{1,13},{2,14},{3,15},{4,8},{5,9},{6,10},{7,11},{8,4},{9,5},... | collective-permute-start | bytes 221192 | tf_op jit(solution)/shard_map/ppermute | solution.py:543
  53.0 4.6 %collective-permute-start.19 = (f32[72,256]{1,0:T(8,128)S(1)}, f32[72,256]{1,0:T(8,128)S(1)}, u32[]{:S(2)}, u32[]{:S(2)}) collective-permute-start(f32[72,256]{1,0:T(8,128)S(1)} %shard_map.155.m0), channel_id=1, source_target_pairs={{0,3},{1,2},{2,1},{3,0},{4,7},{5,6},{6,5},{7,4},{8,11},{9,10},{10,... | collective-permute-start | bytes 221192 | tf_op jit(solution)/shard_map/ppermute | solution.py:543
  53.0 5.5 %collective-permute-start.18 = (f32[72,256]{1,0:T(8,128)S(1)}, f32[72,256]{1,0:T(8,128)S(1)}, u32[]{:S(2)}, u32[]{:S(2)}) collective-permute-start(f32[72,256]{1,0:T(8,128)S(1)} %shard_map.155.m0), channel_id=1, source_target_pairs={{0,2},{1,3},{2,0},{3,1},{4,6},{5,7},{6,4},{7,5},{8,10},{9,11},{10,... | collective-permute-start | bytes 221192 | tf_op jit(solution)/shard_map/ppermute | solution.py:543
  54.2 4.4 %collective-permute-start.17 = (f32[72,256]{1,0:T(8,128)S(1)}, f32[72,256]{1,0:T(8,128)S(1)}, u32[]{:S(2)}, u32[]{:S(2)}) collective-permute-start(f32[72,256]{1,0:T(8,128)S(1)} %shard_map.155.m0), channel_id=1, source_target_pairs={{0,1},{1,0},{2,3},{3,2},{4,5},{5,4},{6,7},{7,6},{8,9},{9,8},{10,11... | collective-permute-start | bytes 221192 | tf_op jit(solution)/shard_map/ppermute | solution.py:543
  (1 other events, 7.1 us)

commit v10 on v9

--- a/solution.py
+++ b/solution.py
@@ -498,7 +498,7 @@
     ).astype(bf16)
 
 
-def grad_out_kernel(own_ref, other_ref, mixed_t_ref, grad_out_ref, token_ref, whole):
+def grad_out_kernel(own_ref, other_ref, mixed_t_ref, _, grad_out_ref, token_ref, whole):
     token_ref[...] = jnp.zeros_like(token_ref)
     place = group_place() & 1
     rows = own_ref.shape[0]
@@ -509,7 +509,7 @@
     grad_out_ref[...] = nn(mixed_t, high) + nn(mixed_t, low)
 
 
-def finish_kernel(depth, m0, m1, m2, m3, grad_mid_ref, slice_ref, temp_ref, extra):
+def finish_kernel(depth, m0, m1, m2, m3, _, grad_mid_ref, slice_ref, temp_ref, extra):
     place = group_place()
     slices = slice_ref.shape[1]
     more = slices // group
@@ -672,16 +672,16 @@
         cost_estimate=cost(unit // 10, rows, rows),
     )(mid, sw, aux, w_slice, w_qkv, wc_sum)
     own = sum_stage(own, 2, 3, count)
-    wc_got = exchange(wc_sum, 2, count)
+    wc_got = exchange(wc_sum, count // 2, count)
     wc_sum = sum_behind([wc_sum, wc_got], own)
     own = sum_over_groups(own, 8, count, token)
     other = exchange(own, 1, count)
-    stride = 4
+    wc_got = exchange(wc_sum, 2, count)
+    stride = 8
     while stride < count // 2:
+        wc_sum = wc_sum + wc_got
         wc_got = exchange(wc_sum, stride, count)
         stride *= 2
-        if stride < count // 2:
-            wc_sum = wc_sum + wc_got
 
     mw, mixed_t, dr, drt, dn, grad_qkv = pl.pallas_call(
         functools.partial(tokens_kernel, heads, slices),
@@ -695,10 +695,8 @@
         ],
         scratch_shapes=[pltpu.VMEM((2,) + half, f32)],
         compiler_params=params(16, False),
-        cost_estimate=cost(100 * width**3, 4 * width * width * 4, hm * hm),
+        cost_estimate=cost(30 * width**3, 4 * width * width * 4, hm * hm),
     )(own, other, w_cat, w_out)
-    wc_sum = sum_behind([wc_sum, wc_got], mw)
-    wc_got = exchange(wc_sum, count // 2, count)
     larger = (width // group + slices // group, width)
     dmt, *sends = pl.pallas_call(
         functools.partial(backward_kernel, heads, slices),
@@ -717,7 +715,7 @@
 
     mid_total = scatter_group(sends, count)
     wc_sum = sum_behind([wc_sum, wc_got], sends[1])
-    wc_other = exchange(wc_sum, 1, count)
+    wc_got = exchange(wc_sum, 4, count)
 
     block = min(1024, rows)
     grid, by_rows = blocks(block)
@@ -737,18 +735,24 @@
         cost_estimate=cost(2 * unit, rows * width * 8),
     )(wt, dmt, mw, w_mid, mid_total)
 
+    wc_sum = sum_behind([wc_sum, wc_got], token)
+    wc_other = exchange(wc_sum, 1, count)
+    mid_total = sum_over_groups(mid_total, group, count, token)
     grad_w_out, token_out = pl.pallas_call(
         grad_out_kernel,
+        in_specs=[whole] * 3 + [pl.BlockSpec(memory_space=pl.ANY)],
+        out_specs=[whole] * 2,
         out_shape=[like((width, width), f32), like((8, 128), f32)],
         scratch_shapes=[pltpu.VMEM((hm, width), f32)],
         compiler_params=params(8, False),
         cost_estimate=cost(4 * width**3, 3 * width * width * 4),
-    )(wc_sum, wc_other, mixed_t)
-    mid_total = sum_over_groups(mid_total, group, count, token, token_out)
+    )(wc_sum, wc_other, mixed_t, mid_total)
 
     mid_parts = gather_group(mid_total, count)
     grad_w_mid, grad_w_slice, grad_temp = pl.pallas_call(
         functools.partial(finish_kernel, depth),
+        in_specs=[whole] * group + [pl.BlockSpec(memory_space=pl.ANY)],
+        out_specs=[whole] * 3,
         out_shape=[
             like((width, width), f32),
             like((depth, slices), f32),
@@ -757,7 +761,7 @@
         scratch_shapes=[pltpu.VMEM((slices, 128), f32)],
         compiler_params=params(8, False),
         cost_estimate=cost(0, 2 * width * width * 4),
-    )(*mid_parts)
+    )(*mid_parts, token_out)
     return (
         attended,
         feats_grad,

time: 59.5 us -> 57.5 us (0.966)
  starting transfers between devices: 22.5 us -> 20.7 us
    ppermute x20, starting transfers between devices: 22.5 us -> 20.7 us  [exchange(): return lax.ppermute(x, 'node', [(i, i ^ k) for i in range(count)])]
  transfers between devices with their start and end apart: 20 -> 20, of which waited for: 10 -> 10; matrix products, arithmetic and copies ran while one was open for 0% -> 0% of each run, Pallas kernels for 23% -> 24%
where the time goes in v10:
time: 57.5 us; the launch traced here: 57.3 us
  Pallas kernels  21.4 us (37%)
  starting transfers between devices  20.7 us (36%)
  waiting for transfers between devices  13.7 us (24%)
  between operations  1.41 us (2%)
    ppermute x20, starting transfers between devices, exchange(): return lax.ppermute(x, 'node', [(i, i ^ k) for i in range(count)])  20.7 us
    ppermute x20, waiting for transfers between devices, exchange(): return lax.ppermute(x, 'node', [(i, i ^ k) for i in range(count)])  13.7 us
    pallas_call x1, Pallas kernels, shards(): pl.pallas_call(functools.partial(stats_kernel, heads, slices), in_specs=[...  7.23 us
    pallas_call x1, Pallas kernels, shards(): pl.pallas_call(functools.partial(backward_kernel, heads, slices), in_spec...  4.91 us
    pallas_call x1, Pallas kernels, shards(): pl.pallas_call(rows_kernel, grid=grid, in_specs=[whole, whole, whole, ful...  3.41 us
    pallas_call x1, Pallas kernels, shards(): pl.pallas_call(functools.partial(tokens_kernel, heads, slices), out_shape...  3.1 us
  transfers between devices with their start and end apart: 20, of which 10 were waited for; matrix products, arithmetic and copies ran while one was open for 0% of the time, Pallas kernels for 24%

profile of v10, /device:TPU:0, one launch (start us, length us, event | category | flops | bytes accessed | tf_op | source)
XLA Modules:
  0.0 57.3 jit_solution(6239158472093981453)
XLA Ops:
  1.3 7.2 %shard_map.144 = (bf16[4096,256]{1,0:T(8,128)(2,1)S(1)}, bf16[256,4096]{1,0:T(8,128)(2,1)S(1)}, f32[24,4096]{1,0:T(8,128)S(1)}, bf16[272,256]{1,0:T(8,128)(2,1)S...) custom-call(s32[1]{0:T(128)S(6)} %copy.16.owned_ref, ...), custom_call_target="tpu_custom_call" | custom-call | flops 2147483648 | bytes 8388608 | tf_op jit(solution)/shard_map/pallas_call | solution.py:626
  9.2 1.1 %collective-permute-done.1 = f32[72,128]{1,0:T(8,128)S(1)} collective-permute-done((f32[72,128]{1,0:T(8,128)S(1)}, f32[72,128]{1,0:T(8,128)S(1)}, u32[]{:S(2)}, u32[]{:S(2)}) %collective-permute-start.1) | collective-permute-done | bytes 36896 | tf_op jit(solution)/shard_map/ppermute | solution.py:543
  10.3 2.7 %collective-permute-start.2 = (f32[72,128]{1,0:T(8,128)S(1)}, f32[72,128]{1,0:T(8,128)S(1)}, u32[]{:S(2)}, u32[]{:S(2)}) collective-permute-start(f32[72,128]{1,0:T(8,128)S(1)} %add.21.refs_2_), channel_id=1, source_target_pairs={{0,2},{1,3},{2,0},{3,1},{4,6},{5,7},{6,4},{7,5},{8,10},{9,11},{10,... | collective-permute-start | bytes 110600 | tf_op jit(solution)/shard_map/ppermute | solution.py:543
  13.0 1.6 %collective-permute-start.3 = (f32[72,128]{1,0:T(8,128)S(1)}, f32[72,128]{1,0:T(8,128)S(1)}, u32[]{:S(2)}, u32[]{:S(2)}) collective-permute-start(f32[72,128]{1,0:T(8,128)S(1)} %add.21.refs_2_), channel_id=1, source_target_pairs={{0,6},{1,7},{2,4},{3,5},{4,2},{5,3},{6,0},{7,1},{8,14},{9,15},{10,... | collective-permute-start | bytes 110600 | tf_op jit(solution)/shard_map/ppermute | solution.py:543
  14.6 3.1 %collective-permute-start.7 = (f32[128,256]{1,0:T(8,128)S(1)}, f32[128,256]{1,0:T(8,128)S(1)}, u32[]{:S(2)}, u32[]{:S(2)}) collective-permute-start(f32[128,256]{1,0:T(8,128)S(1)} %shard_map.145._.refs_0_), channel_id=1, source_target_pairs={{0,8},{1,9},{2,10},{3,11},{4,12},{5,13},{6,14},{7,15},{8,0},{9,1},... | collective-permute-start | bytes 393224 | tf_op jit(solution)/shard_map/ppermute | solution.py:543
  17.9 1.9 %collective-permute-done.4 = f32[72,128]{1,0:T(8,128)S(1)} collective-permute-done((f32[72,128]{1,0:T(8,128)S(1)}, f32[72,128]{1,0:T(8,128)S(1)}, u32[]{:S(2)}, u32[]{:S(2)}) %collective-permute-start.4) | collective-permute-done | bytes 36896 | tf_op jit(solution)/shard_map/ppermute | solution.py:543
  19.8 1.7 %collective-permute-start.5 = (f32[72,128]{1,0:T(8,128)S(1)}, f32[72,128]{1,0:T(8,128)S(1)}, u32[]{:S(2)}, u32[]{:S(2)}) collective-permute-start(f32[72,128]{1,0:T(8,128)S(1)} %add_add_fusion.1.refs_0_.refs_2_), channel_id=1, source_target_pairs={{0,8},{1,9},{2,10},{3,11},{4,12},{5,13},{6,14},{7,15},{8,0},{9,1},... | collective-permute-start | bytes 110600 | tf_op jit(solution)/shard_map/ppermute | solution.py:543
  21.6 1.0 %shard_map.146 = (f32[256,4096]{1,0:T(8,128)S(1)}, f32[256,4096]{1,0:T(8,128)S(1)}, bf16[256,256]{1,0:T(8,128)(2,1)S(1)}, bf16[32,128]{1,0:T(8,128)(2,1)S(1)}, f32[8,128]{1,0:T(8,128)S(1)}) custom-call(bf16[4096,256]{1,0:T(8,128)(2,1)S(1)} %get-tuple-element.43.mid_ref, bf16[272,256]{1,0:T(8,128)(2,1)S(1)} %get-tuple-element.44.sw_ref, ...), custom_call_target="tpu_custom_call" | custom-call | flops 53687092 | bytes 4096 | tf_op jit(solution)/shard_map/pallas_call | solution.py:660
  22.6 2.6 %collective-permute-done.5.refs_1_ = f32[72,128]{1,0:T(8,128)S(1)} collective-permute-done((f32[72,128]{1,0:T(8,128)S(1)}, f32[72,128]{1,0:T(8,128)S(1)}, u32[]{:S(2)}, u32[]{:S(2)}) %collective-permute-start.5) | collective-permute-done | bytes 36896 | tf_op jit(solution)/shard_map/ppermute | solution.py:543
  25.2 1.6 %collective-permute-start.17 = (f32[128,256]{1,0:T(8,128)S(1)}, f32[128,256]{1,0:T(8,128)S(1)}, u32[]{:S(2)}, u32[]{:S(2)}) collective-permute-start(f32[128,256]{1,0:T(8,128)S(1)} %shard_map.149._.refs_0_), channel_id=1, source_target_pairs={{0,2},{1,3},{2,0},{3,1},{4,6},{5,7},{6,4},{7,5},{8,10},{9,11},{10,... | collective-permute-start | bytes 393224 | tf_op jit(solution)/shard_map/ppermute | solution.py:543
  26.8 3.1 %shard_map.148 = (bf16[256,256]{1,0:T(8,128)(2,1)S(1)}, bf16[256,256]{1,0:T(8,128)(2,1)S(1)}, bf16[256,256]{1,0:T(8,128)(2,1)S(1)}, bf16[256,256]{1,0:T(8,128)(2...) custom-call(f32[72,128]{1,0:T(8,128)S(1)} %shard_map.147.own_ref, f32[72,128]{1,0:T(8,128)S(1)} %collective-permute-done.6.got_ref, ...), custom_call_target="tpu_custom_call" | custom-call | flops 503316480 | bytes 1048576 | tf_op jit(solution)/shard_map/pallas_call | solution.py:686
  29.9 4.9 %shard_map.150 = (bf16[256,4096]{1,0:T(8,128)(2,1)S(1)}, f32[72,256]{1,0:T(8,128)S(1)}, f32[72,256]{1,0:T(8,128)S(1)}, f32[72,256]{1,0:T(8,128)S(1)}, f32[72,256]{1,0:T(8,128)S(1)}) custom-call(f32[24,4096]{1,0:T(8,128)S(1)} %get-tuple-element.42.aux_ref, bf16[256,4096]{1,0:T(8,128)(2,1)S(1)} %get-tuple-element.41.wt_ref, ...), custom_call_target="tpu_custom_call" | custom-call | flops 536870912 | bytes 1048576 | tf_op jit(solution)/shard_map/pallas_call | solution.py:701
  34.9 0.9 %collective-permute-start.10 = (f32[72,256]{1,0:T(8,128)S(1)}, f32[72,256]{1,0:T(8,128)S(1)}, u32[]{:S(2)}, u32[]{:S(2)}) collective-permute-start(f32[72,256]{1,0:T(8,128)S(1)} %get-tuple-element.64), channel_id=1, source_target_pairs={{0,3},{1,2},{2,1},{3,0},{4,7},{5,6},{6,5},{7,4},{8,11},{9,10},{10,... | collective-permute-start | bytes 221192 | tf_op jit(solution)/shard_map/ppermute | solution.py:543
  36.1 0.9 %collective-permute-start.9 = (f32[72,256]{1,0:T(8,128)S(1)}, f32[72,256]{1,0:T(8,128)S(1)}, u32[]{:S(2)}, u32[]{:S(2)}) collective-permute-start(f32[72,256]{1,0:T(8,128)S(1)} %get-tuple-element.63), channel_id=1, source_target_pairs={{0,2},{1,3},{2,0},{3,1},{4,6},{5,7},{6,4},{7,5},{8,10},{9,11},{10,... | collective-permute-start | bytes 221192 | tf_op jit(solution)/shard_map/ppermute | solution.py:543
  37.1 0.7 %collective-permute-start.18 = (f32[128,256]{1,0:T(8,128)S(1)}, f32[128,256]{1,0:T(8,128)S(1)}, u32[]{:S(2)}, u32[]{:S(2)}) collective-permute-start(f32[128,256]{1,0:T(8,128)S(1)} %shard_map.153.refs_0_), channel_id=1, source_target_pairs={{0,4},{1,5},{2,6},{3,7},{4,0},{5,1},{6,2},{7,3},{8,12},{9,13},{10,... | collective-permute-start | bytes 393224 | tf_op jit(solution)/shard_map/ppermute | solution.py:543
  37.8 1.4 %collective-permute-done.10 = f32[72,256]{1,0:T(8,128)S(1)} collective-permute-done((f32[72,256]{1,0:T(8,128)S(1)}, f32[72,256]{1,0:T(8,128)S(1)}, u32[]{:S(2)}, u32[]{:S(2)}) %collective-permute-start.10) | collective-permute-done | bytes 73760 | tf_op jit(solution)/shard_map/ppermute | solution.py:543
  39.2 1.9 %collective-permute-done.9 = f32[72,256]{1,0:T(8,128)S(1)} collective-permute-done((f32[72,256]{1,0:T(8,128)S(1)}, f32[72,256]{1,0:T(8,128)S(1)}, u32[]{:S(2)}, u32[]{:S(2)}) %collective-permute-start.9) | collective-permute-done | bytes 73760 | tf_op jit(solution)/shard_map/ppermute | solution.py:543
  41.1 3.6 %collective-permute-start.11 = (f32[72,256]{1,0:T(8,128)S(1)}, f32[72,256]{1,0:T(8,128)S(1)}, u32[]{:S(2)}, u32[]{:S(2)}) collective-permute-start(f32[72,256]{1,0:T(8,128)S(1)} %add_add_fusion._.refs_0_), channel_id=1, source_target_pairs={{0,12},{1,13},{2,14},{3,15},{4,8},{5,9},{6,10},{7,11},{8,4},{9,5},... | collective-permute-start | bytes 221192 | tf_op jit(solution)/shard_map/ppermute | solution.py:543
  44.7 0.9 %collective-permute-start.13 = (f32[72,256]{1,0:T(8,128)S(1)}, f32[72,256]{1,0:T(8,128)S(1)}, u32[]{:S(2)}, u32[]{:S(2)}) collective-permute-start(f32[72,256]{1,0:T(8,128)S(1)} %add_add_fusion._.refs_0_), channel_id=1, source_target_pairs={{0,4},{1,5},{2,6},{3,7},{4,0},{5,1},{6,2},{7,3},{8,12},{9,13},{10,... | collective-permute-start | bytes 221192 | tf_op jit(solution)/shard_map/ppermute | solution.py:543
  45.6 3.4 %shard_map.151 = (bf16[4096,256]{1,0:T(8,128)(2,1)}, bf16[4096,256]{1,0:T(8,128)(2,1)}, f32[8,128]{1,0:T(8,128)S(1)}) custom-call(bf16[256,4096]{1,0:T(8,128)(2,1)S(1)} %get-tuple-element.41.wt_ref, bf16[256,4096]{1,0:T(8,128)(2,1)S(1)} %get-tuple-element.60.dmt_ref, bf16[256,256]{1,0:T(8,128)(2,1)S(1)} %get-tuple-element.56.mw_ref, ...), custom_call_target="tpu_custom_call" | custom-call | flops 1073741824 | bytes 8388608 | tf_op jit(solution)/shard_map/pallas_call | solution.py:722
  49.1 1.4 %collective-permute-done.12.refs_2_ = f32[72,256]{1,0:T(8,128)S(1)} collective-permute-done((f32[72,256]{1,0:T(8,128)S(1)}, f32[72,256]{1,0:T(8,128)S(1)}, u32[]{:S(2)}, u32[]{:S(2)}) %collective-permute-start.12) | collective-permute-done | bytes 73760 | tf_op jit(solution)/shard_map/ppermute | solution.py:543
  50.7 1.2 %collective-permute-start.15 = (f32[72,256]{1,0:T(8,128)S(1)}, f32[72,256]{1,0:T(8,128)S(1)}, u32[]{:S(2)}, u32[]{:S(2)}) collective-permute-start(f32[72,256]{1,0:T(8,128)S(1)} %shard_map.152._.m0), channel_id=1, source_target_pairs={{0,2},{1,3},{2,0},{3,1},{4,6},{5,7},{6,4},{7,5},{8,10},{9,11},{10,... | collective-permute-start | bytes 221192 | tf_op jit(solution)/shard_map/ppermute | solution.py:543
  52.6 1.0 %shard_map.155 = (f32[256,256]{1,0:T(8,128)}, f32[8,128]{1,0:T(8,128)S(1)}) custom-call(f32[128,256]{1,0:T(8,128)S(1)} %shard_map.154.own_ref, f32[128,256]{1,0:T(8,128)S(1)} %collective-permute-done.19.other_ref, bf16[256,256]{1,0:T(8,128)(2,1)S(1)} %get-tuple-element.68.mixed_t_ref, f32[72,256]{1,0:T(8,128)S(1)} %shard_map.152._.m0), custom_call_target="tpu_custom_call" | custom-call | flops 67108864 | bytes 786432 | tf_op jit(solution)/shard_map/pallas_call | solution.py:741
  53.6 2.3 %collective-permute-done.15.m2 = f32[72,256]{1,0:T(8,128)S(1)} collective-permute-done((f32[72,256]{1,0:T(8,128)S(1)}, f32[72,256]{1,0:T(8,128)S(1)}, u32[]{:S(2)}, u32[]{:S(2)}) %collective-permute-start.15) | collective-permute-done | bytes 73760 | tf_op jit(solution)/shard_map/ppermute | solution.py:543
  (42 shorter events, 3.8 us)
Async XLA Ops:
  1.3 20.3 %copy-start.1 = (bf16[3,32,32]{2,1,0:T(8,128)(2,1)S(1)}, bf16[3,32,32]{2,1,0:T(8,128)(2,1)}, u32[]{:S(2)}) copy-start(bf16[3,32,32]{2,1,0:T(8,128)(2,1)} %w_qkv_ref.1) | copy-start | bytes 18436
  1.3 20.3 %copy-start.2 = (bf16[32,32]{1,0:T(8,128)(2,1)S(1)}, bf16[32,32]{1,0:T(8,128)(2,1)}, u32[]{:S(2)}) copy-start(bf16[32,32]{1,0:T(8,128)(2,1)} %w_slice_ref.1) | copy-start | bytes 6148
  8.5 18.3 %copy-start.4 = (bf16[256,256]{1,0:T(8,128)(2,1)S(1)}, bf16[256,256]{1,0:T(8,128)(2,1)}, u32[]{:S(2)}) copy-start(bf16[256,256]{1,0:T(8,128)(2,1)} %w_out_ref.1) | copy-start | bytes 393220
  8.6 6.0 %collective-permute-start = (f32[128,256]{1,0:T(8,128)S(1)}, f32[128,256]{1,0:T(8,128)S(1)}, u32[]{:S(2)}, u32[]{:S(2)}) collective-permute-start(f32[128,256]{1,0:T(8,128)S(1)} %get-tuple-element.46), channel_id=1, source_target_pairs={{0,1},{1,0},{2,3},{3,2},{4,5},{5,4},{6,7},{7,6},{8,9},{9,8},{10,11... | collective-permute-start | bytes 393224 | tf_op jit(solution)/shard_map/ppermute | solution.py:543
  9.1 1.2 %collective-permute-start.1 = (f32[72,128]{1,0:T(8,128)S(1)}, f32[72,128]{1,0:T(8,128)S(1)}, u32[]{:S(2)}, u32[]{:S(2)}) collective-permute-start(f32[72,128]{1,0:T(8,128)S(1)} %get-tuple-element.48), channel_id=1, source_target_pairs={{0,1},{1,0},{2,3},{3,2},{4,5},{5,4},{6,7},{7,6},{8,9},{9,8},{10,11... | collective-permute-start | bytes 110600 | tf_op jit(solution)/shard_map/ppermute | solution.py:543
  10.3 7.4 %collective-permute-start.2 = (f32[72,128]{1,0:T(8,128)S(1)}, f32[72,128]{1,0:T(8,128)S(1)}, u32[]{:S(2)}, u32[]{:S(2)}) collective-permute-start(f32[72,128]{1,0:T(8,128)S(1)} %add.21.refs_2_), channel_id=1, source_target_pairs={{0,2},{1,3},{2,0},{3,1},{4,6},{5,7},{6,4},{7,5},{8,10},{9,11},{10,... | collective-permute-start | bytes 110600 | tf_op jit(solution)/shard_map/ppermute | solution.py:543
  13.0 5.0 %collective-permute-start.3 = (f32[72,128]{1,0:T(8,128)S(1)}, f32[72,128]{1,0:T(8,128)S(1)}, u32[]{:S(2)}, u32[]{:S(2)}) collective-permute-start(f32[72,128]{1,0:T(8,128)S(1)} %add.21.refs_2_), channel_id=1, source_target_pairs={{0,6},{1,7},{2,4},{3,5},{4,2},{5,3},{6,0},{7,1},{8,14},{9,15},{10,... | collective-permute-start | bytes 110600 | tf_op jit(solution)/shard_map/ppermute | solution.py:543
  14.5 5.3 %collective-permute-start.4 = (f32[72,128]{1,0:T(8,128)S(1)}, f32[72,128]{1,0:T(8,128)S(1)}, u32[]{:S(2)}, u32[]{:S(2)}) collective-permute-start(f32[72,128]{1,0:T(8,128)S(1)} %add.21.refs_2_), channel_id=1, source_target_pairs={{0,4},{1,5},{2,6},{3,7},{4,0},{5,1},{6,2},{7,3},{8,12},{9,13},{10,... | collective-permute-start | bytes 110600 | tf_op jit(solution)/shard_map/ppermute | solution.py:543
  14.6 10.6 %collective-permute-start.7 = (f32[128,256]{1,0:T(8,128)S(1)}, f32[128,256]{1,0:T(8,128)S(1)}, u32[]{:S(2)}, u32[]{:S(2)}) collective-permute-start(f32[128,256]{1,0:T(8,128)S(1)} %shard_map.145._.refs_0_), channel_id=1, source_target_pairs={{0,8},{1,9},{2,10},{3,11},{4,12},{5,13},{6,14},{7,15},{8,0},{9,1},... | collective-permute-start | bytes 393224 | tf_op jit(solution)/shard_map/ppermute | solution.py:543
  19.8 5.3 %collective-permute-start.5 = (f32[72,128]{1,0:T(8,128)S(1)}, f32[72,128]{1,0:T(8,128)S(1)}, u32[]{:S(2)}, u32[]{:S(2)}) collective-permute-start(f32[72,128]{1,0:T(8,128)S(1)} %add_add_fusion.1.refs_0_.refs_2_), channel_id=1, source_target_pairs={{0,8},{1,9},{2,10},{3,11},{4,12},{5,13},{6,14},{7,15},{8,0},{9,1},... | collective-permute-start | bytes 110600 | tf_op jit(solution)/shard_map/ppermute | solution.py:543
  25.2 1.6 %collective-permute-start.6 = (f32[72,128]{1,0:T(8,128)S(1)}, f32[72,128]{1,0:T(8,128)S(1)}, u32[]{:S(2)}, u32[]{:S(2)}) collective-permute-start(f32[72,128]{1,0:T(8,128)S(1)} %shard_map.147.own_ref), channel_id=1, source_target_pairs={{0,1},{1,0},{2,3},{3,2},{4,5},{5,4},{6,7},{7,6},{8,9},{9,8},{10,11... | collective-permute-start | bytes 110600 | tf_op jit(solution)/shard_map/ppermute | solution.py:543
  25.2 11.8 %collective-permute-start.17 = (f32[128,256]{1,0:T(8,128)S(1)}, f32[128,256]{1,0:T(8,128)S(1)}, u32[]{:S(2)}, u32[]{:S(2)}) collective-permute-start(f32[128,256]{1,0:T(8,128)S(1)} %shard_map.149._.refs_0_), channel_id=1, source_target_pairs={{0,2},{1,3},{2,0},{3,1},{4,6},{5,7},{6,4},{7,5},{8,10},{9,11},{10,... | collective-permute-start | bytes 393224 | tf_op jit(solution)/shard_map/ppermute | solution.py:543
  29.9 15.6 %copy-start = (bf16[256,256]{1,0:T(8,128)(2,1)S(1)}, bf16[256,256]{1,0:T(8,128)(2,1)}, u32[]{:S(2)}) copy-start(bf16[256,256]{1,0:T(8,128)(2,1)} %w_mid_ref.1) | copy-start | bytes 393220
  34.9 4.3 %collective-permute-start.10 = (f32[72,256]{1,0:T(8,128)S(1)}, f32[72,256]{1,0:T(8,128)S(1)}, u32[]{:S(2)}, u32[]{:S(2)}) collective-permute-start(f32[72,256]{1,0:T(8,128)S(1)} %get-tuple-element.64), channel_id=1, source_target_pairs={{0,3},{1,2},{2,1},{3,0},{4,7},{5,6},{6,5},{7,4},{8,11},{9,10},{10,... | collective-permute-start | bytes 221192 | tf_op jit(solution)/shard_map/ppermute | solution.py:543
  35.8 3.4 %collective-permute-start.8 = (f32[72,256]{1,0:T(8,128)S(1)}, f32[72,256]{1,0:T(8,128)S(1)}, u32[]{:S(2)}, u32[]{:S(2)}) collective-permute-start(f32[72,256]{1,0:T(8,128)S(1)} %get-tuple-element.62.refs_2_), channel_id=1, source_target_pairs={{0,1},{1,0},{2,3},{3,2},{4,5},{5,4},{6,7},{7,6},{8,9},{9,8},{10,11... | collective-permute-start | bytes 221192 | tf_op jit(solution)/shard_map/ppermute | solution.py:543
  36.1 4.9 %collective-permute-start.9 = (f32[72,256]{1,0:T(8,128)S(1)}, f32[72,256]{1,0:T(8,128)S(1)}, u32[]{:S(2)}, u32[]{:S(2)}) collective-permute-start(f32[72,256]{1,0:T(8,128)S(1)} %get-tuple-element.63), channel_id=1, source_target_pairs={{0,2},{1,3},{2,0},{3,1},{4,6},{5,7},{6,4},{7,5},{8,10},{9,11},{10,... | collective-permute-start | bytes 221192 | tf_op jit(solution)/shard_map/ppermute | solution.py:543
  37.1 11.9 %collective-permute-start.18 = (f32[128,256]{1,0:T(8,128)S(1)}, f32[128,256]{1,0:T(8,128)S(1)}, u32[]{:S(2)}, u32[]{:S(2)}) collective-permute-start(f32[128,256]{1,0:T(8,128)S(1)} %shard_map.153.refs_0_), channel_id=1, source_target_pairs={{0,4},{1,5},{2,6},{3,7},{4,0},{5,1},{6,2},{7,3},{8,12},{9,13},{10,... | collective-permute-start | bytes 393224 | tf_op jit(solution)/shard_map/ppermute | solution.py:543
  41.1 8.0 %collective-permute-start.11 = (f32[72,256]{1,0:T(8,128)S(1)}, f32[72,256]{1,0:T(8,128)S(1)}, u32[]{:S(2)}, u32[]{:S(2)}) collective-permute-start(f32[72,256]{1,0:T(8,128)S(1)} %add_add_fusion._.refs_0_), channel_id=1, source_target_pairs={{0,12},{1,13},{2,14},{3,15},{4,8},{5,9},{6,10},{7,11},{8,4},{9,5},... | collective-permute-start | bytes 221192 | tf_op jit(solution)/shard_map/ppermute | solution.py:543
  44.7 5.8 %collective-permute-start.12 = (f32[72,256]{1,0:T(8,128)S(1)}, f32[72,256]{1,0:T(8,128)S(1)}, u32[]{:S(2)}, u32[]{:S(2)}) collective-permute-start(f32[72,256]{1,0:T(8,128)S(1)} %add_add_fusion._.refs_0_), channel_id=1, source_target_pairs={{0,8},{1,9},{2,10},{3,11},{4,12},{5,13},{6,14},{7,15},{8,0},{9,1},... | collective-permute-start | bytes 221192 | tf_op jit(solution)/shard_map/ppermute | solution.py:543
  44.7 6.0 %collective-permute-start.13 = (f32[72,256]{1,0:T(8,128)S(1)}, f32[72,256]{1,0:T(8,128)S(1)}, u32[]{:S(2)}, u32[]{:S(2)}) collective-permute-start(f32[72,256]{1,0:T(8,128)S(1)} %add_add_fusion._.refs_0_), channel_id=1, source_target_pairs={{0,4},{1,5},{2,6},{3,7},{4,0},{5,1},{6,2},{7,3},{8,12},{9,13},{10,... | collective-permute-start | bytes 221192 | tf_op jit(solution)/shard_map/ppermute | solution.py:543
  49.0 3.6 %collective-permute-start.19 = (f32[128,256]{1,0:T(8,128)S(1)}, f32[128,256]{1,0:T(8,128)S(1)}, u32[]{:S(2)}, u32[]{:S(2)}) collective-permute-start(f32[128,256]{1,0:T(8,128)S(1)} %shard_map.154.own_ref), channel_id=1, source_target_pairs={{0,1},{1,0},{2,3},{3,2},{4,5},{5,4},{6,7},{7,6},{8,9},{9,8},{10,11... | collective-permute-start | bytes 393224 | tf_op jit(solution)/shard_map/ppermute | solution.py:543
  50.7 2.9 %collective-permute-start.14 = (f32[72,256]{1,0:T(8,128)S(1)}, f32[72,256]{1,0:T(8,128)S(1)}, u32[]{:S(2)}, u32[]{:S(2)}) collective-permute-start(f32[72,256]{1,0:T(8,128)S(1)} %shard_map.152._.m0), channel_id=1, source_target_pairs={{0,1},{1,0},{2,3},{3,2},{4,5},{5,4},{6,7},{7,6},{8,9},{9,8},{10,11... | collective-permute-start | bytes 221192 | tf_op jit(solution)/shard_map/ppermute | solution.py:543
  50.7 5.1 %collective-permute-start.15 = (f32[72,256]{1,0:T(8,128)S(1)}, f32[72,256]{1,0:T(8,128)S(1)}, u32[]{:S(2)}, u32[]{:S(2)}) collective-permute-start(f32[72,256]{1,0:T(8,128)S(1)} %shard_map.152._.m0), channel_id=1, source_target_pairs={{0,2},{1,3},{2,0},{3,1},{4,6},{5,7},{6,4},{7,5},{8,10},{9,11},{10,... | collective-permute-start | bytes 221192 | tf_op jit(solution)/shard_map/ppermute | solution.py:543
  51.9 4.6 %collective-permute-start.16 = (f32[72,256]{1,0:T(8,128)S(1)}, f32[72,256]{1,0:T(8,128)S(1)}, u32[]{:S(2)}, u32[]{:S(2)}) collective-permute-start(f32[72,256]{1,0:T(8,128)S(1)} %shard_map.152._.m0), channel_id=1, source_target_pairs={{0,3},{1,2},{2,1},{3,0},{4,7},{5,6},{6,5},{7,4},{8,11},{9,10},{10,... | collective-permute-start | bytes 221192 | tf_op jit(solution)/shard_map/ppermute | solution.py:543
  (1 other events, 8.4 us)

commit v11 on v10

--- a/solution.py
+++ b/solution.py
@@ -669,19 +669,19 @@
             near((8, 128), f32),
         ],
         compiler_params=params(16, False),
-        cost_estimate=cost(unit // 10, rows, rows),
-    )(mid, sw, aux, w_slice, w_qkv, wc_sum)
-    own = sum_stage(own, 2, 3, count)
-    wc_got = exchange(wc_sum, count // 2, count)
+        cost_estimate=cost(3 * unit, rows, rows),
+    )(mid, sw, aux, w_slice, w_qkv, own)
+    own = sum_stage(own, 2, 3, count, token)
+    wc_got = exchange(wc_sum, 2, count)
     wc_sum = sum_behind([wc_sum, wc_got], own)
-    own = sum_over_groups(own, 8, count, token)
+    own = sum_over_groups(own, 8, count)
     other = exchange(own, 1, count)
-    wc_got = exchange(wc_sum, 2, count)
     stride = 8
-    while stride < count // 2:
+    wc_got = exchange(wc_sum, stride, count)
+    while 2 * stride < count:
         wc_sum = wc_sum + wc_got
+        stride *= 2
         wc_got = exchange(wc_sum, stride, count)
-        stride *= 2
 
     mw, mixed_t, dr, drt, dn, grad_qkv = pl.pallas_call(
         functools.partial(tokens_kernel, heads, slices),
@@ -695,7 +695,7 @@
         ],
         scratch_shapes=[pltpu.VMEM((2,) + half, f32)],
         compiler_params=params(16, False),
-        cost_estimate=cost(30 * width**3, 4 * width * width * 4, hm * hm),
+        cost_estimate=cost(3 * width**3, 4 * width * width * 4, hm * hm),
     )(own, other, w_cat, w_out)
     larger = (width // group + slices // group, width)
     dmt, *sends = pl.pallas_call(
@@ -710,7 +710,7 @@
             pltpu.VMEM((group,) + larger, f32),
         ],
         compiler_params=params(24, False),
-        cost_estimate=cost(unit, rows * width, rows),
+        cost_estimate=cost(unit * 3 // 10, rows * width, rows),
     )(aux, wt, logits, weights, mid, cot_near, feats_near, sb, mw, dr, drt, dn, temp, wc_sum)
 
     mid_total = scatter_group(sends, count)

time: 57.5 us -> 58.7 us (1.021)
  starting transfers between devices: 20.7 us -> 25.7 us
  waiting for transfers between devices: 13.7 us -> 9.89 us
    ppermute x20, starting transfers between devices: 20.7 us -> 25.7 us  [exchange(): return lax.ppermute(x, 'node', [(i, i ^ k) for i in range(count)])]
    ppermute x20, waiting for transfers between devices: 13.7 us -> 9.89 us  [exchange(): return lax.ppermute(x, 'node', [(i, i ^ k) for i in range(count)])]
  transfers between devices with their start and end apart: 20 -> 20, of which waited for: 10 -> 10; matrix products, arithmetic and copies ran while one was open for 0% -> 0% of each run, Pallas kernels for 24% -> 23%
where the time goes in v11:
time: 58.7 us; the launch traced here: 58.5 us
  starting transfers between devices  25.7 us (44%)
  Pallas kernels  21.4 us (36%)
  waiting for transfers between devices  9.89 us (17%)
  between operations  1.41 us (2%)
    ppermute x20, starting transfers between devices, exchange(): return lax.ppermute(x, 'node', [(i, i ^ k) for i in range(count)])  25.7 us
    ppermute x20, waiting for transfers between devices, exchange(): return lax.ppermute(x, 'node', [(i, i ^ k) for i in range(count)])  9.89 us
    pallas_call x1, Pallas kernels, shards(): pl.pallas_call(functools.partial(stats_kernel, heads, slices), in_specs=[...  7.27 us
    pallas_call x1, Pallas kernels, shards(): pl.pallas_call(functools.partial(backward_kernel, heads, slices), in_spec...  4.86 us
    pallas_call x1, Pallas kernels, shards(): pl.pallas_call(rows_kernel, grid=grid, in_specs=[whole, whole, whole, ful...  3.41 us
    pallas_call x1, Pallas kernels, shards(): pl.pallas_call(functools.partial(tokens_kernel, heads, slices), out_shape...  3.1 us
  transfers between devices with their start and end apart: 20, of which 10 were waited for; matrix products, arithmetic and copies ran while one was open for 0% of the time, Pallas kernels for 23%

profile of v11, /device:TPU:0, one launch (start us, length us, event | category | flops | bytes accessed | tf_op | source)
XLA Modules:
  0.0 58.5 jit_solution(15691402252180838763)
XLA Ops:
  1.3 7.3 %shard_map.144 = (bf16[4096,256]{1,0:T(8,128)(2,1)S(1)}, bf16[256,4096]{1,0:T(8,128)(2,1)S(1)}, f32[24,4096]{1,0:T(8,128)S(1)}, bf16[272,256]{1,0:T(8,128)(2,1)S...) custom-call(s32[1]{0:T(128)S(6)} %copy.16.owned_ref, ...), custom_call_target="tpu_custom_call" | custom-call | flops 2147483648 | bytes 8388608 | tf_op jit(solution)/shard_map/pallas_call | solution.py:626
  9.2 1.1 %collective-permute-done = f32[72,128]{1,0:T(8,128)S(1)} collective-permute-done((f32[72,128]{1,0:T(8,128)S(1)}, f32[72,128]{1,0:T(8,128)S(1)}, u32[]{:S(2)}, u32[]{:S(2)}) %collective-permute-start) | collective-permute-done | bytes 36896 | tf_op jit(solution)/shard_map/ppermute | solution.py:543
  10.3 3.7 %collective-permute-start.1 = (f32[72,128]{1,0:T(8,128)S(1)}, f32[72,128]{1,0:T(8,128)S(1)}, u32[]{:S(2)}, u32[]{:S(2)}) collective-permute-start(f32[72,128]{1,0:T(8,128)S(1)} %add.15._.refs_0_.refs_2_), channel_id=1, source_target_pairs={{0,6},{1,7},{2,4},{3,5},{4,2},{5,3},{6,0},{7,1},{8,14},{9,15},{10,... | collective-permute-start | bytes 110600 | tf_op jit(solution)/shard_map/ppermute | solution.py:543
  14.7 1.9 %collective-permute-start.7 = (f32[128,256]{1,0:T(8,128)S(1)}, f32[128,256]{1,0:T(8,128)S(1)}, u32[]{:S(2)}, u32[]{:S(2)}) collective-permute-start(f32[128,256]{1,0:T(8,128)S(1)} %shard_map.148.refs_0_), channel_id=1, source_target_pairs={{0,2},{1,3},{2,0},{3,1},{4,6},{5,7},{6,4},{7,5},{8,10},{9,11},{10,... | collective-permute-start | bytes 393224 | tf_op jit(solution)/shard_map/ppermute | solution.py:543
  16.6 1.0 %shard_map.145 = (f32[256,4096]{1,0:T(8,128)S(1)}, f32[256,4096]{1,0:T(8,128)S(1)}, bf16[256,256]{1,0:T(8,128)(2,1)S(1)}, bf16[32,128]{1,0:T(8,128)(2,1)S(1)}, f32[8,128]{1,0:T(8,128)S(1)}) custom-call(bf16[4096,256]{1,0:T(8,128)(2,1)S(1)} %get-tuple-element.43.mid_ref, bf16[272,256]{1,0:T(8,128)(2,1)S(1)} %get-tuple-element.44.sw_ref, ...), custom_call_target="tpu_custom_call" | custom-call | flops 1610612736 | bytes 4096 | tf_op jit(solution)/shard_map/pallas_call | solution.py:660
  18.0 0.9 %collective-permute-done.3.refs_3_ = f32[72,128]{1,0:T(8,128)S(1)} collective-permute-done((f32[72,128]{1,0:T(8,128)S(1)}, f32[72,128]{1,0:T(8,128)S(1)}, u32[]{:S(2)}, u32[]{:S(2)}) %collective-permute-start.3) | collective-permute-done | bytes 36896 | tf_op jit(solution)/shard_map/ppermute | solution.py:543
  18.8 2.7 %collective-permute-start.4 = (f32[72,128]{1,0:T(8,128)S(1)}, f32[72,128]{1,0:T(8,128)S(1)}, u32[]{:S(2)}, u32[]{:S(2)}) collective-permute-start(f32[72,128]{1,0:T(8,128)S(1)} %shard_map.146.refs_2_), channel_id=1, source_target_pairs={{0,8},{1,9},{2,10},{3,11},{4,12},{5,13},{6,14},{7,15},{8,0},{9,1},... | collective-permute-start | bytes 110600 | tf_op jit(solution)/shard_map/ppermute | solution.py:543
  21.5 1.6 %collective-permute-start.17 = (f32[128,256]{1,0:T(8,128)S(1)}, f32[128,256]{1,0:T(8,128)S(1)}, u32[]{:S(2)}, u32[]{:S(2)}) collective-permute-start(f32[128,256]{1,0:T(8,128)S(1)} %shard_map.149._.refs_0_), channel_id=1, source_target_pairs={{0,8},{1,9},{2,10},{3,11},{4,12},{5,13},{6,14},{7,15},{8,0},{9,1},... | collective-permute-start | bytes 393224 | tf_op jit(solution)/shard_map/ppermute | solution.py:543
  23.1 1.0 %collective-permute-done.4 = f32[72,128]{1,0:T(8,128)S(1)} collective-permute-done((f32[72,128]{1,0:T(8,128)S(1)}, f32[72,128]{1,0:T(8,128)S(1)}, u32[]{:S(2)}, u32[]{:S(2)}) %collective-permute-start.4) | collective-permute-done | bytes 36896 | tf_op jit(solution)/shard_map/ppermute | solution.py:543
  24.1 1.2 %collective-permute-done.5.got_ref = f32[72,128]{1,0:T(8,128)S(1)} collective-permute-done((f32[72,128]{1,0:T(8,128)S(1)}, f32[72,128]{1,0:T(8,128)S(1)}, u32[]{:S(2)}, u32[]{:S(2)}) %collective-permute-start.5) | collective-permute-done | bytes 36896 | tf_op jit(solution)/shard_map/ppermute | solution.py:543
  25.3 3.1 %shard_map.147 = (bf16[256,256]{1,0:T(8,128)(2,1)S(1)}, bf16[256,256]{1,0:T(8,128)(2,1)S(1)}, bf16[256,256]{1,0:T(8,128)(2,1)S(1)}, bf16[256,256]{1,0:T(8,128)(2...) custom-call(f32[72,128]{1,0:T(8,128)S(1)} %add.16.own_ref, f32[72,128]{1,0:T(8,128)S(1)} %collective-permute-done.5.got_ref, ...), custom_call_target="tpu_custom_call" | custom-call | flops 50331648 | bytes 1048576 | tf_op jit(solution)/shard_map/pallas_call | solution.py:686
  28.4 4.9 %shard_map.150 = (bf16[256,4096]{1,0:T(8,128)(2,1)S(1)}, f32[72,256]{1,0:T(8,128)S(1)}, f32[72,256]{1,0:T(8,128)S(1)}, f32[72,256]{1,0:T(8,128)S(1)}, f32[72,256]{1,0:T(8,128)S(1)}) custom-call(f32[24,4096]{1,0:T(8,128)S(1)} %get-tuple-element.42.aux_ref, bf16[256,4096]{1,0:T(8,128)(2,1)S(1)} %get-tuple-element.41.wt_ref, ...), custom_call_target="tpu_custom_call" | custom-call | flops 161061280 | bytes 1048576 | tf_op jit(solution)/shard_map/pallas_call | solution.py:701
  33.9 1.6 %collective-permute-start.9 = (f32[72,256]{1,0:T(8,128)S(1)}, f32[72,256]{1,0:T(8,128)S(1)}, u32[]{:S(2)}, u32[]{:S(2)}) collective-permute-start(f32[72,256]{1,0:T(8,128)S(1)} %get-tuple-element.63), channel_id=1, source_target_pairs={{0,2},{1,3},{2,0},{3,1},{4,6},{5,7},{6,4},{7,5},{8,10},{9,11},{10,... | collective-permute-start | bytes 221192 | tf_op jit(solution)/shard_map/ppermute | solution.py:543
  35.5 3.4 %collective-permute-start.18 = (f32[128,256]{1,0:T(8,128)S(1)}, f32[128,256]{1,0:T(8,128)S(1)}, u32[]{:S(2)}, u32[]{:S(2)}) collective-permute-start(f32[128,256]{1,0:T(8,128)S(1)} %shard_map.153.refs_0_), channel_id=1, source_target_pairs={{0,4},{1,5},{2,6},{3,7},{4,0},{5,1},{6,2},{7,3},{8,12},{9,13},{10,... | collective-permute-start | bytes 393224 | tf_op jit(solution)/shard_map/ppermute | solution.py:543
  38.9 0.6 collective-permute-done.9
  39.5 6.4 %collective-permute-start.11 = (f32[72,256]{1,0:T(8,128)S(1)}, f32[72,256]{1,0:T(8,128)S(1)}, u32[]{:S(2)}, u32[]{:S(2)}) collective-permute-start(f32[72,256]{1,0:T(8,128)S(1)} %add_add_fusion._.refs_0_), channel_id=1, source_target_pairs={{0,12},{1,13},{2,14},{3,15},{4,8},{5,9},{6,10},{7,11},{8,4},{9,5},... | collective-permute-start | bytes 221192 | tf_op jit(solution)/shard_map/ppermute | solution.py:543
  45.9 0.6 %collective-permute-start.13 = (f32[72,256]{1,0:T(8,128)S(1)}, f32[72,256]{1,0:T(8,128)S(1)}, u32[]{:S(2)}, u32[]{:S(2)}) collective-permute-start(f32[72,256]{1,0:T(8,128)S(1)} %add_add_fusion._.refs_0_), channel_id=1, source_target_pairs={{0,4},{1,5},{2,6},{3,7},{4,0},{5,1},{6,2},{7,3},{8,12},{9,13},{10,... | collective-permute-start | bytes 221192 | tf_op jit(solution)/shard_map/ppermute | solution.py:543
  46.5 3.4 %shard_map.151 = (bf16[4096,256]{1,0:T(8,128)(2,1)}, bf16[4096,256]{1,0:T(8,128)(2,1)}, f32[8,128]{1,0:T(8,128)S(1)}) custom-call(bf16[256,4096]{1,0:T(8,128)(2,1)S(1)} %get-tuple-element.41.wt_ref, bf16[256,4096]{1,0:T(8,128)(2,1)S(1)} %get-tuple-element.60.dmt_ref, bf16[256,256]{1,0:T(8,128)(2,1)S(1)} %get-tuple-element.54.mw_ref, ...), custom_call_target="tpu_custom_call" | custom-call | flops 1073741824 | bytes 8388608 | tf_op jit(solution)/shard_map/pallas_call | solution.py:722
  50.1 1.5 %collective-permute-done.12.refs_2_ = f32[72,256]{1,0:T(8,128)S(1)} collective-permute-done((f32[72,256]{1,0:T(8,128)S(1)}, f32[72,256]{1,0:T(8,128)S(1)}, u32[]{:S(2)}, u32[]{:S(2)}) %collective-permute-start.12) | collective-permute-done | bytes 73760 | tf_op jit(solution)/shard_map/ppermute | solution.py:543
  52.1 1.6 %collective-permute-start.16 = (f32[72,256]{1,0:T(8,128)S(1)}, f32[72,256]{1,0:T(8,128)S(1)}, u32[]{:S(2)}, u32[]{:S(2)}) collective-permute-start(f32[72,256]{1,0:T(8,128)S(1)} %shard_map.152._.m0), channel_id=1, source_target_pairs={{0,3},{1,2},{2,1},{3,0},{4,7},{5,6},{6,5},{7,4},{8,11},{9,10},{10,... | collective-permute-start | bytes 221192 | tf_op jit(solution)/shard_map/ppermute | solution.py:543
  53.8 1.0 %shard_map.155 = (f32[256,256]{1,0:T(8,128)}, f32[8,128]{1,0:T(8,128)S(1)}) custom-call(f32[128,256]{1,0:T(8,128)S(1)} %shard_map.154.own_ref, f32[128,256]{1,0:T(8,128)S(1)} %collective-permute-done.19.other_ref, bf16[256,256]{1,0:T(8,128)(2,1)S(1)} %get-tuple-element.68.mixed_t_ref, f32[72,256]{1,0:T(8,128)S(1)} %shard_map.152._.m0), custom_call_target="tpu_custom_call" | custom-call | flops 67108864 | bytes 786432 | tf_op jit(solution)/shard_map/pallas_call | solution.py:741
  54.8 2.3 %collective-permute-done.15.m2 = f32[72,256]{1,0:T(8,128)S(1)} collective-permute-done((f32[72,256]{1,0:T(8,128)S(1)}, f32[72,256]{1,0:T(8,128)S(1)}, u32[]{:S(2)}, u32[]{:S(2)}) %collective-permute-start.15) | collective-permute-done | bytes 73760 | tf_op jit(solution)/shard_map/ppermute | solution.py:543
  57.1 0.7 %collective-permute-done.16.m3 = f32[72,256]{1,0:T(8,128)S(1)} collective-permute-done((f32[72,256]{1,0:T(8,128)S(1)}, f32[72,256]{1,0:T(8,128)S(1)}, u32[]{:S(2)}, u32[]{:S(2)}) %collective-permute-start.16) | collective-permute-done | bytes 73760 | tf_op jit(solution)/shard_map/ppermute | solution.py:543
  57.7 0.7 %shard_map.156 = (f32[256,256]{1,0:T(8,128)}, f32[32,32]{1,0:T(8,128)}, f32[1,32]{1,0:T(1,128)}) custom-call(f32[72,256]{1,0:T(8,128)S(1)} %shard_map.152._.m0, f32[72,256]{1,0:T(8,128)S(1)} %collective-permute-done.14.m1, f32[72,256]{1,0:T(8,128)S(1)} %collective-permute-done.15.m2, f32[72,256]{1,0:T(8,128)S(1)} %collective-permute-done.16.m3, ...), custom_call_target="tpu_custom_call" | custom-call | bytes 524288 | tf_op jit(solution)/shard_map/pallas_call | solution.py:752
  (42 shorter events, 3.0 us)
Async XLA Ops:
  1.3 15.3 %copy-start.3 = (bf16[3,32,32]{2,1,0:T(8,128)(2,1)S(1)}, bf16[3,32,32]{2,1,0:T(8,128)(2,1)}, u32[]{:S(2)}) copy-start(bf16[3,32,32]{2,1,0:T(8,128)(2,1)} %w_qkv_ref.1) | copy-start | bytes 18436
  1.3 15.3 %copy-start.4 = (bf16[32,32]{1,0:T(8,128)(2,1)S(1)}, bf16[32,32]{1,0:T(8,128)(2,1)}, u32[]{:S(2)}) copy-start(bf16[32,32]{1,0:T(8,128)(2,1)} %w_slice_ref.1) | copy-start | bytes 6148
  8.6 6.1 %collective-permute-start.6 = (f32[128,256]{1,0:T(8,128)S(1)}, f32[128,256]{1,0:T(8,128)S(1)}, u32[]{:S(2)}, u32[]{:S(2)}) collective-permute-start(f32[128,256]{1,0:T(8,128)S(1)} %get-tuple-element.59), channel_id=1, source_target_pairs={{0,1},{1,0},{2,3},{3,2},{4,5},{5,4},{6,7},{7,6},{8,9},{9,8},{10,11... | collective-permute-start | bytes 393224 | tf_op jit(solution)/shard_map/ppermute | solution.py:543
  9.1 1.2 %collective-permute-start = (f32[72,128]{1,0:T(8,128)S(1)}, f32[72,128]{1,0:T(8,128)S(1)}, u32[]{:S(2)}, u32[]{:S(2)}) collective-permute-start(f32[72,128]{1,0:T(8,128)S(1)} %get-tuple-element.46), channel_id=1, source_target_pairs={{0,1},{1,0},{2,3},{3,2},{4,5},{5,4},{6,7},{7,6},{8,9},{9,8},{10,11... | collective-permute-start | bytes 110600 | tf_op jit(solution)/shard_map/ppermute | solution.py:543
  10.3 7.3 %collective-permute-start.1 = (f32[72,128]{1,0:T(8,128)S(1)}, f32[72,128]{1,0:T(8,128)S(1)}, u32[]{:S(2)}, u32[]{:S(2)}) collective-permute-start(f32[72,128]{1,0:T(8,128)S(1)} %add.15._.refs_0_.refs_2_), channel_id=1, source_target_pairs={{0,6},{1,7},{2,4},{3,5},{4,2},{5,3},{6,0},{7,1},{8,14},{9,15},{10,... | collective-permute-start | bytes 110600 | tf_op jit(solution)/shard_map/ppermute | solution.py:543
  14.0 4.0 %collective-permute-start.2 = (f32[72,128]{1,0:T(8,128)S(1)}, f32[72,128]{1,0:T(8,128)S(1)}, u32[]{:S(2)}, u32[]{:S(2)}) collective-permute-start(f32[72,128]{1,0:T(8,128)S(1)} %add.15._.refs_0_.refs_2_), channel_id=1, source_target_pairs={{0,4},{1,5},{2,6},{3,7},{4,0},{5,1},{6,2},{7,3},{8,12},{9,13},{10,... | collective-permute-start | bytes 110600 | tf_op jit(solution)/shard_map/ppermute | solution.py:543
  14.4 4.4 %collective-permute-start.3 = (f32[72,128]{1,0:T(8,128)S(1)}, f32[72,128]{1,0:T(8,128)S(1)}, u32[]{:S(2)}, u32[]{:S(2)}) collective-permute-start(f32[72,128]{1,0:T(8,128)S(1)} %add.15._.refs_0_.refs_2_), channel_id=1, source_target_pairs={{0,2},{1,3},{2,0},{3,1},{4,6},{5,7},{6,4},{7,5},{8,10},{9,11},{10,... | collective-permute-start | bytes 110600 | tf_op jit(solution)/shard_map/ppermute | solution.py:543
  14.7 6.8 %collective-permute-start.7 = (f32[128,256]{1,0:T(8,128)S(1)}, f32[128,256]{1,0:T(8,128)S(1)}, u32[]{:S(2)}, u32[]{:S(2)}) collective-permute-start(f32[128,256]{1,0:T(8,128)S(1)} %shard_map.148.refs_0_), channel_id=1, source_target_pairs={{0,2},{1,3},{2,0},{3,1},{4,6},{5,7},{6,4},{7,5},{8,10},{9,11},{10,... | collective-permute-start | bytes 393224 | tf_op jit(solution)/shard_map/ppermute | solution.py:543
  16.6 11.8 %copy-start.2 = (bf16[32]{0:T(256)(128)(2,1)S(1)}, bf16[32]{0:T(256)(128)(2,1)}, u32[]{:S(2)}) copy-start(bf16[32]{0:T(256)(128)(2,1)} %param.15) | copy-start | bytes 196
  18.8 5.2 %collective-permute-start.4 = (f32[72,128]{1,0:T(8,128)S(1)}, f32[72,128]{1,0:T(8,128)S(1)}, u32[]{:S(2)}, u32[]{:S(2)}) collective-permute-start(f32[72,128]{1,0:T(8,128)S(1)} %shard_map.146.refs_2_), channel_id=1, source_target_pairs={{0,8},{1,9},{2,10},{3,11},{4,12},{5,13},{6,14},{7,15},{8,0},{9,1},... | collective-permute-start | bytes 110600 | tf_op jit(solution)/shard_map/ppermute | solution.py:543
  21.5 14.0 %collective-permute-start.17 = (f32[128,256]{1,0:T(8,128)S(1)}, f32[128,256]{1,0:T(8,128)S(1)}, u32[]{:S(2)}, u32[]{:S(2)}) collective-permute-start(f32[128,256]{1,0:T(8,128)S(1)} %shard_map.149._.refs_0_), channel_id=1, source_target_pairs={{0,8},{1,9},{2,10},{3,11},{4,12},{5,13},{6,14},{7,15},{8,0},{9,1},... | collective-permute-start | bytes 393224 | tf_op jit(solution)/shard_map/ppermute | solution.py:543
  24.1 1.2 %collective-permute-start.5 = (f32[72,128]{1,0:T(8,128)S(1)}, f32[72,128]{1,0:T(8,128)S(1)}, u32[]{:S(2)}, u32[]{:S(2)}) collective-permute-start(f32[72,128]{1,0:T(8,128)S(1)} %add.16.own_ref), channel_id=1, source_target_pairs={{0,1},{1,0},{2,3},{3,2},{4,5},{5,4},{6,7},{7,6},{8,9},{9,8},{10,11... | collective-permute-start | bytes 110600 | tf_op jit(solution)/shard_map/ppermute | solution.py:543
  28.4 18.1 %copy-start = (bf16[256,256]{1,0:T(8,128)(2,1)S(1)}, bf16[256,256]{1,0:T(8,128)(2,1)}, u32[]{:S(2)}) copy-start(bf16[256,256]{1,0:T(8,128)(2,1)} %w_mid_ref.1) | copy-start | bytes 393220
  33.3 5.6 %collective-permute-start.10 = (f32[72,256]{1,0:T(8,128)S(1)}, f32[72,256]{1,0:T(8,128)S(1)}, u32[]{:S(2)}, u32[]{:S(2)}) collective-permute-start(f32[72,256]{1,0:T(8,128)S(1)} %get-tuple-element.64), channel_id=1, source_target_pairs={{0,3},{1,2},{2,1},{3,0},{4,7},{5,6},{6,5},{7,4},{8,11},{9,10},{10,... | collective-permute-start | bytes 221192 | tf_op jit(solution)/shard_map/ppermute | solution.py:543
  33.5 5.4 %collective-permute-start.8 = (f32[72,256]{1,0:T(8,128)S(1)}, f32[72,256]{1,0:T(8,128)S(1)}, u32[]{:S(2)}, u32[]{:S(2)}) collective-permute-start(f32[72,256]{1,0:T(8,128)S(1)} %get-tuple-element.62.refs_2_), channel_id=1, source_target_pairs={{0,1},{1,0},{2,3},{3,2},{4,5},{5,4},{6,7},{7,6},{8,9},{9,8},{10,11... | collective-permute-start | bytes 221192 | tf_op jit(solution)/shard_map/ppermute | solution.py:543
  33.9 5.6 %collective-permute-start.9 = (f32[72,256]{1,0:T(8,128)S(1)}, f32[72,256]{1,0:T(8,128)S(1)}, u32[]{:S(2)}, u32[]{:S(2)}) collective-permute-start(f32[72,256]{1,0:T(8,128)S(1)} %get-tuple-element.63), channel_id=1, source_target_pairs={{0,2},{1,3},{2,0},{3,1},{4,6},{5,7},{6,4},{7,5},{8,10},{9,11},{10,... | collective-permute-start | bytes 221192 | tf_op jit(solution)/shard_map/ppermute | solution.py:543
  35.5 14.4 %collective-permute-start.18 = (f32[128,256]{1,0:T(8,128)S(1)}, f32[128,256]{1,0:T(8,128)S(1)}, u32[]{:S(2)}, u32[]{:S(2)}) collective-permute-start(f32[128,256]{1,0:T(8,128)S(1)} %shard_map.153.refs_0_), channel_id=1, source_target_pairs={{0,4},{1,5},{2,6},{3,7},{4,0},{5,1},{6,2},{7,3},{8,12},{9,13},{10,... | collective-permute-start | bytes 393224 | tf_op jit(solution)/shard_map/ppermute | solution.py:543
  39.5 10.5 %collective-permute-start.11 = (f32[72,256]{1,0:T(8,128)S(1)}, f32[72,256]{1,0:T(8,128)S(1)}, u32[]{:S(2)}, u32[]{:S(2)}) collective-permute-start(f32[72,256]{1,0:T(8,128)S(1)} %add_add_fusion._.refs_0_), channel_id=1, source_target_pairs={{0,12},{1,13},{2,14},{3,15},{4,8},{5,9},{6,10},{7,11},{8,4},{9,5},... | collective-permute-start | bytes 221192 | tf_op jit(solution)/shard_map/ppermute | solution.py:543
  45.9 5.7 %collective-permute-start.12 = (f32[72,256]{1,0:T(8,128)S(1)}, f32[72,256]{1,0:T(8,128)S(1)}, u32[]{:S(2)}, u32[]{:S(2)}) collective-permute-start(f32[72,256]{1,0:T(8,128)S(1)} %add_add_fusion._.refs_0_), channel_id=1, source_target_pairs={{0,8},{1,9},{2,10},{3,11},{4,12},{5,13},{6,14},{7,15},{8,0},{9,1},... | collective-permute-start | bytes 221192 | tf_op jit(solution)/shard_map/ppermute | solution.py:543
  45.9 5.9 %collective-permute-start.13 = (f32[72,256]{1,0:T(8,128)S(1)}, f32[72,256]{1,0:T(8,128)S(1)}, u32[]{:S(2)}, u32[]{:S(2)}) collective-permute-start(f32[72,256]{1,0:T(8,128)S(1)} %add_add_fusion._.refs_0_), channel_id=1, source_target_pairs={{0,4},{1,5},{2,6},{3,7},{4,0},{5,1},{6,2},{7,3},{8,12},{9,13},{10,... | collective-permute-start | bytes 221192 | tf_op jit(solution)/shard_map/ppermute | solution.py:543
  50.0 3.8 %collective-permute-start.19 = (f32[128,256]{1,0:T(8,128)S(1)}, f32[128,256]{1,0:T(8,128)S(1)}, u32[]{:S(2)}, u32[]{:S(2)}) collective-permute-start(f32[128,256]{1,0:T(8,128)S(1)} %shard_map.154.own_ref), channel_id=1, source_target_pairs={{0,1},{1,0},{2,3},{3,2},{4,5},{5,4},{6,7},{7,6},{8,9},{9,8},{10,11... | collective-permute-start | bytes 393224 | tf_op jit(solution)/shard_map/ppermute | solution.py:543
  51.9 2.9 %collective-permute-start.14 = (f32[72,256]{1,0:T(8,128)S(1)}, f32[72,256]{1,0:T(8,128)S(1)}, u32[]{:S(2)}, u32[]{:S(2)}) collective-permute-start(f32[72,256]{1,0:T(8,128)S(1)} %shard_map.152._.m0), channel_id=1, source_target_pairs={{0,1},{1,0},{2,3},{3,2},{4,5},{5,4},{6,7},{7,6},{8,9},{9,8},{10,11... | collective-permute-start | bytes 221192 | tf_op jit(solution)/shard_map/ppermute | solution.py:543
  51.9 5.1 %collective-permute-start.15 = (f32[72,256]{1,0:T(8,128)S(1)}, f32[72,256]{1,0:T(8,128)S(1)}, u32[]{:S(2)}, u32[]{:S(2)}) collective-permute-start(f32[72,256]{1,0:T(8,128)S(1)} %shard_map.152._.m0), channel_id=1, source_target_pairs={{0,2},{1,3},{2,0},{3,1},{4,6},{5,7},{6,4},{7,5},{8,10},{9,11},{10,... | collective-permute-start | bytes 221192 | tf_op jit(solution)/shard_map/ppermute | solution.py:543
  52.1 5.6 %collective-permute-start.16 = (f32[72,256]{1,0:T(8,128)S(1)}, f32[72,256]{1,0:T(8,128)S(1)}, u32[]{:S(2)}, u32[]{:S(2)}) collective-permute-start(f32[72,256]{1,0:T(8,128)S(1)} %shard_map.152._.m0), channel_id=1, source_target_pairs={{0,3},{1,2},{2,1},{3,0},{4,7},{5,6},{6,5},{7,4},{8,11},{9,10},{10,... | collective-permute-start | bytes 221192 | tf_op jit(solution)/shard_map/ppermute | solution.py:543
  (1 other events, 8.7 us)

commit v12 on v11

--- a/solution.py
+++ b/solution.py
@@ -108,7 +108,7 @@
     depth = width // heads
     hm = heads * slices
     rows = feats_ref.shape[0]
-    piece = min(sub_block, rows)
+    piece = min(2 * sub_block, rows)
     count = rows // piece
     small = [
         pltpu.make_async_copy(source, target, sems.at[i])
@@ -280,11 +280,12 @@
     w_cat_ref,
     w_out_ref,
     mw_ref,
-    mixed_t_ref,
     dr_ref,
     drt_ref,
     dn_ref,
-    grad_qkv_ref,
+    mixed_ref,
+    tokens_ref,
+    d_qkv_ref,
     pack,
 ):
     width = w_out_ref.shape[0]
@@ -348,7 +349,8 @@
     diagonal_t = same_block(width, hm, depth, slices)
     mixed_block = jnp.where(diagonal, nt(mixed_b, spread_d), 0.0).astype(bf16)
     mw_ref[...] = nn(mixed_block, w_out_ref[...]).astype(bf16)
-    mixed_t_ref[...] = jnp.where(diagonal_t, nt(spread_d, mixed_b), 0.0).astype(bf16)
+    mixed_ref[...] = mixed_b
+    tokens_ref[...] = tokens
 
     d_probs = nt(g_left, v_right)
     d_v = times_pair(tn, probs, g_pair)
@@ -356,6 +358,7 @@
     d_q = times_pair(nn, d_scores, k_pair)
     d_k = times_pair(tn, d_scores, q_pair)
     d_qkv = d_q + pltpu.roll(d_k, depth, 1) + pltpu.roll(d_v, 2 * depth, 1)
+    d_qkv_ref[...] = d_qkv
     d_high, d_low = two_pieces(d_qkv)
     d_tokens = nt(d_high, w_cat) + nt(d_low, w_cat)
     raw = raw[:, 0:depth]
@@ -365,12 +368,6 @@
     spread_d = spread_matrix(width, depth)
     dr_ref[...] = jnp.where(diagonal, nt(d_raw_b, spread_d), 0.0).astype(bf16)
     drt_ref[...] = jnp.where(diagonal_t, nt(spread_d, d_raw_b), 0.0).astype(bf16)
-
-    t_high, t_low = two_pieces(tokens)
-    grads = tn(t_high, d_high) + tn(t_high, d_low) + tn(t_low, d_high)
-    for i in range(3):
-        at = pltpu.roll(grads, 128 - i * depth, 1) if i else grads
-        grad_qkv_ref[i] = at[0:depth, 0:depth]
 
 
 def backward_kernel(
@@ -498,14 +495,40 @@
     ).astype(bf16)
 
 
-def grad_out_kernel(own_ref, other_ref, mixed_t_ref, _, grad_out_ref, token_ref, whole):
+def grad_out_kernel(
+    heads,
+    slices,
+    own_ref,
+    other_ref,
+    mixed_ref,
+    tokens_ref,
+    d_qkv_ref,
+    _,
+    grad_out_ref,
+    grad_qkv_ref,
+    token_ref,
+    whole,
+):
     token_ref[...] = jnp.zeros_like(token_ref)
+    hm = heads * slices
+    depth = grad_qkv_ref.shape[1]
+    width = heads * depth
+    t_high, t_low = two_pieces(tokens_ref[...])
+    d_high, d_low = two_pieces(d_qkv_ref[...])
+    grads = tn(t_high, d_high) + tn(t_high, d_low) + tn(t_low, d_high)
+    for i in range(3):
+        at = pltpu.roll(grads, 128 - i * depth, 1) if i else grads
+        grad_qkv_ref[i] = at[0:depth, 0:depth]
+    spread_d = jnp.where(
+        (rows_of((width, 128)) & (depth - 1)) == cols_of((width, 128)), 1.0, 0.0
+    ).astype(bf16)
+    diagonal_t = same_block(width, hm, depth, slices)
+    mixed_t = jnp.where(diagonal_t, nt(spread_d, mixed_ref[...]), 0.0).astype(bf16)
     place = group_place() & 1
     rows = own_ref.shape[0]
     for k, part in enumerate((own_ref, other_ref)):
         whole[pl.ds(pl.multiple_of((place ^ k) * rows, 8), rows), :] = part[...]
     high, low = two_pieces(whole[...])
-    mixed_t = mixed_t_ref[...]
     grad_out_ref[...] = nn(mixed_t, high) + nn(mixed_t, low)
 
 
@@ -676,22 +699,23 @@
     wc_sum = sum_behind([wc_sum, wc_got], own)
     own = sum_over_groups(own, 8, count)
     other = exchange(own, 1, count)
-    stride = 8
+    stride = 4
     wc_got = exchange(wc_sum, stride, count)
-    while 2 * stride < count:
+    while 4 * stride < count:
         wc_sum = wc_sum + wc_got
         stride *= 2
         wc_got = exchange(wc_sum, stride, count)
 
-    mw, mixed_t, dr, drt, dn, grad_qkv = pl.pallas_call(
+    mw, dr, drt, dn, mixed, tokens, d_qkv = pl.pallas_call(
         functools.partial(tokens_kernel, heads, slices),
         out_shape=[
             near((hm, width), bf16),
-            near((width, hm), bf16),
             near((hm, width), bf16),
             near((width, hm), bf16),
             near((hm, 128), f32),
-            like((3, depth, depth), f32),
+            near((hm, 128), bf16),
+            near((hm, 128), f32),
+            near((hm, 128), f32),
         ],
         scratch_shapes=[pltpu.VMEM((2,) + half, f32)],
         compiler_params=params(16, False),
@@ -715,7 +739,7 @@
 
     mid_total = scatter_group(sends, count)
     wc_sum = sum_behind([wc_sum, wc_got], sends[1])
-    wc_got = exchange(wc_sum, 4, count)
+    wc_got = exchange(wc_sum, count // 2, count)
 
     block = min(1024, rows)
     grid, by_rows = blocks(block)
@@ -738,15 +762,19 @@
     wc_sum = sum_behind([wc_sum, wc_got], token)
     wc_other = exchange(wc_sum, 1, count)
     mid_total = sum_over_groups(mid_total, group, count, token)
-    grad_w_out, token_out = pl.pallas_call(
-        grad_out_kernel,
-        in_specs=[whole] * 3 + [pl.BlockSpec(memory_space=pl.ANY)],
-        out_specs=[whole] * 2,
-        out_shape=[like((width, width), f32), like((8, 128), f32)],
+    grad_w_out, grad_qkv, token_out = pl.pallas_call(
+        functools.partial(grad_out_kernel, heads, slices),
+        in_specs=[whole] * 5 + [pl.BlockSpec(memory_space=pl.ANY)],
+        out_specs=[whole] * 3,
+        out_shape=[
+            like((width, width), f32),
+            like((3, depth, depth), f32),
+            like((8, 128), f32),
+        ],
         scratch_shapes=[pltpu.VMEM((hm, width), f32)],
         compiler_params=params(8, False),
         cost_estimate=cost(4 * width**3, 3 * width * width * 4),
-    )(wc_sum, wc_other, mixed_t, mid_total)
+    )(wc_sum, wc_other, mixed, tokens, d_qkv, mid_total)
 
     mid_parts = gather_group(mid_total, count)
     grad_w_mid, grad_w_slice, grad_temp = pl.pallas_call(

time: 58.7 us -> 56.2 us (0.957)
  starting transfers between devices: 25.7 us -> 22.5 us
  waiting for transfers between devices: 9.89 us -> 11.8 us
  Pallas kernels: 21.4 us -> 20.2 us
    ppermute x20, starting transfers between devices: 25.7 us -> 22.5 us  [exchange(): return lax.ppermute(x, 'node', [(i, i ^ k) for i in range(count)])]
    ppermute x20, waiting for transfers between devices: 9.89 us -> 11.8 us  [exchange(): return lax.ppermute(x, 'node', [(i, i ^ k) for i in range(count)])]
    pallas_call x1, Pallas kernels: 3.1 us -> 2.29 us  [shards(): pl.pallas_call(functools.partial(tokens_kernel, heads, slices), out_shape...]
    pallas_call x1, Pallas kernels: 7.27 us -> 6.68 us  [shards(): pl.pallas_call(functools.partial(stats_kernel, heads, slices), in_specs=[...]
where the time goes in v12:
time: 56.2 us; the launch traced here: 56 us
  starting transfers between devices  22.5 us (40%)
  Pallas kernels  20.2 us (36%)
  waiting for transfers between devices  11.8 us (21%)
  between operations  1.44 us (3%)
    ppermute x20, starting transfers between devices, exchange(): return lax.ppermute(x, 'node', [(i, i ^ k) for i in range(count)])  22.5 us
    ppermute x20, waiting for transfers between devices, exchange(): return lax.ppermute(x, 'node', [(i, i ^ k) for i in range(count)])  11.8 us
    pallas_call x1, Pallas kernels, shards(): pl.pallas_call(functools.partial(stats_kernel, heads, slices), in_specs=[...  6.68 us
    pallas_call x1, Pallas kernels, shards(): pl.pallas_call(functools.partial(backward_kernel, heads, slices), in_spec...  4.87 us
    pallas_call x1, Pallas kernels, shards(): pl.pallas_call(rows_kernel, grid=grid, in_specs=[whole, whole, whole, ful...  3.41 us
    pallas_call x1, Pallas kernels, shards(): pl.pallas_call(functools.partial(tokens_kernel, heads, slices), out_shape...  2.29 us
    pallas_call x1, Pallas kernels, shards(): pl.pallas_call(functools.partial(grad_out_kernel, heads, slices), in_spec...  1.14 us
  transfers between devices with their start and end apart: 20, of which 10 were waited for; matrix products, arithmetic and copies ran while one was open for 0% of the time, Pallas kernels for 23%

profile of v12, /device:TPU:0, one launch (start us, length us, event | category | flops | bytes accessed | tf_op | source)
XLA Modules:
  0.0 56.0 jit_solution(11827908803178667083)
XLA Ops:
  1.3 6.7 %shard_map.144 = (bf16[4096,256]{1,0:T(8,128)(2,1)S(1)}, bf16[256,4096]{1,0:T(8,128)(2,1)S(1)}, f32[24,4096]{1,0:T(8,128)S(1)}, bf16[272,256]{1,0:T(8,128)(2,1)S...) custom-call(s32[1]{0:T(128)S(6)} %copy.16.owned_ref, ...), custom_call_target="tpu_custom_call" | custom-call | flops 2147483648 | bytes 8388608 | tf_op jit(solution)/shard_map/pallas_call | solution.py:649
  8.6 1.1 %collective-permute-done = f32[72,128]{1,0:T(8,128)S(1)} collective-permute-done((f32[72,128]{1,0:T(8,128)S(1)}, f32[72,128]{1,0:T(8,128)S(1)}, u32[]{:S(2)}, u32[]{:S(2)}) %collective-permute-start) | collective-permute-done | bytes 36896 | tf_op jit(solution)/shard_map/ppermute | solution.py:566
  9.7 3.7 %collective-permute-start.1 = (f32[72,128]{1,0:T(8,128)S(1)}, f32[72,128]{1,0:T(8,128)S(1)}, u32[]{:S(2)}, u32[]{:S(2)}) collective-permute-start(f32[72,128]{1,0:T(8,128)S(1)} %add.15._.refs_0_.refs_2_), channel_id=1, source_target_pairs={{0,6},{1,7},{2,4},{3,5},{4,2},{5,3},{6,0},{7,1},{8,14},{9,15},{10,... | collective-permute-start | bytes 110600 | tf_op jit(solution)/shard_map/ppermute | solution.py:566
  14.1 1.9 %collective-permute-start.7 = (f32[128,256]{1,0:T(8,128)S(1)}, f32[128,256]{1,0:T(8,128)S(1)}, u32[]{:S(2)}, u32[]{:S(2)}) collective-permute-start(f32[128,256]{1,0:T(8,128)S(1)} %shard_map.148.refs_0_), channel_id=1, source_target_pairs={{0,2},{1,3},{2,0},{3,1},{4,6},{5,7},{6,4},{7,5},{8,10},{9,11},{10,... | collective-permute-start | bytes 393224 | tf_op jit(solution)/shard_map/ppermute | solution.py:566
  16.0 1.0 %shard_map.145 = (f32[256,4096]{1,0:T(8,128)S(1)}, f32[256,4096]{1,0:T(8,128)S(1)}, bf16[256,256]{1,0:T(8,128)(2,1)S(1)}, bf16[32,128]{1,0:T(8,128)(2,1)S(1)}, f32[8,128]{1,0:T(8,128)S(1)}) custom-call(bf16[4096,256]{1,0:T(8,128)(2,1)S(1)} %get-tuple-element.45.mid_ref, bf16[272,256]{1,0:T(8,128)(2,1)S(1)} %get-tuple-element.46.sw_ref, ...), custom_call_target="tpu_custom_call" | custom-call | flops 1610612736 | bytes 4096 | tf_op jit(solution)/shard_map/pallas_call | solution.py:683
  17.4 0.9 %collective-permute-done.3.refs_3_ = f32[72,128]{1,0:T(8,128)S(1)} collective-permute-done((f32[72,128]{1,0:T(8,128)S(1)}, f32[72,128]{1,0:T(8,128)S(1)}, u32[]{:S(2)}, u32[]{:S(2)}) %collective-permute-start.3) | collective-permute-done | bytes 36896 | tf_op jit(solution)/shard_map/ppermute | solution.py:566
  18.3 2.7 %collective-permute-start.4 = (f32[72,128]{1,0:T(8,128)S(1)}, f32[72,128]{1,0:T(8,128)S(1)}, u32[]{:S(2)}, u32[]{:S(2)}) collective-permute-start(f32[72,128]{1,0:T(8,128)S(1)} %shard_map.146.refs_2_), channel_id=1, source_target_pairs={{0,8},{1,9},{2,10},{3,11},{4,12},{5,13},{6,14},{7,15},{8,0},{9,1},... | collective-permute-start | bytes 110600 | tf_op jit(solution)/shard_map/ppermute | solution.py:566
  20.9 1.6 %collective-permute-start.17 = (f32[128,256]{1,0:T(8,128)S(1)}, f32[128,256]{1,0:T(8,128)S(1)}, u32[]{:S(2)}, u32[]{:S(2)}) collective-permute-start(f32[128,256]{1,0:T(8,128)S(1)} %shard_map.149._.refs_0_), channel_id=1, source_target_pairs={{0,4},{1,5},{2,6},{3,7},{4,0},{5,1},{6,2},{7,3},{8,12},{9,13},{10,... | collective-permute-start | bytes 393224 | tf_op jit(solution)/shard_map/ppermute | solution.py:566
  22.6 0.7 %collective-permute-done.4 = f32[72,128]{1,0:T(8,128)S(1)} collective-permute-done((f32[72,128]{1,0:T(8,128)S(1)}, f32[72,128]{1,0:T(8,128)S(1)}, u32[]{:S(2)}, u32[]{:S(2)}) %collective-permute-start.4) | collective-permute-done | bytes 36896 | tf_op jit(solution)/shard_map/ppermute | solution.py:566
  23.3 1.2 %collective-permute-done.5.got_ref = f32[72,128]{1,0:T(8,128)S(1)} collective-permute-done((f32[72,128]{1,0:T(8,128)S(1)}, f32[72,128]{1,0:T(8,128)S(1)}, u32[]{:S(2)}, u32[]{:S(2)}) %collective-permute-start.5) | collective-permute-done | bytes 36896 | tf_op jit(solution)/shard_map/ppermute | solution.py:566
  24.5 2.3 %shard_map.147 = (bf16[256,256]{1,0:T(8,128)(2,1)S(1)}, bf16[256,256]{1,0:T(8,128)(2,1)S(1)}, bf16[256,256]{1,0:T(8,128)(2,1)S(1)}, f32[256,128]{1,0:T(8,128)S(1...) custom-call(f32[72,128]{1,0:T(8,128)S(1)} %add.16.own_ref, ...), custom_call_target="tpu_custom_call" | custom-call | flops 50331648 | bytes 1048576 | tf_op jit(solution)/shard_map/pallas_call | solution.py:709
  26.8 4.9 %shard_map.150 = (bf16[256,4096]{1,0:T(8,128)(2,1)S(1)}, f32[72,256]{1,0:T(8,128)S(1)}, f32[72,256]{1,0:T(8,128)S(1)}, f32[72,256]{1,0:T(8,128)S(1)}, f32[72,256]{1,0:T(8,128)S(1)}) custom-call(f32[24,4096]{1,0:T(8,128)S(1)} %get-tuple-element.44.aux_ref, bf16[256,4096]{1,0:T(8,128)(2,1)S(1)} %get-tuple-element.43.wt_ref, ...), custom_call_target="tpu_custom_call" | custom-call | flops 161061280 | bytes 1048576 | tf_op jit(solution)/shard_map/pallas_call | solution.py:725
  32.0 1.9 %collective-permute-start.9 = (f32[72,256]{1,0:T(8,128)S(1)}, f32[72,256]{1,0:T(8,128)S(1)}, u32[]{:S(2)}, u32[]{:S(2)}) collective-permute-start(f32[72,256]{1,0:T(8,128)S(1)} %get-tuple-element.65), channel_id=1, source_target_pairs={{0,2},{1,3},{2,0},{3,1},{4,6},{5,7},{6,4},{7,5},{8,10},{9,11},{10,... | collective-permute-start | bytes 221192 | tf_op jit(solution)/shard_map/ppermute | solution.py:566
  33.9 2.6 %collective-permute-start.18 = (f32[128,256]{1,0:T(8,128)S(1)}, f32[128,256]{1,0:T(8,128)S(1)}, u32[]{:S(2)}, u32[]{:S(2)}) collective-permute-start(f32[128,256]{1,0:T(8,128)S(1)} %shard_map.153.refs_0_), channel_id=1, source_target_pairs={{0,8},{1,9},{2,10},{3,11},{4,12},{5,13},{6,14},{7,15},{8,0},{9,1},... | collective-permute-start | bytes 393224 | tf_op jit(solution)/shard_map/ppermute | solution.py:566
  36.5 1.4 %collective-permute-done.9 = f32[72,256]{1,0:T(8,128)S(1)} collective-permute-done((f32[72,256]{1,0:T(8,128)S(1)}, f32[72,256]{1,0:T(8,128)S(1)}, u32[]{:S(2)}, u32[]{:S(2)}) %collective-permute-start.9) | collective-permute-done | bytes 73760 | tf_op jit(solution)/shard_map/ppermute | solution.py:566
  37.9 3.9 %collective-permute-start.11 = (f32[72,256]{1,0:T(8,128)S(1)}, f32[72,256]{1,0:T(8,128)S(1)}, u32[]{:S(2)}, u32[]{:S(2)}) collective-permute-start(f32[72,256]{1,0:T(8,128)S(1)} %add_add_fusion._.refs_0_), channel_id=1, source_target_pairs={{0,12},{1,13},{2,14},{3,15},{4,8},{5,9},{6,10},{7,11},{8,4},{9,5},... | collective-permute-start | bytes 221192 | tf_op jit(solution)/shard_map/ppermute | solution.py:566
  42.5 3.4 %shard_map.151 = (bf16[4096,256]{1,0:T(8,128)(2,1)}, bf16[4096,256]{1,0:T(8,128)(2,1)}, f32[8,128]{1,0:T(8,128)S(1)}) custom-call(bf16[256,4096]{1,0:T(8,128)(2,1)S(1)} %get-tuple-element.43.wt_ref, bf16[256,4096]{1,0:T(8,128)(2,1)S(1)} %get-tuple-element.62.dmt_ref, bf16[256,256]{1,0:T(8,128)(2,1)S(1)} %get-tuple-element.56.mw_ref, ...), custom_call_target="tpu_custom_call" | custom-call | flops 1073741824 | bytes 8388608 | tf_op jit(solution)/shard_map/pallas_call | solution.py:746
  45.9 1.4 %collective-permute-done.18.refs_1_ = f32[128,256]{1,0:T(8,128)S(1)} collective-permute-done((f32[128,256]{1,0:T(8,128)S(1)}, f32[128,256]{1,0:T(8,128)S(1)}, u32[]{:S(2)}, u32[]{:S(2)}) %collective-permute-start.18) | collective-permute-done | bytes 131104 | tf_op jit(solution)/shard_map/ppermute | solution.py:566
  47.4 2.0 %collective-permute-done.12.refs_2_ = f32[72,256]{1,0:T(8,128)S(1)} collective-permute-done((f32[72,256]{1,0:T(8,128)S(1)}, f32[72,256]{1,0:T(8,128)S(1)}, u32[]{:S(2)}, u32[]{:S(2)}) %collective-permute-start.12) | collective-permute-done | bytes 73760 | tf_op jit(solution)/shard_map/ppermute | solution.py:566
  50.1 1.2 %collective-permute-start.16 = (f32[72,256]{1,0:T(8,128)S(1)}, f32[72,256]{1,0:T(8,128)S(1)}, u32[]{:S(2)}, u32[]{:S(2)}) collective-permute-start(f32[72,256]{1,0:T(8,128)S(1)} %shard_map.152._.m0), channel_id=1, source_target_pairs={{0,3},{1,2},{2,1},{3,0},{4,7},{5,6},{6,5},{7,4},{8,11},{9,10},{10,... | collective-permute-start | bytes 221192 | tf_op jit(solution)/shard_map/ppermute | solution.py:566
  51.3 1.1 %shard_map.155 = (f32[256,256]{1,0:T(8,128)}, f32[3,32,32]{2,1,0:T(8,128)}, f32[8,128]{1,0:T(8,128)S(1)}) custom-call(f32[128,256]{1,0:T(8,128)S(1)} %shard_map.154.own_ref, f32[128,256]{1,0:T(8,128)S(1)} %collective-permute-done.19.other_ref, bf16[256,128]{1,0:T(8,128)(2,1)S(1)} %get-tuple-element.70.mixed_ref, ...), custom_call_target="tpu_custom_call" | custom-call | flops 67108864 | bytes 786432 | tf_op jit(solution)/shard_map/pallas_call | solution.py:765
  52.4 2.1 %collective-permute-done.15.m2 = f32[72,256]{1,0:T(8,128)S(1)} collective-permute-done((f32[72,256]{1,0:T(8,128)S(1)}, f32[72,256]{1,0:T(8,128)S(1)}, u32[]{:S(2)}, u32[]{:S(2)}) %collective-permute-start.15) | collective-permute-done | bytes 73760 | tf_op jit(solution)/shard_map/ppermute | solution.py:566
  54.5 0.7 %collective-permute-done.16.m3 = f32[72,256]{1,0:T(8,128)S(1)} collective-permute-done((f32[72,256]{1,0:T(8,128)S(1)}, f32[72,256]{1,0:T(8,128)S(1)}, u32[]{:S(2)}, u32[]{:S(2)}) %collective-permute-start.16) | collective-permute-done | bytes 73760 | tf_op jit(solution)/shard_map/ppermute | solution.py:566
  55.2 0.7 %shard_map.156 = (f32[256,256]{1,0:T(8,128)}, f32[32,32]{1,0:T(8,128)}, f32[1,32]{1,0:T(1,128)}) custom-call(f32[72,256]{1,0:T(8,128)S(1)} %shard_map.152._.m0, f32[72,256]{1,0:T(8,128)S(1)} %collective-permute-done.14.m1, f32[72,256]{1,0:T(8,128)S(1)} %collective-permute-done.15.m2, f32[72,256]{1,0:T(8,128)S(1)} %collective-permute-done.16.m3, ...), custom_call_target="tpu_custom_call" | custom-call | bytes 524288 | tf_op jit(solution)/shard_map/pallas_call | solution.py:780
  (42 shorter events, 3.5 us)
Async XLA Ops:
  1.3 14.7 %copy-start.3 = (bf16[3,32,32]{2,1,0:T(8,128)(2,1)S(1)}, bf16[3,32,32]{2,1,0:T(8,128)(2,1)}, u32[]{:S(2)}) copy-start(bf16[3,32,32]{2,1,0:T(8,128)(2,1)} %w_qkv_ref.1) | copy-start | bytes 18436
  1.3 14.7 %copy-start.4 = (bf16[32,32]{1,0:T(8,128)(2,1)S(1)}, bf16[32,32]{1,0:T(8,128)(2,1)}, u32[]{:S(2)}) copy-start(bf16[32,32]{1,0:T(8,128)(2,1)} %w_slice_ref.1) | copy-start | bytes 6148
  8.0 6.1 %collective-permute-start.6 = (f32[128,256]{1,0:T(8,128)S(1)}, f32[128,256]{1,0:T(8,128)S(1)}, u32[]{:S(2)}, u32[]{:S(2)}) collective-permute-start(f32[128,256]{1,0:T(8,128)S(1)} %get-tuple-element.61), channel_id=1, source_target_pairs={{0,1},{1,0},{2,3},{3,2},{4,5},{5,4},{6,7},{7,6},{8,9},{9,8},{10,11... | collective-permute-start | bytes 393224 | tf_op jit(solution)/shard_map/ppermute | solution.py:566
  8.5 1.2 %collective-permute-start = (f32[72,128]{1,0:T(8,128)S(1)}, f32[72,128]{1,0:T(8,128)S(1)}, u32[]{:S(2)}, u32[]{:S(2)}) collective-permute-start(f32[72,128]{1,0:T(8,128)S(1)} %get-tuple-element.48), channel_id=1, source_target_pairs={{0,1},{1,0},{2,3},{3,2},{4,5},{5,4},{6,7},{7,6},{8,9},{9,8},{10,11... | collective-permute-start | bytes 110600 | tf_op jit(solution)/shard_map/ppermute | solution.py:566
  9.7 7.3 %collective-permute-start.1 = (f32[72,128]{1,0:T(8,128)S(1)}, f32[72,128]{1,0:T(8,128)S(1)}, u32[]{:S(2)}, u32[]{:S(2)}) collective-permute-start(f32[72,128]{1,0:T(8,128)S(1)} %add.15._.refs_0_.refs_2_), channel_id=1, source_target_pairs={{0,6},{1,7},{2,4},{3,5},{4,2},{5,3},{6,0},{7,1},{8,14},{9,15},{10,... | collective-permute-start | bytes 110600 | tf_op jit(solution)/shard_map/ppermute | solution.py:566
  13.4 4.0 %collective-permute-start.2 = (f32[72,128]{1,0:T(8,128)S(1)}, f32[72,128]{1,0:T(8,128)S(1)}, u32[]{:S(2)}, u32[]{:S(2)}) collective-permute-start(f32[72,128]{1,0:T(8,128)S(1)} %add.15._.refs_0_.refs_2_), channel_id=1, source_target_pairs={{0,4},{1,5},{2,6},{3,7},{4,0},{5,1},{6,2},{7,3},{8,12},{9,13},{10,... | collective-permute-start | bytes 110600 | tf_op jit(solution)/shard_map/ppermute | solution.py:566
  13.9 4.4 %collective-permute-start.3 = (f32[72,128]{1,0:T(8,128)S(1)}, f32[72,128]{1,0:T(8,128)S(1)}, u32[]{:S(2)}, u32[]{:S(2)}) collective-permute-start(f32[72,128]{1,0:T(8,128)S(1)} %add.15._.refs_0_.refs_2_), channel_id=1, source_target_pairs={{0,2},{1,3},{2,0},{3,1},{4,6},{5,7},{6,4},{7,5},{8,10},{9,11},{10,... | collective-permute-start | bytes 110600 | tf_op jit(solution)/shard_map/ppermute | solution.py:566
  14.1 6.8 %collective-permute-start.7 = (f32[128,256]{1,0:T(8,128)S(1)}, f32[128,256]{1,0:T(8,128)S(1)}, u32[]{:S(2)}, u32[]{:S(2)}) collective-permute-start(f32[128,256]{1,0:T(8,128)S(1)} %shard_map.148.refs_0_), channel_id=1, source_target_pairs={{0,2},{1,3},{2,0},{3,1},{4,6},{5,7},{6,4},{7,5},{8,10},{9,11},{10,... | collective-permute-start | bytes 393224 | tf_op jit(solution)/shard_map/ppermute | solution.py:566
  16.0 10.8 %copy-start.2 = (bf16[32]{0:T(256)(128)(2,1)S(1)}, bf16[32]{0:T(256)(128)(2,1)}, u32[]{:S(2)}) copy-start(bf16[32]{0:T(256)(128)(2,1)} %param.15) | copy-start | bytes 196
  18.3 5.0 %collective-permute-start.4 = (f32[72,128]{1,0:T(8,128)S(1)}, f32[72,128]{1,0:T(8,128)S(1)}, u32[]{:S(2)}, u32[]{:S(2)}) collective-permute-start(f32[72,128]{1,0:T(8,128)S(1)} %shard_map.146.refs_2_), channel_id=1, source_target_pairs={{0,8},{1,9},{2,10},{3,11},{4,12},{5,13},{6,14},{7,15},{8,0},{9,1},... | collective-permute-start | bytes 110600 | tf_op jit(solution)/shard_map/ppermute | solution.py:566
  20.9 13.0 %collective-permute-start.17 = (f32[128,256]{1,0:T(8,128)S(1)}, f32[128,256]{1,0:T(8,128)S(1)}, u32[]{:S(2)}, u32[]{:S(2)}) collective-permute-start(f32[128,256]{1,0:T(8,128)S(1)} %shard_map.149._.refs_0_), channel_id=1, source_target_pairs={{0,4},{1,5},{2,6},{3,7},{4,0},{5,1},{6,2},{7,3},{8,12},{9,13},{10,... | collective-permute-start | bytes 393224 | tf_op jit(solution)/shard_map/ppermute | solution.py:566
  23.3 1.2 %collective-permute-start.5 = (f32[72,128]{1,0:T(8,128)S(1)}, f32[72,128]{1,0:T(8,128)S(1)}, u32[]{:S(2)}, u32[]{:S(2)}) collective-permute-start(f32[72,128]{1,0:T(8,128)S(1)} %add.16.own_ref), channel_id=1, source_target_pairs={{0,1},{1,0},{2,3},{3,2},{4,5},{5,4},{6,7},{7,6},{8,9},{9,8},{10,11... | collective-permute-start | bytes 110600 | tf_op jit(solution)/shard_map/ppermute | solution.py:566
  26.8 15.6 %copy-start = (bf16[256,256]{1,0:T(8,128)(2,1)S(1)}, bf16[256,256]{1,0:T(8,128)(2,1)}, u32[]{:S(2)}) copy-start(bf16[256,256]{1,0:T(8,128)(2,1)} %w_mid_ref.1) | copy-start | bytes 393220
  31.7 4.8 %collective-permute-start.10 = (f32[72,256]{1,0:T(8,128)S(1)}, f32[72,256]{1,0:T(8,128)S(1)}, u32[]{:S(2)}, u32[]{:S(2)}) collective-permute-start(f32[72,256]{1,0:T(8,128)S(1)} %get-tuple-element.66), channel_id=1, source_target_pairs={{0,3},{1,2},{2,1},{3,0},{4,7},{5,6},{6,5},{7,4},{8,11},{9,10},{10,... | collective-permute-start | bytes 221192 | tf_op jit(solution)/shard_map/ppermute | solution.py:566
  31.8 4.8 %collective-permute-start.8 = (f32[72,256]{1,0:T(8,128)S(1)}, f32[72,256]{1,0:T(8,128)S(1)}, u32[]{:S(2)}, u32[]{:S(2)}) collective-permute-start(f32[72,256]{1,0:T(8,128)S(1)} %get-tuple-element.64.refs_2_), channel_id=1, source_target_pairs={{0,1},{1,0},{2,3},{3,2},{4,5},{5,4},{6,7},{7,6},{8,9},{9,8},{10,11... | collective-permute-start | bytes 221192 | tf_op jit(solution)/shard_map/ppermute | solution.py:566
  32.0 5.9 %collective-permute-start.9 = (f32[72,256]{1,0:T(8,128)S(1)}, f32[72,256]{1,0:T(8,128)S(1)}, u32[]{:S(2)}, u32[]{:S(2)}) collective-permute-start(f32[72,256]{1,0:T(8,128)S(1)} %get-tuple-element.65), channel_id=1, source_target_pairs={{0,2},{1,3},{2,0},{3,1},{4,6},{5,7},{6,4},{7,5},{8,10},{9,11},{10,... | collective-permute-start | bytes 221192 | tf_op jit(solution)/shard_map/ppermute | solution.py:566
  33.9 13.3 %collective-permute-start.18 = (f32[128,256]{1,0:T(8,128)S(1)}, f32[128,256]{1,0:T(8,128)S(1)}, u32[]{:S(2)}, u32[]{:S(2)}) collective-permute-start(f32[128,256]{1,0:T(8,128)S(1)} %shard_map.153.refs_0_), channel_id=1, source_target_pairs={{0,8},{1,9},{2,10},{3,11},{4,12},{5,13},{6,14},{7,15},{8,0},{9,1},... | collective-permute-start | bytes 393224 | tf_op jit(solution)/shard_map/ppermute | solution.py:566
  37.9 9.4 %collective-permute-start.11 = (f32[72,256]{1,0:T(8,128)S(1)}, f32[72,256]{1,0:T(8,128)S(1)}, u32[]{:S(2)}, u32[]{:S(2)}) collective-permute-start(f32[72,256]{1,0:T(8,128)S(1)} %add_add_fusion._.refs_0_), channel_id=1, source_target_pairs={{0,12},{1,13},{2,14},{3,15},{4,8},{5,9},{6,10},{7,11},{8,4},{9,5},... | collective-permute-start | bytes 221192 | tf_op jit(solution)/shard_map/ppermute | solution.py:566
  41.8 7.5 %collective-permute-start.12 = (f32[72,256]{1,0:T(8,128)S(1)}, f32[72,256]{1,0:T(8,128)S(1)}, u32[]{:S(2)}, u32[]{:S(2)}) collective-permute-start(f32[72,256]{1,0:T(8,128)S(1)} %add_add_fusion._.refs_0_), channel_id=1, source_target_pairs={{0,8},{1,9},{2,10},{3,11},{4,12},{5,13},{6,14},{7,15},{8,0},{9,1},... | collective-permute-start | bytes 221192 | tf_op jit(solution)/shard_map/ppermute | solution.py:566
  41.8 7.5 %collective-permute-start.13 = (f32[72,256]{1,0:T(8,128)S(1)}, f32[72,256]{1,0:T(8,128)S(1)}, u32[]{:S(2)}, u32[]{:S(2)}) collective-permute-start(f32[72,256]{1,0:T(8,128)S(1)} %add_add_fusion._.refs_0_), channel_id=1, source_target_pairs={{0,4},{1,5},{2,6},{3,7},{4,0},{5,1},{6,2},{7,3},{8,12},{9,13},{10,... | collective-permute-start | bytes 221192 | tf_op jit(solution)/shard_map/ppermute | solution.py:566
  47.3 4.0 %collective-permute-start.19 = (f32[128,256]{1,0:T(8,128)S(1)}, f32[128,256]{1,0:T(8,128)S(1)}, u32[]{:S(2)}, u32[]{:S(2)}) collective-permute-start(f32[128,256]{1,0:T(8,128)S(1)} %shard_map.154.own_ref), channel_id=1, source_target_pairs={{0,1},{1,0},{2,3},{3,2},{4,5},{5,4},{6,7},{7,6},{8,9},{9,8},{10,11... | collective-permute-start | bytes 393224 | tf_op jit(solution)/shard_map/ppermute | solution.py:566
  49.3 3.1 %collective-permute-start.14 = (f32[72,256]{1,0:T(8,128)S(1)}, f32[72,256]{1,0:T(8,128)S(1)}, u32[]{:S(2)}, u32[]{:S(2)}) collective-permute-start(f32[72,256]{1,0:T(8,128)S(1)} %shard_map.152._.m0), channel_id=1, source_target_pairs={{0,1},{1,0},{2,3},{3,2},{4,5},{5,4},{6,7},{7,6},{8,9},{9,8},{10,11... | collective-permute-start | bytes 221192 | tf_op jit(solution)/shard_map/ppermute | solution.py:566
  49.4 5.1 %collective-permute-start.15 = (f32[72,256]{1,0:T(8,128)S(1)}, f32[72,256]{1,0:T(8,128)S(1)}, u32[]{:S(2)}, u32[]{:S(2)}) collective-permute-start(f32[72,256]{1,0:T(8,128)S(1)} %shard_map.152._.m0), channel_id=1, source_target_pairs={{0,2},{1,3},{2,0},{3,1},{4,6},{5,7},{6,4},{7,5},{8,10},{9,11},{10,... | collective-permute-start | bytes 221192 | tf_op jit(solution)/shard_map/ppermute | solution.py:566
  50.1 5.1 %collective-permute-start.16 = (f32[72,256]{1,0:T(8,128)S(1)}, f32[72,256]{1,0:T(8,128)S(1)}, u32[]{:S(2)}, u32[]{:S(2)}) collective-permute-start(f32[72,256]{1,0:T(8,128)S(1)} %shard_map.152._.m0), channel_id=1, source_target_pairs={{0,3},{1,2},{2,1},{3,0},{4,7},{5,6},{6,5},{7,4},{8,11},{9,10},{10,... | collective-permute-start | bytes 221192 | tf_op jit(solution)/shard_map/ppermute | solution.py:566
  (1 other events, 8.5 us)

commit v13 on v12

--- a/solution.py
+++ b/solution.py
@@ -108,7 +108,7 @@
     depth = width // heads
     hm = heads * slices
     rows = feats_ref.shape[0]
-    piece = min(2 * sub_block, rows)
+    piece = min(4 * sub_block, rows)
     count = rows // piece
     small = [
         pltpu.make_async_copy(source, target, sems.at[i])
@@ -410,7 +410,7 @@
     temp = jnp.broadcast_to(temp_ref[...].astype(f32), (16, depth)).astype(bf16)
     same = (rows_of((depth, depth)) == cols_of((depth, depth))).astype(f32).astype(bf16)
     temp = nt(same, temp)[:, 0:1]
-    piece = min(sub_block, block)
+    piece = min(2 * sub_block, block)
     pieces = [slice(i * piece, (i + 1) * piece) for i in range(block // piece)]
 
     def products(at):

time: 56.2 us -> 56.5 us (level)
  transfers between devices with their start and end apart: 20 -> 20, of which waited for: 10 -> 10; matrix products, arithmetic and copies ran while one was open for 0% -> 0% of each run, Pallas kernels for 23% -> 22%
where the time goes in v13:
time: 56.5 us; the launch traced here: 56.2 us
  starting transfers between devices  22.4 us (40%)
  Pallas kernels  20.5 us (36%)
  waiting for transfers between devices  11.8 us (21%)
  between operations  1.44 us (3%)
    ppermute x20, starting transfers between devices, exchange(): return lax.ppermute(x, 'node', [(i, i ^ k) for i in range(count)])  22.4 us
    ppermute x20, waiting for transfers between devices, exchange(): return lax.ppermute(x, 'node', [(i, i ^ k) for i in range(count)])  11.8 us
    pallas_call x1, Pallas kernels, shards(): pl.pallas_call(functools.partial(stats_kernel, heads, slices), in_specs=[...  7.13 us
    pallas_call x1, Pallas kernels, shards(): pl.pallas_call(functools.partial(backward_kernel, heads, slices), in_spec...  4.72 us
    pallas_call x1, Pallas kernels, shards(): pl.pallas_call(rows_kernel, grid=grid, in_specs=[whole, whole, whole, ful...  3.41 us
    pallas_call x1, Pallas kernels, shards(): pl.pallas_call(functools.partial(tokens_kernel, heads, slices), out_shape...  2.29 us
    pallas_call x1, Pallas kernels, shards(): pl.pallas_call(functools.partial(grad_out_kernel, heads, slices), in_spec...  1.14 us
  transfers between devices with their start and end apart: 20, of which 10 were waited for; matrix products, arithmetic and copies ran while one was open for 0% of the time, Pallas kernels for 22%

profile of v13, /device:TPU:0, one launch (start us, length us, event | category | flops | bytes accessed | tf_op | source)
XLA Modules:
  0.0 56.2 jit_solution(8951251294437463189)
XLA Ops:
  1.3 7.1 %shard_map.144 = (bf16[4096,256]{1,0:T(8,128)(2,1)S(1)}, bf16[256,4096]{1,0:T(8,128)(2,1)S(1)}, f32[24,4096]{1,0:T(8,128)S(1)}, bf16[272,256]{1,0:T(8,128)(2,1)S...) custom-call(s32[1]{0:T(128)S(6)} %copy.16.owned_ref, ...), custom_call_target="tpu_custom_call" | custom-call | flops 2147483648 | bytes 8388608 | tf_op jit(solution)/shard_map/pallas_call | solution.py:649
  9.0 1.1 %collective-permute-done = f32[72,128]{1,0:T(8,128)S(1)} collective-permute-done((f32[72,128]{1,0:T(8,128)S(1)}, f32[72,128]{1,0:T(8,128)S(1)}, u32[]{:S(2)}, u32[]{:S(2)}) %collective-permute-start) | collective-permute-done | bytes 36896 | tf_op jit(solution)/shard_map/ppermute | solution.py:566
  10.2 3.7 %collective-permute-start.1 = (f32[72,128]{1,0:T(8,128)S(1)}, f32[72,128]{1,0:T(8,128)S(1)}, u32[]{:S(2)}, u32[]{:S(2)}) collective-permute-start(f32[72,128]{1,0:T(8,128)S(1)} %add.15._.refs_0_.refs_2_), channel_id=1, source_target_pairs={{0,6},{1,7},{2,4},{3,5},{4,2},{5,3},{6,0},{7,1},{8,14},{9,15},{10,... | collective-permute-start | bytes 110600 | tf_op jit(solution)/shard_map/ppermute | solution.py:566
  14.5 1.9 %collective-permute-start.7 = (f32[128,256]{1,0:T(8,128)S(1)}, f32[128,256]{1,0:T(8,128)S(1)}, u32[]{:S(2)}, u32[]{:S(2)}) collective-permute-start(f32[128,256]{1,0:T(8,128)S(1)} %shard_map.148.refs_0_), channel_id=1, source_target_pairs={{0,2},{1,3},{2,0},{3,1},{4,6},{5,7},{6,4},{7,5},{8,10},{9,11},{10,... | collective-permute-start | bytes 393224 | tf_op jit(solution)/shard_map/ppermute | solution.py:566
  16.4 1.0 %shard_map.145 = (f32[256,4096]{1,0:T(8,128)S(1)}, f32[256,4096]{1,0:T(8,128)S(1)}, bf16[256,256]{1,0:T(8,128)(2,1)S(1)}, bf16[32,128]{1,0:T(8,128)(2,1)S(1)}, f32[8,128]{1,0:T(8,128)S(1)}) custom-call(bf16[4096,256]{1,0:T(8,128)(2,1)S(1)} %get-tuple-element.45.mid_ref, bf16[272,256]{1,0:T(8,128)(2,1)S(1)} %get-tuple-element.46.sw_ref, ...), custom_call_target="tpu_custom_call" | custom-call | flops 1610612736 | bytes 4096 | tf_op jit(solution)/shard_map/pallas_call | solution.py:683
  17.8 0.9 %collective-permute-done.3.refs_3_ = f32[72,128]{1,0:T(8,128)S(1)} collective-permute-done((f32[72,128]{1,0:T(8,128)S(1)}, f32[72,128]{1,0:T(8,128)S(1)}, u32[]{:S(2)}, u32[]{:S(2)}) %collective-permute-start.3) | collective-permute-done | bytes 36896 | tf_op jit(solution)/shard_map/ppermute | solution.py:566
  18.7 2.7 %collective-permute-start.4 = (f32[72,128]{1,0:T(8,128)S(1)}, f32[72,128]{1,0:T(8,128)S(1)}, u32[]{:S(2)}, u32[]{:S(2)}) collective-permute-start(f32[72,128]{1,0:T(8,128)S(1)} %shard_map.146.refs_2_), channel_id=1, source_target_pairs={{0,8},{1,9},{2,10},{3,11},{4,12},{5,13},{6,14},{7,15},{8,0},{9,1},... | collective-permute-start | bytes 110600 | tf_op jit(solution)/shard_map/ppermute | solution.py:566
  21.4 1.6 %collective-permute-start.17 = (f32[128,256]{1,0:T(8,128)S(1)}, f32[128,256]{1,0:T(8,128)S(1)}, u32[]{:S(2)}, u32[]{:S(2)}) collective-permute-start(f32[128,256]{1,0:T(8,128)S(1)} %shard_map.149._.refs_0_), channel_id=1, source_target_pairs={{0,4},{1,5},{2,6},{3,7},{4,0},{5,1},{6,2},{7,3},{8,12},{9,13},{10,... | collective-permute-start | bytes 393224 | tf_op jit(solution)/shard_map/ppermute | solution.py:566
  23.0 0.7 %collective-permute-done.4 = f32[72,128]{1,0:T(8,128)S(1)} collective-permute-done((f32[72,128]{1,0:T(8,128)S(1)}, f32[72,128]{1,0:T(8,128)S(1)}, u32[]{:S(2)}, u32[]{:S(2)}) %collective-permute-start.4) | collective-permute-done | bytes 36896 | tf_op jit(solution)/shard_map/ppermute | solution.py:566
  23.7 1.2 %collective-permute-done.5.got_ref = f32[72,128]{1,0:T(8,128)S(1)} collective-permute-done((f32[72,128]{1,0:T(8,128)S(1)}, f32[72,128]{1,0:T(8,128)S(1)}, u32[]{:S(2)}, u32[]{:S(2)}) %collective-permute-start.5) | collective-permute-done | bytes 36896 | tf_op jit(solution)/shard_map/ppermute | solution.py:566
  24.9 2.3 %shard_map.147 = (bf16[256,256]{1,0:T(8,128)(2,1)S(1)}, bf16[256,256]{1,0:T(8,128)(2,1)S(1)}, bf16[256,256]{1,0:T(8,128)(2,1)S(1)}, f32[256,128]{1,0:T(8,128)S(1...) custom-call(f32[72,128]{1,0:T(8,128)S(1)} %add.16.own_ref, ...), custom_call_target="tpu_custom_call" | custom-call | flops 50331648 | bytes 1048576 | tf_op jit(solution)/shard_map/pallas_call | solution.py:709
  27.3 4.7 %shard_map.150 = (bf16[256,4096]{1,0:T(8,128)(2,1)S(1)}, f32[72,256]{1,0:T(8,128)S(1)}, f32[72,256]{1,0:T(8,128)S(1)}, f32[72,256]{1,0:T(8,128)S(1)}, f32[72,256]{1,0:T(8,128)S(1)}) custom-call(f32[24,4096]{1,0:T(8,128)S(1)} %get-tuple-element.44.aux_ref, bf16[256,4096]{1,0:T(8,128)(2,1)S(1)} %get-tuple-element.43.wt_ref, ...), custom_call_target="tpu_custom_call" | custom-call | flops 161061280 | bytes 1048576 | tf_op jit(solution)/shard_map/pallas_call | solution.py:725
  32.3 1.9 %collective-permute-start.9 = (f32[72,256]{1,0:T(8,128)S(1)}, f32[72,256]{1,0:T(8,128)S(1)}, u32[]{:S(2)}, u32[]{:S(2)}) collective-permute-start(f32[72,256]{1,0:T(8,128)S(1)} %get-tuple-element.65), channel_id=1, source_target_pairs={{0,2},{1,3},{2,0},{3,1},{4,6},{5,7},{6,4},{7,5},{8,10},{9,11},{10,... | collective-permute-start | bytes 221192 | tf_op jit(solution)/shard_map/ppermute | solution.py:566
  34.2 2.6 %collective-permute-start.18 = (f32[128,256]{1,0:T(8,128)S(1)}, f32[128,256]{1,0:T(8,128)S(1)}, u32[]{:S(2)}, u32[]{:S(2)}) collective-permute-start(f32[128,256]{1,0:T(8,128)S(1)} %shard_map.153.refs_0_), channel_id=1, source_target_pairs={{0,8},{1,9},{2,10},{3,11},{4,12},{5,13},{6,14},{7,15},{8,0},{9,1},... | collective-permute-start | bytes 393224 | tf_op jit(solution)/shard_map/ppermute | solution.py:566
  36.8 1.4 %collective-permute-done.9 = f32[72,256]{1,0:T(8,128)S(1)} collective-permute-done((f32[72,256]{1,0:T(8,128)S(1)}, f32[72,256]{1,0:T(8,128)S(1)}, u32[]{:S(2)}, u32[]{:S(2)}) %collective-permute-start.9) | collective-permute-done | bytes 73760 | tf_op jit(solution)/shard_map/ppermute | solution.py:566
  38.2 3.9 %collective-permute-start.11 = (f32[72,256]{1,0:T(8,128)S(1)}, f32[72,256]{1,0:T(8,128)S(1)}, u32[]{:S(2)}, u32[]{:S(2)}) collective-permute-start(f32[72,256]{1,0:T(8,128)S(1)} %add_add_fusion._.refs_0_), channel_id=1, source_target_pairs={{0,12},{1,13},{2,14},{3,15},{4,8},{5,9},{6,10},{7,11},{8,4},{9,5},... | collective-permute-start | bytes 221192 | tf_op jit(solution)/shard_map/ppermute | solution.py:566
  42.7 3.4 %shard_map.151 = (bf16[4096,256]{1,0:T(8,128)(2,1)}, bf16[4096,256]{1,0:T(8,128)(2,1)}, f32[8,128]{1,0:T(8,128)S(1)}) custom-call(bf16[256,4096]{1,0:T(8,128)(2,1)S(1)} %get-tuple-element.43.wt_ref, bf16[256,4096]{1,0:T(8,128)(2,1)S(1)} %get-tuple-element.62.dmt_ref, bf16[256,256]{1,0:T(8,128)(2,1)S(1)} %get-tuple-element.56.mw_ref, ...), custom_call_target="tpu_custom_call" | custom-call | flops 1073741824 | bytes 8388608 | tf_op jit(solution)/shard_map/pallas_call | solution.py:746
  46.2 1.4 %collective-permute-done.18.refs_1_ = f32[128,256]{1,0:T(8,128)S(1)} collective-permute-done((f32[128,256]{1,0:T(8,128)S(1)}, f32[128,256]{1,0:T(8,128)S(1)}, u32[]{:S(2)}, u32[]{:S(2)}) %collective-permute-start.18) | collective-permute-done | bytes 131104 | tf_op jit(solution)/shard_map/ppermute | solution.py:566
  47.6 1.9 %collective-permute-done.12.refs_2_ = f32[72,256]{1,0:T(8,128)S(1)} collective-permute-done((f32[72,256]{1,0:T(8,128)S(1)}, f32[72,256]{1,0:T(8,128)S(1)}, u32[]{:S(2)}, u32[]{:S(2)}) %collective-permute-start.12) | collective-permute-done | bytes 73760 | tf_op jit(solution)/shard_map/ppermute | solution.py:566
  50.4 1.2 %collective-permute-start.16 = (f32[72,256]{1,0:T(8,128)S(1)}, f32[72,256]{1,0:T(8,128)S(1)}, u32[]{:S(2)}, u32[]{:S(2)}) collective-permute-start(f32[72,256]{1,0:T(8,128)S(1)} %shard_map.152._.m0), channel_id=1, source_target_pairs={{0,3},{1,2},{2,1},{3,0},{4,7},{5,6},{6,5},{7,4},{8,11},{9,10},{10,... | collective-permute-start | bytes 221192 | tf_op jit(solution)/shard_map/ppermute | solution.py:566
  51.6 1.1 %shard_map.155 = (f32[256,256]{1,0:T(8,128)}, f32[3,32,32]{2,1,0:T(8,128)}, f32[8,128]{1,0:T(8,128)S(1)}) custom-call(f32[128,256]{1,0:T(8,128)S(1)} %shard_map.154.own_ref, f32[128,256]{1,0:T(8,128)S(1)} %collective-permute-done.19.other_ref, bf16[256,128]{1,0:T(8,128)(2,1)S(1)} %get-tuple-element.70.mixed_ref, ...), custom_call_target="tpu_custom_call" | custom-call | flops 67108864 | bytes 786432 | tf_op jit(solution)/shard_map/pallas_call | solution.py:765
  52.7 2.1 %collective-permute-done.15.m2 = f32[72,256]{1,0:T(8,128)S(1)} collective-permute-done((f32[72,256]{1,0:T(8,128)S(1)}, f32[72,256]{1,0:T(8,128)S(1)}, u32[]{:S(2)}, u32[]{:S(2)}) %collective-permute-start.15) | collective-permute-done | bytes 73760 | tf_op jit(solution)/shard_map/ppermute | solution.py:566
  54.8 0.7 %collective-permute-done.16.m3 = f32[72,256]{1,0:T(8,128)S(1)} collective-permute-done((f32[72,256]{1,0:T(8,128)S(1)}, f32[72,256]{1,0:T(8,128)S(1)}, u32[]{:S(2)}, u32[]{:S(2)}) %collective-permute-start.16) | collective-permute-done | bytes 73760 | tf_op jit(solution)/shard_map/ppermute | solution.py:566
  55.5 0.7 %shard_map.156 = (f32[256,256]{1,0:T(8,128)}, f32[32,32]{1,0:T(8,128)}, f32[1,32]{1,0:T(1,128)}) custom-call(f32[72,256]{1,0:T(8,128)S(1)} %shard_map.152._.m0, f32[72,256]{1,0:T(8,128)S(1)} %collective-permute-done.14.m1, f32[72,256]{1,0:T(8,128)S(1)} %collective-permute-done.15.m2, f32[72,256]{1,0:T(8,128)S(1)} %collective-permute-done.16.m3, ...), custom_call_target="tpu_custom_call" | custom-call | bytes 524288 | tf_op jit(solution)/shard_map/pallas_call | solution.py:780
  (42 shorter events, 3.5 us)
Async XLA Ops:
  1.3 15.1 %copy-start.3 = (bf16[3,32,32]{2,1,0:T(8,128)(2,1)S(1)}, bf16[3,32,32]{2,1,0:T(8,128)(2,1)}, u32[]{:S(2)}) copy-start(bf16[3,32,32]{2,1,0:T(8,128)(2,1)} %w_qkv_ref.1) | copy-start | bytes 18436
  1.3 15.1 %copy-start.4 = (bf16[32,32]{1,0:T(8,128)(2,1)S(1)}, bf16[32,32]{1,0:T(8,128)(2,1)}, u32[]{:S(2)}) copy-start(bf16[32,32]{1,0:T(8,128)(2,1)} %w_slice_ref.1) | copy-start | bytes 6148
  8.4 6.1 %collective-permute-start.6 = (f32[128,256]{1,0:T(8,128)S(1)}, f32[128,256]{1,0:T(8,128)S(1)}, u32[]{:S(2)}, u32[]{:S(2)}) collective-permute-start(f32[128,256]{1,0:T(8,128)S(1)} %get-tuple-element.61), channel_id=1, source_target_pairs={{0,1},{1,0},{2,3},{3,2},{4,5},{5,4},{6,7},{7,6},{8,9},{9,8},{10,11... | collective-permute-start | bytes 393224 | tf_op jit(solution)/shard_map/ppermute | solution.py:566
  9.0 1.2 %collective-permute-start = (f32[72,128]{1,0:T(8,128)S(1)}, f32[72,128]{1,0:T(8,128)S(1)}, u32[]{:S(2)}, u32[]{:S(2)}) collective-permute-start(f32[72,128]{1,0:T(8,128)S(1)} %get-tuple-element.48), channel_id=1, source_target_pairs={{0,1},{1,0},{2,3},{3,2},{4,5},{5,4},{6,7},{7,6},{8,9},{9,8},{10,11... | collective-permute-start | bytes 110600 | tf_op jit(solution)/shard_map/ppermute | solution.py:566
  10.2 7.3 %collective-permute-start.1 = (f32[72,128]{1,0:T(8,128)S(1)}, f32[72,128]{1,0:T(8,128)S(1)}, u32[]{:S(2)}, u32[]{:S(2)}) collective-permute-start(f32[72,128]{1,0:T(8,128)S(1)} %add.15._.refs_0_.refs_2_), channel_id=1, source_target_pairs={{0,6},{1,7},{2,4},{3,5},{4,2},{5,3},{6,0},{7,1},{8,14},{9,15},{10,... | collective-permute-start | bytes 110600 | tf_op jit(solution)/shard_map/ppermute | solution.py:566
  13.9 4.0 %collective-permute-start.2 = (f32[72,128]{1,0:T(8,128)S(1)}, f32[72,128]{1,0:T(8,128)S(1)}, u32[]{:S(2)}, u32[]{:S(2)}) collective-permute-start(f32[72,128]{1,0:T(8,128)S(1)} %add.15._.refs_0_.refs_2_), channel_id=1, source_target_pairs={{0,4},{1,5},{2,6},{3,7},{4,0},{5,1},{6,2},{7,3},{8,12},{9,13},{10,... | collective-permute-start | bytes 110600 | tf_op jit(solution)/shard_map/ppermute | solution.py:566
  14.3 4.4 %collective-permute-start.3 = (f32[72,128]{1,0:T(8,128)S(1)}, f32[72,128]{1,0:T(8,128)S(1)}, u32[]{:S(2)}, u32[]{:S(2)}) collective-permute-start(f32[72,128]{1,0:T(8,128)S(1)} %add.15._.refs_0_.refs_2_), channel_id=1, source_target_pairs={{0,2},{1,3},{2,0},{3,1},{4,6},{5,7},{6,4},{7,5},{8,10},{9,11},{10,... | collective-permute-start | bytes 110600 | tf_op jit(solution)/shard_map/ppermute | solution.py:566
  14.5 6.8 %collective-permute-start.7 = (f32[128,256]{1,0:T(8,128)S(1)}, f32[128,256]{1,0:T(8,128)S(1)}, u32[]{:S(2)}, u32[]{:S(2)}) collective-permute-start(f32[128,256]{1,0:T(8,128)S(1)} %shard_map.148.refs_0_), channel_id=1, source_target_pairs={{0,2},{1,3},{2,0},{3,1},{4,6},{5,7},{6,4},{7,5},{8,10},{9,11},{10,... | collective-permute-start | bytes 393224 | tf_op jit(solution)/shard_map/ppermute | solution.py:566
  16.4 10.8 %copy-start.2 = (bf16[32]{0:T(256)(128)(2,1)S(1)}, bf16[32]{0:T(256)(128)(2,1)}, u32[]{:S(2)}) copy-start(bf16[32]{0:T(256)(128)(2,1)} %param.15) | copy-start | bytes 196
  18.7 5.0 %collective-permute-start.4 = (f32[72,128]{1,0:T(8,128)S(1)}, f32[72,128]{1,0:T(8,128)S(1)}, u32[]{:S(2)}, u32[]{:S(2)}) collective-permute-start(f32[72,128]{1,0:T(8,128)S(1)} %shard_map.146.refs_2_), channel_id=1, source_target_pairs={{0,8},{1,9},{2,10},{3,11},{4,12},{5,13},{6,14},{7,15},{8,0},{9,1},... | collective-permute-start | bytes 110600 | tf_op jit(solution)/shard_map/ppermute | solution.py:566
  21.4 12.8 %collective-permute-start.17 = (f32[128,256]{1,0:T(8,128)S(1)}, f32[128,256]{1,0:T(8,128)S(1)}, u32[]{:S(2)}, u32[]{:S(2)}) collective-permute-start(f32[128,256]{1,0:T(8,128)S(1)} %shard_map.149._.refs_0_), channel_id=1, source_target_pairs={{0,4},{1,5},{2,6},{3,7},{4,0},{5,1},{6,2},{7,3},{8,12},{9,13},{10,... | collective-permute-start | bytes 393224 | tf_op jit(solution)/shard_map/ppermute | solution.py:566
  23.7 1.2 %collective-permute-start.5 = (f32[72,128]{1,0:T(8,128)S(1)}, f32[72,128]{1,0:T(8,128)S(1)}, u32[]{:S(2)}, u32[]{:S(2)}) collective-permute-start(f32[72,128]{1,0:T(8,128)S(1)} %add.16.own_ref), channel_id=1, source_target_pairs={{0,1},{1,0},{2,3},{3,2},{4,5},{5,4},{6,7},{7,6},{8,9},{9,8},{10,11... | collective-permute-start | bytes 110600 | tf_op jit(solution)/shard_map/ppermute | solution.py:566
  27.3 15.5 %copy-start = (bf16[256,256]{1,0:T(8,128)(2,1)S(1)}, bf16[256,256]{1,0:T(8,128)(2,1)}, u32[]{:S(2)}) copy-start(bf16[256,256]{1,0:T(8,128)(2,1)} %w_mid_ref.1) | copy-start | bytes 393220
  32.0 4.8 %collective-permute-start.10 = (f32[72,256]{1,0:T(8,128)S(1)}, f32[72,256]{1,0:T(8,128)S(1)}, u32[]{:S(2)}, u32[]{:S(2)}) collective-permute-start(f32[72,256]{1,0:T(8,128)S(1)} %get-tuple-element.66), channel_id=1, source_target_pairs={{0,3},{1,2},{2,1},{3,0},{4,7},{5,6},{6,5},{7,4},{8,11},{9,10},{10,... | collective-permute-start | bytes 221192 | tf_op jit(solution)/shard_map/ppermute | solution.py:566
  32.1 4.8 %collective-permute-start.8 = (f32[72,256]{1,0:T(8,128)S(1)}, f32[72,256]{1,0:T(8,128)S(1)}, u32[]{:S(2)}, u32[]{:S(2)}) collective-permute-start(f32[72,256]{1,0:T(8,128)S(1)} %get-tuple-element.64.refs_2_), channel_id=1, source_target_pairs={{0,1},{1,0},{2,3},{3,2},{4,5},{5,4},{6,7},{7,6},{8,9},{9,8},{10,11... | collective-permute-start | bytes 221192 | tf_op jit(solution)/shard_map/ppermute | solution.py:566
  32.3 5.9 %collective-permute-start.9 = (f32[72,256]{1,0:T(8,128)S(1)}, f32[72,256]{1,0:T(8,128)S(1)}, u32[]{:S(2)}, u32[]{:S(2)}) collective-permute-start(f32[72,256]{1,0:T(8,128)S(1)} %get-tuple-element.65), channel_id=1, source_target_pairs={{0,2},{1,3},{2,0},{3,1},{4,6},{5,7},{6,4},{7,5},{8,10},{9,11},{10,... | collective-permute-start | bytes 221192 | tf_op jit(solution)/shard_map/ppermute | solution.py:566
  34.2 13.3 %collective-permute-start.18 = (f32[128,256]{1,0:T(8,128)S(1)}, f32[128,256]{1,0:T(8,128)S(1)}, u32[]{:S(2)}, u32[]{:S(2)}) collective-permute-start(f32[128,256]{1,0:T(8,128)S(1)} %shard_map.153.refs_0_), channel_id=1, source_target_pairs={{0,8},{1,9},{2,10},{3,11},{4,12},{5,13},{6,14},{7,15},{8,0},{9,1},... | collective-permute-start | bytes 393224 | tf_op jit(solution)/shard_map/ppermute | solution.py:566
  38.2 9.4 %collective-permute-start.11 = (f32[72,256]{1,0:T(8,128)S(1)}, f32[72,256]{1,0:T(8,128)S(1)}, u32[]{:S(2)}, u32[]{:S(2)}) collective-permute-start(f32[72,256]{1,0:T(8,128)S(1)} %add_add_fusion._.refs_0_), channel_id=1, source_target_pairs={{0,12},{1,13},{2,14},{3,15},{4,8},{5,9},{6,10},{7,11},{8,4},{9,5},... | collective-permute-start | bytes 221192 | tf_op jit(solution)/shard_map/ppermute | solution.py:566
  42.1 7.5 %collective-permute-start.12 = (f32[72,256]{1,0:T(8,128)S(1)}, f32[72,256]{1,0:T(8,128)S(1)}, u32[]{:S(2)}, u32[]{:S(2)}) collective-permute-start(f32[72,256]{1,0:T(8,128)S(1)} %add_add_fusion._.refs_0_), channel_id=1, source_target_pairs={{0,8},{1,9},{2,10},{3,11},{4,12},{5,13},{6,14},{7,15},{8,0},{9,1},... | collective-permute-start | bytes 221192 | tf_op jit(solution)/shard_map/ppermute | solution.py:566
  42.1 7.5 %collective-permute-start.13 = (f32[72,256]{1,0:T(8,128)S(1)}, f32[72,256]{1,0:T(8,128)S(1)}, u32[]{:S(2)}, u32[]{:S(2)}) collective-permute-start(f32[72,256]{1,0:T(8,128)S(1)} %add_add_fusion._.refs_0_), channel_id=1, source_target_pairs={{0,4},{1,5},{2,6},{3,7},{4,0},{5,1},{6,2},{7,3},{8,12},{9,13},{10,... | collective-permute-start | bytes 221192 | tf_op jit(solution)/shard_map/ppermute | solution.py:566
  47.6 4.0 %collective-permute-start.19 = (f32[128,256]{1,0:T(8,128)S(1)}, f32[128,256]{1,0:T(8,128)S(1)}, u32[]{:S(2)}, u32[]{:S(2)}) collective-permute-start(f32[128,256]{1,0:T(8,128)S(1)} %shard_map.154.own_ref), channel_id=1, source_target_pairs={{0,1},{1,0},{2,3},{3,2},{4,5},{5,4},{6,7},{7,6},{8,9},{9,8},{10,11... | collective-permute-start | bytes 393224 | tf_op jit(solution)/shard_map/ppermute | solution.py:566
  49.6 3.1 %collective-permute-start.14 = (f32[72,256]{1,0:T(8,128)S(1)}, f32[72,256]{1,0:T(8,128)S(1)}, u32[]{:S(2)}, u32[]{:S(2)}) collective-permute-start(f32[72,256]{1,0:T(8,128)S(1)} %shard_map.152._.m0), channel_id=1, source_target_pairs={{0,1},{1,0},{2,3},{3,2},{4,5},{5,4},{6,7},{7,6},{8,9},{9,8},{10,11... | collective-permute-start | bytes 221192 | tf_op jit(solution)/shard_map/ppermute | solution.py:566
  49.7 5.1 %collective-permute-start.15 = (f32[72,256]{1,0:T(8,128)S(1)}, f32[72,256]{1,0:T(8,128)S(1)}, u32[]{:S(2)}, u32[]{:S(2)}) collective-permute-start(f32[72,256]{1,0:T(8,128)S(1)} %shard_map.152._.m0), channel_id=1, source_target_pairs={{0,2},{1,3},{2,0},{3,1},{4,6},{5,7},{6,4},{7,5},{8,10},{9,11},{10,... | collective-permute-start | bytes 221192 | tf_op jit(solution)/shard_map/ppermute | solution.py:566
  50.4 5.1 %collective-permute-start.16 = (f32[72,256]{1,0:T(8,128)S(1)}, f32[72,256]{1,0:T(8,128)S(1)}, u32[]{:S(2)}, u32[]{:S(2)}) collective-permute-start(f32[72,256]{1,0:T(8,128)S(1)} %shard_map.152._.m0), channel_id=1, source_target_pairs={{0,3},{1,2},{2,1},{3,0},{4,7},{5,6},{6,5},{7,4},{8,11},{9,10},{10,... | collective-permute-start | bytes 221192 | tf_op jit(solution)/shard_map/ppermute | solution.py:566
  (1 other events, 8.5 us)

commit v14 on v13

--- a/solution.py
+++ b/solution.py
@@ -108,7 +108,7 @@
     depth = width // heads
     hm = heads * slices
     rows = feats_ref.shape[0]
-    piece = min(4 * sub_block, rows)
+    piece = min(2 * sub_block, rows)
     count = rows // piece
     small = [
         pltpu.make_async_copy(source, target, sems.at[i])
@@ -140,7 +140,7 @@
     wc_acc[...] = jnp.zeros_like(wc_acc)
     spread_d = spread_matrix(width, depth)
     spread_m = spread_matrix(hm, slices)
-    for copy in small + large[:1]:
+    for copy in small[:2] + large[:1]:
         copy.wait()
     temp = jnp.broadcast_to(temp_ref[...].astype(f32), (16, depth)).astype(bf16)
     half = nt(spread_m, w_slice_ref[...]).astype(bf16)
@@ -187,8 +187,8 @@
         wc_acc[...] += nn(wt, cot_ref[at, :])
 
     ready = products(0)
-    large[1].wait()
-    large[2].wait()
+    for copy in small[2:] + large[1:]:
+        copy.wait()
     for i in range(count):
         current = ready
         if i + 1 < count:

time: 56.5 us -> 56 us (level)
  transfers between devices with their start and end apart: 20 -> 20, of which waited for: 10 -> 10; matrix products, arithmetic and copies ran while one was open for 0% -> 0% of each run, Pallas kernels for 22% -> 23%
where the time goes in v14:
time: 56 us; the launch traced here: 55.8 us
  starting transfers between devices  22.4 us (40%)
  Pallas kernels  20.1 us (36%)
  waiting for transfers between devices  11.8 us (21%)
  between operations  1.44 us (3%)
    ppermute x20, starting transfers between devices, exchange(): return lax.ppermute(x, 'node', [(i, i ^ k) for i in range(count)])  22.4 us
    ppermute x20, waiting for transfers between devices, exchange(): return lax.ppermute(x, 'node', [(i, i ^ k) for i in range(count)])  11.8 us
    pallas_call x1, Pallas kernels, shards(): pl.pallas_call(functools.partial(stats_kernel, heads, slices), in_specs=[...  6.68 us
    pallas_call x1, Pallas kernels, shards(): pl.pallas_call(functools.partial(backward_kernel, heads, slices), in_spec...  4.72 us
    pallas_call x1, Pallas kernels, shards(): pl.pallas_call(rows_kernel, grid=grid, in_specs=[whole, whole, whole, ful...  3.41 us
    pallas_call x1, Pallas kernels, shards(): pl.pallas_call(functools.partial(tokens_kernel, heads, slices), out_shape...  2.29 us
    pallas_call x1, Pallas kernels, shards(): pl.pallas_call(functools.partial(grad_out_kernel, heads, slices), in_spec...  1.14 us
  transfers between devices with their start and end apart: 20, of which 10 were waited for; matrix products, arithmetic and copies ran while one was open for 0% of the time, Pallas kernels for 23%

profile of v14, /device:TPU:0, one launch (start us, length us, event | category | flops | bytes accessed | tf_op | source)
XLA Modules:
  0.0 55.8 jit_solution(2654217868472852469)
XLA Ops:
  1.3 6.7 %shard_map.144 = (bf16[4096,256]{1,0:T(8,128)(2,1)S(1)}, bf16[256,4096]{1,0:T(8,128)(2,1)S(1)}, f32[24,4096]{1,0:T(8,128)S(1)}, bf16[272,256]{1,0:T(8,128)(2,1)S...) custom-call(s32[1]{0:T(128)S(6)} %copy.16.owned_ref, ...), custom_call_target="tpu_custom_call" | custom-call | flops 2147483648 | bytes 8388608 | tf_op jit(solution)/shard_map/pallas_call | solution.py:649
  8.6 1.1 %collective-permute-done = f32[72,128]{1,0:T(8,128)S(1)} collective-permute-done((f32[72,128]{1,0:T(8,128)S(1)}, f32[72,128]{1,0:T(8,128)S(1)}, u32[]{:S(2)}, u32[]{:S(2)}) %collective-permute-start) | collective-permute-done | bytes 36896 | tf_op jit(solution)/shard_map/ppermute | solution.py:566
  9.7 3.7 %collective-permute-start.1 = (f32[72,128]{1,0:T(8,128)S(1)}, f32[72,128]{1,0:T(8,128)S(1)}, u32[]{:S(2)}, u32[]{:S(2)}) collective-permute-start(f32[72,128]{1,0:T(8,128)S(1)} %add.15._.refs_0_.refs_2_), channel_id=1, source_target_pairs={{0,6},{1,7},{2,4},{3,5},{4,2},{5,3},{6,0},{7,1},{8,14},{9,15},{10,... | collective-permute-start | bytes 110600 | tf_op jit(solution)/shard_map/ppermute | solution.py:566
  14.1 1.9 %collective-permute-start.7 = (f32[128,256]{1,0:T(8,128)S(1)}, f32[128,256]{1,0:T(8,128)S(1)}, u32[]{:S(2)}, u32[]{:S(2)}) collective-permute-start(f32[128,256]{1,0:T(8,128)S(1)} %shard_map.148.refs_0_), channel_id=1, source_target_pairs={{0,2},{1,3},{2,0},{3,1},{4,6},{5,7},{6,4},{7,5},{8,10},{9,11},{10,... | collective-permute-start | bytes 393224 | tf_op jit(solution)/shard_map/ppermute | solution.py:566
  16.0 1.0 %shard_map.145 = (f32[256,4096]{1,0:T(8,128)S(1)}, f32[256,4096]{1,0:T(8,128)S(1)}, bf16[256,256]{1,0:T(8,128)(2,1)S(1)}, bf16[32,128]{1,0:T(8,128)(2,1)S(1)}, f32[8,128]{1,0:T(8,128)S(1)}) custom-call(bf16[4096,256]{1,0:T(8,128)(2,1)S(1)} %get-tuple-element.45.mid_ref, bf16[272,256]{1,0:T(8,128)(2,1)S(1)} %get-tuple-element.46.sw_ref, ...), custom_call_target="tpu_custom_call" | custom-call | flops 1610612736 | bytes 4096 | tf_op jit(solution)/shard_map/pallas_call | solution.py:683
  17.4 0.9 %collective-permute-done.3.refs_3_ = f32[72,128]{1,0:T(8,128)S(1)} collective-permute-done((f32[72,128]{1,0:T(8,128)S(1)}, f32[72,128]{1,0:T(8,128)S(1)}, u32[]{:S(2)}, u32[]{:S(2)}) %collective-permute-start.3) | collective-permute-done | bytes 36896 | tf_op jit(solution)/shard_map/ppermute | solution.py:566
  18.3 2.7 %collective-permute-start.4 = (f32[72,128]{1,0:T(8,128)S(1)}, f32[72,128]{1,0:T(8,128)S(1)}, u32[]{:S(2)}, u32[]{:S(2)}) collective-permute-start(f32[72,128]{1,0:T(8,128)S(1)} %shard_map.146.refs_2_), channel_id=1, source_target_pairs={{0,8},{1,9},{2,10},{3,11},{4,12},{5,13},{6,14},{7,15},{8,0},{9,1},... | collective-permute-start | bytes 110600 | tf_op jit(solution)/shard_map/ppermute | solution.py:566
  20.9 1.6 %collective-permute-start.17 = (f32[128,256]{1,0:T(8,128)S(1)}, f32[128,256]{1,0:T(8,128)S(1)}, u32[]{:S(2)}, u32[]{:S(2)}) collective-permute-start(f32[128,256]{1,0:T(8,128)S(1)} %shard_map.149._.refs_0_), channel_id=1, source_target_pairs={{0,4},{1,5},{2,6},{3,7},{4,0},{5,1},{6,2},{7,3},{8,12},{9,13},{10,... | collective-permute-start | bytes 393224 | tf_op jit(solution)/shard_map/ppermute | solution.py:566
  22.6 0.7 %collective-permute-done.4 = f32[72,128]{1,0:T(8,128)S(1)} collective-permute-done((f32[72,128]{1,0:T(8,128)S(1)}, f32[72,128]{1,0:T(8,128)S(1)}, u32[]{:S(2)}, u32[]{:S(2)}) %collective-permute-start.4) | collective-permute-done | bytes 36896 | tf_op jit(solution)/shard_map/ppermute | solution.py:566
  23.3 1.2 %collective-permute-done.5.got_ref = f32[72,128]{1,0:T(8,128)S(1)} collective-permute-done((f32[72,128]{1,0:T(8,128)S(1)}, f32[72,128]{1,0:T(8,128)S(1)}, u32[]{:S(2)}, u32[]{:S(2)}) %collective-permute-start.5) | collective-permute-done | bytes 36896 | tf_op jit(solution)/shard_map/ppermute | solution.py:566
  24.5 2.3 %shard_map.147 = (bf16[256,256]{1,0:T(8,128)(2,1)S(1)}, bf16[256,256]{1,0:T(8,128)(2,1)S(1)}, bf16[256,256]{1,0:T(8,128)(2,1)S(1)}, f32[256,128]{1,0:T(8,128)S(1...) custom-call(f32[72,128]{1,0:T(8,128)S(1)} %add.16.own_ref, ...), custom_call_target="tpu_custom_call" | custom-call | flops 50331648 | bytes 1048576 | tf_op jit(solution)/shard_map/pallas_call | solution.py:709
  26.8 4.7 %shard_map.150 = (bf16[256,4096]{1,0:T(8,128)(2,1)S(1)}, f32[72,256]{1,0:T(8,128)S(1)}, f32[72,256]{1,0:T(8,128)S(1)}, f32[72,256]{1,0:T(8,128)S(1)}, f32[72,256]{1,0:T(8,128)S(1)}) custom-call(f32[24,4096]{1,0:T(8,128)S(1)} %get-tuple-element.44.aux_ref, bf16[256,4096]{1,0:T(8,128)(2,1)S(1)} %get-tuple-element.43.wt_ref, ...), custom_call_target="tpu_custom_call" | custom-call | flops 161061280 | bytes 1048576 | tf_op jit(solution)/shard_map/pallas_call | solution.py:725
  31.9 1.9 %collective-permute-start.9 = (f32[72,256]{1,0:T(8,128)S(1)}, f32[72,256]{1,0:T(8,128)S(1)}, u32[]{:S(2)}, u32[]{:S(2)}) collective-permute-start(f32[72,256]{1,0:T(8,128)S(1)} %get-tuple-element.65), channel_id=1, source_target_pairs={{0,2},{1,3},{2,0},{3,1},{4,6},{5,7},{6,4},{7,5},{8,10},{9,11},{10,... | collective-permute-start | bytes 221192 | tf_op jit(solution)/shard_map/ppermute | solution.py:566
  33.8 2.6 %collective-permute-start.18 = (f32[128,256]{1,0:T(8,128)S(1)}, f32[128,256]{1,0:T(8,128)S(1)}, u32[]{:S(2)}, u32[]{:S(2)}) collective-permute-start(f32[128,256]{1,0:T(8,128)S(1)} %shard_map.153.refs_0_), channel_id=1, source_target_pairs={{0,8},{1,9},{2,10},{3,11},{4,12},{5,13},{6,14},{7,15},{8,0},{9,1},... | collective-permute-start | bytes 393224 | tf_op jit(solution)/shard_map/ppermute | solution.py:566
  36.4 1.4 %collective-permute-done.9 = f32[72,256]{1,0:T(8,128)S(1)} collective-permute-done((f32[72,256]{1,0:T(8,128)S(1)}, f32[72,256]{1,0:T(8,128)S(1)}, u32[]{:S(2)}, u32[]{:S(2)}) %collective-permute-start.9) | collective-permute-done | bytes 73760 | tf_op jit(solution)/shard_map/ppermute | solution.py:566
  37.8 3.9 %collective-permute-start.11 = (f32[72,256]{1,0:T(8,128)S(1)}, f32[72,256]{1,0:T(8,128)S(1)}, u32[]{:S(2)}, u32[]{:S(2)}) collective-permute-start(f32[72,256]{1,0:T(8,128)S(1)} %add_add_fusion._.refs_0_), channel_id=1, source_target_pairs={{0,12},{1,13},{2,14},{3,15},{4,8},{5,9},{6,10},{7,11},{8,4},{9,5},... | collective-permute-start | bytes 221192 | tf_op jit(solution)/shard_map/ppermute | solution.py:566
  42.3 3.4 %shard_map.151 = (bf16[4096,256]{1,0:T(8,128)(2,1)}, bf16[4096,256]{1,0:T(8,128)(2,1)}, f32[8,128]{1,0:T(8,128)S(1)}) custom-call(bf16[256,4096]{1,0:T(8,128)(2,1)S(1)} %get-tuple-element.43.wt_ref, bf16[256,4096]{1,0:T(8,128)(2,1)S(1)} %get-tuple-element.62.dmt_ref, bf16[256,256]{1,0:T(8,128)(2,1)S(1)} %get-tuple-element.56.mw_ref, ...), custom_call_target="tpu_custom_call" | custom-call | flops 1073741824 | bytes 8388608 | tf_op jit(solution)/shard_map/pallas_call | solution.py:746
  45.7 1.4 %collective-permute-done.18.refs_1_ = f32[128,256]{1,0:T(8,128)S(1)} collective-permute-done((f32[128,256]{1,0:T(8,128)S(1)}, f32[128,256]{1,0:T(8,128)S(1)}, u32[]{:S(2)}, u32[]{:S(2)}) %collective-permute-start.18) | collective-permute-done | bytes 131104 | tf_op jit(solution)/shard_map/ppermute | solution.py:566
  47.2 2.0 %collective-permute-done.12.refs_2_ = f32[72,256]{1,0:T(8,128)S(1)} collective-permute-done((f32[72,256]{1,0:T(8,128)S(1)}, f32[72,256]{1,0:T(8,128)S(1)}, u32[]{:S(2)}, u32[]{:S(2)}) %collective-permute-start.12) | collective-permute-done | bytes 73760 | tf_op jit(solution)/shard_map/ppermute | solution.py:566
  49.9 1.2 %collective-permute-start.16 = (f32[72,256]{1,0:T(8,128)S(1)}, f32[72,256]{1,0:T(8,128)S(1)}, u32[]{:S(2)}, u32[]{:S(2)}) collective-permute-start(f32[72,256]{1,0:T(8,128)S(1)} %shard_map.152._.m0), channel_id=1, source_target_pairs={{0,3},{1,2},{2,1},{3,0},{4,7},{5,6},{6,5},{7,4},{8,11},{9,10},{10,... | collective-permute-start | bytes 221192 | tf_op jit(solution)/shard_map/ppermute | solution.py:566
  51.1 1.1 %shard_map.155 = (f32[256,256]{1,0:T(8,128)}, f32[3,32,32]{2,1,0:T(8,128)}, f32[8,128]{1,0:T(8,128)S(1)}) custom-call(f32[128,256]{1,0:T(8,128)S(1)} %shard_map.154.own_ref, f32[128,256]{1,0:T(8,128)S(1)} %collective-permute-done.19.other_ref, bf16[256,128]{1,0:T(8,128)(2,1)S(1)} %get-tuple-element.70.mixed_ref, ...), custom_call_target="tpu_custom_call" | custom-call | flops 67108864 | bytes 786432 | tf_op jit(solution)/shard_map/pallas_call | solution.py:765
  52.3 2.1 %collective-permute-done.15.m2 = f32[72,256]{1,0:T(8,128)S(1)} collective-permute-done((f32[72,256]{1,0:T(8,128)S(1)}, f32[72,256]{1,0:T(8,128)S(1)}, u32[]{:S(2)}, u32[]{:S(2)}) %collective-permute-start.15) | collective-permute-done | bytes 73760 | tf_op jit(solution)/shard_map/ppermute | solution.py:566
  54.4 0.7 %collective-permute-done.16.m3 = f32[72,256]{1,0:T(8,128)S(1)} collective-permute-done((f32[72,256]{1,0:T(8,128)S(1)}, f32[72,256]{1,0:T(8,128)S(1)}, u32[]{:S(2)}, u32[]{:S(2)}) %collective-permute-start.16) | collective-permute-done | bytes 73760 | tf_op jit(solution)/shard_map/ppermute | solution.py:566
  55.1 0.7 %shard_map.156 = (f32[256,256]{1,0:T(8,128)}, f32[32,32]{1,0:T(8,128)}, f32[1,32]{1,0:T(1,128)}) custom-call(f32[72,256]{1,0:T(8,128)S(1)} %shard_map.152._.m0, f32[72,256]{1,0:T(8,128)S(1)} %collective-permute-done.14.m1, f32[72,256]{1,0:T(8,128)S(1)} %collective-permute-done.15.m2, f32[72,256]{1,0:T(8,128)S(1)} %collective-permute-done.16.m3, ...), custom_call_target="tpu_custom_call" | custom-call | bytes 524288 | tf_op jit(solution)/shard_map/pallas_call | solution.py:780
  (42 shorter events, 3.5 us)
Async XLA Ops:
  1.3 14.7 %copy-start.3 = (bf16[3,32,32]{2,1,0:T(8,128)(2,1)S(1)}, bf16[3,32,32]{2,1,0:T(8,128)(2,1)}, u32[]{:S(2)}) copy-start(bf16[3,32,32]{2,1,0:T(8,128)(2,1)} %w_qkv_ref.1) | copy-start | bytes 18436
  1.3 14.7 %copy-start.4 = (bf16[32,32]{1,0:T(8,128)(2,1)S(1)}, bf16[32,32]{1,0:T(8,128)(2,1)}, u32[]{:S(2)}) copy-start(bf16[32,32]{1,0:T(8,128)(2,1)} %w_slice_ref.1) | copy-start | bytes 6148
  8.0 6.1 %collective-permute-start.6 = (f32[128,256]{1,0:T(8,128)S(1)}, f32[128,256]{1,0:T(8,128)S(1)}, u32[]{:S(2)}, u32[]{:S(2)}) collective-permute-start(f32[128,256]{1,0:T(8,128)S(1)} %get-tuple-element.61), channel_id=1, source_target_pairs={{0,1},{1,0},{2,3},{3,2},{4,5},{5,4},{6,7},{7,6},{8,9},{9,8},{10,11... | collective-permute-start | bytes 393224 | tf_op jit(solution)/shard_map/ppermute | solution.py:566
  8.5 1.2 %collective-permute-start = (f32[72,128]{1,0:T(8,128)S(1)}, f32[72,128]{1,0:T(8,128)S(1)}, u32[]{:S(2)}, u32[]{:S(2)}) collective-permute-start(f32[72,128]{1,0:T(8,128)S(1)} %get-tuple-element.48), channel_id=1, source_target_pairs={{0,1},{1,0},{2,3},{3,2},{4,5},{5,4},{6,7},{7,6},{8,9},{9,8},{10,11... | collective-permute-start | bytes 110600 | tf_op jit(solution)/shard_map/ppermute | solution.py:566
  9.7 7.3 %collective-permute-start.1 = (f32[72,128]{1,0:T(8,128)S(1)}, f32[72,128]{1,0:T(8,128)S(1)}, u32[]{:S(2)}, u32[]{:S(2)}) collective-permute-start(f32[72,128]{1,0:T(8,128)S(1)} %add.15._.refs_0_.refs_2_), channel_id=1, source_target_pairs={{0,6},{1,7},{2,4},{3,5},{4,2},{5,3},{6,0},{7,1},{8,14},{9,15},{10,... | collective-permute-start | bytes 110600 | tf_op jit(solution)/shard_map/ppermute | solution.py:566
  13.4 4.0 %collective-permute-start.2 = (f32[72,128]{1,0:T(8,128)S(1)}, f32[72,128]{1,0:T(8,128)S(1)}, u32[]{:S(2)}, u32[]{:S(2)}) collective-permute-start(f32[72,128]{1,0:T(8,128)S(1)} %add.15._.refs_0_.refs_2_), channel_id=1, source_target_pairs={{0,4},{1,5},{2,6},{3,7},{4,0},{5,1},{6,2},{7,3},{8,12},{9,13},{10,... | collective-permute-start | bytes 110600 | tf_op jit(solution)/shard_map/ppermute | solution.py:566
  13.9 4.4 %collective-permute-start.3 = (f32[72,128]{1,0:T(8,128)S(1)}, f32[72,128]{1,0:T(8,128)S(1)}, u32[]{:S(2)}, u32[]{:S(2)}) collective-permute-start(f32[72,128]{1,0:T(8,128)S(1)} %add.15._.refs_0_.refs_2_), channel_id=1, source_target_pairs={{0,2},{1,3},{2,0},{3,1},{4,6},{5,7},{6,4},{7,5},{8,10},{9,11},{10,... | collective-permute-start | bytes 110600 | tf_op jit(solution)/shard_map/ppermute | solution.py:566
  14.1 6.8 %collective-permute-start.7 = (f32[128,256]{1,0:T(8,128)S(1)}, f32[128,256]{1,0:T(8,128)S(1)}, u32[]{:S(2)}, u32[]{:S(2)}) collective-permute-start(f32[128,256]{1,0:T(8,128)S(1)} %shard_map.148.refs_0_), channel_id=1, source_target_pairs={{0,2},{1,3},{2,0},{3,1},{4,6},{5,7},{6,4},{7,5},{8,10},{9,11},{10,... | collective-permute-start | bytes 393224 | tf_op jit(solution)/shard_map/ppermute | solution.py:566
  16.0 10.8 %copy-start.2 = (bf16[32]{0:T(256)(128)(2,1)S(1)}, bf16[32]{0:T(256)(128)(2,1)}, u32[]{:S(2)}) copy-start(bf16[32]{0:T(256)(128)(2,1)} %param.15) | copy-start | bytes 196
  18.3 5.0 %collective-permute-start.4 = (f32[72,128]{1,0:T(8,128)S(1)}, f32[72,128]{1,0:T(8,128)S(1)}, u32[]{:S(2)}, u32[]{:S(2)}) collective-permute-start(f32[72,128]{1,0:T(8,128)S(1)} %shard_map.146.refs_2_), channel_id=1, source_target_pairs={{0,8},{1,9},{2,10},{3,11},{4,12},{5,13},{6,14},{7,15},{8,0},{9,1},... | collective-permute-start | bytes 110600 | tf_op jit(solution)/shard_map/ppermute | solution.py:566
  20.9 12.8 %collective-permute-start.17 = (f32[128,256]{1,0:T(8,128)S(1)}, f32[128,256]{1,0:T(8,128)S(1)}, u32[]{:S(2)}, u32[]{:S(2)}) collective-permute-start(f32[128,256]{1,0:T(8,128)S(1)} %shard_map.149._.refs_0_), channel_id=1, source_target_pairs={{0,4},{1,5},{2,6},{3,7},{4,0},{5,1},{6,2},{7,3},{8,12},{9,13},{10,... | collective-permute-start | bytes 393224 | tf_op jit(solution)/shard_map/ppermute | solution.py:566
  23.3 1.2 %collective-permute-start.5 = (f32[72,128]{1,0:T(8,128)S(1)}, f32[72,128]{1,0:T(8,128)S(1)}, u32[]{:S(2)}, u32[]{:S(2)}) collective-permute-start(f32[72,128]{1,0:T(8,128)S(1)} %add.16.own_ref), channel_id=1, source_target_pairs={{0,1},{1,0},{2,3},{3,2},{4,5},{5,4},{6,7},{7,6},{8,9},{9,8},{10,11... | collective-permute-start | bytes 110600 | tf_op jit(solution)/shard_map/ppermute | solution.py:566
  26.8 15.5 %copy-start = (bf16[256,256]{1,0:T(8,128)(2,1)S(1)}, bf16[256,256]{1,0:T(8,128)(2,1)}, u32[]{:S(2)}) copy-start(bf16[256,256]{1,0:T(8,128)(2,1)} %w_mid_ref.1) | copy-start | bytes 393220
  31.5 4.8 %collective-permute-start.10 = (f32[72,256]{1,0:T(8,128)S(1)}, f32[72,256]{1,0:T(8,128)S(1)}, u32[]{:S(2)}, u32[]{:S(2)}) collective-permute-start(f32[72,256]{1,0:T(8,128)S(1)} %get-tuple-element.66), channel_id=1, source_target_pairs={{0,3},{1,2},{2,1},{3,0},{4,7},{5,6},{6,5},{7,4},{8,11},{9,10},{10,... | collective-permute-start | bytes 221192 | tf_op jit(solution)/shard_map/ppermute | solution.py:566
  31.6 4.8 %collective-permute-start.8 = (f32[72,256]{1,0:T(8,128)S(1)}, f32[72,256]{1,0:T(8,128)S(1)}, u32[]{:S(2)}, u32[]{:S(2)}) collective-permute-start(f32[72,256]{1,0:T(8,128)S(1)} %get-tuple-element.64.refs_2_), channel_id=1, source_target_pairs={{0,1},{1,0},{2,3},{3,2},{4,5},{5,4},{6,7},{7,6},{8,9},{9,8},{10,11... | collective-permute-start | bytes 221192 | tf_op jit(solution)/shard_map/ppermute | solution.py:566
  31.9 5.9 %collective-permute-start.9 = (f32[72,256]{1,0:T(8,128)S(1)}, f32[72,256]{1,0:T(8,128)S(1)}, u32[]{:S(2)}, u32[]{:S(2)}) collective-permute-start(f32[72,256]{1,0:T(8,128)S(1)} %get-tuple-element.65), channel_id=1, source_target_pairs={{0,2},{1,3},{2,0},{3,1},{4,6},{5,7},{6,4},{7,5},{8,10},{9,11},{10,... | collective-permute-start | bytes 221192 | tf_op jit(solution)/shard_map/ppermute | solution.py:566
  33.8 13.3 %collective-permute-start.18 = (f32[128,256]{1,0:T(8,128)S(1)}, f32[128,256]{1,0:T(8,128)S(1)}, u32[]{:S(2)}, u32[]{:S(2)}) collective-permute-start(f32[128,256]{1,0:T(8,128)S(1)} %shard_map.153.refs_0_), channel_id=1, source_target_pairs={{0,8},{1,9},{2,10},{3,11},{4,12},{5,13},{6,14},{7,15},{8,0},{9,1},... | collective-permute-start | bytes 393224 | tf_op jit(solution)/shard_map/ppermute | solution.py:566
  37.8 9.4 %collective-permute-start.11 = (f32[72,256]{1,0:T(8,128)S(1)}, f32[72,256]{1,0:T(8,128)S(1)}, u32[]{:S(2)}, u32[]{:S(2)}) collective-permute-start(f32[72,256]{1,0:T(8,128)S(1)} %add_add_fusion._.refs_0_), channel_id=1, source_target_pairs={{0,12},{1,13},{2,14},{3,15},{4,8},{5,9},{6,10},{7,11},{8,4},{9,5},... | collective-permute-start | bytes 221192 | tf_op jit(solution)/shard_map/ppermute | solution.py:566
  41.7 7.5 %collective-permute-start.12 = (f32[72,256]{1,0:T(8,128)S(1)}, f32[72,256]{1,0:T(8,128)S(1)}, u32[]{:S(2)}, u32[]{:S(2)}) collective-permute-start(f32[72,256]{1,0:T(8,128)S(1)} %add_add_fusion._.refs_0_), channel_id=1, source_target_pairs={{0,8},{1,9},{2,10},{3,11},{4,12},{5,13},{6,14},{7,15},{8,0},{9,1},... | collective-permute-start | bytes 221192 | tf_op jit(solution)/shard_map/ppermute | solution.py:566
  41.7 7.5 %collective-permute-start.13 = (f32[72,256]{1,0:T(8,128)S(1)}, f32[72,256]{1,0:T(8,128)S(1)}, u32[]{:S(2)}, u32[]{:S(2)}) collective-permute-start(f32[72,256]{1,0:T(8,128)S(1)} %add_add_fusion._.refs_0_), channel_id=1, source_target_pairs={{0,4},{1,5},{2,6},{3,7},{4,0},{5,1},{6,2},{7,3},{8,12},{9,13},{10,... | collective-permute-start | bytes 221192 | tf_op jit(solution)/shard_map/ppermute | solution.py:566
  47.1 4.0 %collective-permute-start.19 = (f32[128,256]{1,0:T(8,128)S(1)}, f32[128,256]{1,0:T(8,128)S(1)}, u32[]{:S(2)}, u32[]{:S(2)}) collective-permute-start(f32[128,256]{1,0:T(8,128)S(1)} %shard_map.154.own_ref), channel_id=1, source_target_pairs={{0,1},{1,0},{2,3},{3,2},{4,5},{5,4},{6,7},{7,6},{8,9},{9,8},{10,11... | collective-permute-start | bytes 393224 | tf_op jit(solution)/shard_map/ppermute | solution.py:566
  49.2 3.1 %collective-permute-start.14 = (f32[72,256]{1,0:T(8,128)S(1)}, f32[72,256]{1,0:T(8,128)S(1)}, u32[]{:S(2)}, u32[]{:S(2)}) collective-permute-start(f32[72,256]{1,0:T(8,128)S(1)} %shard_map.152._.m0), channel_id=1, source_target_pairs={{0,1},{1,0},{2,3},{3,2},{4,5},{5,4},{6,7},{7,6},{8,9},{9,8},{10,11... | collective-permute-start | bytes 221192 | tf_op jit(solution)/shard_map/ppermute | solution.py:566
  49.3 5.1 %collective-permute-start.15 = (f32[72,256]{1,0:T(8,128)S(1)}, f32[72,256]{1,0:T(8,128)S(1)}, u32[]{:S(2)}, u32[]{:S(2)}) collective-permute-start(f32[72,256]{1,0:T(8,128)S(1)} %shard_map.152._.m0), channel_id=1, source_target_pairs={{0,2},{1,3},{2,0},{3,1},{4,6},{5,7},{6,4},{7,5},{8,10},{9,11},{10,... | collective-permute-start | bytes 221192 | tf_op jit(solution)/shard_map/ppermute | solution.py:566
  49.9 5.1 %collective-permute-start.16 = (f32[72,256]{1,0:T(8,128)S(1)}, f32[72,256]{1,0:T(8,128)S(1)}, u32[]{:S(2)}, u32[]{:S(2)}) collective-permute-start(f32[72,256]{1,0:T(8,128)S(1)} %shard_map.152._.m0), channel_id=1, source_target_pairs={{0,3},{1,2},{2,1},{3,0},{4,7},{5,6},{6,5},{7,4},{8,11},{9,10},{10,... | collective-permute-start | bytes 221192 | tf_op jit(solution)/shard_map/ppermute | solution.py:566
  (1 other events, 8.5 us)

commit v15 on v14

--- a/solution.py
+++ b/solution.py
@@ -477,9 +477,10 @@
     rows = width // group
     more = slices // group
     for j in range(group):
-        pack[j, 0:rows, :] = grad[j * rows : (j + 1) * rows]
-        pack[j, rows : rows + more, 0:128] = extra[j * more : (j + 1) * more]
-        pack[j, rows : rows + more, 128:] = jnp.zeros((more, width - 128), f32)
+        for i in range(width // 128):
+            part = grad[j * rows : (j + 1) * rows, i * 128 : (i + 1) * 128]
+            pack[j, i * rows : (i + 1) * rows, :] = part
+        pack[j, rows * (width // 128) :, :] = extra[j * more : (j + 1) * more]
     place = group_place()
     for k, send in enumerate((send0, send1, send2, send3)):
         send[...] = pack[place ^ k]
@@ -536,11 +537,13 @@
     place = group_place()
     slices = slice_ref.shape[1]
     more = slices // group
-    rows = m0.shape[0] - more
+    rows, width = grad_mid_ref.shape[0] // group, grad_mid_ref.shape[1]
     for k, part in enumerate((m0, m1, m2, m3)):
         at = pl.ds(pl.multiple_of((place ^ k) * rows, 8), rows)
-        grad_mid_ref[at, :] = part[0:rows, :]
-        extra[pl.ds(pl.multiple_of((place ^ k) * more, 8), more), :] = part[rows:, 0:128]
+        for i in range(width // 128):
+            grad_mid_ref[at, i * 128 : (i + 1) * 128] = part[i * rows : (i + 1) * rows, :]
+        last = part[rows * (width // 128) :, :]
+        extra[pl.ds(pl.multiple_of((place ^ k) * more, 8), more), :] = last
     turned = extra[...].T
     slice_ref[...] = turned[0:depth, 0:slices]
     temp_ref[...] = extra[0:1, depth : 2 * depth]
@@ -721,7 +724,7 @@
         compiler_params=params(16, False),
         cost_estimate=cost(3 * width**3, 4 * width * width * 4, hm * hm),
     )(own, other, w_cat, w_out)
-    larger = (width // group + slices // group, width)
+    larger = (width // group * (width // 128) + slices // group, 128)
     dmt, *sends = pl.pallas_call(
         functools.partial(backward_kernel, heads, slices),
         in_specs=[whole] * 13 + [pl.BlockSpec(memory_space=pl.ANY)],

time: 56 us -> 55.5 us (level)
  no operation moved by 1% of the time
where the time goes in v15:
time: 55.5 us; the launch traced here: 55.3 us
  starting transfers between devices  22.4 us (40%)
  Pallas kernels  20.1 us (36%)
  waiting for transfers between devices  11.3 us (20%)
  between operations  1.44 us (3%)
    ppermute x20, starting transfers between devices, exchange(): return lax.ppermute(x, 'node', [(i, i ^ k) for i in range(count)])  22.4 us
    ppermute x20, waiting for transfers between devices, exchange(): return lax.ppermute(x, 'node', [(i, i ^ k) for i in range(count)])  11.3 us
    pallas_call x1, Pallas kernels, shards(): pl.pallas_call(functools.partial(stats_kernel, heads, slices), in_specs=[...  6.68 us
    pallas_call x1, Pallas kernels, shards(): pl.pallas_call(functools.partial(backward_kernel, heads, slices), in_spec...  4.71 us
    pallas_call x1, Pallas kernels, shards(): pl.pallas_call(rows_kernel, grid=grid, in_specs=[whole, whole, whole, ful...  3.41 us
    pallas_call x1, Pallas kernels, shards(): pl.pallas_call(functools.partial(tokens_kernel, heads, slices), out_shape...  2.29 us
    pallas_call x1, Pallas kernels, shards(): pl.pallas_call(functools.partial(grad_out_kernel, heads, slices), in_spec...  1.14 us
  transfers between devices with their start and end apart: 20, of which 10 were waited for; matrix products, arithmetic and copies ran while one was open for 0% of the time, Pallas kernels for 23%

profile of v15, /device:TPU:0, one launch (start us, length us, event | category | flops | bytes accessed | tf_op | source)
XLA Modules:
  0.0 55.3 jit_solution(2486090031855670711)
XLA Ops:
  1.3 6.7 %shard_map.144 = (bf16[4096,256]{1,0:T(8,128)(2,1)S(1)}, bf16[256,4096]{1,0:T(8,128)(2,1)S(1)}, f32[24,4096]{1,0:T(8,128)S(1)}, bf16[272,256]{1,0:T(8,128)(2,1)S...) custom-call(s32[1]{0:T(128)S(6)} %copy.16.owned_ref, ...), custom_call_target="tpu_custom_call" | custom-call | flops 2147483648 | bytes 8388608 | tf_op jit(solution)/shard_map/pallas_call | solution.py:652
  8.6 1.1 %collective-permute-done = f32[72,128]{1,0:T(8,128)S(1)} collective-permute-done((f32[72,128]{1,0:T(8,128)S(1)}, f32[72,128]{1,0:T(8,128)S(1)}, u32[]{:S(2)}, u32[]{:S(2)}) %collective-permute-start) | collective-permute-done | bytes 36896 | tf_op jit(solution)/shard_map/ppermute | solution.py:569
  9.7 3.7 %collective-permute-start.1 = (f32[72,128]{1,0:T(8,128)S(1)}, f32[72,128]{1,0:T(8,128)S(1)}, u32[]{:S(2)}, u32[]{:S(2)}) collective-permute-start(f32[72,128]{1,0:T(8,128)S(1)} %add.15._.refs_0_.refs_2_), channel_id=1, source_target_pairs={{0,6},{1,7},{2,4},{3,5},{4,2},{5,3},{6,0},{7,1},{8,14},{9,15},{10,... | collective-permute-start | bytes 110600 | tf_op jit(solution)/shard_map/ppermute | solution.py:569
  14.1 1.9 %collective-permute-start.7 = (f32[128,256]{1,0:T(8,128)S(1)}, f32[128,256]{1,0:T(8,128)S(1)}, u32[]{:S(2)}, u32[]{:S(2)}) collective-permute-start(f32[128,256]{1,0:T(8,128)S(1)} %shard_map.148.refs_0_), channel_id=1, source_target_pairs={{0,2},{1,3},{2,0},{3,1},{4,6},{5,7},{6,4},{7,5},{8,10},{9,11},{10,... | collective-permute-start | bytes 393224 | tf_op jit(solution)/shard_map/ppermute | solution.py:569
  16.0 1.0 %shard_map.145 = (f32[256,4096]{1,0:T(8,128)S(1)}, f32[256,4096]{1,0:T(8,128)S(1)}, bf16[256,256]{1,0:T(8,128)(2,1)S(1)}, bf16[32,128]{1,0:T(8,128)(2,1)S(1)}, f32[8,128]{1,0:T(8,128)S(1)}) custom-call(bf16[4096,256]{1,0:T(8,128)(2,1)S(1)} %get-tuple-element.45.mid_ref, bf16[272,256]{1,0:T(8,128)(2,1)S(1)} %get-tuple-element.46.sw_ref, ...), custom_call_target="tpu_custom_call" | custom-call | flops 1610612736 | bytes 4096 | tf_op jit(solution)/shard_map/pallas_call | solution.py:686
  17.4 0.9 %collective-permute-done.3.refs_3_ = f32[72,128]{1,0:T(8,128)S(1)} collective-permute-done((f32[72,128]{1,0:T(8,128)S(1)}, f32[72,128]{1,0:T(8,128)S(1)}, u32[]{:S(2)}, u32[]{:S(2)}) %collective-permute-start.3) | collective-permute-done | bytes 36896 | tf_op jit(solution)/shard_map/ppermute | solution.py:569
  18.3 2.7 %collective-permute-start.4 = (f32[72,128]{1,0:T(8,128)S(1)}, f32[72,128]{1,0:T(8,128)S(1)}, u32[]{:S(2)}, u32[]{:S(2)}) collective-permute-start(f32[72,128]{1,0:T(8,128)S(1)} %shard_map.146.refs_2_), channel_id=1, source_target_pairs={{0,8},{1,9},{2,10},{3,11},{4,12},{5,13},{6,14},{7,15},{8,0},{9,1},... | collective-permute-start | bytes 110600 | tf_op jit(solution)/shard_map/ppermute | solution.py:569
  20.9 1.6 %collective-permute-start.17 = (f32[128,256]{1,0:T(8,128)S(1)}, f32[128,256]{1,0:T(8,128)S(1)}, u32[]{:S(2)}, u32[]{:S(2)}) collective-permute-start(f32[128,256]{1,0:T(8,128)S(1)} %shard_map.149._.refs_0_), channel_id=1, source_target_pairs={{0,4},{1,5},{2,6},{3,7},{4,0},{5,1},{6,2},{7,3},{8,12},{9,13},{10,... | collective-permute-start | bytes 393224 | tf_op jit(solution)/shard_map/ppermute | solution.py:569
  22.6 0.7 %collective-permute-done.4 = f32[72,128]{1,0:T(8,128)S(1)} collective-permute-done((f32[72,128]{1,0:T(8,128)S(1)}, f32[72,128]{1,0:T(8,128)S(1)}, u32[]{:S(2)}, u32[]{:S(2)}) %collective-permute-start.4) | collective-permute-done | bytes 36896 | tf_op jit(solution)/shard_map/ppermute | solution.py:569
  23.3 1.2 %collective-permute-done.5.got_ref = f32[72,128]{1,0:T(8,128)S(1)} collective-permute-done((f32[72,128]{1,0:T(8,128)S(1)}, f32[72,128]{1,0:T(8,128)S(1)}, u32[]{:S(2)}, u32[]{:S(2)}) %collective-permute-start.5) | collective-permute-done | bytes 36896 | tf_op jit(solution)/shard_map/ppermute | solution.py:569
  24.5 2.3 %shard_map.147 = (bf16[256,256]{1,0:T(8,128)(2,1)S(1)}, bf16[256,256]{1,0:T(8,128)(2,1)S(1)}, bf16[256,256]{1,0:T(8,128)(2,1)S(1)}, f32[256,128]{1,0:T(8,128)S(1...) custom-call(f32[72,128]{1,0:T(8,128)S(1)} %add.16.own_ref, ...), custom_call_target="tpu_custom_call" | custom-call | flops 50331648 | bytes 1048576 | tf_op jit(solution)/shard_map/pallas_call | solution.py:712
  26.8 4.7 %shard_map.150 = (bf16[256,4096]{1,0:T(8,128)(2,1)S(1)}, f32[136,128]{1,0:T(8,128)S(1)}, f32[136,128]{1,0:T(8,128)S(1)}, f32[136,128]{1,0:T(8,128)S(1)}, f32[136,128]{1,0:T(8,128)S(1)}) custom-call(f32[24,4096]{1,0:T(8,128)S(1)} %get-tuple-element.44.aux_ref, bf16[256,4096]{1,0:T(8,128)(2,1)S(1)} %get-tuple-element.43.wt_ref, ...), custom_call_target="tpu_custom_call" | custom-call | flops 161061280 | bytes 1048576 | tf_op jit(solution)/shard_map/pallas_call | solution.py:728
  31.9 1.9 %collective-permute-start.9 = (f32[136,128]{1,0:T(8,128)S(1)}, f32[136,128]{1,0:T(8,128)S(1)}, u32[]{:S(2)}, u32[]{:S(2)}) collective-permute-start(f32[136,128]{1,0:T(8,128)S(1)} %get-tuple-element.65), channel_id=1, source_target_pairs={{0,2},{1,3},{2,0},{3,1},{4,6},{5,7},{6,4},{7,5},{8,10},{9,11},{10,... | collective-permute-start | bytes 208904 | tf_op jit(solution)/shard_map/ppermute | solution.py:569
  33.8 2.6 %collective-permute-start.18 = (f32[128,256]{1,0:T(8,128)S(1)}, f32[128,256]{1,0:T(8,128)S(1)}, u32[]{:S(2)}, u32[]{:S(2)}) collective-permute-start(f32[128,256]{1,0:T(8,128)S(1)} %shard_map.153.refs_0_), channel_id=1, source_target_pairs={{0,8},{1,9},{2,10},{3,11},{4,12},{5,13},{6,14},{7,15},{8,0},{9,1},... | collective-permute-start | bytes 393224 | tf_op jit(solution)/shard_map/ppermute | solution.py:569
  36.4 1.2 %collective-permute-done.9 = f32[136,128]{1,0:T(8,128)S(1)} collective-permute-done((f32[136,128]{1,0:T(8,128)S(1)}, f32[136,128]{1,0:T(8,128)S(1)}, u32[]{:S(2)}, u32[]{:S(2)}) %collective-permute-start.9) | collective-permute-done | bytes 69664 | tf_op jit(solution)/shard_map/ppermute | solution.py:569
  37.6 3.9 %collective-permute-start.11 = (f32[136,128]{1,0:T(8,128)S(1)}, f32[136,128]{1,0:T(8,128)S(1)}, u32[]{:S(2)}, u32[]{:S(2)}) collective-permute-start(f32[136,128]{1,0:T(8,128)S(1)} %add_add_fusion._.refs_0_), channel_id=1, source_target_pairs={{0,12},{1,13},{2,14},{3,15},{4,8},{5,9},{6,10},{7,11},{8,4},{9,5},... | collective-permute-start | bytes 208904 | tf_op jit(solution)/shard_map/ppermute | solution.py:569
  42.1 3.4 %shard_map.151 = (bf16[4096,256]{1,0:T(8,128)(2,1)}, bf16[4096,256]{1,0:T(8,128)(2,1)}, f32[8,128]{1,0:T(8,128)S(1)}) custom-call(bf16[256,4096]{1,0:T(8,128)(2,1)S(1)} %get-tuple-element.43.wt_ref, bf16[256,4096]{1,0:T(8,128)(2,1)S(1)} %get-tuple-element.62.dmt_ref, bf16[256,256]{1,0:T(8,128)(2,1)S(1)} %get-tuple-element.56.mw_ref, ...), custom_call_target="tpu_custom_call" | custom-call | flops 1073741824 | bytes 8388608 | tf_op jit(solution)/shard_map/pallas_call | solution.py:749
  45.5 1.4 %collective-permute-done.18.refs_1_ = f32[128,256]{1,0:T(8,128)S(1)} collective-permute-done((f32[128,256]{1,0:T(8,128)S(1)}, f32[128,256]{1,0:T(8,128)S(1)}, u32[]{:S(2)}, u32[]{:S(2)}) %collective-permute-start.18) | collective-permute-done | bytes 131104 | tf_op jit(solution)/shard_map/ppermute | solution.py:569
  47.0 1.8 %collective-permute-done.12.refs_2_ = f32[136,128]{1,0:T(8,128)S(1)} collective-permute-done((f32[136,128]{1,0:T(8,128)S(1)}, f32[136,128]{1,0:T(8,128)S(1)}, u32[]{:S(2)}, u32[]{:S(2)}) %collective-permute-start.12) | collective-permute-done | bytes 69664 | tf_op jit(solution)/shard_map/ppermute | solution.py:569
  48.9 0.7 %collective-permute-start.15 = (f32[136,128]{1,0:T(8,128)S(1)}, f32[136,128]{1,0:T(8,128)S(1)}, u32[]{:S(2)}, u32[]{:S(2)}) collective-permute-start(f32[136,128]{1,0:T(8,128)S(1)} %shard_map.152._.m0), channel_id=1, source_target_pairs={{0,2},{1,3},{2,0},{3,1},{4,6},{5,7},{6,4},{7,5},{8,10},{9,11},{10,... | collective-permute-start | bytes 208904 | tf_op jit(solution)/shard_map/ppermute | solution.py:569
  49.6 1.2 %collective-permute-start.16 = (f32[136,128]{1,0:T(8,128)S(1)}, f32[136,128]{1,0:T(8,128)S(1)}, u32[]{:S(2)}, u32[]{:S(2)}) collective-permute-start(f32[136,128]{1,0:T(8,128)S(1)} %shard_map.152._.m0), channel_id=1, source_target_pairs={{0,3},{1,2},{2,1},{3,0},{4,7},{5,6},{6,5},{7,4},{8,11},{9,10},{10,... | collective-permute-start | bytes 208904 | tf_op jit(solution)/shard_map/ppermute | solution.py:569
  50.8 1.1 %shard_map.155 = (f32[256,256]{1,0:T(8,128)}, f32[3,32,32]{2,1,0:T(8,128)}, f32[8,128]{1,0:T(8,128)S(1)}) custom-call(f32[128,256]{1,0:T(8,128)S(1)} %shard_map.154.own_ref, f32[128,256]{1,0:T(8,128)S(1)} %collective-permute-done.19.other_ref, bf16[256,128]{1,0:T(8,128)(2,1)S(1)} %get-tuple-element.70.mixed_ref, ...), custom_call_target="tpu_custom_call" | custom-call | flops 67108864 | bytes 786432 | tf_op jit(solution)/shard_map/pallas_call | solution.py:768
  51.9 2.0 %collective-permute-done.15.m2 = f32[136,128]{1,0:T(8,128)S(1)} collective-permute-done((f32[136,128]{1,0:T(8,128)S(1)}, f32[136,128]{1,0:T(8,128)S(1)}, u32[]{:S(2)}, u32[]{:S(2)}) %collective-permute-start.15) | collective-permute-done | bytes 69664 | tf_op jit(solution)/shard_map/ppermute | solution.py:569
  54.5 0.7 %shard_map.156 = (f32[256,256]{1,0:T(8,128)}, f32[32,32]{1,0:T(8,128)}, f32[1,32]{1,0:T(1,128)}) custom-call(f32[136,128]{1,0:T(8,128)S(1)} %shard_map.152._.m0, f32[136,128]{1,0:T(8,128)S(1)} %collective-permute-done.14.m1, f32[136,128]{1,0:T(8,128)S(1)} %collective-permute-done.15.m2, f32[136,128]{1,0:T(8,128)S(1)} %collective-permute-done.16.m3, ...), custom_call_target="tpu_custom_call" | custom-call | bytes 524288 | tf_op jit(solution)/shard_map/pallas_call | solution.py:783
  (42 shorter events, 3.4 us)
Async XLA Ops:
  1.3 14.7 %copy-start.3 = (bf16[3,32,32]{2,1,0:T(8,128)(2,1)S(1)}, bf16[3,32,32]{2,1,0:T(8,128)(2,1)}, u32[]{:S(2)}) copy-start(bf16[3,32,32]{2,1,0:T(8,128)(2,1)} %w_qkv_ref.1) | copy-start | bytes 18436
  1.3 14.7 %copy-start.4 = (bf16[32,32]{1,0:T(8,128)(2,1)S(1)}, bf16[32,32]{1,0:T(8,128)(2,1)}, u32[]{:S(2)}) copy-start(bf16[32,32]{1,0:T(8,128)(2,1)} %w_slice_ref.1) | copy-start | bytes 6148
  8.0 6.1 %collective-permute-start.6 = (f32[128,256]{1,0:T(8,128)S(1)}, f32[128,256]{1,0:T(8,128)S(1)}, u32[]{:S(2)}, u32[]{:S(2)}) collective-permute-start(f32[128,256]{1,0:T(8,128)S(1)} %get-tuple-element.61), channel_id=1, source_target_pairs={{0,1},{1,0},{2,3},{3,2},{4,5},{5,4},{6,7},{7,6},{8,9},{9,8},{10,11... | collective-permute-start | bytes 393224 | tf_op jit(solution)/shard_map/ppermute | solution.py:569
  8.5 1.2 %collective-permute-start = (f32[72,128]{1,0:T(8,128)S(1)}, f32[72,128]{1,0:T(8,128)S(1)}, u32[]{:S(2)}, u32[]{:S(2)}) collective-permute-start(f32[72,128]{1,0:T(8,128)S(1)} %get-tuple-element.48), channel_id=1, source_target_pairs={{0,1},{1,0},{2,3},{3,2},{4,5},{5,4},{6,7},{7,6},{8,9},{9,8},{10,11... | collective-permute-start | bytes 110600 | tf_op jit(solution)/shard_map/ppermute | solution.py:569
  9.7 7.3 %collective-permute-start.1 = (f32[72,128]{1,0:T(8,128)S(1)}, f32[72,128]{1,0:T(8,128)S(1)}, u32[]{:S(2)}, u32[]{:S(2)}) collective-permute-start(f32[72,128]{1,0:T(8,128)S(1)} %add.15._.refs_0_.refs_2_), channel_id=1, source_target_pairs={{0,6},{1,7},{2,4},{3,5},{4,2},{5,3},{6,0},{7,1},{8,14},{9,15},{10,... | collective-permute-start | bytes 110600 | tf_op jit(solution)/shard_map/ppermute | solution.py:569
  13.4 4.0 %collective-permute-start.2 = (f32[72,128]{1,0:T(8,128)S(1)}, f32[72,128]{1,0:T(8,128)S(1)}, u32[]{:S(2)}, u32[]{:S(2)}) collective-permute-start(f32[72,128]{1,0:T(8,128)S(1)} %add.15._.refs_0_.refs_2_), channel_id=1, source_target_pairs={{0,4},{1,5},{2,6},{3,7},{4,0},{5,1},{6,2},{7,3},{8,12},{9,13},{10,... | collective-permute-start | bytes 110600 | tf_op jit(solution)/shard_map/ppermute | solution.py:569
  13.9 4.4 %collective-permute-start.3 = (f32[72,128]{1,0:T(8,128)S(1)}, f32[72,128]{1,0:T(8,128)S(1)}, u32[]{:S(2)}, u32[]{:S(2)}) collective-permute-start(f32[72,128]{1,0:T(8,128)S(1)} %add.15._.refs_0_.refs_2_), channel_id=1, source_target_pairs={{0,2},{1,3},{2,0},{3,1},{4,6},{5,7},{6,4},{7,5},{8,10},{9,11},{10,... | collective-permute-start | bytes 110600 | tf_op jit(solution)/shard_map/ppermute | solution.py:569
  14.1 6.8 %collective-permute-start.7 = (f32[128,256]{1,0:T(8,128)S(1)}, f32[128,256]{1,0:T(8,128)S(1)}, u32[]{:S(2)}, u32[]{:S(2)}) collective-permute-start(f32[128,256]{1,0:T(8,128)S(1)} %shard_map.148.refs_0_), channel_id=1, source_target_pairs={{0,2},{1,3},{2,0},{3,1},{4,6},{5,7},{6,4},{7,5},{8,10},{9,11},{10,... | collective-permute-start | bytes 393224 | tf_op jit(solution)/shard_map/ppermute | solution.py:569
  16.0 10.8 %copy-start.2 = (bf16[32]{0:T(256)(128)(2,1)S(1)}, bf16[32]{0:T(256)(128)(2,1)}, u32[]{:S(2)}) copy-start(bf16[32]{0:T(256)(128)(2,1)} %param.15) | copy-start | bytes 196
  18.3 5.0 %collective-permute-start.4 = (f32[72,128]{1,0:T(8,128)S(1)}, f32[72,128]{1,0:T(8,128)S(1)}, u32[]{:S(2)}, u32[]{:S(2)}) collective-permute-start(f32[72,128]{1,0:T(8,128)S(1)} %shard_map.146.refs_2_), channel_id=1, source_target_pairs={{0,8},{1,9},{2,10},{3,11},{4,12},{5,13},{6,14},{7,15},{8,0},{9,1},... | collective-permute-start | bytes 110600 | tf_op jit(solution)/shard_map/ppermute | solution.py:569
  20.9 12.8 %collective-permute-start.17 = (f32[128,256]{1,0:T(8,128)S(1)}, f32[128,256]{1,0:T(8,128)S(1)}, u32[]{:S(2)}, u32[]{:S(2)}) collective-permute-start(f32[128,256]{1,0:T(8,128)S(1)} %shard_map.149._.refs_0_), channel_id=1, source_target_pairs={{0,4},{1,5},{2,6},{3,7},{4,0},{5,1},{6,2},{7,3},{8,12},{9,13},{10,... | collective-permute-start | bytes 393224 | tf_op jit(solution)/shard_map/ppermute | solution.py:569
  23.3 1.2 %collective-permute-start.5 = (f32[72,128]{1,0:T(8,128)S(1)}, f32[72,128]{1,0:T(8,128)S(1)}, u32[]{:S(2)}, u32[]{:S(2)}) collective-permute-start(f32[72,128]{1,0:T(8,128)S(1)} %add.16.own_ref), channel_id=1, source_target_pairs={{0,1},{1,0},{2,3},{3,2},{4,5},{5,4},{6,7},{7,6},{8,9},{9,8},{10,11... | collective-permute-start | bytes 110600 | tf_op jit(solution)/shard_map/ppermute | solution.py:569
  26.8 15.3 %copy-start = (bf16[256,256]{1,0:T(8,128)(2,1)S(1)}, bf16[256,256]{1,0:T(8,128)(2,1)}, u32[]{:S(2)}) copy-start(bf16[256,256]{1,0:T(8,128)(2,1)} %w_mid_ref.1) | copy-start | bytes 393220
  31.5 4.8 %collective-permute-start.10 = (f32[136,128]{1,0:T(8,128)S(1)}, f32[136,128]{1,0:T(8,128)S(1)}, u32[]{:S(2)}, u32[]{:S(2)}) collective-permute-start(f32[136,128]{1,0:T(8,128)S(1)} %get-tuple-element.66), channel_id=1, source_target_pairs={{0,3},{1,2},{2,1},{3,0},{4,7},{5,6},{6,5},{7,4},{8,11},{9,10},{10,... | collective-permute-start | bytes 208904 | tf_op jit(solution)/shard_map/ppermute | solution.py:569
  31.6 4.8 %collective-permute-start.8 = (f32[136,128]{1,0:T(8,128)S(1)}, f32[136,128]{1,0:T(8,128)S(1)}, u32[]{:S(2)}, u32[]{:S(2)}) collective-permute-start(f32[136,128]{1,0:T(8,128)S(1)} %get-tuple-element.64.refs_2_), channel_id=1, source_target_pairs={{0,1},{1,0},{2,3},{3,2},{4,5},{5,4},{6,7},{7,6},{8,9},{9,8},{10,11... | collective-permute-start | bytes 208904 | tf_op jit(solution)/shard_map/ppermute | solution.py:569
  31.9 5.7 %collective-permute-start.9 = (f32[136,128]{1,0:T(8,128)S(1)}, f32[136,128]{1,0:T(8,128)S(1)}, u32[]{:S(2)}, u32[]{:S(2)}) collective-permute-start(f32[136,128]{1,0:T(8,128)S(1)} %get-tuple-element.65), channel_id=1, source_target_pairs={{0,2},{1,3},{2,0},{3,1},{4,6},{5,7},{6,4},{7,5},{8,10},{9,11},{10,... | collective-permute-start | bytes 208904 | tf_op jit(solution)/shard_map/ppermute | solution.py:569
  33.8 13.1 %collective-permute-start.18 = (f32[128,256]{1,0:T(8,128)S(1)}, f32[128,256]{1,0:T(8,128)S(1)}, u32[]{:S(2)}, u32[]{:S(2)}) collective-permute-start(f32[128,256]{1,0:T(8,128)S(1)} %shard_map.153.refs_0_), channel_id=1, source_target_pairs={{0,8},{1,9},{2,10},{3,11},{4,12},{5,13},{6,14},{7,15},{8,0},{9,1},... | collective-permute-start | bytes 393224 | tf_op jit(solution)/shard_map/ppermute | solution.py:569
  37.6 9.4 %collective-permute-start.11 = (f32[136,128]{1,0:T(8,128)S(1)}, f32[136,128]{1,0:T(8,128)S(1)}, u32[]{:S(2)}, u32[]{:S(2)}) collective-permute-start(f32[136,128]{1,0:T(8,128)S(1)} %add_add_fusion._.refs_0_), channel_id=1, source_target_pairs={{0,12},{1,13},{2,14},{3,15},{4,8},{5,9},{6,10},{7,11},{8,4},{9,5},... | collective-permute-start | bytes 208904 | tf_op jit(solution)/shard_map/ppermute | solution.py:569
  41.5 7.3 %collective-permute-start.12 = (f32[136,128]{1,0:T(8,128)S(1)}, f32[136,128]{1,0:T(8,128)S(1)}, u32[]{:S(2)}, u32[]{:S(2)}) collective-permute-start(f32[136,128]{1,0:T(8,128)S(1)} %add_add_fusion._.refs_0_), channel_id=1, source_target_pairs={{0,8},{1,9},{2,10},{3,11},{4,12},{5,13},{6,14},{7,15},{8,0},{9,1},... | collective-permute-start | bytes 208904 | tf_op jit(solution)/shard_map/ppermute | solution.py:569
  41.5 7.3 %collective-permute-start.13 = (f32[136,128]{1,0:T(8,128)S(1)}, f32[136,128]{1,0:T(8,128)S(1)}, u32[]{:S(2)}, u32[]{:S(2)}) collective-permute-start(f32[136,128]{1,0:T(8,128)S(1)} %add_add_fusion._.refs_0_), channel_id=1, source_target_pairs={{0,4},{1,5},{2,6},{3,7},{4,0},{5,1},{6,2},{7,3},{8,12},{9,13},{10,... | collective-permute-start | bytes 208904 | tf_op jit(solution)/shard_map/ppermute | solution.py:569
  46.9 3.8 %collective-permute-start.19 = (f32[128,256]{1,0:T(8,128)S(1)}, f32[128,256]{1,0:T(8,128)S(1)}, u32[]{:S(2)}, u32[]{:S(2)}) collective-permute-start(f32[128,256]{1,0:T(8,128)S(1)} %shard_map.154.own_ref), channel_id=1, source_target_pairs={{0,1},{1,0},{2,3},{3,2},{4,5},{5,4},{6,7},{7,6},{8,9},{9,8},{10,11... | collective-permute-start | bytes 393224 | tf_op jit(solution)/shard_map/ppermute | solution.py:569
  48.8 3.1 %collective-permute-start.14 = (f32[136,128]{1,0:T(8,128)S(1)}, f32[136,128]{1,0:T(8,128)S(1)}, u32[]{:S(2)}, u32[]{:S(2)}) collective-permute-start(f32[136,128]{1,0:T(8,128)S(1)} %shard_map.152._.m0), channel_id=1, source_target_pairs={{0,1},{1,0},{2,3},{3,2},{4,5},{5,4},{6,7},{7,6},{8,9},{9,8},{10,11... | collective-permute-start | bytes 208904 | tf_op jit(solution)/shard_map/ppermute | solution.py:569
  48.9 5.0 %collective-permute-start.15 = (f32[136,128]{1,0:T(8,128)S(1)}, f32[136,128]{1,0:T(8,128)S(1)}, u32[]{:S(2)}, u32[]{:S(2)}) collective-permute-start(f32[136,128]{1,0:T(8,128)S(1)} %shard_map.152._.m0), channel_id=1, source_target_pairs={{0,2},{1,3},{2,0},{3,1},{4,6},{5,7},{6,4},{7,5},{8,10},{9,11},{10,... | collective-permute-start | bytes 208904 | tf_op jit(solution)/shard_map/ppermute | solution.py:569
  49.6 5.0 %collective-permute-start.16 = (f32[136,128]{1,0:T(8,128)S(1)}, f32[136,128]{1,0:T(8,128)S(1)}, u32[]{:S(2)}, u32[]{:S(2)}) collective-permute-start(f32[136,128]{1,0:T(8,128)S(1)} %shard_map.152._.m0), channel_id=1, source_target_pairs={{0,3},{1,2},{2,1},{3,0},{4,7},{5,6},{6,5},{7,4},{8,11},{9,10},{10,... | collective-permute-start | bytes 208904 | tf_op jit(solution)/shard_map/ppermute | solution.py:569
  (1 other events, 8.5 us)
